TPU v7x, 128 devices: a whole 4x4x4 slice. The times are simulated.
128 devices in a mesh: dp: 32 (over z_lo, x, y), expert: 4 (over z_hi, core).
Axes of the slice: x: 4, y: 4, z: 4 (z_hi: 2, z_lo: 2; z = z_hi * 2 + z_lo), core: 2. Of those that a mesh axis runs over, the one named last changes fastest.
Arguments:
- tokens: bfloat16 [16384, 4096], P(('dp', 'expert')), may hold values from -24 to 24
- cotangent: bfloat16 [16384, 4096], P(('dp', 'expert')), may hold values from -0.59765625 to 0.59765625
- routes: int32 [16384, 8], P(('dp', 'expert')), may hold values from 0 to 127, as said below
- route_gates: float32 [16384, 8], P(('dp', 'expert')), may hold values from 0.05 to 0.4
- gate_up: bfloat16 [4, 4096, 1536], P('expert'), may hold values from -0.09375 to 0.09375
- down_proj: bfloat16 [4, 768, 4096], P('expert'), may hold values from -0.21875 to 0.21875
Outputs:
- token_grad: bfloat16 [16384, 4096], P(('dp', 'expert'))
- gate_up_grad: bfloat16 [4, 4096, 1536], P('expert', 'dp')
- down_grad: bfloat16 [4, 768, 4096], P('expert', 'dp')
Inputs may be any that keep to these rules, and one draw needn't show every extreme that they name: A row of routes names 8 different ids. In the tokens of one device (aligned blocks of 128 rows) each expert e < 4 is named by at most 48 rows. In every draw some expert is named by exactly 48 rows in every block of one data group of 4 blocks.
All inputs are finite; a program needn't handle non-finite values.
Results may differ from a plain program's by a relative error of at most 0.006.
Values may be sent and summed in bfloat16 or wider, within the bound.
No kernel may reach another device: no remote copies, remote signals or barrier semaphores. Data moves between devices by JAX's collectives and lax.ppermute only.
A program may use at most 192 MiB of HBM per device.

v0:
```python
import jax
import jax.numpy as jnp
from jax import lax
from jax.experimental import pallas as pl
from jax.experimental.pallas import tpu as pltpu
from jax.sharding import Mesh, PartitionSpec as P

CAP = 48
BF = jnp.bfloat16
F32 = jnp.float32
MB = 1024 * 1024
AXES = ("w", "x", "y", "v", "c")
VMEM = pl.BlockSpec(memory_space=pltpu.VMEM)
SMEM = pl.BlockSpec(memory_space=pltpu.SMEM)
ANY = pl.BlockSpec(memory_space=pl.ANY)
HBM = pl.BlockSpec(memory_space=pltpu.HBM)
MARK = jax.ShapeDtypeStruct((8, 128), F32)


def swap_expert(a, k):
    return lax.ppermute(a, ("v", "c"), [(i, i ^ k) for i in range(4)])


def shift(a, axis, j):
    if j == 0:
        return a
    return lax.ppermute(a, axis, [(i, (i + j) % 4) for i in range(4)])


def swap_w(a):
    return lax.ppermute(a, "w", [(0, 1), (1, 0)])


def rows_dot(a, b):
    return lax.dot_general(a, b, (((0,), (0,)), ((), ())), preferred_element_type=F32)


def wide_dot(a, b):
    return lax.dot_general(a, b, (((1,), (1,)), ((), ())), preferred_element_type=F32)


def shape(*dims, dtype=BF):
    return jax.ShapeDtypeStruct(dims, dtype)


def aligned(i, size):
    return pl.ds(pl.multiple_of(i * size, size), size)


def call(body, ins, outs, scratch=(), flops=0, moved=0, limit=8, placed=()):
    specs = {"s": SMEM, "v": VMEM, "a": ANY}
    return pl.pallas_call(
        body,
        out_shape=[pltpu.HBM(o.shape, o.dtype) if i in placed else o for i, o in enumerate(outs)],
        in_specs=[specs[i] for i in ins],
        out_specs=[HBM if o in placed else VMEM for o in range(len(outs))],
        scratch_shapes=list(scratch),
        compiler_params=pltpu.CompilerParams(vmem_limit_bytes=limit * MB),
        cost_estimate=pl.CostEstimate(flops=flops, bytes_accessed=moved, transcendentals=0),
    )


def fetch(pairs, sems):
    copies = [pltpu.make_async_copy(s, d, sems.at[i]) for i, (s, d) in enumerate(pairs)]
    for copy in copies:
        copy.start()
    return copies


def land(pairs, sems):
    for copy in fetch(pairs, sems):
        copy.wait()


def sems(n):
    return pltpu.SemaphoreType.DMA((n,))


def pack_x(at, x0, x1, x2, x3, *outs):
    whole = outs[4]
    for k, piece in enumerate((x0, x1, x2, x3)):
        rows = slice(k * CAP, k * CAP + CAP)
        whole[rows, :] = piece[...]
        for j in range(4):
            for b in range(2):
                cols = aligned(b * 4 + lax.rem(at[1] + j, 4), 512)
                outs[j][rows, b * 512 : b * 512 + 512] = piece[:, cols]


def pack_g(g0, g1, g2, g3, hidden, *rest):
    out, mark, sem = rest[-3:]
    part, inner = g0.shape[1] // 4, hidden.shape[1]
    mark[...] = jnp.zeros_like(mark)
    pairs = []
    for i in range(4):
        for k, piece in enumerate((g0, g1, g2, g3)):
            to = out.at[i, pl.ds(k * CAP, CAP), pl.ds(0, part)]
            pairs.append((piece.at[:, pl.ds(i * part, part)], to))
        pairs.append((hidden, out.at[i, :, pl.ds(part, inner)]))
    land(pairs, sem)


def act_step(x, weights, hidden, slope, silu, buf, sem):
    inner, step = hidden.shape[1], buf.shape[2]
    n = inner // step
    cuts = [(i, h) for i in range(n) for h in range(2)]
    copies = fetch(
        [
            (weights.at[:, pl.ds(h * inner + i * step, step)], buf.at[2 * i + h])
            for i, h in cuts
        ],
        sem,
    )
    for i in range(n):
        cols = slice(i * step, i * step + step)
        copies[2 * i].wait()
        gpart = jnp.dot(x[...], buf[2 * i], preferred_element_type=F32)
        copies[2 * i + 1].wait()
        upart = jnp.dot(x[...], buf[2 * i + 1], preferred_element_type=F32)
        sig = jax.nn.sigmoid(gpart)
        soft = gpart * sig
        hidden[:, cols] = (soft * upart).astype(BF)
        slope[:, cols] = upart * (sig * (1.0 + gpart * (1.0 - sig)))
        silu[:, cols] = soft


def dh_step(g0, g1, g2, g3, slope, silu, weights, *rest):
    dact, whole, buf, sem, gsem = rest[-5:]
    n, step = buf.shape[:2]
    copies = fetch([(weights.at[pl.ds(i * step, step), :], buf.at[i]) for i in range(n)], sem)
    land([(g, whole.at[pl.ds(k * CAP, CAP), :]) for k, g in enumerate((g0, g1, g2, g3))], gsem)
    for i in range(n):
        cols = slice(i * step, i * step + step)
        copies[i].wait()
        dh = wide_dot(whole[...], buf[i])
        dact[0, :, cols] = (dh * slope[:, cols]).astype(BF)
        dact[1, :, cols] = (dh * silu[:, cols]).astype(BF)


def back_step(dact, weights, *rest):
    outs, mark, buf, sem = rest[-7:-3], *rest[-3:]
    n, step, inner = buf.shape[0], buf.shape[1], dact.shape[2]
    copies = fetch([(weights.at[pl.ds(i * step, step), :], buf.at[i]) for i in range(n)], sem)
    mark[...] = jnp.zeros_like(mark)
    for i in range(n):
        copies[i].wait()
        got = wide_dot(dact[0], buf[i, :, :inner]) + wide_dot(dact[1], buf[i, :, inner:])
        for k in range(4):
            outs[k][:, i * step : i * step + step] = got[k * CAP : k * CAP + CAP].astype(BF)


def tok_step(mask, a0, a1, a2, a3, out, mark, whole, sem):
    pieces = (a0, a1, a2, a3)
    land([(a, whole.at[pl.ds(k * CAP, CAP), :]) for k, a in enumerate(pieces)], sem)
    mark[...] = jnp.zeros_like(mark)
    out[...] = jnp.dot(mask[...], whole[...], preferred_element_type=F32).astype(BF)


def tile_step(*refs):
    xs, ds = refs[:4], refs[4:8]
    out, mark, xall, dall, buf, sem, osem = refs[-7:]
    rows = xs[0].shape[0]
    part = [pl.ds(p * rows, rows) for p in range(4)]
    inner = ds[0].shape[2]
    land(
        [(xs[p], xall.at[part[p], :]) for p in range(4)]
        + [
            (ds[p].at[h], dall.at[part[p], pl.ds(h * inner, inner)])
            for p in range(4)
            for h in range(2)
        ],
        sem,
    )
    mark[...] = jnp.zeros_like(mark)
    copies = []
    for j in range(4):
        for b in range(2):
            got = rows_dot(xall[:, b * 512 + j * 128 : b * 512 + j * 128 + 128], dall[...])
            buf[j, b * 128 : b * 128 + 128, :] = got.astype(BF)
        copies.append(pltpu.make_async_copy(buf.at[j], out.at[j], osem.at[j]))
        copies[-1].start()
    for copy in copies:
        copy.wait()


def tile_call(xs, ds, after):
    rows, part = xs[0].shape
    wide = 2 * ds[0].shape[2]
    return call(
        tile_step,
        "a" * (8 + len(after)),
        [shape(4, 256, wide), MARK],
        [
            pltpu.VMEM((4 * rows, part), BF),
            pltpu.VMEM((4 * rows, wide), BF),
            pltpu.VMEM((4, 256, wide), BF),
            sems(12),
            sems(4),
        ],
        flops=8 * rows * part * wide,
        moved=8 * rows * (part + wide),
        limit=16,
        placed=(0,),
    )(*xs, *ds, *after)


def down_step(at, both, *rest):
    outs, mark, gall, hall, total, sem = rest[-9:-5], *rest[-5:]
    rows, part, inner = both.shape[1], gall.shape[1], hall.shape[1]
    pairs = []
    for i in range(4):
        pairs.append((both.at[i, :, pl.ds(0, part)], gall.at[pl.ds(i * rows, rows), :]))
        pairs.append((both.at[i, :, pl.ds(part, inner)], hall.at[pl.ds(i * rows, rows), :]))
    land(pairs, sem)
    mark[...] = jnp.zeros_like(mark)
    for b in range(inner // 128):
        cols = slice(b * 128, b * 128 + 128)
        total[cols, :] = rows_dot(hall[:, cols], gall[...])
    for j in (1, 2, 3, 0):
        other = lax.rem(at[1] + j, 4)
        for b in range(2):
            outs[j][b * 96 : b * 96 + 96, :] = total[aligned(b * 4 + other, 96), :].astype(
                outs[j].dtype
            )


def gate_sum(at, parts, *rest):
    keep, send, g, sem = rest[-4:]
    half = keep.shape[0]
    land([(parts, g)], sem)

    def part(i):
        return sum(g[p, aligned(i, half), :].astype(F32) for p in range(4))

    send[...] = part(1 - at[0]).astype(BF)
    keep[...] = part(at[0])


def sum_step(at, own, r1, r2, r3, *rest):
    keep, send, f, g, sem = rest[-5:]
    half = keep.shape[0]
    land([(own, f), (r1, g.at[0]), (r2, g.at[1]), (r3, g.at[2])], sem)

    def part(i):
        rows = aligned(i, half)
        return f[rows, :] + sum(g[p, rows, :].astype(F32) for p in range(3))

    send[...] = part(1 - at[0]).astype(BF)
    keep[...] = part(at[0])


def sum_call(at, parts, after):
    rows, cols = parts[0].shape
    return call(
        sum_step,
        "saaaa" + "a" * len(after),
        [shape(rows // 2, cols, dtype=F32), shape(rows // 2, cols)],
        [pltpu.VMEM((rows, cols), F32), pltpu.VMEM((3, rows, cols), BF), sems(4)],
        moved=10 * rows * cols,
        limit=12,
    )(at, *parts, *after)


def shards(tokens, cotangent, routes, gates, gate_up, down_proj):
    gate_up = pltpu.with_memory_space_constraint(gate_up[0], pltpu.HBM)
    down_proj = pltpu.with_memory_space_constraint(down_proj[0], pltpu.HBM)
    w, x, y = lax.axis_index("w"), lax.axis_index("x"), lax.axis_index("y")
    me = lax.axis_index(("v", "c"))
    at = jnp.stack([w, x, y, me]).astype(jnp.int32)
    toks, width = tokens.shape
    inner = down_proj.shape[0]
    rows, part = 4 * CAP, width // 4
    experts = jnp.bitwise_xor(me, jnp.arange(4, dtype=jnp.int32))
    matches = routes[:, :, None] == experts[None, None, :]
    member = jnp.any(matches, axis=1)
    weight = jnp.sum(jnp.where(matches, gates[:, :, None], F32(0.0)), axis=1)
    position = jnp.cumsum(member.astype(jnp.int32), axis=0) - 1
    select = member[:, :, None] & (
        position[:, :, None] == jnp.arange(CAP, dtype=jnp.int32)[None, None, :]
    )
    mask = select.astype(BF).reshape(toks, rows)
    slot_gate = jnp.sum(jnp.where(select, weight[:, :, None], F32(0.0)), axis=0).reshape(rows, 1)
    send_x = rows_dot(mask, tokens).astype(BF).reshape(4, CAP, width)
    send_g = (rows_dot(mask, cotangent) * slot_gate).astype(BF).reshape(4, CAP, width)
    xs = [send_x[0]] + [swap_expert(send_x[k], k) for k in (1, 2, 3)]
    gs = [send_g[0]] + [swap_expert(send_g[k], k) for k in (1, 2, 3)]

    packed = call(
        pack_x, "svvvv", [shape(rows, part)] * 4 + [shape(rows, width)], moved=4 * rows * width
    )(at, *xs)
    xa = [shift(packed[j], "x", j) for j in range(4)]
    n = 2 * inner // 256
    hidden, slope, silu = call(
        act_step,
        "va",
        [shape(rows, inner), shape(rows, inner, dtype=F32), shape(rows, inner, dtype=F32)],
        [pltpu.VMEM((n, width, 256), BF), sems(n)],
        flops=4 * rows * width * inner,
        moved=4 * width * inner,
        limit=18,
    )(packed[4], gate_up)
    sent, sent_mark = call(
        pack_g,
        "aaaaaaa",
        [shape(4, rows, part + inner), MARK],
        [sems(20)],
        moved=4 * rows * width,
        placed=(0,),
    )(*gs, hidden, xa[1], xa[3])
    both = lax.all_to_all(sent, "y", split_axis=0, concat_axis=0, tiled=True)
    n = inner // 256
    dact = call(
        dh_step,
        "aaaavvaa",
        [shape(2, rows, inner)],
        [pltpu.VMEM((rows, width), BF), pltpu.VMEM((n, 256, width), BF), sems(n), sems(4)],
        flops=2 * rows * width * inner,
        moved=2 * width * inner,
        limit=12,
    )(*gs, slope, silu, down_proj, sent_mark)[0]
    da = [shift(dact, "x", j) for j in range(4)]
    n = width // 512
    *back, back_mark = call(
        back_step,
        "vaa",
        [shape(CAP, width)] * 4 + [MARK],
        [pltpu.VMEM((n, 512, 2 * inner), BF), sems(n)],
        flops=4 * rows * width * inner,
        moved=4 * width * inner,
        limit=18,
    )(dact, gate_up, da[1])
    *parts, mark = call(
        down_step,
        "saa",
        [shape(192, part, dtype=F32)] + [shape(192, part)] * 3 + [MARK],
        [
            pltpu.VMEM((4 * rows, part), BF),
            pltpu.VMEM((4 * rows, inner), BF),
            pltpu.VMEM((inner, part), F32),
            sems(8),
        ],
        flops=8 * rows * part * inner,
        moved=8 * rows * (part + inner),
        limit=16,
    )(at, both, back_mark)
    down = [parts[0]] + [shift(parts[j], "x", j) for j in (1, 2, 3)]
    parts, _ = tile_call(xa, da, [mark])
    gate = lax.all_to_all(parts, "y", split_axis=0, concat_axis=0, tiled=True)
    arrived = [back[0]] + [swap_expert(back[k], k) for k in (1, 2, 3)]
    token_grad, tok_mark = call(
        tok_step,
        "vaaaa",
        [shape(toks, width), MARK],
        [pltpu.VMEM((rows, width), BF), sems(4)],
        flops=2 * toks * rows * width,
        moved=2 * (rows + toks) * width,
    )(mask, *arrived)

    keep, send = sum_call(at, down, [])
    down_grad = (keep + swap_w(send).astype(F32)).astype(BF).reshape(4, 24, part)
    cols = [
        shift(lax.dynamic_index_in_dim(down_grad, (y + j) % 4, 0, False), "y", j) for j in range(4)
    ]
    turned = jnp.stack(cols[::-1] + cols[::-1])
    mine = lax.dynamic_slice_in_dim(turned, 3 - y, 4, 0)
    down_grad = jnp.concatenate([mine[i] for i in range(4)], axis=1)

    keep, send = call(
        gate_sum,
        "saa",
        [shape(128, 2 * inner, dtype=F32), shape(128, 2 * inner)],
        [pltpu.VMEM((4, 256, 2 * inner), BF), sems(1)],
        moved=16 * 256 * inner,
    )(at, gate, tok_mark)
    gate_up_grad = (keep + swap_w(send).astype(F32)).astype(BF)
    return token_grad, gate_up_grad[None], down_grad[None]


def solution(mesh):
    fine = Mesh(mesh.devices.reshape(2, 4, 4, 2, 2), AXES)
    rows, expert, dp = P(AXES, None), ("v", "c"), ("w", "x", "y")
    in_specs = (rows, rows, rows, rows, P(expert, None, None), P(expert, None, None))
    out_specs = (rows, P(expert, dp, None), P(expert, dp, None))
    return jax.shard_map(
        shards, mesh=fine, in_specs=in_specs, out_specs=out_specs, check_vma=False
    )
```

profile of v0, /device:TPU:0, one launch (start us, length us, event | category | flops | bytes accessed | tf_op | source)
XLA Modules:
  0.0 167.0 jit_solution(4627548109607029109)
XLA Ops:
  4.0 4.0 %collective-permute-start.4 = (bf16[48,4096]{1,0:T(8,128)(2,1)}, bf16[48,4096]{1,0:T(8,128)(2,1)}, u32[]{:S(2)}, u32[]{:S(2)}) collective-permute-start(bf16[48,4096]{1,0:T(8,128)(2,1)} %get-tuple-element.60), channel_id=1, source_target_pairs={{0,2},{1,3},{2,0},{3,1},{4,6},{5,7},{6,4},{7,5},{8,10},{9,11},{10,... | collective-permute-start | bytes 1179656 | tf_op jit(solution)/shard_map/ppermute | solution.py:21
  8.4 1.8 %fusion = bf16[192,4096]{1,0:T(8,128)(2,1)S(1)} fusion(pred[128,192]{1,0:T(32,128)(4,1)S(1)} %get-tuple-element.58, bf16[128,4096]{1,0:T(8,128)(2,1)} %param.7, f32[192]{0:T(256)S(1)} %mul.14), kind=kOutput, calls=%fused_computation.1 | convolution fusion | flops 202899456 | bytes 2646784 | tf_op jit(solution)/shard_map/dot_general | solution.py:35
  11.3 3.4 %collective-permute-start.1 = (bf16[48,4096]{1,0:T(8,128)(2,1)}, bf16[48,4096]{1,0:T(8,128)(2,1)S(1)}, u32[]{:S(2)}, u32[]{:S(2)}) collective-permute-start(bf16[48,4096]{1,0:T(8,128)(2,1)} %get-tuple-element.64), channel_id=1, source_target_pairs={{0,2},{1,3},{2,0},{3,1},{4,6},{5,7},{6,4},{7,5},{8,10},{9,11},{10,... | collective-permute-start | bytes 1179656 | tf_op jit(solution)/shard_map/ppermute | solution.py:21
  15.6 2.6 %collective-permute-done.4.x2 = bf16[48,4096]{1,0:T(8,128)(2,1)} collective-permute-done((bf16[48,4096]{1,0:T(8,128)(2,1)}, bf16[48,4096]{1,0:T(8,128)(2,1)}, u32[]{:S(2)}, u32[]{:S(2)}) %collective-permute-start.4) | collective-permute-done | bytes 393248 | tf_op jit(solution)/shard_map/ppermute | solution.py:21
  18.2 8.1 %collective-permute-done.5.x3 = bf16[48,4096]{1,0:T(8,128)(2,1)} collective-permute-done((bf16[48,4096]{1,0:T(8,128)(2,1)}, bf16[48,4096]{1,0:T(8,128)(2,1)}, u32[]{:S(2)}, u32[]{:S(2)}) %collective-permute-start.5) | collective-permute-done | bytes 393248 | tf_op jit(solution)/shard_map/ppermute | solution.py:21
  27.3 2.0 %shard_map.85 = (bf16[192,1024]{1,0:T(8,128)(2,1)S(1)}, bf16[192,1024]{1,0:T(8,128)(2,1)S(1)}, bf16[192,1024]{1,0:T(8,128)(2,1)}, bf16[192,1024]{1,0:T(8,128)(2,1)S(1)}, bf16[192,4096]{1,0:T(8,128)(2,1)S(1)}) custom-call(s32[4]{0:T(128)S(1)} %pad_add_fusion.at, bf16[48,4096]{1,0:T(8,128)(2,1)S(1)} %get-tuple-element.62.x0, bf16[48,4096]{1,0:T(8,128)(2,1)S(1)} %copy-done.8, ...), custom_call_target="tpu_custom_call" | custom-call | bytes 3145728 | tf_op jit(solution)/shard_map/pallas_call | solution.py:288
  33.3 7.4 %shard_map.86 = (bf16[192,768]{1,0:T(8,128)(2,1)S(1)}, f32[192,768]{1,0:T(8,128)S(1)}, f32[192,768]{1,0:T(8,128)S(1)}) custom-call(bf16[192,4096]{1,0:T(8,128)(2,1)S(1)} %get-tuple-element.30.x, bf16[4096,1536]{1,0:T(8,128)(2,1)} %bitcast.40), custom_call_target="tpu_custom_call" | custom-call | flops 2415919104 | bytes 12582912 | tf_op jit(solution)/shard_map/pallas_call | solution.py:293
  45.6 4.6 %all-to-all-start = ((bf16[4,192,1792]{2,1,0:T(8,128)(2,1)}), bf16[4,192,1792]{2,1,0:T(8,128)(2,1)}, u32[]{:S(2)}, u32[]{:S(2)}) async-start(bf16[4,192,1792]{2,1,0:T(8,128)(2,1)} %get-tuple-element.44), calls=%async_computation | async-start | bytes 5505024 | tf_op jit(solution)/shard_map/all_to_all | solution.py:310
  52.3 5.1 %shard_map.88.dact.refs_4_ = bf16[2,192,768]{2,1,0:T(8,128)(2,1)S(1)} custom-call(bf16[48,4096]{1,0:T(8,128)(2,1)S(1)} %get-tuple-element.66.g0, bf16[48,4096]{1,0:T(8,128)(2,1)S(1)} %collective-permute-done.g1, bf16[48,4096]{1,0:T(8,128)(2,1)S(1)} %collective-permute-done.1.g2, bf16[48,4096]{1,0:T(8,128)(2,1)S(1)} %collective-permute-done.2.g3, ...), custom_call_target="tpu_custom_call" | custom-call | flops 1207959552 | bytes 6291456 | tf_op jit(solution)/shard_map/pallas_call | solution.py:312
  59.0 2.7 %collective-permute-start.13 = (bf16[2,192,768]{2,1,0:T(8,128)(2,1)S(1)}, bf16[2,192,768]{2,1,0:T(8,128)(2,1)}, u32[]{:S(2)}, u32[]{:S(2)}) collective-permute-start(bf16[2,192,768]{2,1,0:T(8,128)(2,1)S(1)} %shard_map.88.dact.refs_4_), channel_id=1, source_target_pairs={{0,32},{16,48},{32,0},{48,16},{1,33},{17,49},{33,1},{49,17},{2,34}... | collective-permute-start | bytes 1769480 | tf_op jit(solution)/shard_map/ppermute | solution.py:27
  63.6 10.4 %collective-permute-done.8.rest_0_.refs_5_ = bf16[2,192,768]{2,1,0:T(8,128)(2,1)S(1)} collective-permute-done((bf16[2,192,768]{2,1,0:T(8,128)(2,1)S(1)}, bf16[2,192,768]{2,1,0:T(8,128)(2,1)S(1)}, u32[]{:S(2)}, u32[]{:S(2)}) %collective-permute-start.8) | collective-permute-done | bytes 589856 | tf_op jit(solution)/shard_map/ppermute | solution.py:27
  74.0 6.8 %shard_map.89 = (bf16[48,4096]{1,0:T(8,128)(2,1)S(1)}, bf16[48,4096]{1,0:T(8,128)(2,1)S(1)}, bf16[48,4096]{1,0:T(8,128)(2,1)S(1)}, bf16[48,4096]{1,0:T(8,128)(2,1)S(1)}, f32[8,128]{1,0:T(8,128)S(1)}) custom-call(bf16[2,192,768]{2,1,0:T(8,128)(2,1)S(1)} %shard_map.88.dact.refs_4_, bf16[4096,1536]{1,0:T(8,128)(2,1)} %bitcast.41, ...), custom_call_target="tpu_custom_call" | custom-call | flops 2415919104 | bytes 12582912 | tf_op jit(solution)/shard_map/pallas_call | solution.py:323
  82.3 1.8 %all-to-all-done.both = bf16[4,192,1792]{2,1,0:T(8,128)(2,1)} async-done(((bf16[4,192,1792]{2,1,0:T(8,128)(2,1)}), bf16[4,192,1792]{2,1,0:T(8,128)(2,1)}, u32[]{:S(2)}, u32[]{:S(2)}) %all-to-all-start) | async-done | bytes 2752544 | tf_op jit(solution)/shard_map/all_to_all | solution.py:310
  84.2 5.0 %shard_map.91 = (f32[192,1024]{1,0:T(8,128)S(1)}, bf16[192,1024]{1,0:T(8,128)(2,1)}, bf16[192,1024]{1,0:T(8,128)(2,1)}, bf16[192,1024]{1,0:T(8,128)(2,1)}, f32[8,128]{1,0:T(8,128)S(1)}) custom-call(s32[4]{0:T(128)S(1)} %pad_add_fusion.at, bf16[4,192,1792]{2,1,0:T(8,128)(2,1)} %all-to-all-done.both, f32[8,128]{1,0:T(8,128)S(1)} %get-tuple-element.45.rest_0_), custom_call_target="tpu_custom_call" | custom-call | flops 1207959552 | bytes 2752512 | tf_op jit(solution)/shard_map/pallas_call | solution.py:332
  90.8 2.7 %collective-permute-start.17 = (bf16[192,1024]{1,0:T(8,128)(2,1)}, bf16[192,1024]{1,0:T(8,128)(2,1)}, u32[]{:S(2)}, u32[]{:S(2)}) collective-permute-start(bf16[192,1024]{1,0:T(8,128)(2,1)} %get-tuple-element.53), channel_id=1, source_target_pairs={{0,32},{16,48},{32,0},{48,16},{1,33},{17,49},{33,1},{49,17},{2,34}... | collective-permute-start | bytes 1179656 | tf_op jit(solution)/shard_map/ppermute | solution.py:27
  93.5 3.6 %collective-permute-done.12.refs_2_ = bf16[192,1024]{1,0:T(8,128)(2,1)} collective-permute-done((bf16[192,1024]{1,0:T(8,128)(2,1)}, bf16[192,1024]{1,0:T(8,128)(2,1)}, u32[]{:S(2)}, u32[]{:S(2)}) %collective-permute-start.12) | collective-permute-done | bytes 393248 | tf_op jit(solution)/shard_map/ppermute | solution.py:27
  97.1 2.6 %collective-permute-start.18 = (bf16[192,1024]{1,0:T(8,128)(2,1)}, bf16[192,1024]{1,0:T(8,128)(2,1)}, u32[]{:S(2)}, u32[]{:S(2)}) collective-permute-start(bf16[192,1024]{1,0:T(8,128)(2,1)} %get-tuple-element.54), channel_id=1, source_target_pairs={{0,48},{16,0},{32,16},{48,32},{1,49},{17,1},{33,17},{49,33},{2,50}... | collective-permute-start | bytes 1179656 | tf_op jit(solution)/shard_map/ppermute | solution.py:27
  99.7 6.2 %shard_map.92 = (bf16[4,256,1536]{2,1,0:T(8,128)(2,1)}, f32[8,128]{1,0:T(8,128)}) custom-call(bf16[192,1024]{1,0:T(8,128)(2,1)S(1)} %copy-done.18, bf16[192,1024]{1,0:T(8,128)(2,1)S(1)} %copy-done.10, bf16[192,1024]{1,0:T(8,128)(2,1)} %collective-permute-done.12.refs_2_, bf16[192,1024]{1,0:T(8,128)(2,1)S(1)} %copy-done.12, ...), custom_call_target="tpu_custom_call" | custom-call | flops 2415919104 | bytes 3932160 | tf_op jit(solution)/shard_map/pallas_call | solution.py:189
  105.9 4.9 %all-to-all-start.1 = ((bf16[4,256,1536]{2,1,0:T(8,128)(2,1)}), bf16[4,256,1536]{2,1,0:T(8,128)(2,1)}, u32[]{:S(2)}, u32[]{:S(2)}) async-start(bf16[4,256,1536]{2,1,0:T(8,128)(2,1)} %get-tuple-element.47), calls=%async_computation.1 | async-start | bytes 6291456 | tf_op jit(solution)/shard_map/all_to_all | solution.py:348
  110.8 2.3 %collective-permute-done.17.r2 = bf16[192,1024]{1,0:T(8,128)(2,1)} collective-permute-done((bf16[192,1024]{1,0:T(8,128)(2,1)}, bf16[192,1024]{1,0:T(8,128)(2,1)}, u32[]{:S(2)}, u32[]{:S(2)}) %collective-permute-start.17) | collective-permute-done | bytes 393248 | tf_op jit(solution)/shard_map/ppermute | solution.py:27
  113.1 2.6 %shard_map.94 = (f32[96,1024]{1,0:T(8,128)S(1)}, bf16[96,1024]{1,0:T(8,128)(2,1)}) custom-call(s32[4]{0:T(128)S(1)} %pad_add_fusion.at, f32[192,1024]{1,0:T(8,128)S(1)} %get-tuple-element.51.own, bf16[192,1024]{1,0:T(8,128)(2,1)} %collective-permute-done.16.r1, bf16[192,1024]{1,0:T(8,128)(2,1)} %collective-permute-done.17.r2, ...), custom_call_target="tpu_custom_call" | custom-call | bytes 1966080 | tf_op jit(solution)/shard_map/pallas_call | solution.py:254
  117.0 3.6 %collective-permute-start.10 = (bf16[48,4096]{1,0:T(8,128)(2,1)}, bf16[48,4096]{1,0:T(8,128)(2,1)S(1)}, u32[]{:S(2)}, u32[]{:S(2)}) collective-permute-start(bf16[48,4096]{1,0:T(8,128)(2,1)} %copy-done.16), channel_id=1, source_target_pairs={{0,2},{1,3},{2,0},{3,1},{4,6},{5,7},{6,4},{7,5},{8,10},{9,11},{10,... | collective-permute-start | bytes 1179656 | tf_op jit(solution)/shard_map/ppermute | solution.py:21
  120.7 3.2 %collective-permute-done.19 = bf16[96,1024]{1,0:T(8,128)(2,1)} collective-permute-done((bf16[96,1024]{1,0:T(8,128)(2,1)}, bf16[96,1024]{1,0:T(8,128)(2,1)}, u32[]{:S(2)}, u32[]{:S(2)}) %collective-permute-start.19) | collective-permute-done | bytes 196640 | tf_op jit(solution)/shard_map/ppermute | solution.py:31
  125.6 3.0 %collective-permute-start.20 = (bf16[24,1024]{1,0:T(8,128)(2,1)S(1)}, bf16[24,1024]{1,0:T(8,128)(2,1)S(1)}, u32[]{:S(2)}, u32[]{:S(2)}) collective-permute-start(bf16[24,1024]{1,0:T(8,128)(2,1)S(1)} %get-tuple-element.73), channel_id=1, source_target_pairs={{0,12},{4,0},{8,4},{12,8},{1,13},{5,1},{9,5},{13,9},{2,14},{6,2},{... | collective-permute-start | bytes 147464 | tf_op jit(solution)/shard_map/ppermute | solution.py:27
  128.6 6.4 %collective-permute-done.10.a2 = bf16[48,4096]{1,0:T(8,128)(2,1)S(1)} collective-permute-done((bf16[48,4096]{1,0:T(8,128)(2,1)}, bf16[48,4096]{1,0:T(8,128)(2,1)S(1)}, u32[]{:S(2)}, u32[]{:S(2)}) %collective-permute-start.10) | collective-permute-done | bytes 393248 | tf_op jit(solution)/shard_map/ppermute | solution.py:21
  135.0 5.0 %collective-permute-done.11.a3 = bf16[48,4096]{1,0:T(8,128)(2,1)S(1)} collective-permute-done((bf16[48,4096]{1,0:T(8,128)(2,1)}, bf16[48,4096]{1,0:T(8,128)(2,1)S(1)}, u32[]{:S(2)}, u32[]{:S(2)}) %collective-permute-start.11) | collective-permute-done | bytes 393248 | tf_op jit(solution)/shard_map/ppermute | solution.py:21
  140.0 2.2 %shard_map.90 = (bf16[128,4096]{1,0:T(8,128)(2,1)}, f32[8,128]{1,0:T(8,128)S(1)}) custom-call(bf16[128,192]{1,0:T(8,128)(2,1)S(1)} %get-tuple-element.57.mask, bf16[48,4096]{1,0:T(8,128)(2,1)S(1)} %copy-done.6, bf16[48,4096]{1,0:T(8,128)(2,1)S(1)} %collective-permute-done.9.a1, bf16[48,4096]{1,0:T(8,128)(2,1)S(1)} %collective-permute-done.10.a2, ...), custom_call_target="tpu_custom_call" | custom-call | flops 201326592 | bytes 2621440 | tf_op jit(solution)/shard_map/pallas_call | solution.py:350
  142.2 2.7 %collective-permute-start.21 = (bf16[24,1024]{1,0:T(8,128)(2,1)S(1)}, bf16[24,1024]{1,0:T(8,128)(2,1)S(1)}, u32[]{:S(2)}, u32[]{:S(2)}) collective-permute-start(bf16[24,1024]{1,0:T(8,128)(2,1)S(1)} %get-tuple-element.72), channel_id=1, source_target_pairs={{0,8},{4,12},{8,0},{12,4},{1,9},{5,13},{9,1},{13,5},{2,10},{6,14},... | collective-permute-start | bytes 147464 | tf_op jit(solution)/shard_map/ppermute | solution.py:27
  145.8 2.1 %collective-permute-done.21 = bf16[24,1024]{1,0:T(8,128)(2,1)S(1)} collective-permute-done((bf16[24,1024]{1,0:T(8,128)(2,1)S(1)}, bf16[24,1024]{1,0:T(8,128)(2,1)S(1)}, u32[]{:S(2)}, u32[]{:S(2)}) %collective-permute-start.21) | collective-permute-done | bytes 49184 | tf_op jit(solution)/shard_map/ppermute | solution.py:27
  147.9 2.3 %collective-permute-done.22 = bf16[24,1024]{1,0:T(8,128)(2,1)S(1)} collective-permute-done((bf16[24,1024]{1,0:T(8,128)(2,1)S(1)}, bf16[24,1024]{1,0:T(8,128)(2,1)S(1)}, u32[]{:S(2)}, u32[]{:S(2)}) %collective-permute-start.22) | collective-permute-done | bytes 49184 | tf_op jit(solution)/shard_map/ppermute | solution.py:27
  151.9 2.8 %shard_map.93 = (f32[128,1536]{1,0:T(8,128)S(1)}, bf16[128,1536]{1,0:T(8,128)(2,1)S(1)}) custom-call(s32[4]{0:T(128)S(1)} %pad_add_fusion.at, bf16[4,256,1536]{2,1,0:T(8,128)(2,1)} %all-to-all-done.1.parts, f32[8,128]{1,0:T(8,128)S(1)} %get-tuple-element.48.rest_0_), custom_call_target="tpu_custom_call" | custom-call | bytes 3145728 | tf_op jit(solution)/shard_map/pallas_call | solution.py:368
  155.5 10.7 %collective-permute-done.15 = bf16[128,1536]{1,0:T(8,128)(2,1)S(1)} collective-permute-done((bf16[128,1536]{1,0:T(8,128)(2,1)S(1)}, bf16[128,1536]{1,0:T(8,128)(2,1)S(1)}, u32[]{:S(2)}, u32[]{:S(2)}) %collective-permute-start.15) | collective-permute-done | bytes 393248 | tf_op jit(solution)/shard_map/ppermute | solution.py:31
  (107 shorter events, 31.4 us)
Async XLA Ops:
  2.3 5.8 %copy-start.20 = (s32[128,8]{0,1:T(8,128)S(1)}, s32[128,8]{0,1:T(8,128)}, u32[]{:S(2)}) copy-start(s32[128,8]{0,1:T(8,128)} %param.8) | copy-start | bytes 12292
  4.0 10.8 %collective-permute-start.3 = (bf16[48,4096]{1,0:T(8,128)(2,1)}, bf16[48,4096]{1,0:T(8,128)(2,1)S(1)}, u32[]{:S(2)}, u32[]{:S(2)}) collective-permute-start(bf16[48,4096]{1,0:T(8,128)(2,1)} %get-tuple-element.61), channel_id=1, source_target_pairs={{0,1},{1,0},{2,3},{3,2},{4,5},{5,4},{6,7},{7,6},{8,9},{9,8},{10,11... | collective-permute-start | bytes 1179656 | tf_op jit(solution)/shard_map/ppermute | solution.py:21
  4.0 14.2 %collective-permute-start.4 = (bf16[48,4096]{1,0:T(8,128)(2,1)}, bf16[48,4096]{1,0:T(8,128)(2,1)}, u32[]{:S(2)}, u32[]{:S(2)}) collective-permute-start(bf16[48,4096]{1,0:T(8,128)(2,1)} %get-tuple-element.60), channel_id=1, source_target_pairs={{0,2},{1,3},{2,0},{3,1},{4,6},{5,7},{6,4},{7,5},{8,10},{9,11},{10,... | collective-permute-start | bytes 1179656 | tf_op jit(solution)/shard_map/ppermute | solution.py:21
  8.0 18.3 %collective-permute-start.5 = (bf16[48,4096]{1,0:T(8,128)(2,1)}, bf16[48,4096]{1,0:T(8,128)(2,1)}, u32[]{:S(2)}, u32[]{:S(2)}) collective-permute-start(bf16[48,4096]{1,0:T(8,128)(2,1)} %get-tuple-element.59), channel_id=1, source_target_pairs={{0,3},{1,2},{2,1},{3,0},{4,7},{5,6},{6,5},{7,4},{8,11},{9,10},{10,... | collective-permute-start | bytes 1179656 | tf_op jit(solution)/shard_map/ppermute | solution.py:21
  11.3 30.3 %collective-permute-start = (bf16[48,4096]{1,0:T(8,128)(2,1)}, bf16[48,4096]{1,0:T(8,128)(2,1)S(1)}, u32[]{:S(2)}, u32[]{:S(2)}) collective-permute-start(bf16[48,4096]{1,0:T(8,128)(2,1)} %get-tuple-element.65), channel_id=1, source_target_pairs={{0,1},{1,0},{2,3},{3,2},{4,5},{5,4},{6,7},{7,6},{8,9},{9,8},{10,11... | collective-permute-start | bytes 1179656 | tf_op jit(solution)/shard_map/ppermute | solution.py:21
  11.3 30.2 %collective-permute-start.1 = (bf16[48,4096]{1,0:T(8,128)(2,1)}, bf16[48,4096]{1,0:T(8,128)(2,1)S(1)}, u32[]{:S(2)}, u32[]{:S(2)}) collective-permute-start(bf16[48,4096]{1,0:T(8,128)(2,1)} %get-tuple-element.64), channel_id=1, source_target_pairs={{0,2},{1,3},{2,0},{3,1},{4,6},{5,7},{6,4},{7,5},{8,10},{9,11},{10,... | collective-permute-start | bytes 1179656 | tf_op jit(solution)/shard_map/ppermute | solution.py:21
  15.6 27.4 %collective-permute-start.2 = (bf16[48,4096]{1,0:T(8,128)(2,1)}, bf16[48,4096]{1,0:T(8,128)(2,1)S(1)}, u32[]{:S(2)}, u32[]{:S(2)}) collective-permute-start(bf16[48,4096]{1,0:T(8,128)(2,1)} %get-tuple-element.63), channel_id=1, source_target_pairs={{0,3},{1,2},{2,1},{3,0},{4,7},{5,6},{6,5},{7,4},{8,11},{9,10},{10,... | collective-permute-start | bytes 1179656 | tf_op jit(solution)/shard_map/ppermute | solution.py:21
  30.1 12.9 %collective-permute-start.6 = (bf16[192,1024]{1,0:T(8,128)(2,1)S(1)}, bf16[192,1024]{1,0:T(8,128)(2,1)S(1)}, u32[]{:S(2)}, u32[]{:S(2)}) collective-permute-start(bf16[192,1024]{1,0:T(8,128)(2,1)S(1)} %get-tuple-element.34), channel_id=1, source_target_pairs={{0,16},{16,32},{32,48},{48,0},{1,17},{17,33},{33,49},{49,1},{2,18}... | collective-permute-start | bytes 1179656 | tf_op jit(solution)/shard_map/ppermute | solution.py:27
  31.6 11.5 %collective-permute-start.7 = (bf16[192,1024]{1,0:T(8,128)(2,1)S(1)}, bf16[192,1024]{1,0:T(8,128)(2,1)S(1)}, u32[]{:S(2)}, u32[]{:S(2)}) collective-permute-start(bf16[192,1024]{1,0:T(8,128)(2,1)S(1)} %get-tuple-element.35), channel_id=1, source_target_pairs={{0,48},{16,0},{32,16},{48,32},{1,49},{17,1},{33,17},{49,33},{2,50}... | collective-permute-start | bytes 1179656 | tf_op jit(solution)/shard_map/ppermute | solution.py:27
  45.6 38.6 %all-to-all-start = ((bf16[4,192,1792]{2,1,0:T(8,128)(2,1)}), bf16[4,192,1792]{2,1,0:T(8,128)(2,1)}, u32[]{:S(2)}, u32[]{:S(2)}) async-start(bf16[4,192,1792]{2,1,0:T(8,128)(2,1)} %get-tuple-element.44), calls=%async_computation | async-start | bytes 5505024 | tf_op jit(solution)/shard_map/all_to_all | solution.py:310
  57.4 16.6 %collective-permute-start.8 = (bf16[2,192,768]{2,1,0:T(8,128)(2,1)S(1)}, bf16[2,192,768]{2,1,0:T(8,128)(2,1)S(1)}, u32[]{:S(2)}, u32[]{:S(2)}) collective-permute-start(bf16[2,192,768]{2,1,0:T(8,128)(2,1)S(1)} %shard_map.88.dact.refs_4_), channel_id=1, source_target_pairs={{0,16},{16,32},{32,48},{48,0},{1,17},{17,33},{33,49},{49,1},{2,18}... | collective-permute-start | bytes 1769480 | tf_op jit(solution)/shard_map/ppermute | solution.py:27
  59.0 40.7 %collective-permute-start.13 = (bf16[2,192,768]{2,1,0:T(8,128)(2,1)S(1)}, bf16[2,192,768]{2,1,0:T(8,128)(2,1)}, u32[]{:S(2)}, u32[]{:S(2)}) collective-permute-start(bf16[2,192,768]{2,1,0:T(8,128)(2,1)S(1)} %shard_map.88.dact.refs_4_), channel_id=1, source_target_pairs={{0,32},{16,48},{32,0},{48,16},{1,33},{17,49},{33,1},{49,17},{2,34}... | collective-permute-start | bytes 1769480 | tf_op jit(solution)/shard_map/ppermute | solution.py:27
  61.7 38.0 %collective-permute-start.14 = (bf16[2,192,768]{2,1,0:T(8,128)(2,1)S(1)}, bf16[2,192,768]{2,1,0:T(8,128)(2,1)}, u32[]{:S(2)}, u32[]{:S(2)}) collective-permute-start(bf16[2,192,768]{2,1,0:T(8,128)(2,1)S(1)} %shard_map.88.dact.refs_4_), channel_id=1, source_target_pairs={{0,48},{16,0},{32,16},{48,32},{1,49},{17,1},{33,17},{49,33},{2,50}... | collective-permute-start | bytes 1769480 | tf_op jit(solution)/shard_map/ppermute | solution.py:27
  63.1 33.9 %collective-permute-start.12 = (bf16[192,1024]{1,0:T(8,128)(2,1)}, bf16[192,1024]{1,0:T(8,128)(2,1)}, u32[]{:S(2)}, u32[]{:S(2)}) collective-permute-start(bf16[192,1024]{1,0:T(8,128)(2,1)} %get-tuple-element.43), channel_id=1, source_target_pairs={{0,32},{16,48},{32,0},{48,16},{1,33},{17,49},{33,1},{49,17},{2,34}... | collective-permute-start | bytes 1179656 | tf_op jit(solution)/shard_map/ppermute | solution.py:27
  82.3 23.5 %copy-start.5 = (bf16[48,4096]{1,0:T(8,128)(2,1)}, bf16[48,4096]{1,0:T(8,128)(2,1)S(1)}, u32[]{:S(2)}) copy-start(bf16[48,4096]{1,0:T(8,128)(2,1)S(1)} %get-tuple-element.37.a0) | copy-start | bytes 1179652
  84.2 15.5 %copy-start.10 = (bf16[192,1024]{1,0:T(8,128)(2,1)S(1)}, bf16[192,1024]{1,0:T(8,128)(2,1)}, u32[]{:S(2)}) copy-start(bf16[192,1024]{1,0:T(8,128)(2,1)} %copy-done.9) | copy-start | bytes 1179652
  84.2 15.5 %copy-start.12 = (bf16[192,1024]{1,0:T(8,128)(2,1)S(1)}, bf16[192,1024]{1,0:T(8,128)(2,1)}, u32[]{:S(2)}) copy-start(bf16[192,1024]{1,0:T(8,128)(2,1)} %copy-done.11) | copy-start | bytes 1179652
  84.2 15.5 %copy-start.18 = (bf16[192,1024]{1,0:T(8,128)(2,1)S(1)}, bf16[192,1024]{1,0:T(8,128)(2,1)}, u32[]{:S(2)}) copy-start(bf16[192,1024]{1,0:T(8,128)(2,1)} %copy-done.17) | copy-start | bytes 1179652
  89.2 21.6 %collective-permute-start.16 = (bf16[192,1024]{1,0:T(8,128)(2,1)}, bf16[192,1024]{1,0:T(8,128)(2,1)}, u32[]{:S(2)}, u32[]{:S(2)}) collective-permute-start(bf16[192,1024]{1,0:T(8,128)(2,1)} %get-tuple-element.52), channel_id=1, source_target_pairs={{0,16},{16,32},{32,48},{48,0},{1,17},{17,33},{33,49},{49,1},{2,18}... | collective-permute-start | bytes 1179656 | tf_op jit(solution)/shard_map/ppermute | solution.py:27
  90.8 22.3 %collective-permute-start.17 = (bf16[192,1024]{1,0:T(8,128)(2,1)}, bf16[192,1024]{1,0:T(8,128)(2,1)}, u32[]{:S(2)}, u32[]{:S(2)}) collective-permute-start(bf16[192,1024]{1,0:T(8,128)(2,1)} %get-tuple-element.53), channel_id=1, source_target_pairs={{0,32},{16,48},{32,0},{48,16},{1,33},{17,49},{33,1},{49,17},{2,34}... | collective-permute-start | bytes 1179656 | tf_op jit(solution)/shard_map/ppermute | solution.py:27
  97.1 16.0 %collective-permute-start.18 = (bf16[192,1024]{1,0:T(8,128)(2,1)}, bf16[192,1024]{1,0:T(8,128)(2,1)}, u32[]{:S(2)}, u32[]{:S(2)}) collective-permute-start(bf16[192,1024]{1,0:T(8,128)(2,1)} %get-tuple-element.54), channel_id=1, source_target_pairs={{0,48},{16,0},{32,16},{48,32},{1,49},{17,1},{33,17},{49,33},{2,50}... | collective-permute-start | bytes 1179656 | tf_op jit(solution)/shard_map/ppermute | solution.py:27
  105.9 14.7 %copy-start.14 = (bf16[48,4096]{1,0:T(8,128)(2,1)S(1)}, bf16[48,4096]{1,0:T(8,128)(2,1)}, u32[]{:S(2)}) copy-start(bf16[48,4096]{1,0:T(8,128)(2,1)} %copy-done.13) | copy-start | bytes 1179652
  105.9 46.0 %all-to-all-start.1 = ((bf16[4,256,1536]{2,1,0:T(8,128)(2,1)}), bf16[4,256,1536]{2,1,0:T(8,128)(2,1)}, u32[]{:S(2)}, u32[]{:S(2)}) async-start(bf16[4,256,1536]{2,1,0:T(8,128)(2,1)} %get-tuple-element.47), calls=%async_computation.1 | async-start | bytes 6291456 | tf_op jit(solution)/shard_map/all_to_all | solution.py:348
  110.8 29.2 %copy-start.6 = (bf16[48,4096]{1,0:T(8,128)(2,1)S(1)}, bf16[48,4096]{1,0:T(8,128)(2,1)}, u32[]{:S(2)}) copy-start(bf16[48,4096]{1,0:T(8,128)(2,1)} %copy-done.5) | copy-start | bytes 1179652
  115.7 8.2 %collective-permute-start.19 = (bf16[96,1024]{1,0:T(8,128)(2,1)}, bf16[96,1024]{1,0:T(8,128)(2,1)}, u32[]{:S(2)}, u32[]{:S(2)}) collective-permute-start(bf16[96,1024]{1,0:T(8,128)(2,1)} %get-tuple-element.56), channel_id=1, source_target_pairs={{0,64},{64,0},{1,65},{65,1},{2,66},{66,2},{3,67},{67,3},{4,68},{68... | collective-permute-start | bytes 589832 | tf_op jit(solution)/shard_map/ppermute | solution.py:31
  117.0 18.0 %collective-permute-start.10 = (bf16[48,4096]{1,0:T(8,128)(2,1)}, bf16[48,4096]{1,0:T(8,128)(2,1)S(1)}, u32[]{:S(2)}, u32[]{:S(2)}) collective-permute-start(bf16[48,4096]{1,0:T(8,128)(2,1)} %copy-done.16), channel_id=1, source_target_pairs={{0,2},{1,3},{2,0},{3,1},{4,6},{5,7},{6,4},{7,5},{8,10},{9,11},{10,... | collective-permute-start | bytes 1179656 | tf_op jit(solution)/shard_map/ppermute | solution.py:21
  120.6 19.5 %collective-permute-start.11 = (bf16[48,4096]{1,0:T(8,128)(2,1)}, bf16[48,4096]{1,0:T(8,128)(2,1)S(1)}, u32[]{:S(2)}, u32[]{:S(2)}) collective-permute-start(bf16[48,4096]{1,0:T(8,128)(2,1)} %copy-done.15), channel_id=1, source_target_pairs={{0,3},{1,2},{2,1},{3,0},{4,7},{5,6},{6,5},{7,4},{8,11},{9,10},{10,... | collective-permute-start | bytes 1179656 | tf_op jit(solution)/shard_map/ppermute | solution.py:21
  120.6 19.5 %collective-permute-start.9 = (bf16[48,4096]{1,0:T(8,128)(2,1)S(1)}, bf16[48,4096]{1,0:T(8,128)(2,1)S(1)}, u32[]{:S(2)}, u32[]{:S(2)}) collective-permute-start(bf16[48,4096]{1,0:T(8,128)(2,1)S(1)} %copy-done.14), channel_id=1, source_target_pairs={{0,1},{1,0},{2,3},{3,2},{4,5},{5,4},{6,7},{7,6},{8,9},{9,8},{10,11... | collective-permute-start | bytes 1179656 | tf_op jit(solution)/shard_map/ppermute | solution.py:21
  125.6 20.1 %collective-permute-start.20 = (bf16[24,1024]{1,0:T(8,128)(2,1)S(1)}, bf16[24,1024]{1,0:T(8,128)(2,1)S(1)}, u32[]{:S(2)}, u32[]{:S(2)}) collective-permute-start(bf16[24,1024]{1,0:T(8,128)(2,1)S(1)} %get-tuple-element.73), channel_id=1, source_target_pairs={{0,12},{4,0},{8,4},{12,8},{1,13},{5,1},{9,5},{13,9},{2,14},{6,2},{... | collective-permute-start | bytes 147464 | tf_op jit(solution)/shard_map/ppermute | solution.py:27
  142.2 5.7 %collective-permute-start.21 = (bf16[24,1024]{1,0:T(8,128)(2,1)S(1)}, bf16[24,1024]{1,0:T(8,128)(2,1)S(1)}, u32[]{:S(2)}, u32[]{:S(2)}) collective-permute-start(bf16[24,1024]{1,0:T(8,128)(2,1)S(1)} %get-tuple-element.72), channel_id=1, source_target_pairs={{0,8},{4,12},{8,0},{12,4},{1,9},{5,13},{9,1},{13,5},{2,10},{6,14},... | collective-permute-start | bytes 147464 | tf_op jit(solution)/shard_map/ppermute | solution.py:27
  144.9 5.3 %collective-permute-start.22 = (bf16[24,1024]{1,0:T(8,128)(2,1)S(1)}, bf16[24,1024]{1,0:T(8,128)(2,1)S(1)}, u32[]{:S(2)}, u32[]{:S(2)}) collective-permute-start(bf16[24,1024]{1,0:T(8,128)(2,1)S(1)} %get-tuple-element.71), channel_id=1, source_target_pairs={{0,4},{4,8},{8,12},{12,0},{1,5},{5,9},{9,13},{13,1},{2,6},{6,10},{... | collective-permute-start | bytes 147464 | tf_op jit(solution)/shard_map/ppermute | solution.py:27
  154.7 11.5 %collective-permute-start.15 = (bf16[128,1536]{1,0:T(8,128)(2,1)S(1)}, bf16[128,1536]{1,0:T(8,128)(2,1)S(1)}, u32[]{:S(2)}, u32[]{:S(2)}) collective-permute-start(bf16[128,1536]{1,0:T(8,128)(2,1)S(1)} %get-tuple-element.50), channel_id=1, source_target_pairs={{0,64},{64,0},{1,65},{65,1},{2,66},{66,2},{3,67},{67,3},{4,68},{68... | collective-permute-start | bytes 1179656 | tf_op jit(solution)/shard_map/ppermute | solution.py:31
  (15 other events, 23.5 us)
where the time goes:
time: 170 us; the launch traced here: 167 us
  waiting for transfers between devices  60.1 us (35%)
  starting transfers between devices  45.1 us (27%)
  Pallas kernels  41.9 us (25%)
  local copies, waits for them, and re-layouts  12.8 us (8%)
  other arithmetic  3.82 us (2%)
  matrix products  2.45 us (1%)
    ppermute x9, waiting for transfers between devices, swap_expert(): return lax.ppermute(a, ('v', 'c'), [(i, i ^ k) for i in range(4)])  23.6 us
    ppermute x12, starting transfers between devices, shift(): return lax.ppermute(a, axis, [(i, (i + j) % 4) for i in range(4)])  22.8 us
    ppermute x12, waiting for transfers between devices, shift(): return lax.ppermute(a, axis, [(i, (i + j) % 4) for i in range(4)])  20.7 us
    ppermute x2, waiting for transfers between devices, swap_w(): return lax.ppermute(a, 'w', [(0, 1), (1, 0)])  14 us
    ppermute x9, starting transfers between devices, swap_expert(): return lax.ppermute(a, ('v', 'c'), [(i, i ^ k) for i in range(4)])  11.3 us
    unnamed x51, local copies, waits for them, and re-layouts  9.27 us
    pallas_call x1, Pallas kernels, shards(): call(act_step, 'va', [shape(rows, inner), shape(rows, inner, dtype=F32),...  7.4 us
    pallas_call x1, Pallas kernels, shards(): call(back_step, 'vaa', [shape(CAP, width)] * 4 + [MARK], [pltpu.VMEM((n,...  6.8 us
  transfers between devices with their start and end apart: 25, of which 13 were waited for; matrix products, arithmetic and copies ran while one was open for 4% of the time, Pallas kernels for 22%

commit v1 on v0

--- a/solution.py
+++ b/solution.py
@@ -125,16 +125,17 @@
 
 
 def dh_step(g0, g1, g2, g3, slope, silu, weights, *rest):
-    dact, whole, buf, sem, gsem = rest[-5:]
+    dact, whole, factors, buf, sem, gsem = rest[-6:]
     n, step = buf.shape[:2]
     copies = fetch([(weights.at[pl.ds(i * step, step), :], buf.at[i]) for i in range(n)], sem)
-    land([(g, whole.at[pl.ds(k * CAP, CAP), :]) for k, g in enumerate((g0, g1, g2, g3))], gsem)
+    pieces = [(g, whole.at[pl.ds(k * CAP, CAP), :]) for k, g in enumerate((g0, g1, g2, g3))]
+    land(pieces + [(slope, factors.at[0]), (silu, factors.at[1])], gsem)
     for i in range(n):
         cols = slice(i * step, i * step + step)
         copies[i].wait()
         dh = wide_dot(whole[...], buf[i])
-        dact[0, :, cols] = (dh * slope[:, cols]).astype(BF)
-        dact[1, :, cols] = (dh * silu[:, cols]).astype(BF)
+        dact[0, :, cols] = (dh * factors[0, :, cols]).astype(BF)
+        dact[1, :, cols] = (dh * factors[1, :, cols]).astype(BF)
 
 
 def back_step(dact, weights, *rest):
@@ -149,10 +150,10 @@
             outs[k][:, i * step : i * step + step] = got[k * CAP : k * CAP + CAP].astype(BF)
 
 
-def tok_step(mask, a0, a1, a2, a3, out, mark, whole, sem):
+def tok_step(mask, a0, a1, a2, a3, *rest):
+    out, whole, sem = rest[-3:]
     pieces = (a0, a1, a2, a3)
     land([(a, whole.at[pl.ds(k * CAP, CAP), :]) for k, a in enumerate(pieces)], sem)
-    mark[...] = jnp.zeros_like(mark)
     out[...] = jnp.dot(mask[...], whole[...], preferred_element_type=F32).astype(BF)
 
 
@@ -173,12 +174,13 @@
     )
     mark[...] = jnp.zeros_like(mark)
     copies = []
-    for j in range(4):
-        for b in range(2):
-            got = rows_dot(xall[:, b * 512 + j * 128 : b * 512 + j * 128 + 128], dall[...])
-            buf[j, b * 128 : b * 128 + 128, :] = got.astype(BF)
-        copies.append(pltpu.make_async_copy(buf.at[j], out.at[j], osem.at[j]))
-        copies[-1].start()
+    for b in range(2):
+        got = rows_dot(xall[:, b * 512 : b * 512 + 512], dall[...])
+        for j in range(4):
+            buf[j, b * 128 : b * 128 + 128, :] = got[j * 128 : j * 128 + 128].astype(BF)
+            if b == 1:
+                copies.append(pltpu.make_async_copy(buf.at[j], out.at[j], osem.at[j]))
+                copies[-1].start()
     for copy in copies:
         copy.wait()
 
@@ -199,7 +201,7 @@
         ],
         flops=8 * rows * part * wide,
         moved=8 * rows * (part + wide),
-        limit=16,
+        limit=24,
         placed=(0,),
     )(*xs, *ds, *after)
 
@@ -213,8 +215,8 @@
         pairs.append((both.at[i, :, pl.ds(part, inner)], hall.at[pl.ds(i * rows, rows), :]))
     land(pairs, sem)
     mark[...] = jnp.zeros_like(mark)
-    for b in range(inner // 128):
-        cols = slice(b * 128, b * 128 + 128)
+    for b in range(2):
+        cols = slice(b * inner // 2, (b + 1) * inner // 2)
         total[cols, :] = rows_dot(hall[:, cols], gall[...])
     for j in (1, 2, 3, 0):
         other = lax.rem(at[1] + j, 4)
@@ -224,10 +226,12 @@
             )
 
 
-def gate_sum(at, parts, *rest):
-    keep, send, g, sem = rest[-4:]
+def gate_sum(at, parts, keep, send, mark, g, sem):
     half = keep.shape[0]
-    land([(parts, g)], sem)
+    copies = fetch([(parts.at[i], g.at[i]) for i in range(4)], sem)
+    for copy in copies:
+        copy.wait()
+    mark[...] = jnp.zeros_like(mark)
 
     def part(i):
         return sum(g[p, aligned(i, half), :].astype(F32) for p in range(4))
@@ -311,24 +315,30 @@
     n = inner // 256
     dact = call(
         dh_step,
-        "aaaavvaa",
+        "aaaaaaaa",
         [shape(2, rows, inner)],
-        [pltpu.VMEM((rows, width), BF), pltpu.VMEM((n, 256, width), BF), sems(n), sems(4)],
+        [
+            pltpu.VMEM((rows, width), BF),
+            pltpu.VMEM((2, rows, inner), F32),
+            pltpu.VMEM((n, 256, width), BF),
+            sems(n),
+            sems(6),
+        ],
         flops=2 * rows * width * inner,
         moved=2 * width * inner,
-        limit=12,
+        limit=14,
     )(*gs, slope, silu, down_proj, sent_mark)[0]
     da = [shift(dact, "x", j) for j in range(4)]
     n = width // 512
     *back, back_mark = call(
         back_step,
-        "vaa",
+        "vaaa",
         [shape(CAP, width)] * 4 + [MARK],
         [pltpu.VMEM((n, 512, 2 * inner), BF), sems(n)],
         flops=4 * rows * width * inner,
         moved=4 * width * inner,
         limit=18,
-    )(dact, gate_up, da[1])
+    )(dact, gate_up, da[1], xa[2])
     *parts, mark = call(
         down_step,
         "saa",
@@ -347,14 +357,23 @@
     parts, _ = tile_call(xa, da, [mark])
     gate = lax.all_to_all(parts, "y", split_axis=0, concat_axis=0, tiled=True)
     arrived = [back[0]] + [swap_expert(back[k], k) for k in (1, 2, 3)]
-    token_grad, tok_mark = call(
+    keep, send, mark = call(
+        gate_sum,
+        "sa",
+        [shape(128, 2 * inner, dtype=F32), shape(128, 2 * inner), MARK],
+        [pltpu.VMEM((4, 256, 2 * inner), BF), sems(4)],
+        moved=16 * 256 * inner,
+        limit=12,
+    )(at, gate)
+    gate_up_grad = (keep + swap_w(send).astype(F32)).astype(BF)
+    token_grad = call(
         tok_step,
-        "vaaaa",
-        [shape(toks, width), MARK],
+        "vaaaaa",
+        [shape(toks, width)],
         [pltpu.VMEM((rows, width), BF), sems(4)],
         flops=2 * toks * rows * width,
         moved=2 * (rows + toks) * width,
-    )(mask, *arrived)
+    )(mask, *arrived, mark)[0]
 
     keep, send = sum_call(at, down, [])
     down_grad = (keep + swap_w(send).astype(F32)).astype(BF).reshape(4, 24, part)
@@ -365,14 +384,6 @@
     mine = lax.dynamic_slice_in_dim(turned, 3 - y, 4, 0)
     down_grad = jnp.concatenate([mine[i] for i in range(4)], axis=1)
 
-    keep, send = call(
-        gate_sum,
-        "saa",
-        [shape(128, 2 * inner, dtype=F32), shape(128, 2 * inner)],
-        [pltpu.VMEM((4, 256, 2 * inner), BF), sems(1)],
-        moved=16 * 256 * inner,
-    )(at, gate, tok_mark)
-    gate_up_grad = (keep + swap_w(send).astype(F32)).astype(BF)
     return token_grad, gate_up_grad[None], down_grad[None]
 
 

time: 170 us -> 168 us (0.988); the launches traced: 167 us -> 167 us
  waiting for transfers between devices: 60.1 us -> 66.4 us
  starting transfers between devices: 45.1 us -> 40.1 us
    ppermute x12, waiting for transfers between devices: 20.7 us -> 46.4 us  [shift(): return lax.ppermute(a, axis, [(i, (i + j) % 4) for i in range(4)])]
    ppermute x9, waiting for transfers between devices: 23.6 us -> 12.1 us  [swap_expert(): return lax.ppermute(a, ('v', 'c'), [(i, i ^ k) for i in range(4)])]
    ppermute x2, waiting for transfers between devices: 14 us -> 8.01 us  [swap_w(): return lax.ppermute(a, 'w', [(0, 1), (1, 0)])]
    ppermute x12, starting transfers between devices: 22.8 us -> 17 us  [shift(): return lax.ppermute(a, axis, [(i, (i + j) % 4) for i in range(4)])]
    all_to_all x1, waiting for transfers between devices: 1.83 us -> 0.01 us  [shards(): both = lax.all_to_all(sent, 'y', split_axis=0, concat_axis=0, tiled=True)]
    unnamed x51 -> x53, local copies, waits for them, and re-layouts: 9.27 us -> 10.1 us
  transfers between devices with their start and end apart: 25 -> 25, of which waited for: 13 -> 11; matrix products, arithmetic and copies ran while one was open for 4% -> 2% of each run, Pallas kernels for 22% -> 24%
where the time goes in v1:
time: 168 us; the launch traced here: 167 us
  waiting for transfers between devices  66.4 us (40%)
  Pallas kernels  41.4 us (25%)
  starting transfers between devices  40.1 us (24%)
  local copies, waits for them, and re-layouts  12.8 us (8%)
  other arithmetic  2.91 us (2%)
  matrix products  2.45 us (1%)
    ppermute x12, waiting for transfers between devices, shift(): return lax.ppermute(a, axis, [(i, (i + j) % 4) for i in range(4)])  46.4 us
    ppermute x12, starting transfers between devices, shift(): return lax.ppermute(a, axis, [(i, (i + j) % 4) for i in range(4)])  17 us
    ppermute x9, waiting for transfers between devices, swap_expert(): return lax.ppermute(a, ('v', 'c'), [(i, i ^ k) for i in range(4)])  12.1 us
    ppermute x9, starting transfers between devices, swap_expert(): return lax.ppermute(a, ('v', 'c'), [(i, i ^ k) for i in range(4)])  11 us
    unnamed x53, local copies, waits for them, and re-layouts  10.1 us
    ppermute x2, waiting for transfers between devices, swap_w(): return lax.ppermute(a, 'w', [(0, 1), (1, 0)])  8.01 us
    pallas_call x1, Pallas kernels, shards(): call(act_step, 'va', [shape(rows, inner), shape(rows, inner, dtype=F32),...  7.4 us
    pallas_call x1, Pallas kernels, tile_call(): call(tile_step, 'a' * (8 + len(after)), [shape(4, 256, wide), MARK], [plt...  6.95 us
  transfers between devices with their start and end apart: 25, of which 11 were waited for; matrix products, arithmetic and copies ran while one was open for 2% of the time, Pallas kernels for 24%

profile of v1, /device:TPU:0, one launch (start us, length us, event | category | flops | bytes accessed | tf_op | source)
XLA Modules:
  0.0 167.2 jit_solution(16886346599086171515)
XLA Ops:
  4.0 4.0 %collective-permute-start.4 = (bf16[48,4096]{1,0:T(8,128)(2,1)}, bf16[48,4096]{1,0:T(8,128)(2,1)}, u32[]{:S(2)}, u32[]{:S(2)}) collective-permute-start(bf16[48,4096]{1,0:T(8,128)(2,1)} %get-tuple-element.58), channel_id=1, source_target_pairs={{0,2},{1,3},{2,0},{3,1},{4,6},{5,7},{6,4},{7,5},{8,10},{9,11},{10,... | collective-permute-start | bytes 1179656 | tf_op jit(solution)/shard_map/ppermute | solution.py:21
  8.4 1.8 %fusion = bf16[192,4096]{1,0:T(8,128)(2,1)S(1)} fusion(pred[128,192]{1,0:T(32,128)(4,1)S(1)} %get-tuple-element.56, bf16[128,4096]{1,0:T(8,128)(2,1)} %param.7, f32[192]{0:T(256)S(1)} %mul.14), kind=kOutput, calls=%fused_computation.1 | convolution fusion | flops 202899456 | bytes 2646784 | tf_op jit(solution)/shard_map/dot_general | solution.py:35
  11.4 3.4 %collective-permute-start.1 = (bf16[48,4096]{1,0:T(8,128)(2,1)}, bf16[48,4096]{1,0:T(8,128)(2,1)S(1)}, u32[]{:S(2)}, u32[]{:S(2)}) collective-permute-start(bf16[48,4096]{1,0:T(8,128)(2,1)} %get-tuple-element.62), channel_id=1, source_target_pairs={{0,2},{1,3},{2,0},{3,1},{4,6},{5,7},{6,4},{7,5},{8,10},{9,11},{10,... | collective-permute-start | bytes 1179656 | tf_op jit(solution)/shard_map/ppermute | solution.py:21
  15.7 2.6 %collective-permute-done.4.x2 = bf16[48,4096]{1,0:T(8,128)(2,1)} collective-permute-done((bf16[48,4096]{1,0:T(8,128)(2,1)}, bf16[48,4096]{1,0:T(8,128)(2,1)}, u32[]{:S(2)}, u32[]{:S(2)}) %collective-permute-start.4) | collective-permute-done | bytes 393248 | tf_op jit(solution)/shard_map/ppermute | solution.py:21
  18.3 8.1 %collective-permute-done.5.x3 = bf16[48,4096]{1,0:T(8,128)(2,1)} collective-permute-done((bf16[48,4096]{1,0:T(8,128)(2,1)}, bf16[48,4096]{1,0:T(8,128)(2,1)}, u32[]{:S(2)}, u32[]{:S(2)}) %collective-permute-start.5) | collective-permute-done | bytes 393248 | tf_op jit(solution)/shard_map/ppermute | solution.py:21
  30.2 1.5 collective-permute-start.6
  31.7 1.7 %collective-permute-start.7 = (bf16[192,1024]{1,0:T(8,128)(2,1)S(1)}, bf16[192,1024]{1,0:T(8,128)(2,1)S(1)}, u32[]{:S(2)}, u32[]{:S(2)}) collective-permute-start(bf16[192,1024]{1,0:T(8,128)(2,1)S(1)} %get-tuple-element.34), channel_id=1, source_target_pairs={{0,48},{16,0},{32,16},{48,32},{1,49},{17,1},{33,17},{49,33},{2,50}... | collective-permute-start | bytes 1179656 | tf_op jit(solution)/shard_map/ppermute | solution.py:27
  33.4 7.4 %shard_map.86 = (bf16[192,768]{1,0:T(8,128)(2,1)S(1)}, f32[192,768]{1,0:T(8,128)S(1)}, f32[192,768]{1,0:T(8,128)S(1)}) custom-call(bf16[192,4096]{1,0:T(8,128)(2,1)S(1)} %get-tuple-element.29.x, bf16[4096,1536]{1,0:T(8,128)(2,1)} %bitcast.40), custom_call_target="tpu_custom_call" | custom-call | flops 2415919104 | bytes 12582912 | tf_op jit(solution)/shard_map/pallas_call | solution.py:297
  41.7 1.4 collective-permute-done.2.g3
  43.1 1.8 %shard_map.87 = (bf16[4,192,1792]{2,1,0:T(8,128)(2,1)}, f32[8,128]{1,0:T(8,128)S(1)}) custom-call(bf16[48,4096]{1,0:T(8,128)(2,1)S(1)} %get-tuple-element.64.g0, bf16[48,4096]{1,0:T(8,128)(2,1)S(1)} %collective-permute-done.g1, bf16[48,4096]{1,0:T(8,128)(2,1)S(1)} %collective-permute-done.1.g2, bf16[48,4096]{1,0:T(8,128)(2,1)S(1)} %collective-permute-done.2.g3, ...), custom_call_target="tpu_custom_call" | custom-call | bytes 3145728 | tf_op jit(solution)/shard_map/pallas_call | solution.py:306
  45.6 4.6 %all-to-all-start = ((bf16[4,192,1792]{2,1,0:T(8,128)(2,1)}), bf16[4,192,1792]{2,1,0:T(8,128)(2,1)}, u32[]{:S(2)}, u32[]{:S(2)}) async-start(bf16[4,192,1792]{2,1,0:T(8,128)(2,1)} %get-tuple-element.42), calls=%async_computation | async-start | bytes 5505024 | tf_op jit(solution)/shard_map/all_to_all | solution.py:314
  52.4 5.1 %shard_map.88.dact.refs_4_ = bf16[2,192,768]{2,1,0:T(8,128)(2,1)S(1)} custom-call(bf16[48,4096]{1,0:T(8,128)(2,1)S(1)} %get-tuple-element.64.g0, bf16[48,4096]{1,0:T(8,128)(2,1)S(1)} %collective-permute-done.g1, bf16[48,4096]{1,0:T(8,128)(2,1)S(1)} %collective-permute-done.1.g2, bf16[48,4096]{1,0:T(8,128)(2,1)S(1)} %collective-permute-done.2.g3, ...), custom_call_target="tpu_custom_call" | custom-call | flops 1207959552 | bytes 6291456 | tf_op jit(solution)/shard_map/pallas_call | solution.py:316
  57.5 1.6 collective-permute-start.8
  59.1 2.7 %collective-permute-start.9 = (bf16[192,1024]{1,0:T(8,128)(2,1)S(1)}, bf16[192,1024]{1,0:T(8,128)(2,1)S(1)}, u32[]{:S(2)}, u32[]{:S(2)}) collective-permute-start(bf16[192,1024]{1,0:T(8,128)(2,1)S(1)} %copy-done.20), channel_id=1, source_target_pairs={{0,32},{16,48},{32,0},{48,16},{1,33},{17,49},{33,1},{49,17},{2,34}... | collective-permute-start | bytes 1179656 | tf_op jit(solution)/shard_map/ppermute | solution.py:27
  62.6 1.7 %collective-permute-start.14 = (bf16[2,192,768]{2,1,0:T(8,128)(2,1)S(1)}, bf16[2,192,768]{2,1,0:T(8,128)(2,1)}, u32[]{:S(2)}, u32[]{:S(2)}) collective-permute-start(bf16[2,192,768]{2,1,0:T(8,128)(2,1)S(1)} %shard_map.88.dact.refs_4_), channel_id=1, source_target_pairs={{0,48},{16,0},{32,16},{48,32},{1,49},{17,1},{33,17},{49,33},{2,50}... | collective-permute-start | bytes 1769480 | tf_op jit(solution)/shard_map/ppermute | solution.py:27
  64.4 20.0 %collective-permute-done.9.rest_1_.refs_2_ = bf16[192,1024]{1,0:T(8,128)(2,1)S(1)} collective-permute-done((bf16[192,1024]{1,0:T(8,128)(2,1)S(1)}, bf16[192,1024]{1,0:T(8,128)(2,1)S(1)}, u32[]{:S(2)}, u32[]{:S(2)}) %collective-permute-start.9) | collective-permute-done | bytes 393248 | tf_op jit(solution)/shard_map/ppermute | solution.py:27
  84.4 6.8 %shard_map.89 = (bf16[48,4096]{1,0:T(8,128)(2,1)S(1)}, bf16[48,4096]{1,0:T(8,128)(2,1)S(1)}, bf16[48,4096]{1,0:T(8,128)(2,1)S(1)}, bf16[48,4096]{1,0:T(8,128)(2,1)S(1)}, f32[8,128]{1,0:T(8,128)S(1)}) custom-call(bf16[2,192,768]{2,1,0:T(8,128)(2,1)S(1)} %shard_map.88.dact.refs_4_, bf16[4096,1536]{1,0:T(8,128)(2,1)} %bitcast.41, ...), custom_call_target="tpu_custom_call" | custom-call | flops 2415919104 | bytes 12582912 | tf_op jit(solution)/shard_map/pallas_call | solution.py:333
  94.2 5.0 %shard_map.90 = (f32[192,1024]{1,0:T(8,128)S(1)}, bf16[192,1024]{1,0:T(8,128)(2,1)}, bf16[192,1024]{1,0:T(8,128)(2,1)}, bf16[192,1024]{1,0:T(8,128)(2,1)}, f32[8,128]{1,0:T(8,128)S(1)}) custom-call(s32[4]{0:T(128)S(1)} %pad_add_fusion.at, bf16[4,192,1792]{2,1,0:T(8,128)(2,1)} %all-to-all-done.both, f32[8,128]{1,0:T(8,128)S(1)} %get-tuple-element.43.rest_0_), custom_call_target="tpu_custom_call" | custom-call | flops 1207959552 | bytes 2752512 | tf_op jit(solution)/shard_map/pallas_call | solution.py:342
  100.3 2.5 %collective-permute-start.18 = (bf16[192,1024]{1,0:T(8,128)(2,1)}, bf16[192,1024]{1,0:T(8,128)(2,1)}, u32[]{:S(2)}, u32[]{:S(2)}) collective-permute-start(bf16[192,1024]{1,0:T(8,128)(2,1)} %get-tuple-element.52), channel_id=1, source_target_pairs={{0,48},{16,0},{32,16},{48,32},{1,49},{17,1},{33,17},{49,33},{2,50}... | collective-permute-start | bytes 1179656 | tf_op jit(solution)/shard_map/ppermute | solution.py:27
  102.8 7.0 %shard_map.91 = (bf16[4,256,1536]{2,1,0:T(8,128)(2,1)}, f32[8,128]{1,0:T(8,128)}) custom-call(bf16[192,1024]{1,0:T(8,128)(2,1)S(1)} %copy-done.18, bf16[192,1024]{1,0:T(8,128)(2,1)S(1)} %copy-done.10, bf16[192,1024]{1,0:T(8,128)(2,1)S(1)} %collective-permute-done.9.rest_1_.refs_2_, bf16[192,1024]{1,0:T(8,128)(2,1)S(1)} %copy-done.12, ...), custom_call_target="tpu_custom_call" | custom-call | flops 2415919104 | bytes 3932160 | tf_op jit(solution)/shard_map/pallas_call | solution.py:191
  109.8 4.8 %all-to-all-start.1 = ((bf16[4,256,1536]{2,1,0:T(8,128)(2,1)}), bf16[4,256,1536]{2,1,0:T(8,128)(2,1)}, u32[]{:S(2)}, u32[]{:S(2)}) async-start(bf16[4,256,1536]{2,1,0:T(8,128)(2,1)} %get-tuple-element.45), calls=%async_computation.1 | async-start | bytes 6291456 | tf_op jit(solution)/shard_map/all_to_all | solution.py:358
  114.6 4.3 %collective-permute-done.16.r1 = bf16[192,1024]{1,0:T(8,128)(2,1)} collective-permute-done((bf16[192,1024]{1,0:T(8,128)(2,1)}, bf16[192,1024]{1,0:T(8,128)(2,1)}, u32[]{:S(2)}, u32[]{:S(2)}) %collective-permute-start.16) | collective-permute-done | bytes 393248 | tf_op jit(solution)/shard_map/ppermute | solution.py:27
  119.5 2.0 %shard_map.94 = (f32[96,1024]{1,0:T(8,128)S(1)}, bf16[96,1024]{1,0:T(8,128)(2,1)S(1)}) custom-call(s32[4]{0:T(128)S(1)} %pad_add_fusion.at, f32[192,1024]{1,0:T(8,128)S(1)} %get-tuple-element.49.own, bf16[192,1024]{1,0:T(8,128)(2,1)} %collective-permute-done.16.r1, bf16[192,1024]{1,0:T(8,128)(2,1)} %collective-permute-done.17.r2, ...), custom_call_target="tpu_custom_call" | custom-call | bytes 1966080 | tf_op jit(solution)/shard_map/pallas_call | solution.py:258
  122.9 4.4 %collective-permute-done.19 = bf16[96,1024]{1,0:T(8,128)(2,1)S(1)} collective-permute-done((bf16[96,1024]{1,0:T(8,128)(2,1)S(1)}, bf16[96,1024]{1,0:T(8,128)(2,1)S(1)}, u32[]{:S(2)}, u32[]{:S(2)}) %collective-permute-start.19) | collective-permute-done | bytes 196640 | tf_op jit(solution)/shard_map/ppermute | solution.py:31
  127.3 2.7 %collective-permute-start.20 = (bf16[24,1024]{1,0:T(8,128)(2,1)S(1)}, bf16[24,1024]{1,0:T(8,128)(2,1)S(1)}, u32[]{:S(2)}, u32[]{:S(2)}) collective-permute-start(bf16[24,1024]{1,0:T(8,128)(2,1)S(1)} %get-tuple-element.71), channel_id=1, source_target_pairs={{0,12},{4,0},{8,4},{12,8},{1,13},{5,1},{9,5},{13,9},{2,14},{6,2},{... | collective-permute-start | bytes 147464 | tf_op jit(solution)/shard_map/ppermute | solution.py:27
  130.1 3.2 %collective-permute-start.11 = (bf16[48,4096]{1,0:T(8,128)(2,1)}, bf16[48,4096]{1,0:T(8,128)(2,1)S(1)}, u32[]{:S(2)}, u32[]{:S(2)}) collective-permute-start(bf16[48,4096]{1,0:T(8,128)(2,1)} %copy-done.15), channel_id=1, source_target_pairs={{0,2},{1,3},{2,0},{3,1},{4,6},{5,7},{6,4},{7,5},{8,10},{9,11},{10,... | collective-permute-start | bytes 1179656 | tf_op jit(solution)/shard_map/ppermute | solution.py:21
  134.1 16.1 %collective-permute-done.20 = bf16[24,1024]{1,0:T(8,128)(2,1)S(1)} collective-permute-done((bf16[24,1024]{1,0:T(8,128)(2,1)S(1)}, bf16[24,1024]{1,0:T(8,128)(2,1)S(1)}, u32[]{:S(2)}, u32[]{:S(2)}) %collective-permute-start.20) | collective-permute-done | bytes 49184 | tf_op jit(solution)/shard_map/ppermute | solution.py:27
  150.3 1.6 collective-permute-done.21
  151.9 3.7 %collective-permute-done.22 = bf16[24,1024]{1,0:T(8,128)(2,1)S(1)} collective-permute-done((bf16[24,1024]{1,0:T(8,128)(2,1)S(1)}, bf16[24,1024]{1,0:T(8,128)(2,1)S(1)}, u32[]{:S(2)}, u32[]{:S(2)}) %collective-permute-start.22) | collective-permute-done | bytes 49184 | tf_op jit(solution)/shard_map/ppermute | solution.py:27
  155.7 2.8 %shard_map.92 = (f32[128,1536]{1,0:T(8,128)S(1)}, bf16[128,1536]{1,0:T(8,128)(2,1)S(1)}, f32[8,128]{1,0:T(8,128)S(1)}) custom-call(s32[4]{0:T(128)S(1)} %pad_add_fusion.at, bf16[4,256,1536]{2,1,0:T(8,128)(2,1)} %all-to-all-done.1.parts), custom_call_target="tpu_custom_call" | custom-call | bytes 3145728 | tf_op jit(solution)/shard_map/pallas_call | solution.py:360
  160.5 2.2 %shard_map.93 = bf16[128,4096]{1,0:T(8,128)(2,1)} custom-call(bf16[128,192]{1,0:T(8,128)(2,1)S(1)} %get-tuple-element.55.mask, bf16[48,4096]{1,0:T(8,128)(2,1)S(1)} %copy-done.8, bf16[48,4096]{1,0:T(8,128)(2,1)S(1)} %collective-permute-done.10.a1, bf16[48,4096]{1,0:T(8,128)(2,1)S(1)} %collective-permute-done.11.a2, ...), custom_call_target="tpu_custom_call" | custom-call | flops 201326592 | bytes 2621440 | tf_op jit(solution)/shard_map/pallas_call | solution.py:369
  162.7 3.6 %collective-permute-done.15 = bf16[128,1536]{1,0:T(8,128)(2,1)S(1)} collective-permute-done((bf16[128,1536]{1,0:T(8,128)(2,1)S(1)}, bf16[128,1536]{1,0:T(8,128)(2,1)S(1)}, u32[]{:S(2)}, u32[]{:S(2)}) %collective-permute-start.15) | collective-permute-done | bytes 393248 | tf_op jit(solution)/shard_map/ppermute | solution.py:31
  (109 shorter events, 23.9 us)
Async XLA Ops:
  2.3 5.8 %copy-start.21 = (s32[128,8]{0,1:T(8,128)S(1)}, s32[128,8]{0,1:T(8,128)}, u32[]{:S(2)}) copy-start(s32[128,8]{0,1:T(8,128)} %param.8) | copy-start | bytes 12292
  4.0 10.8 %collective-permute-start.3 = (bf16[48,4096]{1,0:T(8,128)(2,1)}, bf16[48,4096]{1,0:T(8,128)(2,1)S(1)}, u32[]{:S(2)}, u32[]{:S(2)}) collective-permute-start(bf16[48,4096]{1,0:T(8,128)(2,1)} %get-tuple-element.59), channel_id=1, source_target_pairs={{0,1},{1,0},{2,3},{3,2},{4,5},{5,4},{6,7},{7,6},{8,9},{9,8},{10,11... | collective-permute-start | bytes 1179656 | tf_op jit(solution)/shard_map/ppermute | solution.py:21
  4.0 14.2 %collective-permute-start.4 = (bf16[48,4096]{1,0:T(8,128)(2,1)}, bf16[48,4096]{1,0:T(8,128)(2,1)}, u32[]{:S(2)}, u32[]{:S(2)}) collective-permute-start(bf16[48,4096]{1,0:T(8,128)(2,1)} %get-tuple-element.58), channel_id=1, source_target_pairs={{0,2},{1,3},{2,0},{3,1},{4,6},{5,7},{6,4},{7,5},{8,10},{9,11},{10,... | collective-permute-start | bytes 1179656 | tf_op jit(solution)/shard_map/ppermute | solution.py:21
  8.0 18.3 %collective-permute-start.5 = (bf16[48,4096]{1,0:T(8,128)(2,1)}, bf16[48,4096]{1,0:T(8,128)(2,1)}, u32[]{:S(2)}, u32[]{:S(2)}) collective-permute-start(bf16[48,4096]{1,0:T(8,128)(2,1)} %get-tuple-element.57), channel_id=1, source_target_pairs={{0,3},{1,2},{2,1},{3,0},{4,7},{5,6},{6,5},{7,4},{8,11},{9,10},{10,... | collective-permute-start | bytes 1179656 | tf_op jit(solution)/shard_map/ppermute | solution.py:21
  11.3 30.4 %collective-permute-start = (bf16[48,4096]{1,0:T(8,128)(2,1)}, bf16[48,4096]{1,0:T(8,128)(2,1)S(1)}, u32[]{:S(2)}, u32[]{:S(2)}) collective-permute-start(bf16[48,4096]{1,0:T(8,128)(2,1)} %get-tuple-element.63), channel_id=1, source_target_pairs={{0,1},{1,0},{2,3},{3,2},{4,5},{5,4},{6,7},{7,6},{8,9},{9,8},{10,11... | collective-permute-start | bytes 1179656 | tf_op jit(solution)/shard_map/ppermute | solution.py:21
  11.4 30.3 %collective-permute-start.1 = (bf16[48,4096]{1,0:T(8,128)(2,1)}, bf16[48,4096]{1,0:T(8,128)(2,1)S(1)}, u32[]{:S(2)}, u32[]{:S(2)}) collective-permute-start(bf16[48,4096]{1,0:T(8,128)(2,1)} %get-tuple-element.62), channel_id=1, source_target_pairs={{0,2},{1,3},{2,0},{3,1},{4,6},{5,7},{6,4},{7,5},{8,10},{9,11},{10,... | collective-permute-start | bytes 1179656 | tf_op jit(solution)/shard_map/ppermute | solution.py:21
  15.7 27.4 %collective-permute-start.2 = (bf16[48,4096]{1,0:T(8,128)(2,1)}, bf16[48,4096]{1,0:T(8,128)(2,1)S(1)}, u32[]{:S(2)}, u32[]{:S(2)}) collective-permute-start(bf16[48,4096]{1,0:T(8,128)(2,1)} %get-tuple-element.61), channel_id=1, source_target_pairs={{0,3},{1,2},{2,1},{3,0},{4,7},{5,6},{6,5},{7,4},{8,11},{9,10},{10,... | collective-permute-start | bytes 1179656 | tf_op jit(solution)/shard_map/ppermute | solution.py:21
  30.2 12.9 %collective-permute-start.6 = (bf16[192,1024]{1,0:T(8,128)(2,1)S(1)}, bf16[192,1024]{1,0:T(8,128)(2,1)S(1)}, u32[]{:S(2)}, u32[]{:S(2)}) collective-permute-start(bf16[192,1024]{1,0:T(8,128)(2,1)S(1)} %get-tuple-element.33), channel_id=1, source_target_pairs={{0,16},{16,32},{32,48},{48,0},{1,17},{17,33},{33,49},{49,1},{2,18}... | collective-permute-start | bytes 1179656 | tf_op jit(solution)/shard_map/ppermute | solution.py:27
  31.7 11.4 %collective-permute-start.7 = (bf16[192,1024]{1,0:T(8,128)(2,1)S(1)}, bf16[192,1024]{1,0:T(8,128)(2,1)S(1)}, u32[]{:S(2)}, u32[]{:S(2)}) collective-permute-start(bf16[192,1024]{1,0:T(8,128)(2,1)S(1)} %get-tuple-element.34), channel_id=1, source_target_pairs={{0,48},{16,0},{32,16},{48,32},{1,49},{17,1},{33,17},{49,33},{2,50}... | collective-permute-start | bytes 1179656 | tf_op jit(solution)/shard_map/ppermute | solution.py:27
  45.6 47.8 %all-to-all-start = ((bf16[4,192,1792]{2,1,0:T(8,128)(2,1)}), bf16[4,192,1792]{2,1,0:T(8,128)(2,1)}, u32[]{:S(2)}, u32[]{:S(2)}) async-start(bf16[4,192,1792]{2,1,0:T(8,128)(2,1)} %get-tuple-element.42), calls=%async_computation | async-start | bytes 5505024 | tf_op jit(solution)/shard_map/all_to_all | solution.py:314
  52.4 6.7 %copy-start.20 = (bf16[192,1024]{1,0:T(8,128)(2,1)S(1)}, bf16[192,1024]{1,0:T(8,128)(2,1)}, u32[]{:S(2)}) copy-start(bf16[192,1024]{1,0:T(8,128)(2,1)} %copy-done.19) | copy-start | bytes 1179652
  57.5 26.9 %collective-permute-start.8 = (bf16[2,192,768]{2,1,0:T(8,128)(2,1)S(1)}, bf16[2,192,768]{2,1,0:T(8,128)(2,1)S(1)}, u32[]{:S(2)}, u32[]{:S(2)}) collective-permute-start(bf16[2,192,768]{2,1,0:T(8,128)(2,1)S(1)} %shard_map.88.dact.refs_4_), channel_id=1, source_target_pairs={{0,16},{16,32},{32,48},{48,0},{1,17},{17,33},{33,49},{49,1},{2,18}... | collective-permute-start | bytes 1769480 | tf_op jit(solution)/shard_map/ppermute | solution.py:27
  59.1 25.3 %collective-permute-start.9 = (bf16[192,1024]{1,0:T(8,128)(2,1)S(1)}, bf16[192,1024]{1,0:T(8,128)(2,1)S(1)}, u32[]{:S(2)}, u32[]{:S(2)}) collective-permute-start(bf16[192,1024]{1,0:T(8,128)(2,1)S(1)} %copy-done.20), channel_id=1, source_target_pairs={{0,32},{16,48},{32,0},{48,16},{1,33},{17,49},{33,1},{49,17},{2,34}... | collective-permute-start | bytes 1179656 | tf_op jit(solution)/shard_map/ppermute | solution.py:27
  61.8 41.0 %collective-permute-start.13 = (bf16[2,192,768]{2,1,0:T(8,128)(2,1)S(1)}, bf16[2,192,768]{2,1,0:T(8,128)(2,1)}, u32[]{:S(2)}, u32[]{:S(2)}) collective-permute-start(bf16[2,192,768]{2,1,0:T(8,128)(2,1)S(1)} %shard_map.88.dact.refs_4_), channel_id=1, source_target_pairs={{0,32},{16,48},{32,0},{48,16},{1,33},{17,49},{33,1},{49,17},{2,34}... | collective-permute-start | bytes 1769480 | tf_op jit(solution)/shard_map/ppermute | solution.py:27
  62.6 40.2 %collective-permute-start.14 = (bf16[2,192,768]{2,1,0:T(8,128)(2,1)S(1)}, bf16[2,192,768]{2,1,0:T(8,128)(2,1)}, u32[]{:S(2)}, u32[]{:S(2)}) collective-permute-start(bf16[2,192,768]{2,1,0:T(8,128)(2,1)S(1)} %shard_map.88.dact.refs_4_), channel_id=1, source_target_pairs={{0,48},{16,0},{32,16},{48,32},{1,49},{17,1},{33,17},{49,33},{2,50}... | collective-permute-start | bytes 1769480 | tf_op jit(solution)/shard_map/ppermute | solution.py:27
  94.2 8.6 %copy-start.10 = (bf16[192,1024]{1,0:T(8,128)(2,1)S(1)}, bf16[192,1024]{1,0:T(8,128)(2,1)}, u32[]{:S(2)}) copy-start(bf16[192,1024]{1,0:T(8,128)(2,1)} %copy-done.9) | copy-start | bytes 1179652
  94.2 8.6 %copy-start.12 = (bf16[192,1024]{1,0:T(8,128)(2,1)S(1)}, bf16[192,1024]{1,0:T(8,128)(2,1)}, u32[]{:S(2)}) copy-start(bf16[192,1024]{1,0:T(8,128)(2,1)} %copy-done.11) | copy-start | bytes 1179652
  94.2 8.6 %copy-start.18 = (bf16[192,1024]{1,0:T(8,128)(2,1)S(1)}, bf16[192,1024]{1,0:T(8,128)(2,1)}, u32[]{:S(2)}) copy-start(bf16[192,1024]{1,0:T(8,128)(2,1)} %copy-done.17) | copy-start | bytes 1179652
  99.3 19.6 %collective-permute-start.16 = (bf16[192,1024]{1,0:T(8,128)(2,1)}, bf16[192,1024]{1,0:T(8,128)(2,1)}, u32[]{:S(2)}, u32[]{:S(2)}) collective-permute-start(bf16[192,1024]{1,0:T(8,128)(2,1)} %get-tuple-element.50), channel_id=1, source_target_pairs={{0,16},{16,32},{32,48},{48,0},{1,17},{17,33},{33,49},{49,1},{2,18}... | collective-permute-start | bytes 1179656 | tf_op jit(solution)/shard_map/ppermute | solution.py:27
  99.3 19.5 %collective-permute-start.17 = (bf16[192,1024]{1,0:T(8,128)(2,1)}, bf16[192,1024]{1,0:T(8,128)(2,1)}, u32[]{:S(2)}, u32[]{:S(2)}) collective-permute-start(bf16[192,1024]{1,0:T(8,128)(2,1)} %get-tuple-element.51), channel_id=1, source_target_pairs={{0,32},{16,48},{32,0},{48,16},{1,33},{17,49},{33,1},{49,17},{2,34}... | collective-permute-start | bytes 1179656 | tf_op jit(solution)/shard_map/ppermute | solution.py:27
  100.3 19.2 %collective-permute-start.18 = (bf16[192,1024]{1,0:T(8,128)(2,1)}, bf16[192,1024]{1,0:T(8,128)(2,1)}, u32[]{:S(2)}, u32[]{:S(2)}) collective-permute-start(bf16[192,1024]{1,0:T(8,128)(2,1)} %get-tuple-element.52), channel_id=1, source_target_pairs={{0,48},{16,0},{32,16},{48,32},{1,49},{17,1},{33,17},{49,33},{2,50}... | collective-permute-start | bytes 1179656 | tf_op jit(solution)/shard_map/ppermute | solution.py:27
  109.8 45.9 %all-to-all-start.1 = ((bf16[4,256,1536]{2,1,0:T(8,128)(2,1)}), bf16[4,256,1536]{2,1,0:T(8,128)(2,1)}, u32[]{:S(2)}, u32[]{:S(2)}) async-start(bf16[4,256,1536]{2,1,0:T(8,128)(2,1)} %get-tuple-element.45), calls=%async_computation.1 | async-start | bytes 6291456 | tf_op jit(solution)/shard_map/all_to_all | solution.py:358
  114.6 18.7 %copy-start.14 = (bf16[48,4096]{1,0:T(8,128)(2,1)S(1)}, bf16[48,4096]{1,0:T(8,128)(2,1)}, u32[]{:S(2)}) copy-start(bf16[48,4096]{1,0:T(8,128)(2,1)} %copy-done.13) | copy-start | bytes 1179652
  121.5 5.8 %collective-permute-start.19 = (bf16[96,1024]{1,0:T(8,128)(2,1)S(1)}, bf16[96,1024]{1,0:T(8,128)(2,1)S(1)}, u32[]{:S(2)}, u32[]{:S(2)}) collective-permute-start(bf16[96,1024]{1,0:T(8,128)(2,1)S(1)} %get-tuple-element.54), channel_id=1, source_target_pairs={{0,64},{64,0},{1,65},{65,1},{2,66},{66,2},{3,67},{67,3},{4,68},{68... | collective-permute-start | bytes 589832 | tf_op jit(solution)/shard_map/ppermute | solution.py:31
  127.3 33.3 %copy-start.8 = (bf16[48,4096]{1,0:T(8,128)(2,1)S(1)}, bf16[48,4096]{1,0:T(8,128)(2,1)}, u32[]{:S(2)}) copy-start(bf16[48,4096]{1,0:T(8,128)(2,1)} %copy-done.7) | copy-start | bytes 1179652
  127.3 22.9 %collective-permute-start.20 = (bf16[24,1024]{1,0:T(8,128)(2,1)S(1)}, bf16[24,1024]{1,0:T(8,128)(2,1)S(1)}, u32[]{:S(2)}, u32[]{:S(2)}) collective-permute-start(bf16[24,1024]{1,0:T(8,128)(2,1)S(1)} %get-tuple-element.71), channel_id=1, source_target_pairs={{0,12},{4,0},{8,4},{12,8},{1,13},{5,1},{9,5},{13,9},{2,14},{6,2},{... | collective-permute-start | bytes 147464 | tf_op jit(solution)/shard_map/ppermute | solution.py:27
  130.1 30.5 %collective-permute-start.10 = (bf16[48,4096]{1,0:T(8,128)(2,1)}, bf16[48,4096]{1,0:T(8,128)(2,1)S(1)}, u32[]{:S(2)}, u32[]{:S(2)}) collective-permute-start(bf16[48,4096]{1,0:T(8,128)(2,1)} %copy-done.16), channel_id=1, source_target_pairs={{0,1},{1,0},{2,3},{3,2},{4,5},{5,4},{6,7},{7,6},{8,9},{9,8},{10,11... | collective-permute-start | bytes 1179656 | tf_op jit(solution)/shard_map/ppermute | solution.py:21
  130.1 30.5 %collective-permute-start.11 = (bf16[48,4096]{1,0:T(8,128)(2,1)}, bf16[48,4096]{1,0:T(8,128)(2,1)S(1)}, u32[]{:S(2)}, u32[]{:S(2)}) collective-permute-start(bf16[48,4096]{1,0:T(8,128)(2,1)} %copy-done.15), channel_id=1, source_target_pairs={{0,2},{1,3},{2,0},{3,1},{4,6},{5,7},{6,4},{7,5},{8,10},{9,11},{10,... | collective-permute-start | bytes 1179656 | tf_op jit(solution)/shard_map/ppermute | solution.py:21
  133.3 27.2 %collective-permute-start.12 = (bf16[48,4096]{1,0:T(8,128)(2,1)S(1)}, bf16[48,4096]{1,0:T(8,128)(2,1)S(1)}, u32[]{:S(2)}, u32[]{:S(2)}) collective-permute-start(bf16[48,4096]{1,0:T(8,128)(2,1)S(1)} %copy-done.14), channel_id=1, source_target_pairs={{0,3},{1,2},{2,1},{3,0},{4,7},{5,6},{6,5},{7,4},{8,11},{9,10},{10,... | collective-permute-start | bytes 1179656 | tf_op jit(solution)/shard_map/ppermute | solution.py:21
  133.5 18.4 %collective-permute-start.21 = (bf16[24,1024]{1,0:T(8,128)(2,1)S(1)}, bf16[24,1024]{1,0:T(8,128)(2,1)S(1)}, u32[]{:S(2)}, u32[]{:S(2)}) collective-permute-start(bf16[24,1024]{1,0:T(8,128)(2,1)S(1)} %get-tuple-element.70), channel_id=1, source_target_pairs={{0,8},{4,12},{8,0},{12,4},{1,9},{5,13},{9,1},{13,5},{2,10},{6,14},... | collective-permute-start | bytes 147464 | tf_op jit(solution)/shard_map/ppermute | solution.py:27
  150.3 5.3 %collective-permute-start.22 = (bf16[24,1024]{1,0:T(8,128)(2,1)S(1)}, bf16[24,1024]{1,0:T(8,128)(2,1)S(1)}, u32[]{:S(2)}, u32[]{:S(2)}) collective-permute-start(bf16[24,1024]{1,0:T(8,128)(2,1)S(1)} %get-tuple-element.69), channel_id=1, source_target_pairs={{0,4},{4,8},{8,12},{12,0},{1,5},{5,9},{9,13},{13,1},{2,6},{6,10},{... | collective-permute-start | bytes 147464 | tf_op jit(solution)/shard_map/ppermute | solution.py:27
  158.5 7.9 %collective-permute-start.15 = (bf16[128,1536]{1,0:T(8,128)(2,1)S(1)}, bf16[128,1536]{1,0:T(8,128)(2,1)S(1)}, u32[]{:S(2)}, u32[]{:S(2)}) collective-permute-start(bf16[128,1536]{1,0:T(8,128)(2,1)S(1)} %get-tuple-element.48), channel_id=1, source_target_pairs={{0,64},{64,0},{1,65},{65,1},{2,66},{66,2},{3,67},{67,3},{4,68},{68... | collective-permute-start | bytes 1179656 | tf_op jit(solution)/shard_map/ppermute | solution.py:31
  (16 other events, 23.3 us)

commit v2 on v1

--- a/solution.py
+++ b/solution.py
@@ -125,7 +125,8 @@
 
 
 def dh_step(g0, g1, g2, g3, slope, silu, weights, *rest):
-    dact, whole, factors, buf, sem, gsem = rest[-6:]
+    dact, mark, whole, factors, buf, sem, gsem = rest[-7:]
+    mark[...] = jnp.zeros_like(mark)
     n, step = buf.shape[:2]
     copies = fetch([(weights.at[pl.ds(i * step, step), :], buf.at[i]) for i in range(n)], sem)
     pieces = [(g, whole.at[pl.ds(k * CAP, CAP), :]) for k, g in enumerate((g0, g1, g2, g3))]
@@ -313,10 +314,10 @@
     )(*gs, hidden, xa[1], xa[3])
     both = lax.all_to_all(sent, "y", split_axis=0, concat_axis=0, tiled=True)
     n = inner // 256
-    dact = call(
+    dact, mark = call(
         dh_step,
         "aaaaaaaa",
-        [shape(2, rows, inner)],
+        [shape(2, rows, inner), MARK],
         [
             pltpu.VMEM((rows, width), BF),
             pltpu.VMEM((2, rows, inner), F32),
@@ -327,18 +328,18 @@
         flops=2 * rows * width * inner,
         moved=2 * width * inner,
         limit=14,
-    )(*gs, slope, silu, down_proj, sent_mark)[0]
+    )(*gs, slope, silu, down_proj, sent_mark)
     da = [shift(dact, "x", j) for j in range(4)]
     n = width // 512
     *back, back_mark = call(
         back_step,
-        "vaaa",
+        "vaa",
         [shape(CAP, width)] * 4 + [MARK],
         [pltpu.VMEM((n, 512, 2 * inner), BF), sems(n)],
         flops=4 * rows * width * inner,
         moved=4 * width * inner,
         limit=18,
-    )(dact, gate_up, da[1], xa[2])
+    )(dact, gate_up, swap_expert(mark, 1))
     *parts, mark = call(
         down_step,
         "saa",

time: 168 us -> 169 us (level)
  waiting for transfers between devices: 66.4 us -> 62.1 us
  local copies, waits for them, and re-layouts: 12.8 us -> 15.3 us
  starting transfers between devices: 40.1 us -> 41.8 us
    ppermute x12, waiting for transfers between devices: 46.4 us -> 30.4 us  [shift(): return lax.ppermute(a, axis, [(i, (i + j) % 4) for i in range(4)])]
    all_to_all x1, waiting for transfers between devices: 0.01 us -> 9.45 us  [shards(): both = lax.all_to_all(sent, 'y', split_axis=0, concat_axis=0, tiled=True)]
    ppermute x9 -> x10, waiting for transfers between devices: 12.1 us -> 14.2 us  [swap_expert(): return lax.ppermute(a, ('v', 'c'), [(i, i ^ k) for i in range(4)])]
    unnamed x53, local copies, waits for them, and re-layouts: 10.1 us -> 12 us
    ppermute x9 -> x10, starting transfers between devices: 11 us -> 11.3 us  [swap_expert(): return lax.ppermute(a, ('v', 'c'), [(i, i ^ k) for i in range(4)])]
  transfers between devices with their start and end apart: 25 -> 26, of which waited for: 11 -> 12; matrix products, arithmetic and copies ran while one was open for 2% -> 3% of each run, Pallas kernels for 24% -> 24%
where the time goes in v2:
time: 169 us; the launch traced here: 168 us
  waiting for transfers between devices  62.1 us (37%)
  Pallas kernels  42.4 us (25%)
  starting transfers between devices  41.8 us (25%)
  local copies, waits for them, and re-layouts  15.3 us (9%)
  other arithmetic  2.91 us (2%)
  matrix products  2.45 us (1%)
    ppermute x12, waiting for transfers between devices, shift(): return lax.ppermute(a, axis, [(i, (i + j) % 4) for i in range(4)])  30.4 us
    ppermute x12, starting transfers between devices, shift(): return lax.ppermute(a, axis, [(i, (i + j) % 4) for i in range(4)])  18.3 us
    ppermute x10, waiting for transfers between devices, swap_expert(): return lax.ppermute(a, ('v', 'c'), [(i, i ^ k) for i in range(4)])  14.2 us
    unnamed x53, local copies, waits for them, and re-layouts  12 us
    ppermute x10, starting transfers between devices, swap_expert(): return lax.ppermute(a, ('v', 'c'), [(i, i ^ k) for i in range(4)])  11.3 us
    all_to_all x1, waiting for transfers between devices, shards(): both = lax.all_to_all(sent, 'y', split_axis=0, concat_axis=0, tiled=True)  9.45 us
    ppermute x2, waiting for transfers between devices, swap_w(): return lax.ppermute(a, 'w', [(0, 1), (1, 0)])  8.04 us
    pallas_call x1, Pallas kernels, shards(): call(act_step, 'va', [shape(rows, inner), shape(rows, inner, dtype=F32),...  7.4 us
  transfers between devices with their start and end apart: 26, of which 12 were waited for; matrix products, arithmetic and copies ran while one was open for 3% of the time, Pallas kernels for 24%

profile of v2, /device:TPU:0, one launch (start us, length us, event | category | flops | bytes accessed | tf_op | source)
XLA Modules:
  0.0 168.0 jit_solution(16134312153207020923)
XLA Ops:
  4.0 4.0 %collective-permute-start.4 = (bf16[48,4096]{1,0:T(8,128)(2,1)}, bf16[48,4096]{1,0:T(8,128)(2,1)}, u32[]{:S(2)}, u32[]{:S(2)}) collective-permute-start(bf16[48,4096]{1,0:T(8,128)(2,1)} %get-tuple-element.62), channel_id=1, source_target_pairs={{0,2},{1,3},{2,0},{3,1},{4,6},{5,7},{6,4},{7,5},{8,10},{9,11},{10,... | collective-permute-start | bytes 1179656 | tf_op jit(solution)/shard_map/ppermute | solution.py:21
  8.4 1.8 %fusion = bf16[192,4096]{1,0:T(8,128)(2,1)S(1)} fusion(pred[128,192]{1,0:T(32,128)(4,1)S(1)} %get-tuple-element.60, bf16[128,4096]{1,0:T(8,128)(2,1)} %param.7, f32[192]{0:T(256)S(1)} %mul.14), kind=kOutput, calls=%fused_computation.1 | convolution fusion | flops 202899456 | bytes 2646784 | tf_op jit(solution)/shard_map/dot_general | solution.py:35
  11.3 3.4 %collective-permute-start.1 = (bf16[48,4096]{1,0:T(8,128)(2,1)}, bf16[48,4096]{1,0:T(8,128)(2,1)S(1)}, u32[]{:S(2)}, u32[]{:S(2)}) collective-permute-start(bf16[48,4096]{1,0:T(8,128)(2,1)} %get-tuple-element.66), channel_id=1, source_target_pairs={{0,2},{1,3},{2,0},{3,1},{4,6},{5,7},{6,4},{7,5},{8,10},{9,11},{10,... | collective-permute-start | bytes 1179656 | tf_op jit(solution)/shard_map/ppermute | solution.py:21
  14.9 3.3 %collective-permute-done.4.x2 = bf16[48,4096]{1,0:T(8,128)(2,1)} collective-permute-done((bf16[48,4096]{1,0:T(8,128)(2,1)}, bf16[48,4096]{1,0:T(8,128)(2,1)}, u32[]{:S(2)}, u32[]{:S(2)}) %collective-permute-start.4) | collective-permute-done | bytes 393248 | tf_op jit(solution)/shard_map/ppermute | solution.py:21
  18.2 8.1 %collective-permute-done.5.x3 = bf16[48,4096]{1,0:T(8,128)(2,1)} collective-permute-done((bf16[48,4096]{1,0:T(8,128)(2,1)}, bf16[48,4096]{1,0:T(8,128)(2,1)}, u32[]{:S(2)}, u32[]{:S(2)}) %collective-permute-start.5) | collective-permute-done | bytes 393248 | tf_op jit(solution)/shard_map/ppermute | solution.py:21
  26.3 2.0 %shard_map.85 = (bf16[192,1024]{1,0:T(8,128)(2,1)S(1)}, bf16[192,1024]{1,0:T(8,128)(2,1)S(1)}, bf16[192,1024]{1,0:T(8,128)(2,1)}, bf16[192,1024]{1,0:T(8,128)(2,1)S(1)}, bf16[192,4096]{1,0:T(8,128)(2,1)S(1)}) custom-call(s32[4]{0:T(128)S(1)} %pad_add_fusion.at, bf16[48,4096]{1,0:T(8,128)(2,1)S(1)} %get-tuple-element.64.x0, ...), custom_call_target="tpu_custom_call" | custom-call | bytes 3145728 | tf_op jit(solution)/shard_map/pallas_call | solution.py:293
  29.1 1.5 collective-permute-start.6
  30.6 1.7 %collective-permute-start.7 = (bf16[192,1024]{1,0:T(8,128)(2,1)S(1)}, bf16[192,1024]{1,0:T(8,128)(2,1)S(1)}, u32[]{:S(2)}, u32[]{:S(2)}) collective-permute-start(bf16[192,1024]{1,0:T(8,128)(2,1)S(1)} %get-tuple-element.36), channel_id=1, source_target_pairs={{0,48},{16,0},{32,16},{48,32},{1,49},{17,1},{33,17},{49,33},{2,50}... | collective-permute-start | bytes 1179656 | tf_op jit(solution)/shard_map/ppermute | solution.py:27
  32.3 7.4 %shard_map.86 = (bf16[192,768]{1,0:T(8,128)(2,1)S(1)}, f32[192,768]{1,0:T(8,128)S(1)}, f32[192,768]{1,0:T(8,128)S(1)}) custom-call(bf16[192,4096]{1,0:T(8,128)(2,1)S(1)} %get-tuple-element.31.x, bf16[4096,1536]{1,0:T(8,128)(2,1)} %bitcast.40), custom_call_target="tpu_custom_call" | custom-call | flops 2415919104 | bytes 12582912 | tf_op jit(solution)/shard_map/pallas_call | solution.py:298
  41.4 1.6 collective-permute-done.2.g3
  43.0 1.8 %shard_map.87 = (bf16[4,192,1792]{2,1,0:T(8,128)(2,1)}, f32[8,128]{1,0:T(8,128)S(1)}) custom-call(bf16[48,4096]{1,0:T(8,128)(2,1)S(1)} %get-tuple-element.68.g0, bf16[48,4096]{1,0:T(8,128)(2,1)S(1)} %collective-permute-done.g1, bf16[48,4096]{1,0:T(8,128)(2,1)S(1)} %collective-permute-done.1.g2, bf16[48,4096]{1,0:T(8,128)(2,1)S(1)} %collective-permute-done.2.g3, ...), custom_call_target="tpu_custom_call" | custom-call | bytes 3145728 | tf_op jit(solution)/shard_map/pallas_call | solution.py:307
  45.6 4.6 %all-to-all-start = ((bf16[4,192,1792]{2,1,0:T(8,128)(2,1)}), bf16[4,192,1792]{2,1,0:T(8,128)(2,1)}, u32[]{:S(2)}, u32[]{:S(2)}) async-start(bf16[4,192,1792]{2,1,0:T(8,128)(2,1)} %get-tuple-element.46), calls=%async_computation | async-start | bytes 5505024 | tf_op jit(solution)/shard_map/all_to_all | solution.py:315
  52.4 5.1 %shard_map.88 = (bf16[2,192,768]{2,1,0:T(8,128)(2,1)S(1)}, f32[8,128]{1,0:T(8,128)S(1)}) custom-call(bf16[48,4096]{1,0:T(8,128)(2,1)S(1)} %get-tuple-element.68.g0, bf16[48,4096]{1,0:T(8,128)(2,1)S(1)} %collective-permute-done.g1, bf16[48,4096]{1,0:T(8,128)(2,1)S(1)} %collective-permute-done.1.g2, bf16[48,4096]{1,0:T(8,128)(2,1)S(1)} %collective-permute-done.2.g3, ...), custom_call_target="tpu_custom_call" | custom-call | flops 1207959552 | bytes 6291456 | tf_op jit(solution)/shard_map/pallas_call | solution.py:317
  57.5 1.6 collective-permute-start.13
  59.0 2.7 %collective-permute-start.14 = (bf16[2,192,768]{2,1,0:T(8,128)(2,1)S(1)}, bf16[2,192,768]{2,1,0:T(8,128)(2,1)}, u32[]{:S(2)}, u32[]{:S(2)}) collective-permute-start(bf16[2,192,768]{2,1,0:T(8,128)(2,1)S(1)} %get-tuple-element.38.dact.refs_4_), channel_id=1, source_target_pairs={{0,32},{16,48},{32,0},{48,16},{1,33},{17,49},{33,1},{49,17},{2,34}... | collective-permute-start | bytes 1769480 | tf_op jit(solution)/shard_map/ppermute | solution.py:27
  64.9 6.8 %shard_map.89 = (bf16[48,4096]{1,0:T(8,128)(2,1)S(1)}, bf16[48,4096]{1,0:T(8,128)(2,1)S(1)}, bf16[48,4096]{1,0:T(8,128)(2,1)S(1)}, bf16[48,4096]{1,0:T(8,128)(2,1)S(1)}, f32[8,128]{1,0:T(8,128)S(1)}) custom-call(bf16[2,192,768]{2,1,0:T(8,128)(2,1)S(1)} %get-tuple-element.38.dact.refs_4_, bf16[4096,1536]{1,0:T(8,128)(2,1)} %bitcast.41, ...), custom_call_target="tpu_custom_call" | custom-call | flops 2415919104 | bytes 12582912 | tf_op jit(solution)/shard_map/pallas_call | solution.py:334
  74.8 9.4 %all-to-all-done.both = bf16[4,192,1792]{2,1,0:T(8,128)(2,1)} async-done(((bf16[4,192,1792]{2,1,0:T(8,128)(2,1)}), bf16[4,192,1792]{2,1,0:T(8,128)(2,1)}, u32[]{:S(2)}, u32[]{:S(2)}) %all-to-all-start) | async-done | bytes 2752544 | tf_op jit(solution)/shard_map/all_to_all | solution.py:315
  84.2 5.1 %shard_map.90 = (f32[192,1024]{1,0:T(8,128)S(1)}, bf16[192,1024]{1,0:T(8,128)(2,1)}, bf16[192,1024]{1,0:T(8,128)(2,1)}, bf16[192,1024]{1,0:T(8,128)(2,1)}, f32[8,128]{1,0:T(8,128)S(1)}) custom-call(s32[4]{0:T(128)S(1)} %pad_add_fusion.at, bf16[4,192,1792]{2,1,0:T(8,128)(2,1)} %all-to-all-done.both, f32[8,128]{1,0:T(8,128)S(1)} %get-tuple-element.47.rest_0_), custom_call_target="tpu_custom_call" | custom-call | flops 1207959552 | bytes 2752512 | tf_op jit(solution)/shard_map/pallas_call | solution.py:343
  89.3 1.6 collective-permute-start.17
  90.8 6.2 %collective-permute-done.12.refs_2_ = bf16[192,1024]{1,0:T(8,128)(2,1)S(1)} collective-permute-done((bf16[192,1024]{1,0:T(8,128)(2,1)}, bf16[192,1024]{1,0:T(8,128)(2,1)S(1)}, u32[]{:S(2)}, u32[]{:S(2)}) %collective-permute-start.12) | collective-permute-done | bytes 393248 | tf_op jit(solution)/shard_map/ppermute | solution.py:27
  98.6 3.1 %collective-permute-start.19 = (bf16[192,1024]{1,0:T(8,128)(2,1)}, bf16[192,1024]{1,0:T(8,128)(2,1)}, u32[]{:S(2)}, u32[]{:S(2)}) collective-permute-start(bf16[192,1024]{1,0:T(8,128)(2,1)} %get-tuple-element.56), channel_id=1, source_target_pairs={{0,48},{16,0},{32,16},{48,32},{1,49},{17,1},{33,17},{49,33},{2,50}... | collective-permute-start | bytes 1179656 | tf_op jit(solution)/shard_map/ppermute | solution.py:27
  102.7 7.1 %shard_map.91 = (bf16[4,256,1536]{2,1,0:T(8,128)(2,1)}, f32[8,128]{1,0:T(8,128)}) custom-call(bf16[192,1024]{1,0:T(8,128)(2,1)S(1)} %copy-done.18, bf16[192,1024]{1,0:T(8,128)(2,1)S(1)} %copy-done.10, bf16[192,1024]{1,0:T(8,128)(2,1)S(1)} %copy-done.20, bf16[192,1024]{1,0:T(8,128)(2,1)S(1)} %copy-done.12, ...), custom_call_target="tpu_custom_call" | custom-call | flops 2415919104 | bytes 3932160 | tf_op jit(solution)/shard_map/pallas_call | solution.py:192
  109.8 4.8 %all-to-all-start.1 = ((bf16[4,256,1536]{2,1,0:T(8,128)(2,1)}), bf16[4,256,1536]{2,1,0:T(8,128)(2,1)}, u32[]{:S(2)}, u32[]{:S(2)}) async-start(bf16[4,256,1536]{2,1,0:T(8,128)(2,1)} %get-tuple-element.49), calls=%async_computation.1 | async-start | bytes 6291456 | tf_op jit(solution)/shard_map/all_to_all | solution.py:359
  117.8 2.2 %shard_map.94 = (f32[96,1024]{1,0:T(8,128)S(1)}, bf16[96,1024]{1,0:T(8,128)(2,1)S(1)}) custom-call(s32[4]{0:T(128)S(1)} %pad_add_fusion.at, f32[192,1024]{1,0:T(8,128)S(1)} %get-tuple-element.53.own, bf16[192,1024]{1,0:T(8,128)(2,1)S(1)} %collective-permute-done.17.r1, bf16[192,1024]{1,0:T(8,128)(2,1)S(1)} %copy-done.6, ...), custom_call_target="tpu_custom_call" | custom-call | bytes 1966080 | tf_op jit(solution)/shard_map/pallas_call | solution.py:259
  121.3 4.5 %collective-permute-done.20 = bf16[96,1024]{1,0:T(8,128)(2,1)S(1)} collective-permute-done((bf16[96,1024]{1,0:T(8,128)(2,1)S(1)}, bf16[96,1024]{1,0:T(8,128)(2,1)S(1)}, u32[]{:S(2)}, u32[]{:S(2)}) %collective-permute-start.20) | collective-permute-done | bytes 196640 | tf_op jit(solution)/shard_map/ppermute | solution.py:31
  126.5 2.8 %collective-permute-start.21 = (bf16[24,1024]{1,0:T(8,128)(2,1)S(1)}, bf16[24,1024]{1,0:T(8,128)(2,1)S(1)}, u32[]{:S(2)}, u32[]{:S(2)}) collective-permute-start(bf16[24,1024]{1,0:T(8,128)(2,1)S(1)} %get-tuple-element.75), channel_id=1, source_target_pairs={{0,12},{4,0},{8,4},{12,8},{1,13},{5,1},{9,5},{13,9},{2,14},{6,2},{... | collective-permute-start | bytes 147464 | tf_op jit(solution)/shard_map/ppermute | solution.py:27
  129.3 3.2 %collective-permute-start.10 = (bf16[48,4096]{1,0:T(8,128)(2,1)}, bf16[48,4096]{1,0:T(8,128)(2,1)S(1)}, u32[]{:S(2)}, u32[]{:S(2)}) collective-permute-start(bf16[48,4096]{1,0:T(8,128)(2,1)} %copy-done.16), channel_id=1, source_target_pairs={{0,2},{1,3},{2,0},{3,1},{4,6},{5,7},{6,4},{7,5},{8,10},{9,11},{10,... | collective-permute-start | bytes 1179656 | tf_op jit(solution)/shard_map/ppermute | solution.py:21
  133.6 17.5 %collective-permute-done.21 = bf16[24,1024]{1,0:T(8,128)(2,1)S(1)} collective-permute-done((bf16[24,1024]{1,0:T(8,128)(2,1)S(1)}, bf16[24,1024]{1,0:T(8,128)(2,1)S(1)}, u32[]{:S(2)}, u32[]{:S(2)}) %collective-permute-start.21) | collective-permute-done | bytes 49184 | tf_op jit(solution)/shard_map/ppermute | solution.py:27
  152.3 4.1 %collective-permute-done.23 = bf16[24,1024]{1,0:T(8,128)(2,1)S(1)} collective-permute-done((bf16[24,1024]{1,0:T(8,128)(2,1)S(1)}, bf16[24,1024]{1,0:T(8,128)(2,1)S(1)}, u32[]{:S(2)}, u32[]{:S(2)}) %collective-permute-start.23) | collective-permute-done | bytes 49184 | tf_op jit(solution)/shard_map/ppermute | solution.py:27
  156.5 2.8 %shard_map.92 = (f32[128,1536]{1,0:T(8,128)S(1)}, bf16[128,1536]{1,0:T(8,128)(2,1)S(1)}, f32[8,128]{1,0:T(8,128)S(1)}) custom-call(s32[4]{0:T(128)S(1)} %pad_add_fusion.at, bf16[4,256,1536]{2,1,0:T(8,128)(2,1)} %all-to-all-done.1.parts), custom_call_target="tpu_custom_call" | custom-call | bytes 3145728 | tf_op jit(solution)/shard_map/pallas_call | solution.py:361
  161.4 2.2 %shard_map.93 = bf16[128,4096]{1,0:T(8,128)(2,1)} custom-call(bf16[128,192]{1,0:T(8,128)(2,1)S(1)} %get-tuple-element.59.mask, bf16[48,4096]{1,0:T(8,128)(2,1)S(1)} %copy-done.8, bf16[48,4096]{1,0:T(8,128)(2,1)S(1)} %collective-permute-done.9.a1, bf16[48,4096]{1,0:T(8,128)(2,1)S(1)} %collective-permute-done.10.a2, ...), custom_call_target="tpu_custom_call" | custom-call | flops 201326592 | bytes 2621440 | tf_op jit(solution)/shard_map/pallas_call | solution.py:370
  163.6 3.6 %collective-permute-done.16 = bf16[128,1536]{1,0:T(8,128)(2,1)S(1)} collective-permute-done((bf16[128,1536]{1,0:T(8,128)(2,1)S(1)}, bf16[128,1536]{1,0:T(8,128)(2,1)S(1)}, u32[]{:S(2)}, u32[]{:S(2)}) %collective-permute-start.16) | collective-permute-done | bytes 393248 | tf_op jit(solution)/shard_map/ppermute | solution.py:31
  (111 shorter events, 29.5 us)
Async XLA Ops:
  2.3 5.8 %copy-start.21 = (s32[128,8]{0,1:T(8,128)S(1)}, s32[128,8]{0,1:T(8,128)}, u32[]{:S(2)}) copy-start(s32[128,8]{0,1:T(8,128)} %param.8) | copy-start | bytes 12292
  4.0 10.9 %collective-permute-start.3 = (bf16[48,4096]{1,0:T(8,128)(2,1)}, bf16[48,4096]{1,0:T(8,128)(2,1)S(1)}, u32[]{:S(2)}, u32[]{:S(2)}) collective-permute-start(bf16[48,4096]{1,0:T(8,128)(2,1)} %get-tuple-element.63), channel_id=1, source_target_pairs={{0,1},{1,0},{2,3},{3,2},{4,5},{5,4},{6,7},{7,6},{8,9},{9,8},{10,11... | collective-permute-start | bytes 1179656 | tf_op jit(solution)/shard_map/ppermute | solution.py:21
  4.0 14.2 %collective-permute-start.4 = (bf16[48,4096]{1,0:T(8,128)(2,1)}, bf16[48,4096]{1,0:T(8,128)(2,1)}, u32[]{:S(2)}, u32[]{:S(2)}) collective-permute-start(bf16[48,4096]{1,0:T(8,128)(2,1)} %get-tuple-element.62), channel_id=1, source_target_pairs={{0,2},{1,3},{2,0},{3,1},{4,6},{5,7},{6,4},{7,5},{8,10},{9,11},{10,... | collective-permute-start | bytes 1179656 | tf_op jit(solution)/shard_map/ppermute | solution.py:21
  7.9 18.3 %collective-permute-start.5 = (bf16[48,4096]{1,0:T(8,128)(2,1)}, bf16[48,4096]{1,0:T(8,128)(2,1)}, u32[]{:S(2)}, u32[]{:S(2)}) collective-permute-start(bf16[48,4096]{1,0:T(8,128)(2,1)} %get-tuple-element.61), channel_id=1, source_target_pairs={{0,3},{1,2},{2,1},{3,0},{4,7},{5,6},{6,5},{7,4},{8,11},{9,10},{10,... | collective-permute-start | bytes 1179656 | tf_op jit(solution)/shard_map/ppermute | solution.py:21
  11.3 30.1 %collective-permute-start = (bf16[48,4096]{1,0:T(8,128)(2,1)}, bf16[48,4096]{1,0:T(8,128)(2,1)S(1)}, u32[]{:S(2)}, u32[]{:S(2)}) collective-permute-start(bf16[48,4096]{1,0:T(8,128)(2,1)} %get-tuple-element.67), channel_id=1, source_target_pairs={{0,1},{1,0},{2,3},{3,2},{4,5},{5,4},{6,7},{7,6},{8,9},{9,8},{10,11... | collective-permute-start | bytes 1179656 | tf_op jit(solution)/shard_map/ppermute | solution.py:21
  11.3 30.1 %collective-permute-start.1 = (bf16[48,4096]{1,0:T(8,128)(2,1)}, bf16[48,4096]{1,0:T(8,128)(2,1)S(1)}, u32[]{:S(2)}, u32[]{:S(2)}) collective-permute-start(bf16[48,4096]{1,0:T(8,128)(2,1)} %get-tuple-element.66), channel_id=1, source_target_pairs={{0,2},{1,3},{2,0},{3,1},{4,6},{5,7},{6,4},{7,5},{8,10},{9,11},{10,... | collective-permute-start | bytes 1179656 | tf_op jit(solution)/shard_map/ppermute | solution.py:21
  14.8 28.2 %collective-permute-start.2 = (bf16[48,4096]{1,0:T(8,128)(2,1)}, bf16[48,4096]{1,0:T(8,128)(2,1)S(1)}, u32[]{:S(2)}, u32[]{:S(2)}) collective-permute-start(bf16[48,4096]{1,0:T(8,128)(2,1)} %get-tuple-element.65), channel_id=1, source_target_pairs={{0,3},{1,2},{2,1},{3,0},{4,7},{5,6},{6,5},{7,4},{8,11},{9,10},{10,... | collective-permute-start | bytes 1179656 | tf_op jit(solution)/shard_map/ppermute | solution.py:21
  29.1 13.9 %collective-permute-start.6 = (bf16[192,1024]{1,0:T(8,128)(2,1)S(1)}, bf16[192,1024]{1,0:T(8,128)(2,1)S(1)}, u32[]{:S(2)}, u32[]{:S(2)}) collective-permute-start(bf16[192,1024]{1,0:T(8,128)(2,1)S(1)} %get-tuple-element.35), channel_id=1, source_target_pairs={{0,16},{16,32},{32,48},{48,0},{1,17},{17,33},{33,49},{49,1},{2,18}... | collective-permute-start | bytes 1179656 | tf_op jit(solution)/shard_map/ppermute | solution.py:27
  30.6 12.4 %collective-permute-start.7 = (bf16[192,1024]{1,0:T(8,128)(2,1)S(1)}, bf16[192,1024]{1,0:T(8,128)(2,1)S(1)}, u32[]{:S(2)}, u32[]{:S(2)}) collective-permute-start(bf16[192,1024]{1,0:T(8,128)(2,1)S(1)} %get-tuple-element.36), channel_id=1, source_target_pairs={{0,48},{16,0},{32,16},{48,32},{1,49},{17,1},{33,17},{49,33},{2,50}... | collective-permute-start | bytes 1179656 | tf_op jit(solution)/shard_map/ppermute | solution.py:27
  45.6 38.6 %all-to-all-start = ((bf16[4,192,1792]{2,1,0:T(8,128)(2,1)}), bf16[4,192,1792]{2,1,0:T(8,128)(2,1)}, u32[]{:S(2)}, u32[]{:S(2)}) async-start(bf16[4,192,1792]{2,1,0:T(8,128)(2,1)} %get-tuple-element.46), calls=%async_computation | async-start | bytes 5505024 | tf_op jit(solution)/shard_map/all_to_all | solution.py:315
  57.5 41.1 %collective-permute-start.13 = (bf16[2,192,768]{2,1,0:T(8,128)(2,1)S(1)}, bf16[2,192,768]{2,1,0:T(8,128)(2,1)}, u32[]{:S(2)}, u32[]{:S(2)}) collective-permute-start(bf16[2,192,768]{2,1,0:T(8,128)(2,1)S(1)} %get-tuple-element.38.dact.refs_4_), channel_id=1, source_target_pairs={{0,16},{16,32},{32,48},{48,0},{1,17},{17,33},{33,49},{49,1},{2,18}... | collective-permute-start | bytes 1769480 | tf_op jit(solution)/shard_map/ppermute | solution.py:27
  59.0 42.6 %collective-permute-start.14 = (bf16[2,192,768]{2,1,0:T(8,128)(2,1)S(1)}, bf16[2,192,768]{2,1,0:T(8,128)(2,1)}, u32[]{:S(2)}, u32[]{:S(2)}) collective-permute-start(bf16[2,192,768]{2,1,0:T(8,128)(2,1)S(1)} %get-tuple-element.38.dact.refs_4_), channel_id=1, source_target_pairs={{0,32},{16,48},{32,0},{48,16},{1,33},{17,49},{33,1},{49,17},{2,34}... | collective-permute-start | bytes 1769480 | tf_op jit(solution)/shard_map/ppermute | solution.py:27
  61.8 39.9 %collective-permute-start.15 = (bf16[2,192,768]{2,1,0:T(8,128)(2,1)S(1)}, bf16[2,192,768]{2,1,0:T(8,128)(2,1)}, u32[]{:S(2)}, u32[]{:S(2)}) collective-permute-start(bf16[2,192,768]{2,1,0:T(8,128)(2,1)S(1)} %get-tuple-element.38.dact.refs_4_), channel_id=1, source_target_pairs={{0,48},{16,0},{32,16},{48,32},{1,49},{17,1},{33,17},{49,33},{2,50}... | collective-permute-start | bytes 1769480 | tf_op jit(solution)/shard_map/ppermute | solution.py:27
  63.2 33.8 %collective-permute-start.12 = (bf16[192,1024]{1,0:T(8,128)(2,1)}, bf16[192,1024]{1,0:T(8,128)(2,1)S(1)}, u32[]{:S(2)}, u32[]{:S(2)}) collective-permute-start(bf16[192,1024]{1,0:T(8,128)(2,1)} %get-tuple-element.45), channel_id=1, source_target_pairs={{0,32},{16,48},{32,0},{48,16},{1,33},{17,49},{33,1},{49,17},{2,34}... | collective-permute-start | bytes 1179656 | tf_op jit(solution)/shard_map/ppermute | solution.py:27
  63.7 1.2 collective-permute-start.8
  84.2 17.4 %copy-start.10 = (bf16[192,1024]{1,0:T(8,128)(2,1)S(1)}, bf16[192,1024]{1,0:T(8,128)(2,1)}, u32[]{:S(2)}) copy-start(bf16[192,1024]{1,0:T(8,128)(2,1)} %copy-done.9) | copy-start | bytes 1179652
  84.2 17.4 %copy-start.12 = (bf16[192,1024]{1,0:T(8,128)(2,1)S(1)}, bf16[192,1024]{1,0:T(8,128)(2,1)}, u32[]{:S(2)}) copy-start(bf16[192,1024]{1,0:T(8,128)(2,1)} %copy-done.11) | copy-start | bytes 1179652
  84.2 17.5 %copy-start.18 = (bf16[192,1024]{1,0:T(8,128)(2,1)S(1)}, bf16[192,1024]{1,0:T(8,128)(2,1)}, u32[]{:S(2)}) copy-start(bf16[192,1024]{1,0:T(8,128)(2,1)} %copy-done.17) | copy-start | bytes 1179652
  89.3 25.3 %collective-permute-start.17 = (bf16[192,1024]{1,0:T(8,128)(2,1)}, bf16[192,1024]{1,0:T(8,128)(2,1)S(1)}, u32[]{:S(2)}, u32[]{:S(2)}) collective-permute-start(bf16[192,1024]{1,0:T(8,128)(2,1)} %get-tuple-element.54), channel_id=1, source_target_pairs={{0,16},{16,32},{32,48},{48,0},{1,17},{17,33},{33,49},{49,1},{2,18}... | collective-permute-start | bytes 1179656 | tf_op jit(solution)/shard_map/ppermute | solution.py:27
  97.8 16.8 %collective-permute-start.18 = (bf16[192,1024]{1,0:T(8,128)(2,1)}, bf16[192,1024]{1,0:T(8,128)(2,1)S(1)}, u32[]{:S(2)}, u32[]{:S(2)}) collective-permute-start(bf16[192,1024]{1,0:T(8,128)(2,1)} %get-tuple-element.55), channel_id=1, source_target_pairs={{0,32},{16,48},{32,0},{48,16},{1,33},{17,49},{33,1},{49,17},{2,34}... | collective-permute-start | bytes 1179656 | tf_op jit(solution)/shard_map/ppermute | solution.py:27
  98.6 18.2 %collective-permute-start.19 = (bf16[192,1024]{1,0:T(8,128)(2,1)}, bf16[192,1024]{1,0:T(8,128)(2,1)}, u32[]{:S(2)}, u32[]{:S(2)}) collective-permute-start(bf16[192,1024]{1,0:T(8,128)(2,1)} %get-tuple-element.56), channel_id=1, source_target_pairs={{0,48},{16,0},{32,16},{48,32},{1,49},{17,1},{33,17},{49,33},{2,50}... | collective-permute-start | bytes 1179656 | tf_op jit(solution)/shard_map/ppermute | solution.py:27
  109.8 22.7 %copy-start.14 = (bf16[48,4096]{1,0:T(8,128)(2,1)S(1)}, bf16[48,4096]{1,0:T(8,128)(2,1)}, u32[]{:S(2)}) copy-start(bf16[48,4096]{1,0:T(8,128)(2,1)} %copy-done.13) | copy-start | bytes 1179652
  109.8 46.7 %all-to-all-start.1 = ((bf16[4,256,1536]{2,1,0:T(8,128)(2,1)}), bf16[4,256,1536]{2,1,0:T(8,128)(2,1)}, u32[]{:S(2)}, u32[]{:S(2)}) async-start(bf16[4,256,1536]{2,1,0:T(8,128)(2,1)} %get-tuple-element.49), calls=%async_computation.1 | async-start | bytes 6291456 | tf_op jit(solution)/shard_map/all_to_all | solution.py:359
  120.0 5.8 %collective-permute-start.20 = (bf16[96,1024]{1,0:T(8,128)(2,1)S(1)}, bf16[96,1024]{1,0:T(8,128)(2,1)S(1)}, u32[]{:S(2)}, u32[]{:S(2)}) collective-permute-start(bf16[96,1024]{1,0:T(8,128)(2,1)S(1)} %get-tuple-element.58), channel_id=1, source_target_pairs={{0,64},{64,0},{1,65},{65,1},{2,66},{66,2},{3,67},{67,3},{4,68},{68... | collective-permute-start | bytes 589832 | tf_op jit(solution)/shard_map/ppermute | solution.py:31
  125.8 35.6 %copy-start.8 = (bf16[48,4096]{1,0:T(8,128)(2,1)S(1)}, bf16[48,4096]{1,0:T(8,128)(2,1)}, u32[]{:S(2)}) copy-start(bf16[48,4096]{1,0:T(8,128)(2,1)} %copy-done.7) | copy-start | bytes 1179652
  126.5 24.6 %collective-permute-start.21 = (bf16[24,1024]{1,0:T(8,128)(2,1)S(1)}, bf16[24,1024]{1,0:T(8,128)(2,1)S(1)}, u32[]{:S(2)}, u32[]{:S(2)}) collective-permute-start(bf16[24,1024]{1,0:T(8,128)(2,1)S(1)} %get-tuple-element.75), channel_id=1, source_target_pairs={{0,12},{4,0},{8,4},{12,8},{1,13},{5,1},{9,5},{13,9},{2,14},{6,2},{... | collective-permute-start | bytes 147464 | tf_op jit(solution)/shard_map/ppermute | solution.py:27
  129.3 32.1 %collective-permute-start.10 = (bf16[48,4096]{1,0:T(8,128)(2,1)}, bf16[48,4096]{1,0:T(8,128)(2,1)S(1)}, u32[]{:S(2)}, u32[]{:S(2)}) collective-permute-start(bf16[48,4096]{1,0:T(8,128)(2,1)} %copy-done.16), channel_id=1, source_target_pairs={{0,2},{1,3},{2,0},{3,1},{4,6},{5,7},{6,4},{7,5},{8,10},{9,11},{10,... | collective-permute-start | bytes 1179656 | tf_op jit(solution)/shard_map/ppermute | solution.py:21
  132.5 28.9 %collective-permute-start.11 = (bf16[48,4096]{1,0:T(8,128)(2,1)}, bf16[48,4096]{1,0:T(8,128)(2,1)S(1)}, u32[]{:S(2)}, u32[]{:S(2)}) collective-permute-start(bf16[48,4096]{1,0:T(8,128)(2,1)} %copy-done.15), channel_id=1, source_target_pairs={{0,3},{1,2},{2,1},{3,0},{4,7},{5,6},{6,5},{7,4},{8,11},{9,10},{10,... | collective-permute-start | bytes 1179656 | tf_op jit(solution)/shard_map/ppermute | solution.py:21
  132.5 28.9 %collective-permute-start.9 = (bf16[48,4096]{1,0:T(8,128)(2,1)S(1)}, bf16[48,4096]{1,0:T(8,128)(2,1)S(1)}, u32[]{:S(2)}, u32[]{:S(2)}) collective-permute-start(bf16[48,4096]{1,0:T(8,128)(2,1)S(1)} %copy-done.14), channel_id=1, source_target_pairs={{0,1},{1,0},{2,3},{3,2},{4,5},{5,4},{6,7},{7,6},{8,9},{9,8},{10,11... | collective-permute-start | bytes 1179656 | tf_op jit(solution)/shard_map/ppermute | solution.py:21
  132.9 19.4 %collective-permute-start.22 = (bf16[24,1024]{1,0:T(8,128)(2,1)}, bf16[24,1024]{1,0:T(8,128)(2,1)S(1)}, u32[]{:S(2)}, u32[]{:S(2)}) collective-permute-start(bf16[24,1024]{1,0:T(8,128)(2,1)} %get-tuple-element.74), channel_id=1, source_target_pairs={{0,8},{4,12},{8,0},{12,4},{1,9},{5,13},{9,1},{13,5},{2,10},{6,14},... | collective-permute-start | bytes 147464 | tf_op jit(solution)/shard_map/ppermute | solution.py:27
  151.1 5.3 %collective-permute-start.23 = (bf16[24,1024]{1,0:T(8,128)(2,1)S(1)}, bf16[24,1024]{1,0:T(8,128)(2,1)S(1)}, u32[]{:S(2)}, u32[]{:S(2)}) collective-permute-start(bf16[24,1024]{1,0:T(8,128)(2,1)S(1)} %get-tuple-element.73), channel_id=1, source_target_pairs={{0,4},{4,8},{8,12},{12,0},{1,5},{5,9},{9,13},{13,1},{2,6},{6,10},{... | collective-permute-start | bytes 147464 | tf_op jit(solution)/shard_map/ppermute | solution.py:27
  159.3 7.9 %collective-permute-start.16 = (bf16[128,1536]{1,0:T(8,128)(2,1)S(1)}, bf16[128,1536]{1,0:T(8,128)(2,1)S(1)}, u32[]{:S(2)}, u32[]{:S(2)}) collective-permute-start(bf16[128,1536]{1,0:T(8,128)(2,1)S(1)} %get-tuple-element.52), channel_id=1, source_target_pairs={{0,64},{64,0},{1,65},{65,1},{2,66},{66,2},{3,67},{67,3},{4,68},{68... | collective-permute-start | bytes 1179656 | tf_op jit(solution)/shard_map/ppermute | solution.py:31
  (17 other events, 21.2 us)

commit v3 on v2

--- a/solution.py
+++ b/solution.py
@@ -261,7 +261,6 @@
         "saaaa" + "a" * len(after),
         [shape(rows // 2, cols, dtype=F32), shape(rows // 2, cols)],
         [pltpu.VMEM((rows, cols), F32), pltpu.VMEM((3, rows, cols), BF), sems(4)],
-        moved=10 * rows * cols,
         limit=12,
     )(at, *parts, *after)
 
@@ -304,19 +303,10 @@
         moved=4 * width * inner,
         limit=18,
     )(packed[4], gate_up)
-    sent, sent_mark = call(
-        pack_g,
-        "aaaaaaa",
-        [shape(4, rows, part + inner), MARK],
-        [sems(20)],
-        moved=4 * rows * width,
-        placed=(0,),
-    )(*gs, hidden, xa[1], xa[3])
-    both = lax.all_to_all(sent, "y", split_axis=0, concat_axis=0, tiled=True)
     n = inner // 256
     dact, mark = call(
         dh_step,
-        "aaaaaaaa",
+        "aaaaaaa",
         [shape(2, rows, inner), MARK],
         [
             pltpu.VMEM((rows, width), BF),
@@ -328,8 +318,17 @@
         flops=2 * rows * width * inner,
         moved=2 * width * inner,
         limit=14,
-    )(*gs, slope, silu, down_proj, sent_mark)
+    )(*gs, slope, silu, down_proj)
     da = [shift(dact, "x", j) for j in range(4)]
+    sent, sent_mark = call(
+        pack_g,
+        "aaaaaaaaa",
+        [shape(4, rows, part + inner), MARK],
+        [sems(20)],
+        moved=4 * rows * width,
+        placed=(0,),
+    )(*gs, hidden, *xa[1:], mark)
+    both = lax.all_to_all(sent, "y", split_axis=0, concat_axis=0, tiled=True)
     n = width // 512
     *back, back_mark = call(
         back_step,
@@ -339,8 +338,10 @@
         flops=4 * rows * width * inner,
         moved=4 * width * inner,
         limit=18,
-    )(dact, gate_up, swap_expert(mark, 1))
-    *parts, mark = call(
+    )(dact, gate_up, sent_mark)
+    parts, mark = tile_call(xa, da, [back_mark])
+    gate = lax.all_to_all(parts, "y", split_axis=0, concat_axis=0, tiled=True)
+    *parts, _ = call(
         down_step,
         "saa",
         [shape(192, part, dtype=F32)] + [shape(192, part)] * 3 + [MARK],
@@ -353,17 +354,14 @@
         flops=8 * rows * part * inner,
         moved=8 * rows * (part + inner),
         limit=16,
-    )(at, both, back_mark)
+    )(at, both, mark)
     down = [parts[0]] + [shift(parts[j], "x", j) for j in (1, 2, 3)]
-    parts, _ = tile_call(xa, da, [mark])
-    gate = lax.all_to_all(parts, "y", split_axis=0, concat_axis=0, tiled=True)
     arrived = [back[0]] + [swap_expert(back[k], k) for k in (1, 2, 3)]
     keep, send, mark = call(
         gate_sum,
         "sa",
         [shape(128, 2 * inner, dtype=F32), shape(128, 2 * inner), MARK],
         [pltpu.VMEM((4, 256, 2 * inner), BF), sems(4)],
-        moved=16 * 256 * inner,
         limit=12,
     )(at, gate)
     gate_up_grad = (keep + swap_w(send).astype(F32)).astype(BF)
@@ -372,8 +370,6 @@
         "vaaaaa",
         [shape(toks, width)],
         [pltpu.VMEM((rows, width), BF), sems(4)],
-        flops=2 * toks * rows * width,
-        moved=2 * (rows + toks) * width,
     )(mask, *arrived, mark)[0]
 
     keep, send = sum_call(at, down, [])

time: 169 us -> 164 us (0.970); the launches traced: 168 us -> 161 us
  local copies, waits for them, and re-layouts: 15.3 us -> 5.66 us
  starting transfers between devices: 41.8 us -> 46.4 us
  Pallas kernels: 42.4 us -> 40 us
    unnamed x53 -> x43, local copies, waits for them, and re-layouts: 12 us -> 2.29 us
    all_to_all x1, waiting for transfers between devices: 9.45 us -> 0.01 us  [shards(): both = lax.all_to_all(sent, 'y', split_axis=0, concat_axis=0, tiled=True)]
    ppermute x12, waiting for transfers between devices: 30.4 us -> 39.1 us  [shift(): return lax.ppermute(a, axis, [(i, (i + j) % 4) for i in range(4)])]
    ppermute x10 -> x9, waiting for transfers between devices: 14.2 us -> 22.8 us  [swap_expert(): return lax.ppermute(a, ('v', 'c'), [(i, i ^ k) for i in range(4)])]
    ppermute x2, waiting for transfers between devices: 8.04 us -> 1.04 us  [swap_w(): return lax.ppermute(a, 'w', [(0, 1), (1, 0)])]
    ppermute x12, starting transfers between devices: 18.3 us -> 22 us  [shift(): return lax.ppermute(a, axis, [(i, (i + j) % 4) for i in range(4)])]
    pallas_call x1, Pallas kernels: 7.08 us -> 5.26 us  [tile_call(): call(tile_step, 'a' * (8 + len(after)), [shape(4, 256, wide), MARK], [plt...]
    ppermute x10 -> x9, starting transfers between devices: 11.3 us -> 11.3 us  [swap_expert(): return lax.ppermute(a, ('v', 'c'), [(i, i ^ k) for i in range(4)])]
  transfers between devices with their start and end apart: 26 -> 25, of which waited for: 12 -> 13; matrix products, arithmetic and copies ran while one was open for 3% -> 3% of each run, Pallas kernels for 24% -> 24%
where the time goes in v3:
time: 164 us; the launch traced here: 161 us
  waiting for transfers between devices  63 us (38%)
  starting transfers between devices  46.4 us (28%)
  Pallas kernels  40 us (24%)
  local copies, waits for them, and re-layouts  5.66 us (3%)
  other arithmetic  3.83 us (2%)
    ppermute x12, waiting for transfers between devices, shift(): return lax.ppermute(a, axis, [(i, (i + j) % 4) for i in range(4)])  39.1 us
    ppermute x9, waiting for transfers between devices, swap_expert(): return lax.ppermute(a, ('v', 'c'), [(i, i ^ k) for i in range(4)])  22.8 us
    ppermute x12, starting transfers between devices, shift(): return lax.ppermute(a, axis, [(i, (i + j) % 4) for i in range(4)])  22 us
    ppermute x9, starting transfers between devices, swap_expert(): return lax.ppermute(a, ('v', 'c'), [(i, i ^ k) for i in range(4)])  11.3 us
    pallas_call x1, Pallas kernels, shards(): call(back_step, 'vaa', [shape(CAP, width)] * 4 + [MARK], [pltpu.VMEM((n,...  7.77 us
    pallas_call x1, Pallas kernels, shards(): call(act_step, 'va', [shape(rows, inner), shape(rows, inner, dtype=F32),...  7.42 us
    pallas_call x1, Pallas kernels, tile_call(): call(tile_step, 'a' * (8 + len(after)), [shape(4, 256, wide), MARK], [plt...  5.26 us
    pallas_call x1, Pallas kernels, shards(): call(dh_step, 'aaaaaaa', [shape(2, rows, inner), MARK], [pltpu.VMEM((rows...  5.09 us
  transfers between devices with their start and end apart: 25, of which 13 were waited for; matrix products, arithmetic and copies ran while one was open for 3% of the time, Pallas kernels for 24%

profile of v3, /device:TPU:0, one launch (start us, length us, event | category | flops | bytes accessed | tf_op | source)
XLA Modules:
  0.0 161.2 jit_solution(11373036838030733582)
XLA Ops:
  4.0 4.0 %collective-permute-start.4 = (bf16[48,4096]{1,0:T(8,128)(2,1)}, bf16[48,4096]{1,0:T(8,128)(2,1)}, u32[]{:S(2)}, u32[]{:S(2)}) collective-permute-start(bf16[48,4096]{1,0:T(8,128)(2,1)} %get-tuple-element.62), channel_id=1, source_target_pairs={{0,2},{1,3},{2,0},{3,1},{4,6},{5,7},{6,4},{7,5},{8,10},{9,11},{10,... | collective-permute-start | bytes 1179656 | tf_op jit(solution)/shard_map/ppermute | solution.py:21
  10.2 3.4 %collective-permute-start.1 = (bf16[48,4096]{1,0:T(8,128)(2,1)}, bf16[48,4096]{1,0:T(8,128)(2,1)S(1)}, u32[]{:S(2)}, u32[]{:S(2)}) collective-permute-start(bf16[48,4096]{1,0:T(8,128)(2,1)} %get-tuple-element.66), channel_id=1, source_target_pairs={{0,2},{1,3},{2,0},{3,1},{4,6},{5,7},{6,4},{7,5},{8,10},{9,11},{10,... | collective-permute-start | bytes 1179656 | tf_op jit(solution)/shard_map/ppermute | solution.py:21
  13.6 4.6 %collective-permute-done.4.x2 = bf16[48,4096]{1,0:T(8,128)(2,1)} collective-permute-done((bf16[48,4096]{1,0:T(8,128)(2,1)}, bf16[48,4096]{1,0:T(8,128)(2,1)}, u32[]{:S(2)}, u32[]{:S(2)}) %collective-permute-start.4) | collective-permute-done | bytes 393248 | tf_op jit(solution)/shard_map/ppermute | solution.py:21
  18.2 8.1 %collective-permute-done.5.x3 = bf16[48,4096]{1,0:T(8,128)(2,1)} collective-permute-done((bf16[48,4096]{1,0:T(8,128)(2,1)}, bf16[48,4096]{1,0:T(8,128)(2,1)}, u32[]{:S(2)}, u32[]{:S(2)}) %collective-permute-start.5) | collective-permute-done | bytes 393248 | tf_op jit(solution)/shard_map/ppermute | solution.py:21
  29.9 2.7 %collective-permute-start.7 = (bf16[192,1024]{1,0:T(8,128)(2,1)S(1)}, bf16[192,1024]{1,0:T(8,128)(2,1)S(1)}, u32[]{:S(2)}, u32[]{:S(2)}) collective-permute-start(bf16[192,1024]{1,0:T(8,128)(2,1)S(1)} %get-tuple-element.37), channel_id=1, source_target_pairs={{0,32},{16,48},{32,0},{48,16},{1,33},{17,49},{33,1},{49,17},{2,34}... | collective-permute-start | bytes 1179656 | tf_op jit(solution)/shard_map/ppermute | solution.py:27
  34.1 7.4 %shard_map.86 = (bf16[192,768]{1,0:T(8,128)(2,1)S(1)}, f32[192,768]{1,0:T(8,128)S(1)}, f32[192,768]{1,0:T(8,128)S(1)}) custom-call(bf16[192,4096]{1,0:T(8,128)(2,1)S(1)} %get-tuple-element.31.x, bf16[4096,1536]{1,0:T(8,128)(2,1)} %bitcast.40), custom_call_target="tpu_custom_call" | custom-call | flops 2415919104 | bytes 12582912 | tf_op jit(solution)/shard_map/pallas_call | solution.py:297
  43.1 5.1 %shard_map.87 = (bf16[2,192,768]{2,1,0:T(8,128)(2,1)S(1)}, f32[8,128]{1,0:T(8,128)S(1)}) custom-call(bf16[48,4096]{1,0:T(8,128)(2,1)S(1)} %get-tuple-element.68.g0, bf16[48,4096]{1,0:T(8,128)(2,1)S(1)} %collective-permute-done.g1, bf16[48,4096]{1,0:T(8,128)(2,1)S(1)} %collective-permute-done.1.g2, bf16[48,4096]{1,0:T(8,128)(2,1)S(1)} %collective-permute-done.2.g3, ...), custom_call_target="tpu_custom_call" | custom-call | flops 1207959552 | bytes 6291456 | tf_op jit(solution)/shard_map/pallas_call | solution.py:307
  48.2 2.0 %collective-permute-done.7.rest_1_.refs_2_ = bf16[192,1024]{1,0:T(8,128)(2,1)S(1)} collective-permute-done((bf16[192,1024]{1,0:T(8,128)(2,1)S(1)}, bf16[192,1024]{1,0:T(8,128)(2,1)S(1)}, u32[]{:S(2)}, u32[]{:S(2)}) %collective-permute-start.7) | collective-permute-done | bytes 393248 | tf_op jit(solution)/shard_map/ppermute | solution.py:27
  50.2 1.7 %shard_map.88 = (bf16[4,192,1792]{2,1,0:T(8,128)(2,1)}, f32[8,128]{1,0:T(8,128)S(1)}) custom-call(bf16[48,4096]{1,0:T(8,128)(2,1)S(1)} %get-tuple-element.68.g0, bf16[48,4096]{1,0:T(8,128)(2,1)S(1)} %collective-permute-done.g1, bf16[48,4096]{1,0:T(8,128)(2,1)S(1)} %collective-permute-done.1.g2, bf16[48,4096]{1,0:T(8,128)(2,1)S(1)} %collective-permute-done.2.g3, ...), custom_call_target="tpu_custom_call" | custom-call | bytes 3145728 | tf_op jit(solution)/shard_map/pallas_call | solution.py:323
  52.0 4.6 %all-to-all-start.1 = ((bf16[4,192,1792]{2,1,0:T(8,128)(2,1)}), bf16[4,192,1792]{2,1,0:T(8,128)(2,1)}, u32[]{:S(2)}, u32[]{:S(2)}) async-start(bf16[4,192,1792]{2,1,0:T(8,128)(2,1)} %get-tuple-element.51), calls=%async_computation.1 | async-start | bytes 5505024 | tf_op jit(solution)/shard_map/all_to_all | solution.py:331
  58.0 2.4 %collective-permute-start.13 = (bf16[2,192,768]{2,1,0:T(8,128)(2,1)S(1)}, bf16[2,192,768]{2,1,0:T(8,128)(2,1)S(1)}, u32[]{:S(2)}, u32[]{:S(2)}) collective-permute-start(bf16[2,192,768]{2,1,0:T(8,128)(2,1)S(1)} %get-tuple-element.34.dact.refs_4_), channel_id=1, source_target_pairs={{0,32},{16,48},{32,0},{48,16},{1,33},{17,49},{33,1},{49,17},{2,34}... | collective-permute-start | bytes 1769480 | tf_op jit(solution)/shard_map/ppermute | solution.py:27
  62.0 7.8 %shard_map.89 = (bf16[48,4096]{1,0:T(8,128)(2,1)S(1)}, bf16[48,4096]{1,0:T(8,128)(2,1)}, bf16[48,4096]{1,0:T(8,128)(2,1)}, bf16[48,4096]{1,0:T(8,128)(2,1)S(1)}, f32[8,128]{1,0:T(8,128)S(1)}) custom-call(bf16[2,192,768]{2,1,0:T(8,128)(2,1)S(1)} %get-tuple-element.34.dact.refs_4_, bf16[4096,1536]{1,0:T(8,128)(2,1)} %bitcast.41, ...), custom_call_target="tpu_custom_call" | custom-call | flops 2415919104 | bytes 12582912 | tf_op jit(solution)/shard_map/pallas_call | solution.py:333
  70.5 2.0 %collective-permute-done.12.refs_5_ = bf16[2,192,768]{2,1,0:T(8,128)(2,1)S(1)} collective-permute-done((bf16[2,192,768]{2,1,0:T(8,128)(2,1)S(1)}, bf16[2,192,768]{2,1,0:T(8,128)(2,1)S(1)}, u32[]{:S(2)}, u32[]{:S(2)}) %collective-permute-start.12) | collective-permute-done | bytes 589856 | tf_op jit(solution)/shard_map/ppermute | solution.py:27
  72.5 13.8 %collective-permute-done.13.refs_6_ = bf16[2,192,768]{2,1,0:T(8,128)(2,1)S(1)} collective-permute-done((bf16[2,192,768]{2,1,0:T(8,128)(2,1)S(1)}, bf16[2,192,768]{2,1,0:T(8,128)(2,1)S(1)}, u32[]{:S(2)}, u32[]{:S(2)}) %collective-permute-start.13) | collective-permute-done | bytes 589856 | tf_op jit(solution)/shard_map/ppermute | solution.py:27
  86.3 5.3 %shard_map.90 = (bf16[4,256,1536]{2,1,0:T(8,128)(2,1)}, f32[8,128]{1,0:T(8,128)S(1)}) custom-call(bf16[192,1024]{1,0:T(8,128)(2,1)S(1)} %copy-done.10, bf16[192,1024]{1,0:T(8,128)(2,1)S(1)} %copy-done.2, bf16[192,1024]{1,0:T(8,128)(2,1)S(1)} %copy-done.4, bf16[192,1024]{1,0:T(8,128)(2,1)S(1)} %copy-done.6, ...), custom_call_target="tpu_custom_call" | custom-call | flops 2415919104 | bytes 3932160 | tf_op jit(solution)/shard_map/pallas_call | solution.py:192
  91.6 4.7 %all-to-all-start = ((bf16[4,256,1536]{2,1,0:T(8,128)(2,1)}), bf16[4,256,1536]{2,1,0:T(8,128)(2,1)}, u32[]{:S(2)}, u32[]{:S(2)}) async-start(bf16[4,256,1536]{2,1,0:T(8,128)(2,1)} %get-tuple-element.47), calls=%async_computation | async-start | bytes 6291456 | tf_op jit(solution)/shard_map/all_to_all | solution.py:343
  96.2 4.5 %shard_map.93 = (f32[192,1024]{1,0:T(8,128)S(1)}, bf16[192,1024]{1,0:T(8,128)(2,1)S(1)}, bf16[192,1024]{1,0:T(8,128)(2,1)S(1)}, bf16[192,1024]{1,0:T(8,128)(2,1)S(1)}, f32[8,128]{1,0:T(8,128)}) custom-call(s32[4]{0:T(128)S(1)} %pad_add_fusion.at, bf16[4,192,1792]{2,1,0:T(8,128)(2,1)} %all-to-all-done.1.both, f32[8,128]{1,0:T(8,128)S(1)} %get-tuple-element.52.rest_0_), custom_call_target="tpu_custom_call" | custom-call | flops 1207959552 | bytes 2752512 | tf_op jit(solution)/shard_map/pallas_call | solution.py:344
  102.0 2.4 %collective-permute-start.17 = (bf16[192,1024]{1,0:T(8,128)(2,1)S(1)}, bf16[192,1024]{1,0:T(8,128)(2,1)S(1)}, u32[]{:S(2)}, u32[]{:S(2)}) collective-permute-start(bf16[192,1024]{1,0:T(8,128)(2,1)S(1)} %get-tuple-element.55), channel_id=1, source_target_pairs={{0,32},{16,48},{32,0},{48,16},{1,33},{17,49},{33,1},{49,17},{2,34}... | collective-permute-start | bytes 1179656 | tf_op jit(solution)/shard_map/ppermute | solution.py:27
  105.3 7.1 %collective-permute-done.16.r1 = bf16[192,1024]{1,0:T(8,128)(2,1)S(1)} collective-permute-done((bf16[192,1024]{1,0:T(8,128)(2,1)S(1)}, bf16[192,1024]{1,0:T(8,128)(2,1)S(1)}, u32[]{:S(2)}, u32[]{:S(2)}) %collective-permute-start.16) | collective-permute-done | bytes 393248 | tf_op jit(solution)/shard_map/ppermute | solution.py:27
  112.3 9.6 %collective-permute-done.17.r2 = bf16[192,1024]{1,0:T(8,128)(2,1)S(1)} collective-permute-done((bf16[192,1024]{1,0:T(8,128)(2,1)S(1)}, bf16[192,1024]{1,0:T(8,128)(2,1)S(1)}, u32[]{:S(2)}, u32[]{:S(2)}) %collective-permute-start.17) | collective-permute-done | bytes 393248 | tf_op jit(solution)/shard_map/ppermute | solution.py:27
  122.0 2.0 %shard_map.94 = (f32[96,1024]{1,0:T(8,128)S(1)}, bf16[96,1024]{1,0:T(8,128)(2,1)}) custom-call(s32[4]{0:T(128)S(1)} %pad_add_fusion.at, f32[192,1024]{1,0:T(8,128)S(1)} %get-tuple-element.53.own, bf16[192,1024]{1,0:T(8,128)(2,1)S(1)} %collective-permute-done.16.r1, bf16[192,1024]{1,0:T(8,128)(2,1)S(1)} %collective-permute-done.17.r2, ...), custom_call_target="tpu_custom_call" | custom-call | tf_op jit(solution)/shard_map/pallas_call | solution.py:259
  123.9 2.0 %collective-permute-start.19 = (bf16[96,1024]{1,0:T(8,128)(2,1)}, bf16[96,1024]{1,0:T(8,128)(2,1)}, u32[]{:S(2)}, u32[]{:S(2)}) collective-permute-start(bf16[96,1024]{1,0:T(8,128)(2,1)} %get-tuple-element.58), channel_id=1, source_target_pairs={{0,64},{64,0},{1,65},{65,1},{2,66},{66,2},{3,67},{67,3},{4,68},{68... | collective-permute-start | bytes 589832 | tf_op jit(solution)/shard_map/ppermute | solution.py:31
  125.9 3.6 %collective-permute-start.10 = (bf16[48,4096]{1,0:T(8,128)(2,1)}, bf16[48,4096]{1,0:T(8,128)(2,1)S(1)}, u32[]{:S(2)}, u32[]{:S(2)}) collective-permute-start(bf16[48,4096]{1,0:T(8,128)(2,1)} %get-tuple-element.43), channel_id=1, source_target_pairs={{0,2},{1,3},{2,0},{3,1},{4,6},{5,7},{6,4},{7,5},{8,10},{9,11},{10,... | collective-permute-start | bytes 1179656 | tf_op jit(solution)/shard_map/ppermute | solution.py:21
  133.0 2.8 %collective-permute-start.20 = (bf16[24,1024]{1,0:T(8,128)(2,1)}, bf16[24,1024]{1,0:T(8,128)(2,1)S(1)}, u32[]{:S(2)}, u32[]{:S(2)}) collective-permute-start(bf16[24,1024]{1,0:T(8,128)(2,1)} %get-tuple-element.75), channel_id=1, source_target_pairs={{0,12},{4,0},{8,4},{12,8},{1,13},{5,1},{9,5},{13,9},{2,14},{6,2},{... | collective-permute-start | bytes 147464 | tf_op jit(solution)/shard_map/ppermute | solution.py:27
  135.9 2.8 %shard_map.91 = (f32[128,1536]{1,0:T(8,128)S(1)}, bf16[128,1536]{1,0:T(8,128)(2,1)S(1)}, f32[8,128]{1,0:T(8,128)S(1)}) custom-call(s32[4]{0:T(128)S(1)} %pad_add_fusion.at, bf16[4,256,1536]{2,1,0:T(8,128)(2,1)} %all-to-all-done.parts), custom_call_target="tpu_custom_call" | custom-call | tf_op jit(solution)/shard_map/pallas_call | solution.py:360
  138.7 1.8 %collective-permute-start.15 = (bf16[128,1536]{1,0:T(8,128)(2,1)S(1)}, bf16[128,1536]{1,0:T(8,128)(2,1)S(1)}, u32[]{:S(2)}, u32[]{:S(2)}) collective-permute-start(bf16[128,1536]{1,0:T(8,128)(2,1)S(1)} %get-tuple-element.50), channel_id=1, source_target_pairs={{0,64},{64,0},{1,65},{65,1},{2,66},{66,2},{3,67},{67,3},{4,68},{68... | collective-permute-start | bytes 1179656 | tf_op jit(solution)/shard_map/ppermute | solution.py:31
  140.5 3.5 %collective-permute-done.10.a2 = bf16[48,4096]{1,0:T(8,128)(2,1)S(1)} collective-permute-done((bf16[48,4096]{1,0:T(8,128)(2,1)}, bf16[48,4096]{1,0:T(8,128)(2,1)S(1)}, u32[]{:S(2)}, u32[]{:S(2)}) %collective-permute-start.10) | collective-permute-done | bytes 393248 | tf_op jit(solution)/shard_map/ppermute | solution.py:21
  143.9 5.1 %collective-permute-done.11.a3 = bf16[48,4096]{1,0:T(8,128)(2,1)S(1)} collective-permute-done((bf16[48,4096]{1,0:T(8,128)(2,1)S(1)}, bf16[48,4096]{1,0:T(8,128)(2,1)S(1)}, u32[]{:S(2)}, u32[]{:S(2)}) %collective-permute-start.11) | collective-permute-done | bytes 393248 | tf_op jit(solution)/shard_map/ppermute | solution.py:21
  149.1 2.2 %shard_map.92 = bf16[128,4096]{1,0:T(8,128)(2,1)} custom-call(bf16[128,192]{1,0:T(8,128)(2,1)S(1)} %get-tuple-element.59.mask, bf16[48,4096]{1,0:T(8,128)(2,1)S(1)} %get-tuple-element.41.a0, bf16[48,4096]{1,0:T(8,128)(2,1)S(1)} %collective-permute-done.9.a1, bf16[48,4096]{1,0:T(8,128)(2,1)S(1)} %collective-permute-done.10.a2, ...), custom_call_target="tpu_custom_call" | custom-call | tf_op jit(solution)/shard_map/pallas_call | solution.py:368
  151.3 2.4 %collective-permute-start.21 = (bf16[24,1024]{1,0:T(8,128)(2,1)S(1)}, bf16[24,1024]{1,0:T(8,128)(2,1)S(1)}, u32[]{:S(2)}, u32[]{:S(2)}) collective-permute-start(bf16[24,1024]{1,0:T(8,128)(2,1)S(1)} %copy-done.15), channel_id=1, source_target_pairs={{0,8},{4,12},{8,0},{12,4},{1,9},{5,13},{9,1},{13,5},{2,10},{6,14},... | collective-permute-start | bytes 147464 | tf_op jit(solution)/shard_map/ppermute | solution.py:27
  154.9 2.1 %collective-permute-done.21 = bf16[24,1024]{1,0:T(8,128)(2,1)S(1)} collective-permute-done((bf16[24,1024]{1,0:T(8,128)(2,1)S(1)}, bf16[24,1024]{1,0:T(8,128)(2,1)S(1)}, u32[]{:S(2)}, u32[]{:S(2)}) %collective-permute-start.21) | collective-permute-done | bytes 49184 | tf_op jit(solution)/shard_map/ppermute | solution.py:27
  157.0 2.6 %collective-permute-done.22 = bf16[24,1024]{1,0:T(8,128)(2,1)S(1)} collective-permute-done((bf16[24,1024]{1,0:T(8,128)(2,1)S(1)}, bf16[24,1024]{1,0:T(8,128)(2,1)S(1)}, u32[]{:S(2)}, u32[]{:S(2)}) %collective-permute-start.22) | collective-permute-done | bytes 49184 | tf_op jit(solution)/shard_map/ppermute | solution.py:27
  (99 shorter events, 24.3 us)
Async XLA Ops:
  4.0 9.6 %collective-permute-start.3 = (bf16[48,4096]{1,0:T(8,128)(2,1)S(1)}, bf16[48,4096]{1,0:T(8,128)(2,1)S(1)}, u32[]{:S(2)}, u32[]{:S(2)}) collective-permute-start(bf16[48,4096]{1,0:T(8,128)(2,1)S(1)} %get-tuple-element.63), channel_id=1, source_target_pairs={{0,1},{1,0},{2,3},{3,2},{4,5},{5,4},{6,7},{7,6},{8,9},{9,8},{10,11... | collective-permute-start | bytes 1179656 | tf_op jit(solution)/shard_map/ppermute | solution.py:21
  4.0 14.2 %collective-permute-start.4 = (bf16[48,4096]{1,0:T(8,128)(2,1)}, bf16[48,4096]{1,0:T(8,128)(2,1)}, u32[]{:S(2)}, u32[]{:S(2)}) collective-permute-start(bf16[48,4096]{1,0:T(8,128)(2,1)} %get-tuple-element.62), channel_id=1, source_target_pairs={{0,2},{1,3},{2,0},{3,1},{4,6},{5,7},{6,4},{7,5},{8,10},{9,11},{10,... | collective-permute-start | bytes 1179656 | tf_op jit(solution)/shard_map/ppermute | solution.py:21
  8.0 18.3 %collective-permute-start.5 = (bf16[48,4096]{1,0:T(8,128)(2,1)}, bf16[48,4096]{1,0:T(8,128)(2,1)}, u32[]{:S(2)}, u32[]{:S(2)}) collective-permute-start(bf16[48,4096]{1,0:T(8,128)(2,1)} %get-tuple-element.61), channel_id=1, source_target_pairs={{0,3},{1,2},{2,1},{3,0},{4,7},{5,6},{6,5},{7,4},{8,11},{9,10},{10,... | collective-permute-start | bytes 1179656 | tf_op jit(solution)/shard_map/ppermute | solution.py:21
  10.1 22.6 %collective-permute-start = (bf16[48,4096]{1,0:T(8,128)(2,1)}, bf16[48,4096]{1,0:T(8,128)(2,1)S(1)}, u32[]{:S(2)}, u32[]{:S(2)}) collective-permute-start(bf16[48,4096]{1,0:T(8,128)(2,1)} %get-tuple-element.67), channel_id=1, source_target_pairs={{0,1},{1,0},{2,3},{3,2},{4,5},{5,4},{6,7},{7,6},{8,9},{9,8},{10,11... | collective-permute-start | bytes 1179656 | tf_op jit(solution)/shard_map/ppermute | solution.py:21
  10.2 31.3 %collective-permute-start.1 = (bf16[48,4096]{1,0:T(8,128)(2,1)}, bf16[48,4096]{1,0:T(8,128)(2,1)S(1)}, u32[]{:S(2)}, u32[]{:S(2)}) collective-permute-start(bf16[48,4096]{1,0:T(8,128)(2,1)} %get-tuple-element.66), channel_id=1, source_target_pairs={{0,2},{1,3},{2,0},{3,1},{4,6},{5,7},{6,4},{7,5},{8,10},{9,11},{10,... | collective-permute-start | bytes 1179656 | tf_op jit(solution)/shard_map/ppermute | solution.py:21
  13.6 29.5 %collective-permute-start.2 = (bf16[48,4096]{1,0:T(8,128)(2,1)}, bf16[48,4096]{1,0:T(8,128)(2,1)S(1)}, u32[]{:S(2)}, u32[]{:S(2)}) collective-permute-start(bf16[48,4096]{1,0:T(8,128)(2,1)} %get-tuple-element.65), channel_id=1, source_target_pairs={{0,3},{1,2},{2,1},{3,0},{4,7},{5,6},{6,5},{7,4},{8,11},{9,10},{10,... | collective-permute-start | bytes 1179656 | tf_op jit(solution)/shard_map/ppermute | solution.py:21
  28.4 19.8 %collective-permute-start.6 = (bf16[192,1024]{1,0:T(8,128)(2,1)S(1)}, bf16[192,1024]{1,0:T(8,128)(2,1)S(1)}, u32[]{:S(2)}, u32[]{:S(2)}) collective-permute-start(bf16[192,1024]{1,0:T(8,128)(2,1)S(1)} %get-tuple-element.36), channel_id=1, source_target_pairs={{0,16},{16,32},{32,48},{48,0},{1,17},{17,33},{33,49},{49,1},{2,18}... | collective-permute-start | bytes 1179656 | tf_op jit(solution)/shard_map/ppermute | solution.py:27
  29.9 20.3 %collective-permute-start.7 = (bf16[192,1024]{1,0:T(8,128)(2,1)S(1)}, bf16[192,1024]{1,0:T(8,128)(2,1)S(1)}, u32[]{:S(2)}, u32[]{:S(2)}) collective-permute-start(bf16[192,1024]{1,0:T(8,128)(2,1)S(1)} %get-tuple-element.37), channel_id=1, source_target_pairs={{0,32},{16,48},{32,0},{48,16},{1,33},{17,49},{33,1},{49,17},{2,34}... | collective-permute-start | bytes 1179656 | tf_op jit(solution)/shard_map/ppermute | solution.py:27
  32.6 17.6 %collective-permute-start.8 = (bf16[192,1024]{1,0:T(8,128)(2,1)S(1)}, bf16[192,1024]{1,0:T(8,128)(2,1)S(1)}, u32[]{:S(2)}, u32[]{:S(2)}) collective-permute-start(bf16[192,1024]{1,0:T(8,128)(2,1)S(1)} %get-tuple-element.38), channel_id=1, source_target_pairs={{0,48},{16,0},{32,16},{48,32},{1,49},{17,1},{33,17},{49,33},{2,50}... | collective-permute-start | bytes 1179656 | tf_op jit(solution)/shard_map/ppermute | solution.py:27
  52.0 39.5 %all-to-all-start.1 = ((bf16[4,192,1792]{2,1,0:T(8,128)(2,1)}), bf16[4,192,1792]{2,1,0:T(8,128)(2,1)}, u32[]{:S(2)}, u32[]{:S(2)}) async-start(bf16[4,192,1792]{2,1,0:T(8,128)(2,1)} %get-tuple-element.51), calls=%async_computation.1 | async-start | bytes 5505024 | tf_op jit(solution)/shard_map/all_to_all | solution.py:331
  56.6 15.9 %collective-permute-start.12 = (bf16[2,192,768]{2,1,0:T(8,128)(2,1)S(1)}, bf16[2,192,768]{2,1,0:T(8,128)(2,1)S(1)}, u32[]{:S(2)}, u32[]{:S(2)}) collective-permute-start(bf16[2,192,768]{2,1,0:T(8,128)(2,1)S(1)} %get-tuple-element.34.dact.refs_4_), channel_id=1, source_target_pairs={{0,16},{16,32},{32,48},{48,0},{1,17},{17,33},{33,49},{49,1},{2,18}... | collective-permute-start | bytes 1769480 | tf_op jit(solution)/shard_map/ppermute | solution.py:27
  58.0 28.2 %collective-permute-start.13 = (bf16[2,192,768]{2,1,0:T(8,128)(2,1)S(1)}, bf16[2,192,768]{2,1,0:T(8,128)(2,1)S(1)}, u32[]{:S(2)}, u32[]{:S(2)}) collective-permute-start(bf16[2,192,768]{2,1,0:T(8,128)(2,1)S(1)} %get-tuple-element.34.dact.refs_4_), channel_id=1, source_target_pairs={{0,32},{16,48},{32,0},{48,16},{1,33},{17,49},{33,1},{49,17},{2,34}... | collective-permute-start | bytes 1769480 | tf_op jit(solution)/shard_map/ppermute | solution.py:27
  60.4 25.9 %collective-permute-start.14 = (bf16[2,192,768]{2,1,0:T(8,128)(2,1)S(1)}, bf16[2,192,768]{2,1,0:T(8,128)(2,1)S(1)}, u32[]{:S(2)}, u32[]{:S(2)}) collective-permute-start(bf16[2,192,768]{2,1,0:T(8,128)(2,1)S(1)} %get-tuple-element.34.dact.refs_4_), channel_id=1, source_target_pairs={{0,48},{16,0},{32,16},{48,32},{1,49},{17,1},{33,17},{49,33},{2,50}... | collective-permute-start | bytes 1769480 | tf_op jit(solution)/shard_map/ppermute | solution.py:27
  61.9 24.3 %copy-start.2 = (bf16[192,1024]{1,0:T(8,128)(2,1)S(1)}, bf16[192,1024]{1,0:T(8,128)(2,1)}, u32[]{:S(2)}) copy-start(bf16[192,1024]{1,0:T(8,128)(2,1)} %copy-done.1) | copy-start | bytes 1179652
  62.0 24.3 %copy-start.4 = (bf16[192,1024]{1,0:T(8,128)(2,1)S(1)}, bf16[192,1024]{1,0:T(8,128)(2,1)}, u32[]{:S(2)}) copy-start(bf16[192,1024]{1,0:T(8,128)(2,1)} %copy-done.3) | copy-start | bytes 1179652
  62.0 24.3 %copy-start.6 = (bf16[192,1024]{1,0:T(8,128)(2,1)S(1)}, bf16[192,1024]{1,0:T(8,128)(2,1)}, u32[]{:S(2)}) copy-start(bf16[192,1024]{1,0:T(8,128)(2,1)} %copy-done.5) | copy-start | bytes 1179652
  62.0 24.3 %copy-start.10 = (bf16[192,1024]{1,0:T(8,128)(2,1)S(1)}, bf16[192,1024]{1,0:T(8,128)(2,1)}, u32[]{:S(2)}) copy-start(bf16[192,1024]{1,0:T(8,128)(2,1)} %copy-done.9) | copy-start | bytes 1179652
  91.6 44.3 %all-to-all-start = ((bf16[4,256,1536]{2,1,0:T(8,128)(2,1)}), bf16[4,256,1536]{2,1,0:T(8,128)(2,1)}, u32[]{:S(2)}, u32[]{:S(2)}) async-start(bf16[4,256,1536]{2,1,0:T(8,128)(2,1)} %get-tuple-element.47), calls=%async_computation | async-start | bytes 6291456 | tf_op jit(solution)/shard_map/all_to_all | solution.py:343
  96.2 33.3 %copy-start.8 = (bf16[48,4096]{1,0:T(8,128)(2,1)S(1)}, bf16[48,4096]{1,0:T(8,128)(2,1)}, u32[]{:S(2)}) copy-start(bf16[48,4096]{1,0:T(8,128)(2,1)} %copy-done.7) | copy-start | bytes 1179652
  100.7 11.6 %collective-permute-start.16 = (bf16[192,1024]{1,0:T(8,128)(2,1)S(1)}, bf16[192,1024]{1,0:T(8,128)(2,1)S(1)}, u32[]{:S(2)}, u32[]{:S(2)}) collective-permute-start(bf16[192,1024]{1,0:T(8,128)(2,1)S(1)} %get-tuple-element.54), channel_id=1, source_target_pairs={{0,16},{16,32},{32,48},{48,0},{1,17},{17,33},{33,49},{49,1},{2,18}... | collective-permute-start | bytes 1179656 | tf_op jit(solution)/shard_map/ppermute | solution.py:27
  102.0 20.0 %collective-permute-start.17 = (bf16[192,1024]{1,0:T(8,128)(2,1)S(1)}, bf16[192,1024]{1,0:T(8,128)(2,1)S(1)}, u32[]{:S(2)}, u32[]{:S(2)}) collective-permute-start(bf16[192,1024]{1,0:T(8,128)(2,1)S(1)} %get-tuple-element.55), channel_id=1, source_target_pairs={{0,32},{16,48},{32,0},{48,16},{1,33},{17,49},{33,1},{49,17},{2,34}... | collective-permute-start | bytes 1179656 | tf_op jit(solution)/shard_map/ppermute | solution.py:27
  104.4 17.5 %collective-permute-start.18 = (bf16[192,1024]{1,0:T(8,128)(2,1)S(1)}, bf16[192,1024]{1,0:T(8,128)(2,1)S(1)}, u32[]{:S(2)}, u32[]{:S(2)}) collective-permute-start(bf16[192,1024]{1,0:T(8,128)(2,1)S(1)} %get-tuple-element.56), channel_id=1, source_target_pairs={{0,48},{16,0},{32,16},{48,32},{1,49},{17,1},{33,17},{49,33},{2,50}... | collective-permute-start | bytes 1179656 | tf_op jit(solution)/shard_map/ppermute | solution.py:27
  123.9 6.8 %collective-permute-start.19 = (bf16[96,1024]{1,0:T(8,128)(2,1)}, bf16[96,1024]{1,0:T(8,128)(2,1)}, u32[]{:S(2)}, u32[]{:S(2)}) collective-permute-start(bf16[96,1024]{1,0:T(8,128)(2,1)} %get-tuple-element.58), channel_id=1, source_target_pairs={{0,64},{64,0},{1,65},{65,1},{2,66},{66,2},{3,67},{67,3},{4,68},{68... | collective-permute-start | bytes 589832 | tf_op jit(solution)/shard_map/ppermute | solution.py:31
  125.9 14.6 %collective-permute-start.9 = (bf16[48,4096]{1,0:T(8,128)(2,1)}, bf16[48,4096]{1,0:T(8,128)(2,1)S(1)}, u32[]{:S(2)}, u32[]{:S(2)}) collective-permute-start(bf16[48,4096]{1,0:T(8,128)(2,1)} %get-tuple-element.42), channel_id=1, source_target_pairs={{0,1},{1,0},{2,3},{3,2},{4,5},{5,4},{6,7},{7,6},{8,9},{9,8},{10,11... | collective-permute-start | bytes 1179656 | tf_op jit(solution)/shard_map/ppermute | solution.py:21
  125.9 18.0 %collective-permute-start.10 = (bf16[48,4096]{1,0:T(8,128)(2,1)}, bf16[48,4096]{1,0:T(8,128)(2,1)S(1)}, u32[]{:S(2)}, u32[]{:S(2)}) collective-permute-start(bf16[48,4096]{1,0:T(8,128)(2,1)} %get-tuple-element.43), channel_id=1, source_target_pairs={{0,2},{1,3},{2,0},{3,1},{4,6},{5,7},{6,4},{7,5},{8,10},{9,11},{10,... | collective-permute-start | bytes 1179656 | tf_op jit(solution)/shard_map/ppermute | solution.py:21
  129.5 19.6 %collective-permute-start.11 = (bf16[48,4096]{1,0:T(8,128)(2,1)S(1)}, bf16[48,4096]{1,0:T(8,128)(2,1)S(1)}, u32[]{:S(2)}, u32[]{:S(2)}) collective-permute-start(bf16[48,4096]{1,0:T(8,128)(2,1)S(1)} %copy-done.8), channel_id=1, source_target_pairs={{0,3},{1,2},{2,1},{3,0},{4,7},{5,6},{6,5},{7,4},{8,11},{9,10},{10,... | collective-permute-start | bytes 1179656 | tf_op jit(solution)/shard_map/ppermute | solution.py:21
  133.0 21.9 %collective-permute-start.20 = (bf16[24,1024]{1,0:T(8,128)(2,1)}, bf16[24,1024]{1,0:T(8,128)(2,1)S(1)}, u32[]{:S(2)}, u32[]{:S(2)}) collective-permute-start(bf16[24,1024]{1,0:T(8,128)(2,1)} %get-tuple-element.75), channel_id=1, source_target_pairs={{0,12},{4,0},{8,4},{12,8},{1,13},{5,1},{9,5},{13,9},{2,14},{6,2},{... | collective-permute-start | bytes 147464 | tf_op jit(solution)/shard_map/ppermute | solution.py:27
  135.9 17.9 %copy-start.14 = (bf16[24,1024]{1,0:T(8,128)(2,1)S(1)}, bf16[24,1024]{1,0:T(8,128)(2,1)}, u32[]{:S(2)}) copy-start(bf16[24,1024]{1,0:T(8,128)(2,1)} %get-tuple-element.73) | copy-start | bytes 147460
  135.9 23.7 %copy-start.13 = (bf16[96,1024]{1,0:T(8,128)(2,1)S(1)}, bf16[96,1024]{1,0:T(8,128)(2,1)}, u32[]{:S(2)}) copy-start(bf16[96,1024]{1,0:T(8,128)(2,1)} %copy-done.12) | copy-start | bytes 589828
  138.7 21.7 %collective-permute-start.15 = (bf16[128,1536]{1,0:T(8,128)(2,1)S(1)}, bf16[128,1536]{1,0:T(8,128)(2,1)S(1)}, u32[]{:S(2)}, u32[]{:S(2)}) collective-permute-start(bf16[128,1536]{1,0:T(8,128)(2,1)S(1)} %get-tuple-element.50), channel_id=1, source_target_pairs={{0,64},{64,0},{1,65},{65,1},{2,66},{66,2},{3,67},{67,3},{4,68},{68... | collective-permute-start | bytes 1179656 | tf_op jit(solution)/shard_map/ppermute | solution.py:31
  151.3 5.7 %collective-permute-start.21 = (bf16[24,1024]{1,0:T(8,128)(2,1)S(1)}, bf16[24,1024]{1,0:T(8,128)(2,1)S(1)}, u32[]{:S(2)}, u32[]{:S(2)}) collective-permute-start(bf16[24,1024]{1,0:T(8,128)(2,1)S(1)} %copy-done.15), channel_id=1, source_target_pairs={{0,8},{4,12},{8,0},{12,4},{1,9},{5,13},{9,1},{13,5},{2,10},{6,14},... | collective-permute-start | bytes 147464 | tf_op jit(solution)/shard_map/ppermute | solution.py:27
  153.7 5.8 %collective-permute-start.22 = (bf16[24,1024]{1,0:T(8,128)(2,1)S(1)}, bf16[24,1024]{1,0:T(8,128)(2,1)S(1)}, u32[]{:S(2)}, u32[]{:S(2)}) collective-permute-start(bf16[24,1024]{1,0:T(8,128)(2,1)S(1)} %copy-done.14), channel_id=1, source_target_pairs={{0,4},{4,8},{8,12},{12,0},{1,5},{5,9},{9,13},{13,1},{2,6},{6,10},{... | collective-permute-start | bytes 147464 | tf_op jit(solution)/shard_map/ppermute | solution.py:27
  (11 other events, 44.3 us)

commit v4 on v3

--- a/solution.py
+++ b/solution.py
@@ -151,8 +151,8 @@
             outs[k][:, i * step : i * step + step] = got[k * CAP : k * CAP + CAP].astype(BF)
 
 
-def tok_step(mask, a0, a1, a2, a3, *rest):
-    out, whole, sem = rest[-3:]
+def tok_step(mask, a0, a1, a2, a3, out, mark, whole, sem):
+    mark[...] = jnp.zeros_like(mark)
     pieces = (a0, a1, a2, a3)
     land([(a, whole.at[pl.ds(k * CAP, CAP), :]) for k, a in enumerate(pieces)], sem)
     out[...] = jnp.dot(mask[...], whole[...], preferred_element_type=F32).astype(BF)
@@ -228,11 +228,11 @@
 
 
 def gate_sum(at, parts, keep, send, mark, g, sem):
+    mark[...] = jnp.zeros_like(mark)
     half = keep.shape[0]
     copies = fetch([(parts.at[i], g.at[i]) for i in range(4)], sem)
     for copy in copies:
         copy.wait()
-    mark[...] = jnp.zeros_like(mark)
 
     def part(i):
         return sum(g[p, aligned(i, half), :].astype(F32) for p in range(4))
@@ -263,6 +263,10 @@
         [pltpu.VMEM((rows, cols), F32), pltpu.VMEM((3, rows, cols), BF), sems(4)],
         limit=12,
     )(at, *parts, *after)
+
+
+def join_step(keep, theirs, mark, out):
+    out[...] = (keep[...] + theirs[...].astype(F32)).astype(BF)
 
 
 def shards(tokens, cotangent, routes, gates, gate_up, down_proj):
@@ -339,7 +343,8 @@
         moved=4 * width * inner,
         limit=18,
     )(dact, gate_up, sent_mark)
-    parts, mark = tile_call(xa, da, [back_mark])
+    arrived = [back[0]] + [swap_expert(back[k], k) for k in (1, 2, 3)]
+    parts, mark = tile_call(xa, da, [arrived[2]])
     gate = lax.all_to_all(parts, "y", split_axis=0, concat_axis=0, tiled=True)
     *parts, _ = call(
         down_step,
@@ -356,24 +361,25 @@
         limit=16,
     )(at, both, mark)
     down = [parts[0]] + [shift(parts[j], "x", j) for j in (1, 2, 3)]
-    arrived = [back[0]] + [swap_expert(back[k], k) for k in (1, 2, 3)]
-    keep, send, mark = call(
+    token_grad, tok_mark = call(
+        tok_step,
+        "vaaaa",
+        [shape(toks, width), MARK],
+        [pltpu.VMEM((rows, width), BF), sems(4)],
+    )(mask, *arrived)
+
+    gate_keep, gate_send, mark = call(
         gate_sum,
         "sa",
         [shape(128, 2 * inner, dtype=F32), shape(128, 2 * inner), MARK],
         [pltpu.VMEM((4, 256, 2 * inner), BF), sems(4)],
         limit=12,
     )(at, gate)
-    gate_up_grad = (keep + swap_w(send).astype(F32)).astype(BF)
-    token_grad = call(
-        tok_step,
-        "vaaaaa",
-        [shape(toks, width)],
-        [pltpu.VMEM((rows, width), BF), sems(4)],
-    )(mask, *arrived, mark)[0]
-
-    keep, send = sum_call(at, down, [])
-    down_grad = (keep + swap_w(send).astype(F32)).astype(BF).reshape(4, 24, part)
+    gate_up_grad = (gate_keep + swap_w(gate_send).astype(F32)).astype(BF)
+    keep, send = sum_call(at, down, [tok_mark])
+    down_grad = call(join_step, "vva", [shape(96, part)], moved=800 * part)(
+        keep, swap_w(send), mark
+    )[0].reshape(4, 24, part)
     cols = [
         shift(lax.dynamic_index_in_dim(down_grad, (y + j) % 4, 0, False), "y", j) for j in range(4)
     ]

time: 164 us -> 150 us (0.915)
  waiting for transfers between devices: 63 us -> 52.3 us
    ppermute x9, waiting for transfers between devices: 22.8 us -> 13.1 us  [swap_expert(): return lax.ppermute(a, ('v', 'c'), [(i, i ^ k) for i in range(4)])]
    all_to_all x1, waiting for transfers between devices: 0.01 us -> 5.06 us  [shards(): gate = lax.all_to_all(parts, 'y', split_axis=0, concat_axis=0, tiled=True)]
    ppermute x12, waiting for transfers between devices: 39.1 us -> 34.2 us  [shift(): return lax.ppermute(a, axis, [(i, (i + j) % 4) for i in range(4)])]
    ppermute x9, starting transfers between devices: 11.3 us -> 14.7 us  [swap_expert(): return lax.ppermute(a, ('v', 'c'), [(i, i ^ k) for i in range(4)])]
    ppermute x12, starting transfers between devices: 22 us -> 18.7 us  [shift(): return lax.ppermute(a, axis, [(i, (i + j) % 4) for i in range(4)])]
  transfers between devices with their start and end apart: 25 -> 25, of which waited for: 13 -> 10; matrix products, arithmetic and copies ran while one was open for 3% -> 3% of each run, Pallas kernels for 24% -> 25%
where the time goes in v4:
time: 150 us; the launch traced here: 148 us
  waiting for transfers between devices  52.3 us (35%)
  starting transfers between devices  45.4 us (30%)
  Pallas kernels  38.6 us (26%)
  local copies, waits for them, and re-layouts  5.08 us (3%)
  other arithmetic  2.86 us (2%)
  matrix products  2.45 us (2%)
    ppermute x12, waiting for transfers between devices, shift(): return lax.ppermute(a, axis, [(i, (i + j) % 4) for i in range(4)])  34.2 us
    ppermute x12, starting transfers between devices, shift(): return lax.ppermute(a, axis, [(i, (i + j) % 4) for i in range(4)])  18.7 us
    ppermute x9, starting transfers between devices, swap_expert(): return lax.ppermute(a, ('v', 'c'), [(i, i ^ k) for i in range(4)])  14.7 us
    ppermute x9, waiting for transfers between devices, swap_expert(): return lax.ppermute(a, ('v', 'c'), [(i, i ^ k) for i in range(4)])  13.1 us
    pallas_call x1, Pallas kernels, shards(): call(act_step, 'va', [shape(rows, inner), shape(rows, inner, dtype=F32),...  7.4 us
    pallas_call x1, Pallas kernels, shards(): call(back_step, 'vaa', [shape(CAP, width)] * 4 + [MARK], [pltpu.VMEM((n,...  6.92 us
    pallas_call x1, Pallas kernels, tile_call(): call(tile_step, 'a' * (8 + len(after)), [shape(4, 256, wide), MARK], [plt...  5.27 us
    pallas_call x1, Pallas kernels, shards(): call(dh_step, 'aaaaaaa', [shape(2, rows, inner), MARK], [pltpu.VMEM((rows...  5.09 us
  transfers between devices with their start and end apart: 25, of which 10 were waited for; matrix products, arithmetic and copies ran while one was open for 3% of the time, Pallas kernels for 25%

profile of v4, /device:TPU:0, one launch (start us, length us, event | category | flops | bytes accessed | tf_op | source)
XLA Modules:
  0.0 147.8 jit_solution(9091831327405168020)
XLA Ops:
  4.0 4.0 %collective-permute-start.4 = (bf16[48,4096]{1,0:T(8,128)(2,1)}, bf16[48,4096]{1,0:T(8,128)(2,1)}, u32[]{:S(2)}, u32[]{:S(2)}) collective-permute-start(bf16[48,4096]{1,0:T(8,128)(2,1)} %get-tuple-element.64), channel_id=1, source_target_pairs={{0,2},{1,3},{2,0},{3,1},{4,6},{5,7},{6,4},{7,5},{8,10},{9,11},{10,... | collective-permute-start | bytes 1179656 | tf_op jit(solution)/shard_map/ppermute | solution.py:21
  8.4 1.8 %fusion = bf16[192,4096]{1,0:T(8,128)(2,1)S(1)} fusion(pred[128,192]{1,0:T(32,128)(4,1)S(1)} %get-tuple-element.62, bf16[128,4096]{1,0:T(8,128)(2,1)} %param.7, f32[192]{0:T(256)S(1)} %mul.14), kind=kOutput, calls=%fused_computation.1 | convolution fusion | flops 202899456 | bytes 2646784 | tf_op jit(solution)/shard_map/dot_general | solution.py:35
  11.4 3.4 %collective-permute-start.1 = (bf16[48,4096]{1,0:T(8,128)(2,1)}, bf16[48,4096]{1,0:T(8,128)(2,1)S(1)}, u32[]{:S(2)}, u32[]{:S(2)}) collective-permute-start(bf16[48,4096]{1,0:T(8,128)(2,1)} %get-tuple-element.68), channel_id=1, source_target_pairs={{0,2},{1,3},{2,0},{3,1},{4,6},{5,7},{6,4},{7,5},{8,10},{9,11},{10,... | collective-permute-start | bytes 1179656 | tf_op jit(solution)/shard_map/ppermute | solution.py:21
  14.9 3.4 %collective-permute-done.4.x2 = bf16[48,4096]{1,0:T(8,128)(2,1)} collective-permute-done((bf16[48,4096]{1,0:T(8,128)(2,1)}, bf16[48,4096]{1,0:T(8,128)(2,1)}, u32[]{:S(2)}, u32[]{:S(2)}) %collective-permute-start.4) | collective-permute-done | bytes 393248 | tf_op jit(solution)/shard_map/ppermute | solution.py:21
  18.3 8.1 %collective-permute-done.5.x3 = bf16[48,4096]{1,0:T(8,128)(2,1)} collective-permute-done((bf16[48,4096]{1,0:T(8,128)(2,1)}, bf16[48,4096]{1,0:T(8,128)(2,1)}, u32[]{:S(2)}, u32[]{:S(2)}) %collective-permute-start.5) | collective-permute-done | bytes 393248 | tf_op jit(solution)/shard_map/ppermute | solution.py:21
  28.4 1.5 %collective-permute-start.6 = (bf16[192,1024]{1,0:T(8,128)(2,1)S(1)}, bf16[192,1024]{1,0:T(8,128)(2,1)S(1)}, u32[]{:S(2)}, u32[]{:S(2)}) collective-permute-start(bf16[192,1024]{1,0:T(8,128)(2,1)S(1)} %get-tuple-element.37), channel_id=1, source_target_pairs={{0,16},{16,32},{32,48},{48,0},{1,17},{17,33},{33,49},{49,1},{2,18}... | collective-permute-start | bytes 1179656 | tf_op jit(solution)/shard_map/ppermute | solution.py:27
  29.9 2.7 %collective-permute-start.7 = (bf16[192,1024]{1,0:T(8,128)(2,1)S(1)}, bf16[192,1024]{1,0:T(8,128)(2,1)S(1)}, u32[]{:S(2)}, u32[]{:S(2)}) collective-permute-start(bf16[192,1024]{1,0:T(8,128)(2,1)S(1)} %get-tuple-element.38), channel_id=1, source_target_pairs={{0,32},{16,48},{32,0},{48,16},{1,33},{17,49},{33,1},{49,17},{2,34}... | collective-permute-start | bytes 1179656 | tf_op jit(solution)/shard_map/ppermute | solution.py:27
  34.1 7.4 %shard_map.86 = (bf16[192,768]{1,0:T(8,128)(2,1)S(1)}, f32[192,768]{1,0:T(8,128)S(1)}, f32[192,768]{1,0:T(8,128)S(1)}) custom-call(bf16[192,4096]{1,0:T(8,128)(2,1)S(1)} %get-tuple-element.32.x, bf16[4096,1536]{1,0:T(8,128)(2,1)} %bitcast.43), custom_call_target="tpu_custom_call" | custom-call | flops 2415919104 | bytes 12582912 | tf_op jit(solution)/shard_map/pallas_call | solution.py:301
  41.5 1.6 %collective-permute-done.2.g3 = bf16[48,4096]{1,0:T(8,128)(2,1)S(1)} collective-permute-done((bf16[48,4096]{1,0:T(8,128)(2,1)}, bf16[48,4096]{1,0:T(8,128)(2,1)S(1)}, u32[]{:S(2)}, u32[]{:S(2)}) %collective-permute-start.2) | collective-permute-done | bytes 393248 | tf_op jit(solution)/shard_map/ppermute | solution.py:21
  43.1 5.1 %shard_map.87 = (bf16[2,192,768]{2,1,0:T(8,128)(2,1)S(1)}, f32[8,128]{1,0:T(8,128)S(1)}) custom-call(bf16[48,4096]{1,0:T(8,128)(2,1)S(1)} %get-tuple-element.70.g0, bf16[48,4096]{1,0:T(8,128)(2,1)S(1)} %collective-permute-done.g1, bf16[48,4096]{1,0:T(8,128)(2,1)S(1)} %collective-permute-done.1.g2, bf16[48,4096]{1,0:T(8,128)(2,1)S(1)} %collective-permute-done.2.g3, ...), custom_call_target="tpu_custom_call" | custom-call | flops 1207959552 | bytes 6291456 | tf_op jit(solution)/shard_map/pallas_call | solution.py:311
  48.2 2.0 %collective-permute-done.7.rest_1_.refs_2_ = bf16[192,1024]{1,0:T(8,128)(2,1)S(1)} collective-permute-done((bf16[192,1024]{1,0:T(8,128)(2,1)S(1)}, bf16[192,1024]{1,0:T(8,128)(2,1)S(1)}, u32[]{:S(2)}, u32[]{:S(2)}) %collective-permute-start.7) | collective-permute-done | bytes 393248 | tf_op jit(solution)/shard_map/ppermute | solution.py:27
  50.3 1.8 %shard_map.88 = (bf16[4,192,1792]{2,1,0:T(8,128)(2,1)}, f32[8,128]{1,0:T(8,128)S(1)}) custom-call(bf16[48,4096]{1,0:T(8,128)(2,1)S(1)} %get-tuple-element.70.g0, bf16[48,4096]{1,0:T(8,128)(2,1)S(1)} %collective-permute-done.g1, bf16[48,4096]{1,0:T(8,128)(2,1)S(1)} %collective-permute-done.1.g2, bf16[48,4096]{1,0:T(8,128)(2,1)S(1)} %collective-permute-done.2.g3, ...), custom_call_target="tpu_custom_call" | custom-call | bytes 3145728 | tf_op jit(solution)/shard_map/pallas_call | solution.py:327
  52.0 4.6 %all-to-all-start.1 = ((bf16[4,192,1792]{2,1,0:T(8,128)(2,1)}), bf16[4,192,1792]{2,1,0:T(8,128)(2,1)}, u32[]{:S(2)}, u32[]{:S(2)}) async-start(bf16[4,192,1792]{2,1,0:T(8,128)(2,1)} %get-tuple-element.51), calls=%async_computation.1 | async-start | bytes 5505024 | tf_op jit(solution)/shard_map/all_to_all | solution.py:335
  58.0 2.4 %collective-permute-start.13 = (bf16[2,192,768]{2,1,0:T(8,128)(2,1)S(1)}, bf16[2,192,768]{2,1,0:T(8,128)(2,1)S(1)}, u32[]{:S(2)}, u32[]{:S(2)}) collective-permute-start(bf16[2,192,768]{2,1,0:T(8,128)(2,1)S(1)} %get-tuple-element.35.dact.refs_4_), channel_id=1, source_target_pairs={{0,32},{16,48},{32,0},{48,16},{1,33},{17,49},{33,1},{49,17},{2,34}... | collective-permute-start | bytes 1769480 | tf_op jit(solution)/shard_map/ppermute | solution.py:27
  60.4 1.6 %collective-permute-start.14 = (bf16[2,192,768]{2,1,0:T(8,128)(2,1)S(1)}, bf16[2,192,768]{2,1,0:T(8,128)(2,1)S(1)}, u32[]{:S(2)}, u32[]{:S(2)}) collective-permute-start(bf16[2,192,768]{2,1,0:T(8,128)(2,1)S(1)} %get-tuple-element.35.dact.refs_4_), channel_id=1, source_target_pairs={{0,48},{16,0},{32,16},{48,32},{1,49},{17,1},{33,17},{49,33},{2,50}... | collective-permute-start | bytes 1769480 | tf_op jit(solution)/shard_map/ppermute | solution.py:27
  62.0 6.9 %shard_map.89 = (bf16[48,4096]{1,0:T(8,128)(2,1)S(1)}, bf16[48,4096]{1,0:T(8,128)(2,1)S(1)}, bf16[48,4096]{1,0:T(8,128)(2,1)S(1)}, bf16[48,4096]{1,0:T(8,128)(2,1)S(1)}, f32[8,128]{1,0:T(8,128)}) custom-call(bf16[2,192,768]{2,1,0:T(8,128)(2,1)S(1)} %get-tuple-element.35.dact.refs_4_, bf16[4096,1536]{1,0:T(8,128)(2,1)} %bitcast.44, ...), custom_call_target="tpu_custom_call" | custom-call | flops 2415919104 | bytes 12582912 | tf_op jit(solution)/shard_map/pallas_call | solution.py:337
  70.4 3.4 %collective-permute-start.10 = (bf16[48,4096]{1,0:T(8,128)(2,1)S(1)}, bf16[48,4096]{1,0:T(8,128)(2,1)S(1)}, u32[]{:S(2)}, u32[]{:S(2)}) collective-permute-start(bf16[48,4096]{1,0:T(8,128)(2,1)S(1)} %get-tuple-element.44), channel_id=1, source_target_pairs={{0,2},{1,3},{2,0},{3,1},{4,6},{5,7},{6,4},{7,5},{8,10},{9,11},{10,... | collective-permute-start | bytes 1179656 | tf_op jit(solution)/shard_map/ppermute | solution.py:21
  73.9 12.4 %collective-permute-done.13.refs_6_ = bf16[2,192,768]{2,1,0:T(8,128)(2,1)S(1)} collective-permute-done((bf16[2,192,768]{2,1,0:T(8,128)(2,1)S(1)}, bf16[2,192,768]{2,1,0:T(8,128)(2,1)S(1)}, u32[]{:S(2)}, u32[]{:S(2)}) %collective-permute-start.13) | collective-permute-done | bytes 589856 | tf_op jit(solution)/shard_map/ppermute | solution.py:27
  86.3 5.3 %shard_map.91 = (bf16[4,256,1536]{2,1,0:T(8,128)(2,1)}, f32[8,128]{1,0:T(8,128)S(1)}) custom-call(bf16[192,1024]{1,0:T(8,128)(2,1)S(1)} %copy-done.8, bf16[192,1024]{1,0:T(8,128)(2,1)S(1)} %copy-done.2, bf16[192,1024]{1,0:T(8,128)(2,1)S(1)} %copy-done.4, bf16[192,1024]{1,0:T(8,128)(2,1)S(1)} %copy-done.6, ...), custom_call_target="tpu_custom_call" | custom-call | flops 2415919104 | bytes 3932160 | tf_op jit(solution)/shard_map/pallas_call | solution.py:192
  91.6 4.8 %all-to-all-start = ((bf16[4,256,1536]{2,1,0:T(8,128)(2,1)}), bf16[4,256,1536]{2,1,0:T(8,128)(2,1)}, u32[]{:S(2)}, u32[]{:S(2)}) async-start(bf16[4,256,1536]{2,1,0:T(8,128)(2,1)} %get-tuple-element.48), calls=%async_computation | async-start | bytes 6291456 | tf_op jit(solution)/shard_map/all_to_all | solution.py:348
  96.5 3.6 %collective-permute-start.11 = (bf16[48,4096]{1,0:T(8,128)(2,1)S(1)}, bf16[48,4096]{1,0:T(8,128)(2,1)S(1)}, u32[]{:S(2)}, u32[]{:S(2)}) collective-permute-start(bf16[48,4096]{1,0:T(8,128)(2,1)S(1)} %copy-done.10), channel_id=1, source_target_pairs={{0,3},{1,2},{2,1},{3,0},{4,7},{5,6},{6,5},{7,4},{8,11},{9,10},{10,... | collective-permute-start | bytes 1179656 | tf_op jit(solution)/shard_map/ppermute | solution.py:21
  100.1 4.5 %shard_map.93 = (f32[192,1024]{1,0:T(8,128)S(1)}, bf16[192,1024]{1,0:T(8,128)(2,1)S(1)}, bf16[192,1024]{1,0:T(8,128)(2,1)S(1)}, bf16[192,1024]{1,0:T(8,128)(2,1)S(1)}, f32[8,128]{1,0:T(8,128)}) custom-call(s32[4]{0:T(128)S(1)} %pad_add_fusion.at, bf16[4,192,1792]{2,1,0:T(8,128)(2,1)} %all-to-all-done.1.both, f32[8,128]{1,0:T(8,128)S(1)} %get-tuple-element.52.rest_0_), custom_call_target="tpu_custom_call" | custom-call | flops 1207959552 | bytes 2752512 | tf_op jit(solution)/shard_map/pallas_call | solution.py:349
  104.6 1.7 %collective-permute-start.16 = (bf16[192,1024]{1,0:T(8,128)(2,1)S(1)}, bf16[192,1024]{1,0:T(8,128)(2,1)S(1)}, u32[]{:S(2)}, u32[]{:S(2)}) collective-permute-start(bf16[192,1024]{1,0:T(8,128)(2,1)S(1)} %get-tuple-element.54), channel_id=1, source_target_pairs={{0,16},{16,32},{32,48},{48,0},{1,17},{17,33},{33,49},{49,1},{2,18}... | collective-permute-start | bytes 1179656 | tf_op jit(solution)/shard_map/ppermute | solution.py:27
  106.2 2.4 %collective-permute-start.17 = (bf16[192,1024]{1,0:T(8,128)(2,1)S(1)}, bf16[192,1024]{1,0:T(8,128)(2,1)S(1)}, u32[]{:S(2)}, u32[]{:S(2)}) collective-permute-start(bf16[192,1024]{1,0:T(8,128)(2,1)S(1)} %get-tuple-element.55), channel_id=1, source_target_pairs={{0,32},{16,48},{32,0},{48,16},{1,33},{17,49},{33,1},{49,17},{2,34}... | collective-permute-start | bytes 1179656 | tf_op jit(solution)/shard_map/ppermute | solution.py:27
  109.6 2.2 %shard_map.90 = (bf16[128,4096]{1,0:T(8,128)(2,1)}, f32[8,128]{1,0:T(8,128)S(1)}) custom-call(bf16[128,192]{1,0:T(8,128)(2,1)S(1)} %get-tuple-element.61.mask, bf16[48,4096]{1,0:T(8,128)(2,1)S(1)} %get-tuple-element.42.a0, bf16[48,4096]{1,0:T(8,128)(2,1)S(1)} %collective-permute-done.9.a1, bf16[48,4096]{1,0:T(8,128)(2,1)S(1)} %collective-permute-done.10.a2.refs_8_, ...), custom_call_target="tpu_custom_call" | custom-call | tf_op jit(solution)/shard_map/pallas_call | solution.py:364
  111.8 5.2 %collective-permute-done.16.r1 = bf16[192,1024]{1,0:T(8,128)(2,1)S(1)} collective-permute-done((bf16[192,1024]{1,0:T(8,128)(2,1)S(1)}, bf16[192,1024]{1,0:T(8,128)(2,1)S(1)}, u32[]{:S(2)}, u32[]{:S(2)}) %collective-permute-start.16) | collective-permute-done | bytes 393248 | tf_op jit(solution)/shard_map/ppermute | solution.py:27
  117.0 9.2 %collective-permute-done.17.r2 = bf16[192,1024]{1,0:T(8,128)(2,1)S(1)} collective-permute-done((bf16[192,1024]{1,0:T(8,128)(2,1)S(1)}, bf16[192,1024]{1,0:T(8,128)(2,1)S(1)}, u32[]{:S(2)}, u32[]{:S(2)}) %collective-permute-start.17) | collective-permute-done | bytes 393248 | tf_op jit(solution)/shard_map/ppermute | solution.py:27
  128.7 5.1 %all-to-all-done.parts = bf16[4,256,1536]{2,1,0:T(8,128)(2,1)} async-done(((bf16[4,256,1536]{2,1,0:T(8,128)(2,1)}), bf16[4,256,1536]{2,1,0:T(8,128)(2,1)}, u32[]{:S(2)}, u32[]{:S(2)}) %all-to-all-start) | async-done | bytes 3145760 | tf_op jit(solution)/shard_map/all_to_all | solution.py:348
  133.8 2.8 %shard_map.92 = (f32[128,1536]{1,0:T(8,128)S(1)}, bf16[128,1536]{1,0:T(8,128)(2,1)S(1)}, f32[8,128]{1,0:T(8,128)S(1)}) custom-call(s32[4]{0:T(128)S(1)} %pad_add_fusion.at, bf16[4,256,1536]{2,1,0:T(8,128)(2,1)} %all-to-all-done.parts), custom_call_target="tpu_custom_call" | custom-call | tf_op jit(solution)/shard_map/pallas_call | solution.py:371
  137.9 1.5 %collective-permute-start.15 = (bf16[128,1536]{1,0:T(8,128)(2,1)S(1)}, bf16[128,1536]{1,0:T(8,128)(2,1)S(1)}, u32[]{:S(2)}, u32[]{:S(2)}) collective-permute-start(bf16[128,1536]{1,0:T(8,128)(2,1)S(1)} %get-tuple-element.50), channel_id=1, source_target_pairs={{0,64},{64,0},{1,65},{65,1},{2,66},{66,2},{3,67},{67,3},{4,68},{68... | collective-permute-start | bytes 1179656 | tf_op jit(solution)/shard_map/ppermute | solution.py:31
  139.4 1.5 %collective-permute-start.21 = (bf16[24,1024]{1,0:T(8,128)(2,1)S(1)}, bf16[24,1024]{1,0:T(8,128)(2,1)S(1)}, u32[]{:S(2)}, u32[]{:S(2)}) collective-permute-start(bf16[24,1024]{1,0:T(8,128)(2,1)S(1)} %get-tuple-element.76), channel_id=1, source_target_pairs={{0,8},{4,12},{8,0},{12,4},{1,9},{5,13},{9,1},{13,5},{2,10},{6,14},... | collective-permute-start | bytes 147464 | tf_op jit(solution)/shard_map/ppermute | solution.py:27
  140.9 4.1 %collective-permute-done.21 = bf16[24,1024]{1,0:T(8,128)(2,1)S(1)} collective-permute-done((bf16[24,1024]{1,0:T(8,128)(2,1)S(1)}, bf16[24,1024]{1,0:T(8,128)(2,1)S(1)}, u32[]{:S(2)}, u32[]{:S(2)}) %collective-permute-start.21) | collective-permute-done | bytes 49184 | tf_op jit(solution)/shard_map/ppermute | solution.py:27
  (93 shorter events, 18.9 us)
Async XLA Ops:
  2.3 5.8 %copy-start.13 = (s32[128,8]{0,1:T(8,128)S(1)}, s32[128,8]{0,1:T(8,128)}, u32[]{:S(2)}) copy-start(s32[128,8]{0,1:T(8,128)} %param.8) | copy-start | bytes 12292
  2.3 5.8 %copy-start.14 = (f32[128,8]{0,1:T(8,128)S(1)}, f32[128,8]{0,1:T(8,128)}, u32[]{:S(2)}) copy-start(f32[128,8]{0,1:T(8,128)} %param.9) | copy-start | bytes 12292
  4.0 10.8 %collective-permute-start.3 = (bf16[48,4096]{1,0:T(8,128)(2,1)}, bf16[48,4096]{1,0:T(8,128)(2,1)S(1)}, u32[]{:S(2)}, u32[]{:S(2)}) collective-permute-start(bf16[48,4096]{1,0:T(8,128)(2,1)} %get-tuple-element.65), channel_id=1, source_target_pairs={{0,1},{1,0},{2,3},{3,2},{4,5},{5,4},{6,7},{7,6},{8,9},{9,8},{10,11... | collective-permute-start | bytes 1179656 | tf_op jit(solution)/shard_map/ppermute | solution.py:21
  4.0 14.2 %collective-permute-start.4 = (bf16[48,4096]{1,0:T(8,128)(2,1)}, bf16[48,4096]{1,0:T(8,128)(2,1)}, u32[]{:S(2)}, u32[]{:S(2)}) collective-permute-start(bf16[48,4096]{1,0:T(8,128)(2,1)} %get-tuple-element.64), channel_id=1, source_target_pairs={{0,2},{1,3},{2,0},{3,1},{4,6},{5,7},{6,4},{7,5},{8,10},{9,11},{10,... | collective-permute-start | bytes 1179656 | tf_op jit(solution)/shard_map/ppermute | solution.py:21
  8.0 18.3 %collective-permute-start.5 = (bf16[48,4096]{1,0:T(8,128)(2,1)}, bf16[48,4096]{1,0:T(8,128)(2,1)}, u32[]{:S(2)}, u32[]{:S(2)}) collective-permute-start(bf16[48,4096]{1,0:T(8,128)(2,1)} %get-tuple-element.63), channel_id=1, source_target_pairs={{0,3},{1,2},{2,1},{3,0},{4,7},{5,6},{6,5},{7,4},{8,11},{9,10},{10,... | collective-permute-start | bytes 1179656 | tf_op jit(solution)/shard_map/ppermute | solution.py:21
  11.3 21.3 %collective-permute-start = (bf16[48,4096]{1,0:T(8,128)(2,1)}, bf16[48,4096]{1,0:T(8,128)(2,1)S(1)}, u32[]{:S(2)}, u32[]{:S(2)}) collective-permute-start(bf16[48,4096]{1,0:T(8,128)(2,1)} %get-tuple-element.69), channel_id=1, source_target_pairs={{0,1},{1,0},{2,3},{3,2},{4,5},{5,4},{6,7},{7,6},{8,9},{9,8},{10,11... | collective-permute-start | bytes 1179656 | tf_op jit(solution)/shard_map/ppermute | solution.py:21
  11.4 30.1 %collective-permute-start.1 = (bf16[48,4096]{1,0:T(8,128)(2,1)}, bf16[48,4096]{1,0:T(8,128)(2,1)S(1)}, u32[]{:S(2)}, u32[]{:S(2)}) collective-permute-start(bf16[48,4096]{1,0:T(8,128)(2,1)} %get-tuple-element.68), channel_id=1, source_target_pairs={{0,2},{1,3},{2,0},{3,1},{4,6},{5,7},{6,4},{7,5},{8,10},{9,11},{10,... | collective-permute-start | bytes 1179656 | tf_op jit(solution)/shard_map/ppermute | solution.py:21
  14.8 28.3 %collective-permute-start.2 = (bf16[48,4096]{1,0:T(8,128)(2,1)}, bf16[48,4096]{1,0:T(8,128)(2,1)S(1)}, u32[]{:S(2)}, u32[]{:S(2)}) collective-permute-start(bf16[48,4096]{1,0:T(8,128)(2,1)} %get-tuple-element.67), channel_id=1, source_target_pairs={{0,3},{1,2},{2,1},{3,0},{4,7},{5,6},{6,5},{7,4},{8,11},{9,10},{10,... | collective-permute-start | bytes 1179656 | tf_op jit(solution)/shard_map/ppermute | solution.py:21
  28.4 19.8 %collective-permute-start.6 = (bf16[192,1024]{1,0:T(8,128)(2,1)S(1)}, bf16[192,1024]{1,0:T(8,128)(2,1)S(1)}, u32[]{:S(2)}, u32[]{:S(2)}) collective-permute-start(bf16[192,1024]{1,0:T(8,128)(2,1)S(1)} %get-tuple-element.37), channel_id=1, source_target_pairs={{0,16},{16,32},{32,48},{48,0},{1,17},{17,33},{33,49},{49,1},{2,18}... | collective-permute-start | bytes 1179656 | tf_op jit(solution)/shard_map/ppermute | solution.py:27
  29.9 20.3 %collective-permute-start.7 = (bf16[192,1024]{1,0:T(8,128)(2,1)S(1)}, bf16[192,1024]{1,0:T(8,128)(2,1)S(1)}, u32[]{:S(2)}, u32[]{:S(2)}) collective-permute-start(bf16[192,1024]{1,0:T(8,128)(2,1)S(1)} %get-tuple-element.38), channel_id=1, source_target_pairs={{0,32},{16,48},{32,0},{48,16},{1,33},{17,49},{33,1},{49,17},{2,34}... | collective-permute-start | bytes 1179656 | tf_op jit(solution)/shard_map/ppermute | solution.py:27
  32.6 17.6 %collective-permute-start.8 = (bf16[192,1024]{1,0:T(8,128)(2,1)S(1)}, bf16[192,1024]{1,0:T(8,128)(2,1)S(1)}, u32[]{:S(2)}, u32[]{:S(2)}) collective-permute-start(bf16[192,1024]{1,0:T(8,128)(2,1)S(1)} %get-tuple-element.39), channel_id=1, source_target_pairs={{0,48},{16,0},{32,16},{48,32},{1,49},{17,1},{33,17},{49,33},{2,50}... | collective-permute-start | bytes 1179656 | tf_op jit(solution)/shard_map/ppermute | solution.py:27
  52.0 39.5 %all-to-all-start.1 = ((bf16[4,192,1792]{2,1,0:T(8,128)(2,1)}), bf16[4,192,1792]{2,1,0:T(8,128)(2,1)}, u32[]{:S(2)}, u32[]{:S(2)}) async-start(bf16[4,192,1792]{2,1,0:T(8,128)(2,1)} %get-tuple-element.51), calls=%async_computation.1 | async-start | bytes 5505024 | tf_op jit(solution)/shard_map/all_to_all | solution.py:335
  56.6 17.2 %collective-permute-start.12 = (bf16[2,192,768]{2,1,0:T(8,128)(2,1)S(1)}, bf16[2,192,768]{2,1,0:T(8,128)(2,1)S(1)}, u32[]{:S(2)}, u32[]{:S(2)}) collective-permute-start(bf16[2,192,768]{2,1,0:T(8,128)(2,1)S(1)} %get-tuple-element.35.dact.refs_4_), channel_id=1, source_target_pairs={{0,16},{16,32},{32,48},{48,0},{1,17},{17,33},{33,49},{49,1},{2,18}... | collective-permute-start | bytes 1769480 | tf_op jit(solution)/shard_map/ppermute | solution.py:27
  58.0 28.2 %collective-permute-start.13 = (bf16[2,192,768]{2,1,0:T(8,128)(2,1)S(1)}, bf16[2,192,768]{2,1,0:T(8,128)(2,1)S(1)}, u32[]{:S(2)}, u32[]{:S(2)}) collective-permute-start(bf16[2,192,768]{2,1,0:T(8,128)(2,1)S(1)} %get-tuple-element.35.dact.refs_4_), channel_id=1, source_target_pairs={{0,32},{16,48},{32,0},{48,16},{1,33},{17,49},{33,1},{49,17},{2,34}... | collective-permute-start | bytes 1769480 | tf_op jit(solution)/shard_map/ppermute | solution.py:27
  60.4 25.9 %collective-permute-start.14 = (bf16[2,192,768]{2,1,0:T(8,128)(2,1)S(1)}, bf16[2,192,768]{2,1,0:T(8,128)(2,1)S(1)}, u32[]{:S(2)}, u32[]{:S(2)}) collective-permute-start(bf16[2,192,768]{2,1,0:T(8,128)(2,1)S(1)} %get-tuple-element.35.dact.refs_4_), channel_id=1, source_target_pairs={{0,48},{16,0},{32,16},{48,32},{1,49},{17,1},{33,17},{49,33},{2,50}... | collective-permute-start | bytes 1769480 | tf_op jit(solution)/shard_map/ppermute | solution.py:27
  62.0 24.3 %copy-start.2 = (bf16[192,1024]{1,0:T(8,128)(2,1)S(1)}, bf16[192,1024]{1,0:T(8,128)(2,1)}, u32[]{:S(2)}) copy-start(bf16[192,1024]{1,0:T(8,128)(2,1)} %copy-done.1) | copy-start | bytes 1179652
  62.0 24.3 %copy-start.4 = (bf16[192,1024]{1,0:T(8,128)(2,1)S(1)}, bf16[192,1024]{1,0:T(8,128)(2,1)}, u32[]{:S(2)}) copy-start(bf16[192,1024]{1,0:T(8,128)(2,1)} %copy-done.3) | copy-start | bytes 1179652
  62.0 24.3 %copy-start.6 = (bf16[192,1024]{1,0:T(8,128)(2,1)S(1)}, bf16[192,1024]{1,0:T(8,128)(2,1)}, u32[]{:S(2)}) copy-start(bf16[192,1024]{1,0:T(8,128)(2,1)} %copy-done.5) | copy-start | bytes 1179652
  62.0 24.3 %copy-start.8 = (bf16[192,1024]{1,0:T(8,128)(2,1)S(1)}, bf16[192,1024]{1,0:T(8,128)(2,1)}, u32[]{:S(2)}) copy-start(bf16[192,1024]{1,0:T(8,128)(2,1)} %copy-done.7) | copy-start | bytes 1179652
  70.4 15.9 %collective-permute-start.10 = (bf16[48,4096]{1,0:T(8,128)(2,1)S(1)}, bf16[48,4096]{1,0:T(8,128)(2,1)S(1)}, u32[]{:S(2)}, u32[]{:S(2)}) collective-permute-start(bf16[48,4096]{1,0:T(8,128)(2,1)S(1)} %get-tuple-element.44), channel_id=1, source_target_pairs={{0,2},{1,3},{2,0},{3,1},{4,6},{5,7},{6,4},{7,5},{8,10},{9,11},{10,... | collective-permute-start | bytes 1179656 | tf_op jit(solution)/shard_map/ppermute | solution.py:21
  91.6 4.9 %copy-start.10 = (bf16[48,4096]{1,0:T(8,128)(2,1)S(1)}, bf16[48,4096]{1,0:T(8,128)(2,1)}, u32[]{:S(2)}) copy-start(bf16[48,4096]{1,0:T(8,128)(2,1)} %copy-done.9) | copy-start | bytes 1179652
  91.6 42.1 %all-to-all-start = ((bf16[4,256,1536]{2,1,0:T(8,128)(2,1)}), bf16[4,256,1536]{2,1,0:T(8,128)(2,1)}, u32[]{:S(2)}, u32[]{:S(2)}) async-start(bf16[4,256,1536]{2,1,0:T(8,128)(2,1)} %get-tuple-element.48), calls=%async_computation | async-start | bytes 6291456 | tf_op jit(solution)/shard_map/all_to_all | solution.py:348
  96.4 13.1 %collective-permute-start.9 = (bf16[48,4096]{1,0:T(8,128)(2,1)S(1)}, bf16[48,4096]{1,0:T(8,128)(2,1)S(1)}, u32[]{:S(2)}, u32[]{:S(2)}) collective-permute-start(bf16[48,4096]{1,0:T(8,128)(2,1)S(1)} %copy-done.12), channel_id=1, source_target_pairs={{0,1},{1,0},{2,3},{3,2},{4,5},{5,4},{6,7},{7,6},{8,9},{9,8},{10,11... | collective-permute-start | bytes 1179656 | tf_op jit(solution)/shard_map/ppermute | solution.py:21
  96.5 13.0 %collective-permute-start.11 = (bf16[48,4096]{1,0:T(8,128)(2,1)S(1)}, bf16[48,4096]{1,0:T(8,128)(2,1)S(1)}, u32[]{:S(2)}, u32[]{:S(2)}) collective-permute-start(bf16[48,4096]{1,0:T(8,128)(2,1)S(1)} %copy-done.10), channel_id=1, source_target_pairs={{0,3},{1,2},{2,1},{3,0},{4,7},{5,6},{6,5},{7,4},{8,11},{9,10},{10,... | collective-permute-start | bytes 1179656 | tf_op jit(solution)/shard_map/ppermute | solution.py:21
  104.6 12.4 %collective-permute-start.16 = (bf16[192,1024]{1,0:T(8,128)(2,1)S(1)}, bf16[192,1024]{1,0:T(8,128)(2,1)S(1)}, u32[]{:S(2)}, u32[]{:S(2)}) collective-permute-start(bf16[192,1024]{1,0:T(8,128)(2,1)S(1)} %get-tuple-element.54), channel_id=1, source_target_pairs={{0,16},{16,32},{32,48},{48,0},{1,17},{17,33},{33,49},{49,1},{2,18}... | collective-permute-start | bytes 1179656 | tf_op jit(solution)/shard_map/ppermute | solution.py:27
  106.2 20.0 %collective-permute-start.17 = (bf16[192,1024]{1,0:T(8,128)(2,1)S(1)}, bf16[192,1024]{1,0:T(8,128)(2,1)S(1)}, u32[]{:S(2)}, u32[]{:S(2)}) collective-permute-start(bf16[192,1024]{1,0:T(8,128)(2,1)S(1)} %get-tuple-element.55), channel_id=1, source_target_pairs={{0,32},{16,48},{32,0},{48,16},{1,33},{17,49},{33,1},{49,17},{2,34}... | collective-permute-start | bytes 1179656 | tf_op jit(solution)/shard_map/ppermute | solution.py:27
  108.7 17.6 %collective-permute-start.18 = (bf16[192,1024]{1,0:T(8,128)(2,1)S(1)}, bf16[192,1024]{1,0:T(8,128)(2,1)S(1)}, u32[]{:S(2)}, u32[]{:S(2)}) collective-permute-start(bf16[192,1024]{1,0:T(8,128)(2,1)S(1)} %get-tuple-element.56), channel_id=1, source_target_pairs={{0,48},{16,0},{32,16},{48,32},{1,49},{17,1},{33,17},{49,33},{2,50}... | collective-permute-start | bytes 1179656 | tf_op jit(solution)/shard_map/ppermute | solution.py:27
  127.6 9.0 %collective-permute-start.19 = (bf16[96,1024]{1,0:T(8,128)(2,1)S(1)}, bf16[96,1024]{1,0:T(8,128)(2,1)S(1)}, u32[]{:S(2)}, u32[]{:S(2)}) collective-permute-start(bf16[96,1024]{1,0:T(8,128)(2,1)S(1)} %get-tuple-element.59), channel_id=1, source_target_pairs={{0,64},{64,0},{1,65},{65,1},{2,66},{66,2},{3,67},{67,3},{4,68},{68... | collective-permute-start | bytes 589832 | tf_op jit(solution)/shard_map/ppermute | solution.py:31
  136.6 4.2 %collective-permute-start.20 = (bf16[24,1024]{1,0:T(8,128)(2,1)S(1)}, bf16[24,1024]{1,0:T(8,128)(2,1)S(1)}, u32[]{:S(2)}, u32[]{:S(2)}) collective-permute-start(bf16[24,1024]{1,0:T(8,128)(2,1)S(1)} %get-tuple-element.77), channel_id=1, source_target_pairs={{0,12},{4,0},{8,4},{12,8},{1,13},{5,1},{9,5},{13,9},{2,14},{6,2},{... | collective-permute-start | bytes 147464 | tf_op jit(solution)/shard_map/ppermute | solution.py:27
  137.9 9.1 %collective-permute-start.15 = (bf16[128,1536]{1,0:T(8,128)(2,1)S(1)}, bf16[128,1536]{1,0:T(8,128)(2,1)S(1)}, u32[]{:S(2)}, u32[]{:S(2)}) collective-permute-start(bf16[128,1536]{1,0:T(8,128)(2,1)S(1)} %get-tuple-element.50), channel_id=1, source_target_pairs={{0,64},{64,0},{1,65},{65,1},{2,66},{66,2},{3,67},{67,3},{4,68},{68... | collective-permute-start | bytes 1179656 | tf_op jit(solution)/shard_map/ppermute | solution.py:31
  139.4 5.6 %collective-permute-start.21 = (bf16[24,1024]{1,0:T(8,128)(2,1)S(1)}, bf16[24,1024]{1,0:T(8,128)(2,1)S(1)}, u32[]{:S(2)}, u32[]{:S(2)}) collective-permute-start(bf16[24,1024]{1,0:T(8,128)(2,1)S(1)} %get-tuple-element.76), channel_id=1, source_target_pairs={{0,8},{4,12},{8,0},{12,4},{1,9},{5,13},{9,1},{13,5},{2,10},{6,14},... | collective-permute-start | bytes 147464 | tf_op jit(solution)/shard_map/ppermute | solution.py:27
  140.9 5.3 %collective-permute-start.22 = (bf16[24,1024]{1,0:T(8,128)(2,1)S(1)}, bf16[24,1024]{1,0:T(8,128)(2,1)S(1)}, u32[]{:S(2)}, u32[]{:S(2)}) collective-permute-start(bf16[24,1024]{1,0:T(8,128)(2,1)S(1)} %get-tuple-element.75), channel_id=1, source_target_pairs={{0,4},{4,8},{8,12},{12,0},{1,5},{5,9},{9,13},{13,1},{2,6},{6,10},{... | collective-permute-start | bytes 147464 | tf_op jit(solution)/shard_map/ppermute | solution.py:27
  (8 other events, 16.1 us)

commit v5 on v4

--- a/solution.py
+++ b/solution.py
@@ -178,10 +178,10 @@
     for b in range(2):
         got = rows_dot(xall[:, b * 512 : b * 512 + 512], dall[...])
         for j in range(4):
-            buf[j, b * 128 : b * 128 + 128, :] = got[j * 128 : j * 128 + 128].astype(BF)
-            if b == 1:
-                copies.append(pltpu.make_async_copy(buf.at[j], out.at[j], osem.at[j]))
-                copies[-1].start()
+            i = b * 4 + j
+            buf[i] = got[j * 128 : j * 128 + 128].astype(BF)
+            copies.append(pltpu.make_async_copy(buf.at[i], out.at[i], osem.at[i]))
+            copies[-1].start()
     for copy in copies:
         copy.wait()
 
@@ -192,13 +192,13 @@
     return call(
         tile_step,
         "a" * (8 + len(after)),
-        [shape(4, 256, wide), MARK],
+        [shape(8, 128, wide), MARK],
         [
             pltpu.VMEM((4 * rows, part), BF),
             pltpu.VMEM((4 * rows, wide), BF),
-            pltpu.VMEM((4, 256, wide), BF),
+            pltpu.VMEM((8, 128, wide), BF),
             sems(12),
-            sems(4),
+            sems(8),
         ],
         flops=8 * rows * part * wide,
         moved=8 * rows * (part + wide),
@@ -227,18 +227,12 @@
             )
 
 
-def gate_sum(at, parts, keep, send, mark, g, sem):
-    mark[...] = jnp.zeros_like(mark)
-    half = keep.shape[0]
-    copies = fetch([(parts.at[i], g.at[i]) for i in range(4)], sem)
+def gate_sum(parts, out, mark, g, sem):
+    copies = fetch([(parts.at[i], g.at[i]) for i in range(8)], sem)
+    mark[...] = jnp.zeros_like(mark)
     for copy in copies:
         copy.wait()
-
-    def part(i):
-        return sum(g[p, aligned(i, half), :].astype(F32) for p in range(4))
-
-    send[...] = part(1 - at[0]).astype(BF)
-    keep[...] = part(at[0])
+    out[...] = sum(g[i].astype(F32) for i in range(8)).astype(BF)
 
 
 def sum_step(at, own, r1, r2, r3, *rest):
@@ -265,8 +259,9 @@
     )(at, *parts, *after)
 
 
-def join_step(keep, theirs, mark, out):
-    out[...] = (keep[...] + theirs[...].astype(F32)).astype(BF)
+def join_step(at, c0, c1, c2, c3, mark, out):
+    for j, piece in enumerate((c0, c1, c2, c3)):
+        out[:, aligned(lax.rem(at[2] + 4 - j, 4), piece.shape[1])] = piece[...]
 
 
 def shards(tokens, cotangent, routes, gates, gate_up, down_proj):
@@ -345,7 +340,7 @@
     )(dact, gate_up, sent_mark)
     arrived = [back[0]] + [swap_expert(back[k], k) for k in (1, 2, 3)]
     parts, mark = tile_call(xa, da, [arrived[2]])
-    gate = lax.all_to_all(parts, "y", split_axis=0, concat_axis=0, tiled=True)
+    gate = lax.all_to_all(parts, ("w", "y"), split_axis=0, concat_axis=0, tiled=True)
     *parts, _ = call(
         down_step,
         "saa",
@@ -368,24 +363,19 @@
         [pltpu.VMEM((rows, width), BF), sems(4)],
     )(mask, *arrived)
 
-    gate_keep, gate_send, mark = call(
+    gate_up_grad, mark = call(
         gate_sum,
-        "sa",
-        [shape(128, 2 * inner, dtype=F32), shape(128, 2 * inner), MARK],
-        [pltpu.VMEM((4, 256, 2 * inner), BF), sems(4)],
+        "a",
+        [shape(128, 2 * inner), MARK],
+        [pltpu.VMEM((8, 128, 2 * inner), BF), sems(8)],
         limit=12,
-    )(at, gate)
-    gate_up_grad = (gate_keep + swap_w(gate_send).astype(F32)).astype(BF)
+    )(gate)
     keep, send = sum_call(at, down, [tok_mark])
-    down_grad = call(join_step, "vva", [shape(96, part)], moved=800 * part)(
-        keep, swap_w(send), mark
-    )[0].reshape(4, 24, part)
+    down_grad = (keep + swap_w(send).astype(F32)).astype(BF).reshape(4, 24, part)
     cols = [
         shift(lax.dynamic_index_in_dim(down_grad, (y + j) % 4, 0, False), "y", j) for j in range(4)
     ]
-    turned = jnp.stack(cols[::-1] + cols[::-1])
-    mine = lax.dynamic_slice_in_dim(turned, 3 - y, 4, 0)
-    down_grad = jnp.concatenate([mine[i] for i in range(4)], axis=1)
+    down_grad = call(join_step, "svvvva", [shape(24, width)])(at, *cols, mark)[0]
 
     return token_grad, gate_up_grad[None], down_grad[None]
 

time: 150 us -> 165 us (1.10)
  waiting for transfers between devices: 52.3 us -> 63.8 us
  starting transfers between devices: 45.4 us -> 49.5 us
    ppermute x9, waiting for transfers between devices: 13.1 us -> 43.2 us  [swap_expert(): return lax.ppermute(a, ('v', 'c'), [(i, i ^ k) for i in range(4)])]
    ppermute x12, waiting for transfers between devices: 34.2 us -> 14.5 us  [shift(): return lax.ppermute(a, axis, [(i, (i + j) % 4) for i in range(4)])]
    ppermute x2 -> x1, waiting for transfers between devices: 0.01 us -> 6.11 us  [swap_w(): return lax.ppermute(a, 'w', [(0, 1), (1, 0)])]
    all_to_all x1, waiting for transfers between devices: 5.06 us -> 0.01 us  [shards(): lax.all_to_all(parts, ('w', 'y'), split_axis=0, concat_axis=0, tiled=True)]
    ppermute x12, starting transfers between devices: 18.7 us -> 23.5 us  [shift(): return lax.ppermute(a, axis, [(i, (i + j) % 4) for i in range(4)])]
    ppermute x2 -> x1, starting transfers between devices: 2.6 us -> 0.91 us  [swap_w(): return lax.ppermute(a, 'w', [(0, 1), (1, 0)])]
  transfers between devices with their start and end apart: 25 -> 24, of which waited for: 10 -> 7; matrix products, arithmetic and copies ran while one was open for 3% -> 2% of each run, Pallas kernels for 25% -> 23%
where the time goes in v5:
time: 165 us; the launch traced here: 163 us
  waiting for transfers between devices  63.8 us (39%)
  starting transfers between devices  49.5 us (30%)
  Pallas kernels  39.8 us (24%)
  local copies, waits for them, and re-layouts  5.01 us (3%)
  matrix products  2.46 us (1%)
    ppermute x9, waiting for transfers between devices, swap_expert(): return lax.ppermute(a, ('v', 'c'), [(i, i ^ k) for i in range(4)])  43.2 us
    ppermute x12, starting transfers between devices, shift(): return lax.ppermute(a, axis, [(i, (i + j) % 4) for i in range(4)])  23.5 us
    ppermute x9, starting transfers between devices, swap_expert(): return lax.ppermute(a, ('v', 'c'), [(i, i ^ k) for i in range(4)])  14.8 us
    ppermute x12, waiting for transfers between devices, shift(): return lax.ppermute(a, axis, [(i, (i + j) % 4) for i in range(4)])  14.5 us
    pallas_call x1, Pallas kernels, shards(): call(act_step, 'va', [shape(rows, inner), shape(rows, inner, dtype=F32),...  7.42 us
    pallas_call x1, Pallas kernels, shards(): call(back_step, 'vaa', [shape(CAP, width)] * 4 + [MARK], [pltpu.VMEM((n,...  6.93 us
    ppermute x1, waiting for transfers between devices, swap_w(): return lax.ppermute(a, 'w', [(0, 1), (1, 0)])  6.11 us
    all_to_all x1, starting transfers between devices, shards(): lax.all_to_all(parts, ('w', 'y'), split_axis=0, concat_axis=0, tiled=True)  5.61 us
  transfers between devices with their start and end apart: 24, of which 7 were waited for; matrix products, arithmetic and copies ran while one was open for 2% of the time, Pallas kernels for 23%

profile of v5, /device:TPU:0, one launch (start us, length us, event | category | flops | bytes accessed | tf_op | source)
XLA Modules:
  0.0 163.0 jit_solution(5300929053280261060)
XLA Ops:
  4.0 4.0 %collective-permute-start.4 = (bf16[48,4096]{1,0:T(8,128)(2,1)}, bf16[48,4096]{1,0:T(8,128)(2,1)}, u32[]{:S(2)}, u32[]{:S(2)}) collective-permute-start(bf16[48,4096]{1,0:T(8,128)(2,1)} %get-tuple-element.62), channel_id=1, source_target_pairs={{0,2},{1,3},{2,0},{3,1},{4,6},{5,7},{6,4},{7,5},{8,10},{9,11},{10,... | collective-permute-start | bytes 1179656 | tf_op jit(solution)/shard_map/ppermute | solution.py:21
  8.4 1.8 %fusion = bf16[192,4096]{1,0:T(8,128)(2,1)S(1)} fusion(pred[128,192]{1,0:T(32,128)(4,1)S(1)} %get-tuple-element.60, bf16[128,4096]{1,0:T(8,128)(2,1)} %param.7, f32[192]{0:T(256)S(1)} %mul.14), kind=kOutput, calls=%fused_computation.1 | convolution fusion | flops 202899456 | bytes 2646784 | tf_op jit(solution)/shard_map/dot_general | solution.py:35
  11.4 3.4 %collective-permute-start.1 = (bf16[48,4096]{1,0:T(8,128)(2,1)}, bf16[48,4096]{1,0:T(8,128)(2,1)S(1)}, u32[]{:S(2)}, u32[]{:S(2)}) collective-permute-start(bf16[48,4096]{1,0:T(8,128)(2,1)} %get-tuple-element.66), channel_id=1, source_target_pairs={{0,2},{1,3},{2,0},{3,1},{4,6},{5,7},{6,4},{7,5},{8,10},{9,11},{10,... | collective-permute-start | bytes 1179656 | tf_op jit(solution)/shard_map/ppermute | solution.py:21
  14.9 3.4 %collective-permute-done.4.x2 = bf16[48,4096]{1,0:T(8,128)(2,1)} collective-permute-done((bf16[48,4096]{1,0:T(8,128)(2,1)}, bf16[48,4096]{1,0:T(8,128)(2,1)}, u32[]{:S(2)}, u32[]{:S(2)}) %collective-permute-start.4) | collective-permute-done | bytes 393248 | tf_op jit(solution)/shard_map/ppermute | solution.py:21
  18.3 8.1 %collective-permute-done.5.x3 = bf16[48,4096]{1,0:T(8,128)(2,1)} collective-permute-done((bf16[48,4096]{1,0:T(8,128)(2,1)}, bf16[48,4096]{1,0:T(8,128)(2,1)}, u32[]{:S(2)}, u32[]{:S(2)}) %collective-permute-start.5) | collective-permute-done | bytes 393248 | tf_op jit(solution)/shard_map/ppermute | solution.py:21
  28.4 1.5 collective-permute-start.6
  29.9 2.7 %collective-permute-start.7 = (bf16[192,1024]{1,0:T(8,128)(2,1)S(1)}, bf16[192,1024]{1,0:T(8,128)(2,1)S(1)}, u32[]{:S(2)}, u32[]{:S(2)}) collective-permute-start(bf16[192,1024]{1,0:T(8,128)(2,1)S(1)} %get-tuple-element.37), channel_id=1, source_target_pairs={{0,32},{16,48},{32,0},{48,16},{1,33},{17,49},{33,1},{49,17},{2,34}... | collective-permute-start | bytes 1179656 | tf_op jit(solution)/shard_map/ppermute | solution.py:27
  32.6 1.4 collective-permute-start.8
  34.1 7.4 %shard_map.86 = (bf16[192,768]{1,0:T(8,128)(2,1)S(1)}, f32[192,768]{1,0:T(8,128)S(1)}, f32[192,768]{1,0:T(8,128)S(1)}) custom-call(bf16[192,4096]{1,0:T(8,128)(2,1)S(1)} %get-tuple-element.31.x, bf16[4096,1536]{1,0:T(8,128)(2,1)} %bitcast.23), custom_call_target="tpu_custom_call" | custom-call | flops 2415919104 | bytes 12582912 | tf_op jit(solution)/shard_map/pallas_call | solution.py:296
  41.5 1.6 collective-permute-done.2.g3
  43.1 5.1 %shard_map.87 = (bf16[2,192,768]{2,1,0:T(8,128)(2,1)S(1)}, f32[8,128]{1,0:T(8,128)S(1)}) custom-call(bf16[48,4096]{1,0:T(8,128)(2,1)S(1)} %get-tuple-element.68.g0, bf16[48,4096]{1,0:T(8,128)(2,1)S(1)} %collective-permute-done.g1, bf16[48,4096]{1,0:T(8,128)(2,1)S(1)} %collective-permute-done.1.g2, bf16[48,4096]{1,0:T(8,128)(2,1)S(1)} %collective-permute-done.2.g3, ...), custom_call_target="tpu_custom_call" | custom-call | flops 1207959552 | bytes 6291456 | tf_op jit(solution)/shard_map/pallas_call | solution.py:306
  48.2 2.1 %collective-permute-done.7.rest_1_.refs_2_ = bf16[192,1024]{1,0:T(8,128)(2,1)S(1)} collective-permute-done((bf16[192,1024]{1,0:T(8,128)(2,1)S(1)}, bf16[192,1024]{1,0:T(8,128)(2,1)S(1)}, u32[]{:S(2)}, u32[]{:S(2)}) %collective-permute-start.7) | collective-permute-done | bytes 393248 | tf_op jit(solution)/shard_map/ppermute | solution.py:27
  50.3 1.8 %shard_map.88 = (bf16[4,192,1792]{2,1,0:T(8,128)(2,1)}, f32[8,128]{1,0:T(8,128)S(1)}) custom-call(bf16[48,4096]{1,0:T(8,128)(2,1)S(1)} %get-tuple-element.68.g0, bf16[48,4096]{1,0:T(8,128)(2,1)S(1)} %collective-permute-done.g1, bf16[48,4096]{1,0:T(8,128)(2,1)S(1)} %collective-permute-done.1.g2, bf16[48,4096]{1,0:T(8,128)(2,1)S(1)} %collective-permute-done.2.g3, ...), custom_call_target="tpu_custom_call" | custom-call | bytes 3145728 | tf_op jit(solution)/shard_map/pallas_call | solution.py:322
  52.1 4.6 %all-to-all-start.1 = ((bf16[4,192,1792]{2,1,0:T(8,128)(2,1)}), bf16[4,192,1792]{2,1,0:T(8,128)(2,1)}, u32[]{:S(2)}, u32[]{:S(2)}) async-start(bf16[4,192,1792]{2,1,0:T(8,128)(2,1)} %get-tuple-element.49), calls=%async_computation.1 | async-start | bytes 5505024 | tf_op jit(solution)/shard_map/all_to_all | solution.py:330
  56.7 1.4 collective-permute-start.12
  58.1 2.4 %collective-permute-start.13 = (bf16[2,192,768]{2,1,0:T(8,128)(2,1)S(1)}, bf16[2,192,768]{2,1,0:T(8,128)(2,1)S(1)}, u32[]{:S(2)}, u32[]{:S(2)}) collective-permute-start(bf16[2,192,768]{2,1,0:T(8,128)(2,1)S(1)} %get-tuple-element.34.dact.refs_4_), channel_id=1, source_target_pairs={{0,32},{16,48},{32,0},{48,16},{1,33},{17,49},{33,1},{49,17},{2,34}... | collective-permute-start | bytes 1769480 | tf_op jit(solution)/shard_map/ppermute | solution.py:27
  60.5 1.6 collective-permute-start.14
  62.1 6.9 %shard_map.89 = (bf16[48,4096]{1,0:T(8,128)(2,1)S(1)}, bf16[48,4096]{1,0:T(8,128)(2,1)S(1)}, bf16[48,4096]{1,0:T(8,128)(2,1)S(1)}, bf16[48,4096]{1,0:T(8,128)(2,1)S(1)}, f32[8,128]{1,0:T(8,128)}) custom-call(bf16[2,192,768]{2,1,0:T(8,128)(2,1)S(1)} %get-tuple-element.34.dact.refs_4_, bf16[4096,1536]{1,0:T(8,128)(2,1)} %bitcast.24, ...), custom_call_target="tpu_custom_call" | custom-call | flops 2415919104 | bytes 12582912 | tf_op jit(solution)/shard_map/pallas_call | solution.py:332
  70.5 3.4 %collective-permute-start.10 = (bf16[48,4096]{1,0:T(8,128)(2,1)S(1)}, bf16[48,4096]{1,0:T(8,128)(2,1)S(1)}, u32[]{:S(2)}, u32[]{:S(2)}) collective-permute-start(bf16[48,4096]{1,0:T(8,128)(2,1)S(1)} %get-tuple-element.43), channel_id=1, source_target_pairs={{0,2},{1,3},{2,0},{3,1},{4,6},{5,7},{6,4},{7,5},{8,10},{9,11},{10,... | collective-permute-start | bytes 1179656 | tf_op jit(solution)/shard_map/ppermute | solution.py:21
  73.9 12.4 %collective-permute-done.13.refs_6_ = bf16[2,192,768]{2,1,0:T(8,128)(2,1)S(1)} collective-permute-done((bf16[2,192,768]{2,1,0:T(8,128)(2,1)S(1)}, bf16[2,192,768]{2,1,0:T(8,128)(2,1)S(1)}, u32[]{:S(2)}, u32[]{:S(2)}) %collective-permute-start.13) | collective-permute-done | bytes 589856 | tf_op jit(solution)/shard_map/ppermute | solution.py:27
  86.4 4.9 %shard_map.91 = (bf16[8,128,1536]{2,1,0:T(8,128)(2,1)}, f32[8,128]{1,0:T(8,128)S(1)}) custom-call(bf16[192,1024]{1,0:T(8,128)(2,1)S(1)} %copy-done.8, bf16[192,1024]{1,0:T(8,128)(2,1)S(1)} %copy-done.2, bf16[192,1024]{1,0:T(8,128)(2,1)S(1)} %copy-done.4, bf16[192,1024]{1,0:T(8,128)(2,1)S(1)} %copy-done.6, ...), custom_call_target="tpu_custom_call" | custom-call | flops 2415919104 | bytes 3932160 | tf_op jit(solution)/shard_map/pallas_call | solution.py:192
  91.3 5.6 %all-to-all-start = ((bf16[8,128,1536]{2,1,0:T(8,128)(2,1)}), bf16[8,128,1536]{2,1,0:T(8,128)(2,1)}, u32[]{:S(2)}, u32[]{:S(2)}) async-start(bf16[8,128,1536]{2,1,0:T(8,128)(2,1)} %get-tuple-element.47), calls=%async_computation | async-start | bytes 6291456 | tf_op jit(solution)/shard_map/all_to_all | solution.py:343
  97.0 3.7 %collective-permute-start.11 = (bf16[48,4096]{1,0:T(8,128)(2,1)S(1)}, bf16[48,4096]{1,0:T(8,128)(2,1)S(1)}, u32[]{:S(2)}, u32[]{:S(2)}) collective-permute-start(bf16[48,4096]{1,0:T(8,128)(2,1)S(1)} %copy-done.10), channel_id=1, source_target_pairs={{0,3},{1,2},{2,1},{3,0},{4,7},{5,6},{6,5},{7,4},{8,11},{9,10},{10,... | collective-permute-start | bytes 1179656 | tf_op jit(solution)/shard_map/ppermute | solution.py:21
  100.7 4.5 %shard_map.93 = (f32[192,1024]{1,0:T(8,128)S(1)}, bf16[192,1024]{1,0:T(8,128)(2,1)S(1)}, bf16[192,1024]{1,0:T(8,128)(2,1)S(1)}, bf16[192,1024]{1,0:T(8,128)(2,1)S(1)}, f32[8,128]{1,0:T(8,128)}) custom-call(s32[4]{0:T(128)S(1)} %pad_add_fusion.at, bf16[4,192,1792]{2,1,0:T(8,128)(2,1)} %all-to-all-done.1.both, f32[8,128]{1,0:T(8,128)S(1)} %get-tuple-element.50.rest_0_), custom_call_target="tpu_custom_call" | custom-call | flops 1207959552 | bytes 2752512 | tf_op jit(solution)/shard_map/pallas_call | solution.py:344
  105.2 1.7 %collective-permute-start.15 = (bf16[192,1024]{1,0:T(8,128)(2,1)S(1)}, bf16[192,1024]{1,0:T(8,128)(2,1)S(1)}, u32[]{:S(2)}, u32[]{:S(2)}) collective-permute-start(bf16[192,1024]{1,0:T(8,128)(2,1)S(1)} %get-tuple-element.52), channel_id=1, source_target_pairs={{0,16},{16,32},{32,48},{48,0},{1,17},{17,33},{33,49},{49,1},{2,18}... | collective-permute-start | bytes 1179656 | tf_op jit(solution)/shard_map/ppermute | solution.py:27
  106.9 2.4 %collective-permute-start.16 = (bf16[192,1024]{1,0:T(8,128)(2,1)S(1)}, bf16[192,1024]{1,0:T(8,128)(2,1)S(1)}, u32[]{:S(2)}, u32[]{:S(2)}) collective-permute-start(bf16[192,1024]{1,0:T(8,128)(2,1)S(1)} %get-tuple-element.53), channel_id=1, source_target_pairs={{0,32},{16,48},{32,0},{48,16},{1,33},{17,49},{33,1},{49,17},{2,34}... | collective-permute-start | bytes 1179656 | tf_op jit(solution)/shard_map/ppermute | solution.py:27
  110.2 30.2 %collective-permute-done.11.a3 = bf16[48,4096]{1,0:T(8,128)(2,1)S(1)} collective-permute-done((bf16[48,4096]{1,0:T(8,128)(2,1)S(1)}, bf16[48,4096]{1,0:T(8,128)(2,1)S(1)}, u32[]{:S(2)}, u32[]{:S(2)}) %collective-permute-start.11) | collective-permute-done | bytes 393248 | tf_op jit(solution)/shard_map/ppermute | solution.py:21
  140.4 2.2 %shard_map.90 = (bf16[128,4096]{1,0:T(8,128)(2,1)}, f32[8,128]{1,0:T(8,128)S(1)}) custom-call(bf16[128,192]{1,0:T(8,128)(2,1)S(1)} %get-tuple-element.59.mask, bf16[48,4096]{1,0:T(8,128)(2,1)S(1)} %get-tuple-element.41.a0, bf16[48,4096]{1,0:T(8,128)(2,1)S(1)} %collective-permute-done.9.a1, bf16[48,4096]{1,0:T(8,128)(2,1)S(1)} %collective-permute-done.10.a2.refs_8_, ...), custom_call_target="tpu_custom_call" | custom-call | tf_op jit(solution)/shard_map/pallas_call | solution.py:359
  144.9 6.1 %collective-permute-done.18 = bf16[96,1024]{1,0:T(8,128)(2,1)S(1)} collective-permute-done((bf16[96,1024]{1,0:T(8,128)(2,1)S(1)}, bf16[96,1024]{1,0:T(8,128)(2,1)S(1)}, u32[]{:S(2)}, u32[]{:S(2)}) %collective-permute-start.18) | collective-permute-done | bytes 196640 | tf_op jit(solution)/shard_map/ppermute | solution.py:31
  152.2 4.9 %collective-permute-start.20 = (bf16[24,1024]{1,0:T(8,128)(2,1)S(1)}, bf16[24,1024]{1,0:T(8,128)(2,1)S(1)}, u32[]{:S(2)}, u32[]{:S(2)}) collective-permute-start(bf16[24,1024]{1,0:T(8,128)(2,1)S(1)} %get-tuple-element.70), channel_id=1, source_target_pairs={{0,8},{4,12},{8,0},{12,4},{1,9},{5,13},{9,1},{13,5},{2,10},{6,14},... | collective-permute-start | bytes 147464 | tf_op jit(solution)/shard_map/ppermute | solution.py:27
  157.2 1.4 collective-permute-start.21
  158.6 3.0 %shard_map.92 = (bf16[128,1536]{1,0:T(8,128)(2,1)}, f32[8,128]{1,0:T(8,128)S(1)}) custom-call(bf16[8,128,1536]{2,1,0:T(8,128)(2,1)} %all-to-all-done.parts), custom_call_target="tpu_custom_call" | custom-call | tf_op jit(solution)/shard_map/pallas_call | solution.py:366
  (81 shorter events, 14.3 us)
Async XLA Ops:
  2.3 5.8 %copy-start.13 = (s32[128,8]{0,1:T(8,128)S(1)}, s32[128,8]{0,1:T(8,128)}, u32[]{:S(2)}) copy-start(s32[128,8]{0,1:T(8,128)} %param.8) | copy-start | bytes 12292
  2.3 5.8 %copy-start.14 = (f32[128,8]{0,1:T(8,128)S(1)}, f32[128,8]{0,1:T(8,128)}, u32[]{:S(2)}) copy-start(f32[128,8]{0,1:T(8,128)} %param.9) | copy-start | bytes 12292
  4.0 10.8 %collective-permute-start.3 = (bf16[48,4096]{1,0:T(8,128)(2,1)}, bf16[48,4096]{1,0:T(8,128)(2,1)S(1)}, u32[]{:S(2)}, u32[]{:S(2)}) collective-permute-start(bf16[48,4096]{1,0:T(8,128)(2,1)} %get-tuple-element.63), channel_id=1, source_target_pairs={{0,1},{1,0},{2,3},{3,2},{4,5},{5,4},{6,7},{7,6},{8,9},{9,8},{10,11... | collective-permute-start | bytes 1179656 | tf_op jit(solution)/shard_map/ppermute | solution.py:21
  4.0 14.2 %collective-permute-start.4 = (bf16[48,4096]{1,0:T(8,128)(2,1)}, bf16[48,4096]{1,0:T(8,128)(2,1)}, u32[]{:S(2)}, u32[]{:S(2)}) collective-permute-start(bf16[48,4096]{1,0:T(8,128)(2,1)} %get-tuple-element.62), channel_id=1, source_target_pairs={{0,2},{1,3},{2,0},{3,1},{4,6},{5,7},{6,4},{7,5},{8,10},{9,11},{10,... | collective-permute-start | bytes 1179656 | tf_op jit(solution)/shard_map/ppermute | solution.py:21
  8.0 18.3 %collective-permute-start.5 = (bf16[48,4096]{1,0:T(8,128)(2,1)}, bf16[48,4096]{1,0:T(8,128)(2,1)}, u32[]{:S(2)}, u32[]{:S(2)}) collective-permute-start(bf16[48,4096]{1,0:T(8,128)(2,1)} %get-tuple-element.61), channel_id=1, source_target_pairs={{0,3},{1,2},{2,1},{3,0},{4,7},{5,6},{6,5},{7,4},{8,11},{9,10},{10,... | collective-permute-start | bytes 1179656 | tf_op jit(solution)/shard_map/ppermute | solution.py:21
  11.3 21.4 %collective-permute-start = (bf16[48,4096]{1,0:T(8,128)(2,1)}, bf16[48,4096]{1,0:T(8,128)(2,1)S(1)}, u32[]{:S(2)}, u32[]{:S(2)}) collective-permute-start(bf16[48,4096]{1,0:T(8,128)(2,1)} %get-tuple-element.67), channel_id=1, source_target_pairs={{0,1},{1,0},{2,3},{3,2},{4,5},{5,4},{6,7},{7,6},{8,9},{9,8},{10,11... | collective-permute-start | bytes 1179656 | tf_op jit(solution)/shard_map/ppermute | solution.py:21
  11.4 30.1 %collective-permute-start.1 = (bf16[48,4096]{1,0:T(8,128)(2,1)}, bf16[48,4096]{1,0:T(8,128)(2,1)S(1)}, u32[]{:S(2)}, u32[]{:S(2)}) collective-permute-start(bf16[48,4096]{1,0:T(8,128)(2,1)} %get-tuple-element.66), channel_id=1, source_target_pairs={{0,2},{1,3},{2,0},{3,1},{4,6},{5,7},{6,4},{7,5},{8,10},{9,11},{10,... | collective-permute-start | bytes 1179656 | tf_op jit(solution)/shard_map/ppermute | solution.py:21
  14.8 28.3 %collective-permute-start.2 = (bf16[48,4096]{1,0:T(8,128)(2,1)}, bf16[48,4096]{1,0:T(8,128)(2,1)S(1)}, u32[]{:S(2)}, u32[]{:S(2)}) collective-permute-start(bf16[48,4096]{1,0:T(8,128)(2,1)} %get-tuple-element.65), channel_id=1, source_target_pairs={{0,3},{1,2},{2,1},{3,0},{4,7},{5,6},{6,5},{7,4},{8,11},{9,10},{10,... | collective-permute-start | bytes 1179656 | tf_op jit(solution)/shard_map/ppermute | solution.py:21
  28.4 19.8 %collective-permute-start.6 = (bf16[192,1024]{1,0:T(8,128)(2,1)S(1)}, bf16[192,1024]{1,0:T(8,128)(2,1)S(1)}, u32[]{:S(2)}, u32[]{:S(2)}) collective-permute-start(bf16[192,1024]{1,0:T(8,128)(2,1)S(1)} %get-tuple-element.36), channel_id=1, source_target_pairs={{0,16},{16,32},{32,48},{48,0},{1,17},{17,33},{33,49},{49,1},{2,18}... | collective-permute-start | bytes 1179656 | tf_op jit(solution)/shard_map/ppermute | solution.py:27
  29.9 20.3 %collective-permute-start.7 = (bf16[192,1024]{1,0:T(8,128)(2,1)S(1)}, bf16[192,1024]{1,0:T(8,128)(2,1)S(1)}, u32[]{:S(2)}, u32[]{:S(2)}) collective-permute-start(bf16[192,1024]{1,0:T(8,128)(2,1)S(1)} %get-tuple-element.37), channel_id=1, source_target_pairs={{0,32},{16,48},{32,0},{48,16},{1,33},{17,49},{33,1},{49,17},{2,34}... | collective-permute-start | bytes 1179656 | tf_op jit(solution)/shard_map/ppermute | solution.py:27
  32.6 17.6 %collective-permute-start.8 = (bf16[192,1024]{1,0:T(8,128)(2,1)S(1)}, bf16[192,1024]{1,0:T(8,128)(2,1)S(1)}, u32[]{:S(2)}, u32[]{:S(2)}) collective-permute-start(bf16[192,1024]{1,0:T(8,128)(2,1)S(1)} %get-tuple-element.38), channel_id=1, source_target_pairs={{0,48},{16,0},{32,16},{48,32},{1,49},{17,1},{33,17},{49,33},{2,50}... | collective-permute-start | bytes 1179656 | tf_op jit(solution)/shard_map/ppermute | solution.py:27
  52.1 39.2 %all-to-all-start.1 = ((bf16[4,192,1792]{2,1,0:T(8,128)(2,1)}), bf16[4,192,1792]{2,1,0:T(8,128)(2,1)}, u32[]{:S(2)}, u32[]{:S(2)}) async-start(bf16[4,192,1792]{2,1,0:T(8,128)(2,1)} %get-tuple-element.49), calls=%async_computation.1 | async-start | bytes 5505024 | tf_op jit(solution)/shard_map/all_to_all | solution.py:330
  56.7 17.3 %collective-permute-start.12 = (bf16[2,192,768]{2,1,0:T(8,128)(2,1)S(1)}, bf16[2,192,768]{2,1,0:T(8,128)(2,1)S(1)}, u32[]{:S(2)}, u32[]{:S(2)}) collective-permute-start(bf16[2,192,768]{2,1,0:T(8,128)(2,1)S(1)} %get-tuple-element.34.dact.refs_4_), channel_id=1, source_target_pairs={{0,16},{16,32},{32,48},{48,0},{1,17},{17,33},{33,49},{49,1},{2,18}... | collective-permute-start | bytes 1769480 | tf_op jit(solution)/shard_map/ppermute | solution.py:27
  58.1 28.2 %collective-permute-start.13 = (bf16[2,192,768]{2,1,0:T(8,128)(2,1)S(1)}, bf16[2,192,768]{2,1,0:T(8,128)(2,1)S(1)}, u32[]{:S(2)}, u32[]{:S(2)}) collective-permute-start(bf16[2,192,768]{2,1,0:T(8,128)(2,1)S(1)} %get-tuple-element.34.dact.refs_4_), channel_id=1, source_target_pairs={{0,32},{16,48},{32,0},{48,16},{1,33},{17,49},{33,1},{49,17},{2,34}... | collective-permute-start | bytes 1769480 | tf_op jit(solution)/shard_map/ppermute | solution.py:27
  60.5 25.9 %collective-permute-start.14 = (bf16[2,192,768]{2,1,0:T(8,128)(2,1)S(1)}, bf16[2,192,768]{2,1,0:T(8,128)(2,1)S(1)}, u32[]{:S(2)}, u32[]{:S(2)}) collective-permute-start(bf16[2,192,768]{2,1,0:T(8,128)(2,1)S(1)} %get-tuple-element.34.dact.refs_4_), channel_id=1, source_target_pairs={{0,48},{16,0},{32,16},{48,32},{1,49},{17,1},{33,17},{49,33},{2,50}... | collective-permute-start | bytes 1769480 | tf_op jit(solution)/shard_map/ppermute | solution.py:27
  62.0 24.3 %copy-start.2 = (bf16[192,1024]{1,0:T(8,128)(2,1)S(1)}, bf16[192,1024]{1,0:T(8,128)(2,1)}, u32[]{:S(2)}) copy-start(bf16[192,1024]{1,0:T(8,128)(2,1)} %copy-done.1) | copy-start | bytes 1179652
  62.0 24.3 %copy-start.4 = (bf16[192,1024]{1,0:T(8,128)(2,1)S(1)}, bf16[192,1024]{1,0:T(8,128)(2,1)}, u32[]{:S(2)}) copy-start(bf16[192,1024]{1,0:T(8,128)(2,1)} %copy-done.3) | copy-start | bytes 1179652
  62.0 24.3 %copy-start.6 = (bf16[192,1024]{1,0:T(8,128)(2,1)S(1)}, bf16[192,1024]{1,0:T(8,128)(2,1)}, u32[]{:S(2)}) copy-start(bf16[192,1024]{1,0:T(8,128)(2,1)} %copy-done.5) | copy-start | bytes 1179652
  62.0 24.3 %copy-start.8 = (bf16[192,1024]{1,0:T(8,128)(2,1)S(1)}, bf16[192,1024]{1,0:T(8,128)(2,1)}, u32[]{:S(2)}) copy-start(bf16[192,1024]{1,0:T(8,128)(2,1)} %copy-done.7) | copy-start | bytes 1179652
  70.5 15.9 %collective-permute-start.10 = (bf16[48,4096]{1,0:T(8,128)(2,1)S(1)}, bf16[48,4096]{1,0:T(8,128)(2,1)S(1)}, u32[]{:S(2)}, u32[]{:S(2)}) collective-permute-start(bf16[48,4096]{1,0:T(8,128)(2,1)S(1)} %get-tuple-element.43), channel_id=1, source_target_pairs={{0,2},{1,3},{2,0},{3,1},{4,6},{5,7},{6,4},{7,5},{8,10},{9,11},{10,... | collective-permute-start | bytes 1179656 | tf_op jit(solution)/shard_map/ppermute | solution.py:21
  91.3 5.6 %copy-start.12 = (bf16[48,4096]{1,0:T(8,128)(2,1)S(1)}, bf16[48,4096]{1,0:T(8,128)(2,1)}, u32[]{:S(2)}) copy-start(bf16[48,4096]{1,0:T(8,128)(2,1)} %copy-done.11) | copy-start | bytes 1179652
  91.3 5.7 %copy-start.10 = (bf16[48,4096]{1,0:T(8,128)(2,1)S(1)}, bf16[48,4096]{1,0:T(8,128)(2,1)}, u32[]{:S(2)}) copy-start(bf16[48,4096]{1,0:T(8,128)(2,1)} %copy-done.9) | copy-start | bytes 1179652
  91.3 67.4 %all-to-all-start = ((bf16[8,128,1536]{2,1,0:T(8,128)(2,1)}), bf16[8,128,1536]{2,1,0:T(8,128)(2,1)}, u32[]{:S(2)}, u32[]{:S(2)}) async-start(bf16[8,128,1536]{2,1,0:T(8,128)(2,1)} %get-tuple-element.47), calls=%async_computation | async-start | bytes 6291456 | tf_op jit(solution)/shard_map/all_to_all | solution.py:343
  96.9 13.3 %collective-permute-start.9 = (bf16[48,4096]{1,0:T(8,128)(2,1)S(1)}, bf16[48,4096]{1,0:T(8,128)(2,1)S(1)}, u32[]{:S(2)}, u32[]{:S(2)}) collective-permute-start(bf16[48,4096]{1,0:T(8,128)(2,1)S(1)} %copy-done.12), channel_id=1, source_target_pairs={{0,1},{1,0},{2,3},{3,2},{4,5},{5,4},{6,7},{7,6},{8,9},{9,8},{10,11... | collective-permute-start | bytes 1179656 | tf_op jit(solution)/shard_map/ppermute | solution.py:21
  97.0 43.4 %collective-permute-start.11 = (bf16[48,4096]{1,0:T(8,128)(2,1)S(1)}, bf16[48,4096]{1,0:T(8,128)(2,1)S(1)}, u32[]{:S(2)}, u32[]{:S(2)}) collective-permute-start(bf16[48,4096]{1,0:T(8,128)(2,1)S(1)} %copy-done.10), channel_id=1, source_target_pairs={{0,3},{1,2},{2,1},{3,0},{4,7},{5,6},{6,5},{7,4},{8,11},{9,10},{10,... | collective-permute-start | bytes 1179656 | tf_op jit(solution)/shard_map/ppermute | solution.py:21
  105.2 37.4 %collective-permute-start.15 = (bf16[192,1024]{1,0:T(8,128)(2,1)S(1)}, bf16[192,1024]{1,0:T(8,128)(2,1)S(1)}, u32[]{:S(2)}, u32[]{:S(2)}) collective-permute-start(bf16[192,1024]{1,0:T(8,128)(2,1)S(1)} %get-tuple-element.52), channel_id=1, source_target_pairs={{0,16},{16,32},{32,48},{48,0},{1,17},{17,33},{33,49},{49,1},{2,18}... | collective-permute-start | bytes 1179656 | tf_op jit(solution)/shard_map/ppermute | solution.py:27
  106.9 35.7 %collective-permute-start.16 = (bf16[192,1024]{1,0:T(8,128)(2,1)S(1)}, bf16[192,1024]{1,0:T(8,128)(2,1)S(1)}, u32[]{:S(2)}, u32[]{:S(2)}) collective-permute-start(bf16[192,1024]{1,0:T(8,128)(2,1)S(1)} %get-tuple-element.53), channel_id=1, source_target_pairs={{0,32},{16,48},{32,0},{48,16},{1,33},{17,49},{33,1},{49,17},{2,34}... | collective-permute-start | bytes 1179656 | tf_op jit(solution)/shard_map/ppermute | solution.py:27
  109.3 33.3 %collective-permute-start.17 = (bf16[192,1024]{1,0:T(8,128)(2,1)S(1)}, bf16[192,1024]{1,0:T(8,128)(2,1)S(1)}, u32[]{:S(2)}, u32[]{:S(2)}) collective-permute-start(bf16[192,1024]{1,0:T(8,128)(2,1)S(1)} %get-tuple-element.54), channel_id=1, source_target_pairs={{0,48},{16,0},{32,16},{48,32},{1,49},{17,1},{33,17},{49,33},{2,50}... | collective-permute-start | bytes 1179656 | tf_op jit(solution)/shard_map/ppermute | solution.py:27
  144.0 7.0 %collective-permute-start.18 = (bf16[96,1024]{1,0:T(8,128)(2,1)S(1)}, bf16[96,1024]{1,0:T(8,128)(2,1)S(1)}, u32[]{:S(2)}, u32[]{:S(2)}) collective-permute-start(bf16[96,1024]{1,0:T(8,128)(2,1)S(1)} %get-tuple-element.57), channel_id=1, source_target_pairs={{0,64},{64,0},{1,65},{65,1},{2,66},{66,2},{3,67},{67,3},{4,68},{68... | collective-permute-start | bytes 589832 | tf_op jit(solution)/shard_map/ppermute | solution.py:31
  151.1 10.6 %collective-permute-start.19 = (bf16[24,1024]{1,0:T(8,128)(2,1)S(1)}, bf16[24,1024]{1,0:T(8,128)(2,1)S(1)}, u32[]{:S(2)}, u32[]{:S(2)}) collective-permute-start(bf16[24,1024]{1,0:T(8,128)(2,1)S(1)} %get-tuple-element.71), channel_id=1, source_target_pairs={{0,4},{4,8},{8,12},{12,0},{1,5},{5,9},{9,13},{13,1},{2,6},{6,10},{... | collective-permute-start | bytes 147464 | tf_op jit(solution)/shard_map/ppermute | solution.py:27
  152.2 9.4 %collective-permute-start.20 = (bf16[24,1024]{1,0:T(8,128)(2,1)S(1)}, bf16[24,1024]{1,0:T(8,128)(2,1)S(1)}, u32[]{:S(2)}, u32[]{:S(2)}) collective-permute-start(bf16[24,1024]{1,0:T(8,128)(2,1)S(1)} %get-tuple-element.70), channel_id=1, source_target_pairs={{0,8},{4,12},{8,0},{12,4},{1,9},{5,13},{9,1},{13,5},{2,10},{6,14},... | collective-permute-start | bytes 147464 | tf_op jit(solution)/shard_map/ppermute | solution.py:27
  157.2 4.5 %collective-permute-start.21 = (bf16[24,1024]{1,0:T(8,128)(2,1)S(1)}, bf16[24,1024]{1,0:T(8,128)(2,1)S(1)}, u32[]{:S(2)}, u32[]{:S(2)}) collective-permute-start(bf16[24,1024]{1,0:T(8,128)(2,1)S(1)} %get-tuple-element.69), channel_id=1, source_target_pairs={{0,12},{4,0},{8,4},{12,8},{1,13},{5,1},{9,5},{13,9},{2,14},{6,2},{... | collective-permute-start | bytes 147464 | tf_op jit(solution)/shard_map/ppermute | solution.py:27
  (7 other events, 11.5 us)

commit v6 on v5

--- a/solution.py
+++ b/solution.py
@@ -339,7 +339,7 @@
         limit=18,
     )(dact, gate_up, sent_mark)
     arrived = [back[0]] + [swap_expert(back[k], k) for k in (1, 2, 3)]
-    parts, mark = tile_call(xa, da, [arrived[2]])
+    parts, mark = tile_call(xa, da, arrived[2:])
     gate = lax.all_to_all(parts, ("w", "y"), split_axis=0, concat_axis=0, tiled=True)
     *parts, _ = call(
         down_step,

time: 165 us -> 153 us (0.927)
  starting transfers between devices: 49.5 us -> 44.9 us
  waiting for transfers between devices: 63.8 us -> 59.5 us
    ppermute x9, waiting for transfers between devices: 43.2 us -> 14.8 us  [swap_expert(): return lax.ppermute(a, ('v', 'c'), [(i, i ^ k) for i in range(4)])]
    ppermute x12, waiting for transfers between devices: 14.5 us -> 32 us  [shift(): return lax.ppermute(a, axis, [(i, (i + j) % 4) for i in range(4)])]
    ppermute x1, waiting for transfers between devices: 6.11 us -> 12.7 us  [swap_w(): return lax.ppermute(a, 'w', [(0, 1), (1, 0)])]
    ppermute x9, starting transfers between devices: 14.8 us -> 11.7 us  [swap_expert(): return lax.ppermute(a, ('v', 'c'), [(i, i ^ k) for i in range(4)])]
    ppermute x12, starting transfers between devices: 23.5 us -> 21.6 us  [shift(): return lax.ppermute(a, axis, [(i, (i + j) % 4) for i in range(4)])]
  transfers between devices with their start and end apart: 24 -> 24, of which waited for: 7 -> 10; matrix products, arithmetic and copies ran while one was open for 2% -> 2% of each run, Pallas kernels for 23% -> 24%
where the time goes in v6:
time: 153 us; the launch traced here: 152 us
  waiting for transfers between devices  59.5 us (39%)
  starting transfers between devices  44.9 us (29%)
  Pallas kernels  39.6 us (26%)
  local copies, waits for them, and re-layouts  3.53 us (2%)
  matrix products  2.46 us (2%)
    ppermute x12, waiting for transfers between devices, shift(): return lax.ppermute(a, axis, [(i, (i + j) % 4) for i in range(4)])  32 us
    ppermute x12, starting transfers between devices, shift(): return lax.ppermute(a, axis, [(i, (i + j) % 4) for i in range(4)])  21.6 us
    ppermute x9, waiting for transfers between devices, swap_expert(): return lax.ppermute(a, ('v', 'c'), [(i, i ^ k) for i in range(4)])  14.8 us
    ppermute x1, waiting for transfers between devices, swap_w(): return lax.ppermute(a, 'w', [(0, 1), (1, 0)])  12.7 us
    ppermute x9, starting transfers between devices, swap_expert(): return lax.ppermute(a, ('v', 'c'), [(i, i ^ k) for i in range(4)])  11.7 us
    pallas_call x1, Pallas kernels, shards(): call(act_step, 'va', [shape(rows, inner), shape(rows, inner, dtype=F32),...  7.42 us
    pallas_call x1, Pallas kernels, shards(): call(back_step, 'vaa', [shape(CAP, width)] * 4 + [MARK], [pltpu.VMEM((n,...  6.93 us
    pallas_call x1, Pallas kernels, shards(): call(dh_step, 'aaaaaaa', [shape(2, rows, inner), MARK], [pltpu.VMEM((rows...  5.09 us
  transfers between devices with their start and end apart: 24, of which 10 were waited for; matrix products, arithmetic and copies ran while one was open for 2% of the time, Pallas kernels for 24%

profile of v6, /device:TPU:0, one launch (start us, length us, event | category | flops | bytes accessed | tf_op | source)
XLA Modules:
  0.0 152.3 jit_solution(835798439531596335)
XLA Ops:
  4.0 4.0 %collective-permute-start.4 = (bf16[48,4096]{1,0:T(8,128)(2,1)}, bf16[48,4096]{1,0:T(8,128)(2,1)}, u32[]{:S(2)}, u32[]{:S(2)}) collective-permute-start(bf16[48,4096]{1,0:T(8,128)(2,1)} %get-tuple-element.62), channel_id=1, source_target_pairs={{0,2},{1,3},{2,0},{3,1},{4,6},{5,7},{6,4},{7,5},{8,10},{9,11},{10,... | collective-permute-start | bytes 1179656 | tf_op jit(solution)/shard_map/ppermute | solution.py:21
  8.4 1.8 %fusion = bf16[192,4096]{1,0:T(8,128)(2,1)S(1)} fusion(pred[128,192]{1,0:T(32,128)(4,1)S(1)} %get-tuple-element.60, bf16[128,4096]{1,0:T(8,128)(2,1)} %param.7, f32[192]{0:T(256)S(1)} %mul.14), kind=kOutput, calls=%fused_computation.1 | convolution fusion | flops 202899456 | bytes 2646784 | tf_op jit(solution)/shard_map/dot_general | solution.py:35
  11.4 3.4 %collective-permute-start.1 = (bf16[48,4096]{1,0:T(8,128)(2,1)}, bf16[48,4096]{1,0:T(8,128)(2,1)S(1)}, u32[]{:S(2)}, u32[]{:S(2)}) collective-permute-start(bf16[48,4096]{1,0:T(8,128)(2,1)} %get-tuple-element.66), channel_id=1, source_target_pairs={{0,2},{1,3},{2,0},{3,1},{4,6},{5,7},{6,4},{7,5},{8,10},{9,11},{10,... | collective-permute-start | bytes 1179656 | tf_op jit(solution)/shard_map/ppermute | solution.py:21
  14.9 3.4 %collective-permute-done.4.x2 = bf16[48,4096]{1,0:T(8,128)(2,1)} collective-permute-done((bf16[48,4096]{1,0:T(8,128)(2,1)}, bf16[48,4096]{1,0:T(8,128)(2,1)}, u32[]{:S(2)}, u32[]{:S(2)}) %collective-permute-start.4) | collective-permute-done | bytes 393248 | tf_op jit(solution)/shard_map/ppermute | solution.py:21
  18.2 8.1 %collective-permute-done.5.x3 = bf16[48,4096]{1,0:T(8,128)(2,1)} collective-permute-done((bf16[48,4096]{1,0:T(8,128)(2,1)}, bf16[48,4096]{1,0:T(8,128)(2,1)}, u32[]{:S(2)}, u32[]{:S(2)}) %collective-permute-start.5) | collective-permute-done | bytes 393248 | tf_op jit(solution)/shard_map/ppermute | solution.py:21
  28.4 1.5 collective-permute-start.6
  29.9 2.7 %collective-permute-start.7 = (bf16[192,1024]{1,0:T(8,128)(2,1)S(1)}, bf16[192,1024]{1,0:T(8,128)(2,1)S(1)}, u32[]{:S(2)}, u32[]{:S(2)}) collective-permute-start(bf16[192,1024]{1,0:T(8,128)(2,1)S(1)} %get-tuple-element.37), channel_id=1, source_target_pairs={{0,32},{16,48},{32,0},{48,16},{1,33},{17,49},{33,1},{49,17},{2,34}... | collective-permute-start | bytes 1179656 | tf_op jit(solution)/shard_map/ppermute | solution.py:27
  32.6 1.4 collective-permute-start.8
  34.1 7.4 %shard_map.86 = (bf16[192,768]{1,0:T(8,128)(2,1)S(1)}, f32[192,768]{1,0:T(8,128)S(1)}, f32[192,768]{1,0:T(8,128)S(1)}) custom-call(bf16[192,4096]{1,0:T(8,128)(2,1)S(1)} %get-tuple-element.31.x, bf16[4096,1536]{1,0:T(8,128)(2,1)} %bitcast.23), custom_call_target="tpu_custom_call" | custom-call | flops 2415919104 | bytes 12582912 | tf_op jit(solution)/shard_map/pallas_call | solution.py:296
  41.5 1.6 %collective-permute-done.2.g3 = bf16[48,4096]{1,0:T(8,128)(2,1)S(1)} collective-permute-done((bf16[48,4096]{1,0:T(8,128)(2,1)}, bf16[48,4096]{1,0:T(8,128)(2,1)S(1)}, u32[]{:S(2)}, u32[]{:S(2)}) %collective-permute-start.2) | collective-permute-done | bytes 393248 | tf_op jit(solution)/shard_map/ppermute | solution.py:21
  43.1 5.1 %shard_map.87 = (bf16[2,192,768]{2,1,0:T(8,128)(2,1)S(1)}, f32[8,128]{1,0:T(8,128)S(1)}) custom-call(bf16[48,4096]{1,0:T(8,128)(2,1)S(1)} %get-tuple-element.68.g0, bf16[48,4096]{1,0:T(8,128)(2,1)S(1)} %collective-permute-done.g1, bf16[48,4096]{1,0:T(8,128)(2,1)S(1)} %collective-permute-done.1.g2, bf16[48,4096]{1,0:T(8,128)(2,1)S(1)} %collective-permute-done.2.g3, ...), custom_call_target="tpu_custom_call" | custom-call | flops 1207959552 | bytes 6291456 | tf_op jit(solution)/shard_map/pallas_call | solution.py:306
  48.2 2.1 %collective-permute-done.7.rest_1_.refs_2_ = bf16[192,1024]{1,0:T(8,128)(2,1)S(1)} collective-permute-done((bf16[192,1024]{1,0:T(8,128)(2,1)S(1)}, bf16[192,1024]{1,0:T(8,128)(2,1)S(1)}, u32[]{:S(2)}, u32[]{:S(2)}) %collective-permute-start.7) | collective-permute-done | bytes 393248 | tf_op jit(solution)/shard_map/ppermute | solution.py:27
  50.2 1.7 %shard_map.88 = (bf16[4,192,1792]{2,1,0:T(8,128)(2,1)}, f32[8,128]{1,0:T(8,128)S(1)}) custom-call(bf16[48,4096]{1,0:T(8,128)(2,1)S(1)} %get-tuple-element.68.g0, bf16[48,4096]{1,0:T(8,128)(2,1)S(1)} %collective-permute-done.g1, bf16[48,4096]{1,0:T(8,128)(2,1)S(1)} %collective-permute-done.1.g2, bf16[48,4096]{1,0:T(8,128)(2,1)S(1)} %collective-permute-done.2.g3, ...), custom_call_target="tpu_custom_call" | custom-call | bytes 3145728 | tf_op jit(solution)/shard_map/pallas_call | solution.py:322
  52.0 4.6 %all-to-all-start.1 = ((bf16[4,192,1792]{2,1,0:T(8,128)(2,1)}), bf16[4,192,1792]{2,1,0:T(8,128)(2,1)}, u32[]{:S(2)}, u32[]{:S(2)}) async-start(bf16[4,192,1792]{2,1,0:T(8,128)(2,1)} %get-tuple-element.49), calls=%async_computation.1 | async-start | bytes 5505024 | tf_op jit(solution)/shard_map/all_to_all | solution.py:330
  56.6 1.4 collective-permute-start.12
  58.0 2.4 %collective-permute-start.13 = (bf16[2,192,768]{2,1,0:T(8,128)(2,1)S(1)}, bf16[2,192,768]{2,1,0:T(8,128)(2,1)S(1)}, u32[]{:S(2)}, u32[]{:S(2)}) collective-permute-start(bf16[2,192,768]{2,1,0:T(8,128)(2,1)S(1)} %get-tuple-element.34.dact.refs_4_), channel_id=1, source_target_pairs={{0,32},{16,48},{32,0},{48,16},{1,33},{17,49},{33,1},{49,17},{2,34}... | collective-permute-start | bytes 1769480 | tf_op jit(solution)/shard_map/ppermute | solution.py:27
  60.4 1.6 %collective-permute-start.14 = (bf16[2,192,768]{2,1,0:T(8,128)(2,1)S(1)}, bf16[2,192,768]{2,1,0:T(8,128)(2,1)S(1)}, u32[]{:S(2)}, u32[]{:S(2)}) collective-permute-start(bf16[2,192,768]{2,1,0:T(8,128)(2,1)S(1)} %get-tuple-element.34.dact.refs_4_), channel_id=1, source_target_pairs={{0,48},{16,0},{32,16},{48,32},{1,49},{17,1},{33,17},{49,33},{2,50}... | collective-permute-start | bytes 1769480 | tf_op jit(solution)/shard_map/ppermute | solution.py:27
  62.0 6.9 %shard_map.89 = (bf16[48,4096]{1,0:T(8,128)(2,1)S(1)}, bf16[48,4096]{1,0:T(8,128)(2,1)S(1)}, bf16[48,4096]{1,0:T(8,128)(2,1)S(1)}, bf16[48,4096]{1,0:T(8,128)(2,1)S(1)}, f32[8,128]{1,0:T(8,128)}) custom-call(bf16[2,192,768]{2,1,0:T(8,128)(2,1)S(1)} %get-tuple-element.34.dact.refs_4_, bf16[4096,1536]{1,0:T(8,128)(2,1)} %bitcast.24, ...), custom_call_target="tpu_custom_call" | custom-call | flops 2415919104 | bytes 12582912 | tf_op jit(solution)/shard_map/pallas_call | solution.py:332
  68.9 3.5 %collective-permute-start.10 = (bf16[48,4096]{1,0:T(8,128)(2,1)S(1)}, bf16[48,4096]{1,0:T(8,128)(2,1)S(1)}, u32[]{:S(2)}, u32[]{:S(2)}) collective-permute-start(bf16[48,4096]{1,0:T(8,128)(2,1)S(1)} %get-tuple-element.43), channel_id=1, source_target_pairs={{0,2},{1,3},{2,0},{3,1},{4,6},{5,7},{6,4},{7,5},{8,10},{9,11},{10,... | collective-permute-start | bytes 1179656 | tf_op jit(solution)/shard_map/ppermute | solution.py:21
  72.5 13.8 %collective-permute-done.13.refs_6_ = bf16[2,192,768]{2,1,0:T(8,128)(2,1)S(1)} collective-permute-done((bf16[2,192,768]{2,1,0:T(8,128)(2,1)S(1)}, bf16[2,192,768]{2,1,0:T(8,128)(2,1)S(1)}, u32[]{:S(2)}, u32[]{:S(2)}) %collective-permute-start.13) | collective-permute-done | bytes 589856 | tf_op jit(solution)/shard_map/ppermute | solution.py:27
  86.3 1.8 %collective-permute-done.11.a3.refs_9_ = bf16[48,4096]{1,0:T(8,128)(2,1)S(1)} collective-permute-done((bf16[48,4096]{1,0:T(8,128)(2,1)S(1)}, bf16[48,4096]{1,0:T(8,128)(2,1)S(1)}, u32[]{:S(2)}, u32[]{:S(2)}) %collective-permute-start.11) | collective-permute-done | bytes 393248 | tf_op jit(solution)/shard_map/ppermute | solution.py:21
  88.1 4.8 %shard_map.91 = (bf16[8,128,1536]{2,1,0:T(8,128)(2,1)}, f32[8,128]{1,0:T(8,128)S(1)}) custom-call(bf16[192,1024]{1,0:T(8,128)(2,1)S(1)} %copy-done.8, bf16[192,1024]{1,0:T(8,128)(2,1)S(1)} %copy-done.2, bf16[192,1024]{1,0:T(8,128)(2,1)S(1)} %copy-done.4, bf16[192,1024]{1,0:T(8,128)(2,1)S(1)} %copy-done.6, ...), custom_call_target="tpu_custom_call" | custom-call | flops 2415919104 | bytes 3932160 | tf_op jit(solution)/shard_map/pallas_call | solution.py:192
  92.9 5.0 %all-to-all-start = ((bf16[8,128,1536]{2,1,0:T(8,128)(2,1)}), bf16[8,128,1536]{2,1,0:T(8,128)(2,1)}, u32[]{:S(2)}, u32[]{:S(2)}) async-start(bf16[8,128,1536]{2,1,0:T(8,128)(2,1)} %get-tuple-element.47), calls=%async_computation | async-start | bytes 6291456 | tf_op jit(solution)/shard_map/all_to_all | solution.py:343
  98.5 4.5 %shard_map.93 = (f32[192,1024]{1,0:T(8,128)S(1)}, bf16[192,1024]{1,0:T(8,128)(2,1)S(1)}, bf16[192,1024]{1,0:T(8,128)(2,1)S(1)}, bf16[192,1024]{1,0:T(8,128)(2,1)S(1)}, f32[8,128]{1,0:T(8,128)}) custom-call(s32[4]{0:T(128)S(1)} %pad_add_fusion.at, bf16[4,192,1792]{2,1,0:T(8,128)(2,1)} %all-to-all-done.1.both, f32[8,128]{1,0:T(8,128)S(1)} %get-tuple-element.50.rest_0_), custom_call_target="tpu_custom_call" | custom-call | flops 1207959552 | bytes 2752512 | tf_op jit(solution)/shard_map/pallas_call | solution.py:344
  105.2 1.9 %collective-permute-start.17 = (bf16[192,1024]{1,0:T(8,128)(2,1)S(1)}, bf16[192,1024]{1,0:T(8,128)(2,1)S(1)}, u32[]{:S(2)}, u32[]{:S(2)}) collective-permute-start(bf16[192,1024]{1,0:T(8,128)(2,1)S(1)} %get-tuple-element.54), channel_id=1, source_target_pairs={{0,48},{16,0},{32,16},{48,32},{1,49},{17,1},{33,17},{49,33},{2,50}... | collective-permute-start | bytes 1179656 | tf_op jit(solution)/shard_map/ppermute | solution.py:27
  107.1 2.2 %shard_map.90 = (bf16[128,4096]{1,0:T(8,128)(2,1)}, f32[8,128]{1,0:T(8,128)S(1)}) custom-call(bf16[128,192]{1,0:T(8,128)(2,1)S(1)} %get-tuple-element.59.mask, bf16[48,4096]{1,0:T(8,128)(2,1)S(1)} %get-tuple-element.41.a0, bf16[48,4096]{1,0:T(8,128)(2,1)S(1)} %collective-permute-done.9.a1, bf16[48,4096]{1,0:T(8,128)(2,1)S(1)} %collective-permute-done.10.a2.refs_8_, ...), custom_call_target="tpu_custom_call" | custom-call | tf_op jit(solution)/shard_map/pallas_call | solution.py:359
  109.3 14.5 %collective-permute-done.15.r1 = bf16[192,1024]{1,0:T(8,128)(2,1)S(1)} collective-permute-done((bf16[192,1024]{1,0:T(8,128)(2,1)S(1)}, bf16[192,1024]{1,0:T(8,128)(2,1)S(1)}, u32[]{:S(2)}, u32[]{:S(2)}) %collective-permute-start.15) | collective-permute-done | bytes 393248 | tf_op jit(solution)/shard_map/ppermute | solution.py:27
  125.7 2.0 %collective-permute-start.18 = (bf16[96,1024]{1,0:T(8,128)(2,1)S(1)}, bf16[96,1024]{1,0:T(8,128)(2,1)S(1)}, u32[]{:S(2)}, u32[]{:S(2)}) collective-permute-start(bf16[96,1024]{1,0:T(8,128)(2,1)S(1)} %get-tuple-element.57), channel_id=1, source_target_pairs={{0,64},{64,0},{1,65},{65,1},{2,66},{66,2},{3,67},{67,3},{4,68},{68... | collective-permute-start | bytes 589832 | tf_op jit(solution)/shard_map/ppermute | solution.py:31
  127.8 12.7 %collective-permute-done.18 = bf16[96,1024]{1,0:T(8,128)(2,1)S(1)} collective-permute-done((bf16[96,1024]{1,0:T(8,128)(2,1)S(1)}, bf16[96,1024]{1,0:T(8,128)(2,1)S(1)}, u32[]{:S(2)}, u32[]{:S(2)}) %collective-permute-start.18) | collective-permute-done | bytes 196640 | tf_op jit(solution)/shard_map/ppermute | solution.py:31
  140.5 1.6 %collective-permute-start.19 = (bf16[24,1024]{1,0:T(8,128)(2,1)S(1)}, bf16[24,1024]{1,0:T(8,128)(2,1)S(1)}, u32[]{:S(2)}, u32[]{:S(2)}) collective-permute-start(bf16[24,1024]{1,0:T(8,128)(2,1)S(1)} %get-tuple-element.71), channel_id=1, source_target_pairs={{0,4},{4,8},{8,12},{12,0},{1,5},{5,9},{9,13},{13,1},{2,6},{6,10},{... | collective-permute-start | bytes 147464 | tf_op jit(solution)/shard_map/ppermute | solution.py:27
  142.2 4.9 %collective-permute-start.20 = (bf16[24,1024]{1,0:T(8,128)(2,1)S(1)}, bf16[24,1024]{1,0:T(8,128)(2,1)S(1)}, u32[]{:S(2)}, u32[]{:S(2)}) collective-permute-start(bf16[24,1024]{1,0:T(8,128)(2,1)S(1)} %get-tuple-element.70), channel_id=1, source_target_pairs={{0,8},{4,12},{8,0},{12,4},{1,9},{5,13},{9,1},{13,5},{2,10},{6,14},... | collective-permute-start | bytes 147464 | tf_op jit(solution)/shard_map/ppermute | solution.py:27
  147.0 3.0 %shard_map.92 = (bf16[128,1536]{1,0:T(8,128)(2,1)}, f32[8,128]{1,0:T(8,128)S(1)}) custom-call(bf16[8,128,1536]{2,1,0:T(8,128)(2,1)} %all-to-all-done.parts), custom_call_target="tpu_custom_call" | custom-call | tf_op jit(solution)/shard_map/pallas_call | solution.py:366
  (73 shorter events, 14.2 us)
Async XLA Ops:
  2.3 5.8 %copy-start.9 = (s32[128,8]{0,1:T(8,128)S(1)}, s32[128,8]{0,1:T(8,128)}, u32[]{:S(2)}) copy-start(s32[128,8]{0,1:T(8,128)} %param.8) | copy-start | bytes 12292
  2.3 5.8 %copy-start.10 = (f32[128,8]{0,1:T(8,128)S(1)}, f32[128,8]{0,1:T(8,128)}, u32[]{:S(2)}) copy-start(f32[128,8]{0,1:T(8,128)} %param.9) | copy-start | bytes 12292
  4.0 10.8 %collective-permute-start.3 = (bf16[48,4096]{1,0:T(8,128)(2,1)}, bf16[48,4096]{1,0:T(8,128)(2,1)S(1)}, u32[]{:S(2)}, u32[]{:S(2)}) collective-permute-start(bf16[48,4096]{1,0:T(8,128)(2,1)} %get-tuple-element.63), channel_id=1, source_target_pairs={{0,1},{1,0},{2,3},{3,2},{4,5},{5,4},{6,7},{7,6},{8,9},{9,8},{10,11... | collective-permute-start | bytes 1179656 | tf_op jit(solution)/shard_map/ppermute | solution.py:21
  4.0 14.2 %collective-permute-start.4 = (bf16[48,4096]{1,0:T(8,128)(2,1)}, bf16[48,4096]{1,0:T(8,128)(2,1)}, u32[]{:S(2)}, u32[]{:S(2)}) collective-permute-start(bf16[48,4096]{1,0:T(8,128)(2,1)} %get-tuple-element.62), channel_id=1, source_target_pairs={{0,2},{1,3},{2,0},{3,1},{4,6},{5,7},{6,4},{7,5},{8,10},{9,11},{10,... | collective-permute-start | bytes 1179656 | tf_op jit(solution)/shard_map/ppermute | solution.py:21
  8.0 18.3 %collective-permute-start.5 = (bf16[48,4096]{1,0:T(8,128)(2,1)}, bf16[48,4096]{1,0:T(8,128)(2,1)}, u32[]{:S(2)}, u32[]{:S(2)}) collective-permute-start(bf16[48,4096]{1,0:T(8,128)(2,1)} %get-tuple-element.61), channel_id=1, source_target_pairs={{0,3},{1,2},{2,1},{3,0},{4,7},{5,6},{6,5},{7,4},{8,11},{9,10},{10,... | collective-permute-start | bytes 1179656 | tf_op jit(solution)/shard_map/ppermute | solution.py:21
  11.3 21.3 %collective-permute-start = (bf16[48,4096]{1,0:T(8,128)(2,1)}, bf16[48,4096]{1,0:T(8,128)(2,1)S(1)}, u32[]{:S(2)}, u32[]{:S(2)}) collective-permute-start(bf16[48,4096]{1,0:T(8,128)(2,1)} %get-tuple-element.67), channel_id=1, source_target_pairs={{0,1},{1,0},{2,3},{3,2},{4,5},{5,4},{6,7},{7,6},{8,9},{9,8},{10,11... | collective-permute-start | bytes 1179656 | tf_op jit(solution)/shard_map/ppermute | solution.py:21
  11.4 30.1 %collective-permute-start.1 = (bf16[48,4096]{1,0:T(8,128)(2,1)}, bf16[48,4096]{1,0:T(8,128)(2,1)S(1)}, u32[]{:S(2)}, u32[]{:S(2)}) collective-permute-start(bf16[48,4096]{1,0:T(8,128)(2,1)} %get-tuple-element.66), channel_id=1, source_target_pairs={{0,2},{1,3},{2,0},{3,1},{4,6},{5,7},{6,4},{7,5},{8,10},{9,11},{10,... | collective-permute-start | bytes 1179656 | tf_op jit(solution)/shard_map/ppermute | solution.py:21
  14.8 28.3 %collective-permute-start.2 = (bf16[48,4096]{1,0:T(8,128)(2,1)}, bf16[48,4096]{1,0:T(8,128)(2,1)S(1)}, u32[]{:S(2)}, u32[]{:S(2)}) collective-permute-start(bf16[48,4096]{1,0:T(8,128)(2,1)} %get-tuple-element.65), channel_id=1, source_target_pairs={{0,3},{1,2},{2,1},{3,0},{4,7},{5,6},{6,5},{7,4},{8,11},{9,10},{10,... | collective-permute-start | bytes 1179656 | tf_op jit(solution)/shard_map/ppermute | solution.py:21
  28.4 19.7 %collective-permute-start.6 = (bf16[192,1024]{1,0:T(8,128)(2,1)S(1)}, bf16[192,1024]{1,0:T(8,128)(2,1)S(1)}, u32[]{:S(2)}, u32[]{:S(2)}) collective-permute-start(bf16[192,1024]{1,0:T(8,128)(2,1)S(1)} %get-tuple-element.36), channel_id=1, source_target_pairs={{0,16},{16,32},{32,48},{48,0},{1,17},{17,33},{33,49},{49,1},{2,18}... | collective-permute-start | bytes 1179656 | tf_op jit(solution)/shard_map/ppermute | solution.py:27
  29.9 20.3 %collective-permute-start.7 = (bf16[192,1024]{1,0:T(8,128)(2,1)S(1)}, bf16[192,1024]{1,0:T(8,128)(2,1)S(1)}, u32[]{:S(2)}, u32[]{:S(2)}) collective-permute-start(bf16[192,1024]{1,0:T(8,128)(2,1)S(1)} %get-tuple-element.37), channel_id=1, source_target_pairs={{0,32},{16,48},{32,0},{48,16},{1,33},{17,49},{33,1},{49,17},{2,34}... | collective-permute-start | bytes 1179656 | tf_op jit(solution)/shard_map/ppermute | solution.py:27
  32.6 17.6 %collective-permute-start.8 = (bf16[192,1024]{1,0:T(8,128)(2,1)S(1)}, bf16[192,1024]{1,0:T(8,128)(2,1)S(1)}, u32[]{:S(2)}, u32[]{:S(2)}) collective-permute-start(bf16[192,1024]{1,0:T(8,128)(2,1)S(1)} %get-tuple-element.38), channel_id=1, source_target_pairs={{0,48},{16,0},{32,16},{48,32},{1,49},{17,1},{33,17},{49,33},{2,50}... | collective-permute-start | bytes 1179656 | tf_op jit(solution)/shard_map/ppermute | solution.py:27
  48.2 3.8 %copy-start.1 = (bf16[192,1024]{1,0:T(8,128)(2,1)}, bf16[192,1024]{1,0:T(8,128)(2,1)S(1)}, u32[]{:S(2)}) copy-start(bf16[192,1024]{1,0:T(8,128)(2,1)S(1)} %collective-permute-done.6.rest_0_.refs_1_) | copy-start | bytes 1179652
  50.2 1.8 %copy-start.5 = (bf16[192,1024]{1,0:T(8,128)(2,1)}, bf16[192,1024]{1,0:T(8,128)(2,1)S(1)}, u32[]{:S(2)}) copy-start(bf16[192,1024]{1,0:T(8,128)(2,1)S(1)} %collective-permute-done.8.rest_2_.refs_3_) | copy-start | bytes 1179652
  52.0 40.9 %all-to-all-start.1 = ((bf16[4,192,1792]{2,1,0:T(8,128)(2,1)}), bf16[4,192,1792]{2,1,0:T(8,128)(2,1)}, u32[]{:S(2)}, u32[]{:S(2)}) async-start(bf16[4,192,1792]{2,1,0:T(8,128)(2,1)} %get-tuple-element.49), calls=%async_computation.1 | async-start | bytes 5505024 | tf_op jit(solution)/shard_map/all_to_all | solution.py:330
  56.6 15.9 %collective-permute-start.12 = (bf16[2,192,768]{2,1,0:T(8,128)(2,1)S(1)}, bf16[2,192,768]{2,1,0:T(8,128)(2,1)S(1)}, u32[]{:S(2)}, u32[]{:S(2)}) collective-permute-start(bf16[2,192,768]{2,1,0:T(8,128)(2,1)S(1)} %get-tuple-element.34.dact.refs_4_), channel_id=1, source_target_pairs={{0,16},{16,32},{32,48},{48,0},{1,17},{17,33},{33,49},{49,1},{2,18}... | collective-permute-start | bytes 1769480 | tf_op jit(solution)/shard_map/ppermute | solution.py:27
  58.0 28.2 %collective-permute-start.13 = (bf16[2,192,768]{2,1,0:T(8,128)(2,1)S(1)}, bf16[2,192,768]{2,1,0:T(8,128)(2,1)S(1)}, u32[]{:S(2)}, u32[]{:S(2)}) collective-permute-start(bf16[2,192,768]{2,1,0:T(8,128)(2,1)S(1)} %get-tuple-element.34.dact.refs_4_), channel_id=1, source_target_pairs={{0,32},{16,48},{32,0},{48,16},{1,33},{17,49},{33,1},{49,17},{2,34}... | collective-permute-start | bytes 1769480 | tf_op jit(solution)/shard_map/ppermute | solution.py:27
  60.4 25.9 %collective-permute-start.14 = (bf16[2,192,768]{2,1,0:T(8,128)(2,1)S(1)}, bf16[2,192,768]{2,1,0:T(8,128)(2,1)S(1)}, u32[]{:S(2)}, u32[]{:S(2)}) collective-permute-start(bf16[2,192,768]{2,1,0:T(8,128)(2,1)S(1)} %get-tuple-element.34.dact.refs_4_), channel_id=1, source_target_pairs={{0,48},{16,0},{32,16},{48,32},{1,49},{17,1},{33,17},{49,33},{2,50}... | collective-permute-start | bytes 1769480 | tf_op jit(solution)/shard_map/ppermute | solution.py:27
  62.0 26.1 %copy-start.2 = (bf16[192,1024]{1,0:T(8,128)(2,1)S(1)}, bf16[192,1024]{1,0:T(8,128)(2,1)}, u32[]{:S(2)}) copy-start(bf16[192,1024]{1,0:T(8,128)(2,1)} %copy-done.1) | copy-start | bytes 1179652
  62.0 26.1 %copy-start.4 = (bf16[192,1024]{1,0:T(8,128)(2,1)S(1)}, bf16[192,1024]{1,0:T(8,128)(2,1)}, u32[]{:S(2)}) copy-start(bf16[192,1024]{1,0:T(8,128)(2,1)} %copy-done.3) | copy-start | bytes 1179652
  62.0 26.1 %copy-start.6 = (bf16[192,1024]{1,0:T(8,128)(2,1)S(1)}, bf16[192,1024]{1,0:T(8,128)(2,1)}, u32[]{:S(2)}) copy-start(bf16[192,1024]{1,0:T(8,128)(2,1)} %copy-done.5) | copy-start | bytes 1179652
  62.0 26.1 %copy-start.8 = (bf16[192,1024]{1,0:T(8,128)(2,1)S(1)}, bf16[192,1024]{1,0:T(8,128)(2,1)}, u32[]{:S(2)}) copy-start(bf16[192,1024]{1,0:T(8,128)(2,1)} %copy-done.7) | copy-start | bytes 1179652
  68.9 17.4 %collective-permute-start.10 = (bf16[48,4096]{1,0:T(8,128)(2,1)S(1)}, bf16[48,4096]{1,0:T(8,128)(2,1)S(1)}, u32[]{:S(2)}, u32[]{:S(2)}) collective-permute-start(bf16[48,4096]{1,0:T(8,128)(2,1)S(1)} %get-tuple-element.43), channel_id=1, source_target_pairs={{0,2},{1,3},{2,0},{3,1},{4,6},{5,7},{6,4},{7,5},{8,10},{9,11},{10,... | collective-permute-start | bytes 1179656 | tf_op jit(solution)/shard_map/ppermute | solution.py:21
  72.4 15.6 %collective-permute-start.11 = (bf16[48,4096]{1,0:T(8,128)(2,1)S(1)}, bf16[48,4096]{1,0:T(8,128)(2,1)S(1)}, u32[]{:S(2)}, u32[]{:S(2)}) collective-permute-start(bf16[48,4096]{1,0:T(8,128)(2,1)S(1)} %get-tuple-element.44), channel_id=1, source_target_pairs={{0,3},{1,2},{2,1},{3,0},{4,7},{5,6},{6,5},{7,4},{8,11},{9,10},{10,... | collective-permute-start | bytes 1179656 | tf_op jit(solution)/shard_map/ppermute | solution.py:21
  92.9 54.1 %all-to-all-start = ((bf16[8,128,1536]{2,1,0:T(8,128)(2,1)}), bf16[8,128,1536]{2,1,0:T(8,128)(2,1)}, u32[]{:S(2)}, u32[]{:S(2)}) async-start(bf16[8,128,1536]{2,1,0:T(8,128)(2,1)} %get-tuple-element.47), calls=%async_computation | async-start | bytes 6291456 | tf_op jit(solution)/shard_map/all_to_all | solution.py:343
  97.9 9.2 %collective-permute-start.9 = (bf16[48,4096]{1,0:T(8,128)(2,1)S(1)}, bf16[48,4096]{1,0:T(8,128)(2,1)S(1)}, u32[]{:S(2)}, u32[]{:S(2)}) collective-permute-start(bf16[48,4096]{1,0:T(8,128)(2,1)S(1)} %get-tuple-element.42), channel_id=1, source_target_pairs={{0,1},{1,0},{2,3},{3,2},{4,5},{5,4},{6,7},{7,6},{8,9},{9,8},{10,11... | collective-permute-start | bytes 1179656 | tf_op jit(solution)/shard_map/ppermute | solution.py:21
  103.0 20.7 %collective-permute-start.15 = (bf16[192,1024]{1,0:T(8,128)(2,1)S(1)}, bf16[192,1024]{1,0:T(8,128)(2,1)S(1)}, u32[]{:S(2)}, u32[]{:S(2)}) collective-permute-start(bf16[192,1024]{1,0:T(8,128)(2,1)S(1)} %get-tuple-element.52), channel_id=1, source_target_pairs={{0,16},{16,32},{32,48},{48,0},{1,17},{17,33},{33,49},{49,1},{2,18}... | collective-permute-start | bytes 1179656 | tf_op jit(solution)/shard_map/ppermute | solution.py:27
  104.1 19.7 %collective-permute-start.16 = (bf16[192,1024]{1,0:T(8,128)(2,1)S(1)}, bf16[192,1024]{1,0:T(8,128)(2,1)S(1)}, u32[]{:S(2)}, u32[]{:S(2)}) collective-permute-start(bf16[192,1024]{1,0:T(8,128)(2,1)S(1)} %get-tuple-element.53), channel_id=1, source_target_pairs={{0,32},{16,48},{32,0},{48,16},{1,33},{17,49},{33,1},{49,17},{2,34}... | collective-permute-start | bytes 1179656 | tf_op jit(solution)/shard_map/ppermute | solution.py:27
  105.2 19.1 %collective-permute-start.17 = (bf16[192,1024]{1,0:T(8,128)(2,1)S(1)}, bf16[192,1024]{1,0:T(8,128)(2,1)S(1)}, u32[]{:S(2)}, u32[]{:S(2)}) collective-permute-start(bf16[192,1024]{1,0:T(8,128)(2,1)S(1)} %get-tuple-element.54), channel_id=1, source_target_pairs={{0,48},{16,0},{32,16},{48,32},{1,49},{17,1},{33,17},{49,33},{2,50}... | collective-permute-start | bytes 1179656 | tf_op jit(solution)/shard_map/ppermute | solution.py:27
  125.7 14.7 %collective-permute-start.18 = (bf16[96,1024]{1,0:T(8,128)(2,1)S(1)}, bf16[96,1024]{1,0:T(8,128)(2,1)S(1)}, u32[]{:S(2)}, u32[]{:S(2)}) collective-permute-start(bf16[96,1024]{1,0:T(8,128)(2,1)S(1)} %get-tuple-element.57), channel_id=1, source_target_pairs={{0,64},{64,0},{1,65},{65,1},{2,66},{66,2},{3,67},{67,3},{4,68},{68... | collective-permute-start | bytes 589832 | tf_op jit(solution)/shard_map/ppermute | solution.py:31
  140.5 9.5 %collective-permute-start.19 = (bf16[24,1024]{1,0:T(8,128)(2,1)S(1)}, bf16[24,1024]{1,0:T(8,128)(2,1)S(1)}, u32[]{:S(2)}, u32[]{:S(2)}) collective-permute-start(bf16[24,1024]{1,0:T(8,128)(2,1)S(1)} %get-tuple-element.71), channel_id=1, source_target_pairs={{0,4},{4,8},{8,12},{12,0},{1,5},{5,9},{9,13},{13,1},{2,6},{6,10},{... | collective-permute-start | bytes 147464 | tf_op jit(solution)/shard_map/ppermute | solution.py:27
  142.2 7.9 %collective-permute-start.20 = (bf16[24,1024]{1,0:T(8,128)(2,1)S(1)}, bf16[24,1024]{1,0:T(8,128)(2,1)S(1)}, u32[]{:S(2)}, u32[]{:S(2)}) collective-permute-start(bf16[24,1024]{1,0:T(8,128)(2,1)S(1)} %get-tuple-element.70), channel_id=1, source_target_pairs={{0,8},{4,12},{8,0},{12,4},{1,9},{5,13},{9,1},{13,5},{2,10},{6,14},... | collective-permute-start | bytes 147464 | tf_op jit(solution)/shard_map/ppermute | solution.py:27
  147.0 4.1 %collective-permute-start.21 = (bf16[24,1024]{1,0:T(8,128)(2,1)S(1)}, bf16[24,1024]{1,0:T(8,128)(2,1)S(1)}, u32[]{:S(2)}, u32[]{:S(2)}) collective-permute-start(bf16[24,1024]{1,0:T(8,128)(2,1)S(1)} %get-tuple-element.69), channel_id=1, source_target_pairs={{0,12},{4,0},{8,4},{12,8},{1,13},{5,1},{9,5},{13,9},{2,14},{6,2},{... | collective-permute-start | bytes 147464 | tf_op jit(solution)/shard_map/ppermute | solution.py:27
  (3 other events, 4.2 us)

commit v7 on v4

--- a/solution.py
+++ b/solution.py
@@ -158,12 +158,12 @@
     out[...] = jnp.dot(mask[...], whole[...], preferred_element_type=F32).astype(BF)
 
 
-def tile_step(*refs):
+def tile_step(at, *refs):
     xs, ds = refs[:4], refs[4:8]
-    out, mark, xall, dall, buf, sem, osem = refs[-7:]
-    rows = xs[0].shape[0]
+    out, keep, send, mark, xall, dall, buf, sem, osem = refs[-9:]
+    rows, inner = xs[0].shape[0], ds[0].shape[2]
+    cut = buf.shape[2]
     part = [pl.ds(p * rows, rows) for p in range(4)]
-    inner = ds[0].shape[2]
     land(
         [(xs[p], xall.at[part[p], :]) for p in range(4)]
         + [
@@ -176,27 +176,29 @@
     mark[...] = jnp.zeros_like(mark)
     copies = []
     for b in range(2):
-        got = rows_dot(xall[:, b * 512 : b * 512 + 512], dall[...])
+        got = rows_dot(xall[:, b * 512 : b * 512 + 512], dall[:, :cut])
         for j in range(4):
             buf[j, b * 128 : b * 128 + 128, :] = got[j * 128 : j * 128 + 128].astype(BF)
             if b == 1:
                 copies.append(pltpu.make_async_copy(buf.at[j], out.at[j], osem.at[j]))
                 copies[-1].start()
+    send[...] = rows_dot(xall[:, aligned(1 - at[0], 512)], dall[:, cut:]).astype(BF)
+    keep[...] = rows_dot(xall[:, aligned(at[0], 512)], dall[:, cut:])
     for copy in copies:
         copy.wait()
 
 
-def tile_call(xs, ds, after):
+def tile_call(at, xs, ds, cut, after):
     rows, part = xs[0].shape
     wide = 2 * ds[0].shape[2]
     return call(
         tile_step,
-        "a" * (8 + len(after)),
-        [shape(4, 256, wide), MARK],
+        "s" + "a" * (8 + len(after)),
+        [shape(4, 256, cut), shape(512, wide - cut, dtype=F32), shape(512, wide - cut), MARK],
         [
             pltpu.VMEM((4 * rows, part), BF),
             pltpu.VMEM((4 * rows, wide), BF),
-            pltpu.VMEM((4, 256, wide), BF),
+            pltpu.VMEM((4, 256, cut), BF),
             sems(12),
             sems(4),
         ],
@@ -204,7 +206,22 @@
         moved=8 * rows * (part + wide),
         limit=24,
         placed=(0,),
-    )(*xs, *ds, *after)
+    )(at, *xs, *ds, *after)
+
+
+def middle_step(at, keep, theirs, own, *sends):
+    for j in range(4):
+        rows = aligned(lax.rem(at[2] + j, 4), 128)
+        got = keep[rows, :] + theirs[rows, :].astype(F32)
+        if j:
+            sends[j - 1][...] = got.astype(BF)
+        else:
+            own[...] = got
+
+
+def ring_sum(own, r1, r2, r3, after, out, mark):
+    mark[...] = jnp.zeros_like(mark)
+    out[...] = (own[...] + sum(r[...].astype(F32) for r in (r1, r2, r3))).astype(BF)
 
 
 def down_step(at, both, *rest):
@@ -265,8 +282,9 @@
     )(at, *parts, *after)
 
 
-def join_step(keep, theirs, mark, out):
-    out[...] = (keep[...] + theirs[...].astype(F32)).astype(BF)
+def join_step(at, c0, c1, c2, c3, mark, out):
+    for j, piece in enumerate((c0, c1, c2, c3)):
+        out[:, aligned(lax.rem(at[2] + 4 - j, 4), piece.shape[1])] = piece[...]
 
 
 def shards(tokens, cotangent, routes, gates, gate_up, down_proj):
@@ -344,7 +362,8 @@
         limit=18,
     )(dact, gate_up, sent_mark)
     arrived = [back[0]] + [swap_expert(back[k], k) for k in (1, 2, 3)]
-    parts, mark = tile_call(xa, da, [arrived[2]])
+    cut = 896
+    parts, side_keep, side_send, mark = tile_call(at, xa, da, cut, arrived[2:])
     gate = lax.all_to_all(parts, "y", split_axis=0, concat_axis=0, tiled=True)
     *parts, _ = call(
         down_step,
@@ -368,24 +387,27 @@
         [pltpu.VMEM((rows, width), BF), sems(4)],
     )(mask, *arrived)
 
-    gate_keep, gate_send, mark = call(
+    rest = 2 * inner - cut
+    side = call(
+        middle_step, "svv", [shape(128, rest, dtype=F32)] + [shape(128, rest)] * 3
+    )(at, side_keep, swap_w(side_send))
+    side = [side[0]] + [shift(side[j], "y", j) for j in (1, 2, 3)]
+    gate_keep, gate_send, _ = call(
         gate_sum,
         "sa",
-        [shape(128, 2 * inner, dtype=F32), shape(128, 2 * inner), MARK],
-        [pltpu.VMEM((4, 256, 2 * inner), BF), sems(4)],
+        [shape(128, cut, dtype=F32), shape(128, cut), MARK],
+        [pltpu.VMEM((4, 256, cut), BF), sems(4)],
         limit=12,
     )(at, gate)
+    keep, send = sum_call(at, down, [tok_mark])
+    side_grad, mark = call(ring_sum, "vvvva", [shape(128, rest), MARK])(*side, send)
     gate_up_grad = (gate_keep + swap_w(gate_send).astype(F32)).astype(BF)
-    keep, send = sum_call(at, down, [tok_mark])
-    down_grad = call(join_step, "vva", [shape(96, part)], moved=800 * part)(
-        keep, swap_w(send), mark
-    )[0].reshape(4, 24, part)
+    gate_up_grad = jnp.concatenate([gate_up_grad, side_grad], axis=1)
+    down_grad = (keep + swap_w(send).astype(F32)).astype(BF).reshape(4, 24, part)
     cols = [
         shift(lax.dynamic_index_in_dim(down_grad, (y + j) % 4, 0, False), "y", j) for j in range(4)
     ]
-    turned = jnp.stack(cols[::-1] + cols[::-1])
-    mine = lax.dynamic_slice_in_dim(turned, 3 - y, 4, 0)
-    down_grad = jnp.concatenate([mine[i] for i in range(4)], axis=1)
+    down_grad = call(join_step, "svvvva", [shape(24, width)])(at, *cols, mark)[0]
 
     return token_grad, gate_up_grad[None], down_grad[None]
 

time: 150 us -> 160 us (1.067)
  local copies, waits for them, and re-layouts: 5.08 us -> 11.5 us
  Pallas kernels: 38.6 us -> 43.8 us
  starting transfers between devices: 45.4 us -> 47.1 us
    ppermute x12 -> x15, waiting for transfers between devices: 34.2 us -> 20.1 us  [shift(): return lax.ppermute(a, axis, [(i, (i + j) % 4) for i in range(4)])]
    all_to_all x1, waiting for transfers between devices: 5.06 us -> 13.1 us  [shards(): gate = lax.all_to_all(parts, 'y', split_axis=0, concat_axis=0, tiled=True)]
    unnamed x37 -> x50, local copies, waits for them, and re-layouts: 2.32 us -> 8.8 us
    ppermute x12 -> x15, starting transfers between devices: 18.7 us -> 23.6 us  [shift(): return lax.ppermute(a, axis, [(i, (i + j) % 4) for i in range(4)])]
    ppermute x9, waiting for transfers between devices: 13.1 us -> 17.4 us  [swap_expert(): return lax.ppermute(a, ('v', 'c'), [(i, i ^ k) for i in range(4)])]
    ppermute x9, starting transfers between devices: 14.7 us -> 11.3 us  [swap_expert(): return lax.ppermute(a, ('v', 'c'), [(i, i ^ k) for i in range(4)])]
    pallas_call x3 -> x5, Pallas kernels: 8.09 us -> 10.8 us  [the longest x1 5.66 us: tile_call(): call(tile_step, 's' + 'a' * (8 + len(after)), [shape(4, 256, cut), shape(...]
  transfers between devices with their start and end apart: 25 -> 29, of which waited for: 10 -> 12; matrix products, arithmetic and copies ran while one was open for 3% -> 2% of each run, Pallas kernels for 25% -> 26%
where the time goes in v7:
time: 160 us; the launch traced here: 159 us
  waiting for transfers between devices  50.8 us (32%)
  starting transfers between devices  47.1 us (29%)
  Pallas kernels  43.8 us (27%)
  local copies, waits for them, and re-layouts  11.5 us (7%)
  other arithmetic  3.79 us (2%)
    ppermute x15, starting transfers between devices, shift(): return lax.ppermute(a, axis, [(i, (i + j) % 4) for i in range(4)])  23.6 us
    ppermute x15, waiting for transfers between devices, shift(): return lax.ppermute(a, axis, [(i, (i + j) % 4) for i in range(4)])  20.1 us
    ppermute x9, waiting for transfers between devices, swap_expert(): return lax.ppermute(a, ('v', 'c'), [(i, i ^ k) for i in range(4)])  17.4 us
    all_to_all x1, waiting for transfers between devices, shards(): gate = lax.all_to_all(parts, 'y', split_axis=0, concat_axis=0, tiled=True)  13.1 us
    ppermute x9, starting transfers between devices, swap_expert(): return lax.ppermute(a, ('v', 'c'), [(i, i ^ k) for i in range(4)])  11.3 us
    unnamed x50, local copies, waits for them, and re-layouts  8.8 us
    pallas_call x1, Pallas kernels, shards(): call(back_step, 'vaa', [shape(CAP, width)] * 4 + [MARK], [pltpu.VMEM((n,...  7.64 us
    pallas_call x1, Pallas kernels, shards(): call(act_step, 'va', [shape(rows, inner), shape(rows, inner, dtype=F32),...  7.42 us
  transfers between devices with their start and end apart: 29, of which 12 were waited for; matrix products, arithmetic and copies ran while one was open for 2% of the time, Pallas kernels for 26%

profile of v7, /device:TPU:0, one launch (start us, length us, event | category | flops | bytes accessed | tf_op | source)
XLA Modules:
  0.0 159.2 jit_solution(8290155076712677847)
XLA Ops:
  4.6 4.0 %collective-permute-start.4 = (bf16[48,4096]{1,0:T(8,128)(2,1)}, bf16[48,4096]{1,0:T(8,128)(2,1)}, u32[]{:S(2)}, u32[]{:S(2)}) collective-permute-start(bf16[48,4096]{1,0:T(8,128)(2,1)} %get-tuple-element.78), channel_id=1, source_target_pairs={{0,2},{1,3},{2,0},{3,1},{4,6},{5,7},{6,4},{7,5},{8,10},{9,11},{10,... | collective-permute-start | bytes 1179656 | tf_op jit(solution)/shard_map/ppermute | solution.py:21
  10.7 3.4 %collective-permute-start.1 = (bf16[48,4096]{1,0:T(8,128)(2,1)}, bf16[48,4096]{1,0:T(8,128)(2,1)S(1)}, u32[]{:S(2)}, u32[]{:S(2)}) collective-permute-start(bf16[48,4096]{1,0:T(8,128)(2,1)} %get-tuple-element.82), channel_id=1, source_target_pairs={{0,2},{1,3},{2,0},{3,1},{4,6},{5,7},{6,4},{7,5},{8,10},{9,11},{10,... | collective-permute-start | bytes 1179656 | tf_op jit(solution)/shard_map/ppermute | solution.py:21
  14.2 4.6 %collective-permute-done.4.x2 = bf16[48,4096]{1,0:T(8,128)(2,1)} collective-permute-done((bf16[48,4096]{1,0:T(8,128)(2,1)}, bf16[48,4096]{1,0:T(8,128)(2,1)}, u32[]{:S(2)}, u32[]{:S(2)}) %collective-permute-start.4) | collective-permute-done | bytes 393248 | tf_op jit(solution)/shard_map/ppermute | solution.py:21
  18.8 8.1 %collective-permute-done.5.x3 = bf16[48,4096]{1,0:T(8,128)(2,1)} collective-permute-done((bf16[48,4096]{1,0:T(8,128)(2,1)}, bf16[48,4096]{1,0:T(8,128)(2,1)}, u32[]{:S(2)}, u32[]{:S(2)}) %collective-permute-start.5) | collective-permute-done | bytes 393248 | tf_op jit(solution)/shard_map/ppermute | solution.py:21
  29.0 1.5 collective-permute-start.6
  30.5 2.7 %collective-permute-start.7 = (bf16[192,1024]{1,0:T(8,128)(2,1)S(1)}, bf16[192,1024]{1,0:T(8,128)(2,1)S(1)}, u32[]{:S(2)}, u32[]{:S(2)}) collective-permute-start(bf16[192,1024]{1,0:T(8,128)(2,1)S(1)} %get-tuple-element.45), channel_id=1, source_target_pairs={{0,32},{16,48},{32,0},{48,16},{1,33},{17,49},{33,1},{49,17},{2,34}... | collective-permute-start | bytes 1179656 | tf_op jit(solution)/shard_map/ppermute | solution.py:27
  33.2 1.4 collective-permute-start.8
  34.7 7.4 %shard_map.86 = (bf16[192,768]{1,0:T(8,128)(2,1)S(1)}, f32[192,768]{1,0:T(8,128)S(1)}, f32[192,768]{1,0:T(8,128)S(1)}) custom-call(bf16[192,4096]{1,0:T(8,128)(2,1)S(1)} %get-tuple-element.39.x, bf16[4096,1536]{1,0:T(8,128)(2,1)} %bitcast.24), custom_call_target="tpu_custom_call" | custom-call | flops 2415919104 | bytes 12582912 | tf_op jit(solution)/shard_map/pallas_call | solution.py:319
  42.1 1.6 collective-permute-done.2.g3
  43.6 5.1 %shard_map.87 = (bf16[2,192,768]{2,1,0:T(8,128)(2,1)S(1)}, f32[8,128]{1,0:T(8,128)S(1)}) custom-call(bf16[48,4096]{1,0:T(8,128)(2,1)S(1)} %get-tuple-element.84.g0, bf16[48,4096]{1,0:T(8,128)(2,1)S(1)} %collective-permute-done.g1, bf16[48,4096]{1,0:T(8,128)(2,1)S(1)} %collective-permute-done.1.g2, bf16[48,4096]{1,0:T(8,128)(2,1)S(1)} %collective-permute-done.2.g3, ...), custom_call_target="tpu_custom_call" | custom-call | flops 1207959552 | bytes 6291456 | tf_op jit(solution)/shard_map/pallas_call | solution.py:329
  48.8 2.1 %collective-permute-done.7.rest_1_.refs_2_ = bf16[192,1024]{1,0:T(8,128)(2,1)S(1)} collective-permute-done((bf16[192,1024]{1,0:T(8,128)(2,1)S(1)}, bf16[192,1024]{1,0:T(8,128)(2,1)S(1)}, u32[]{:S(2)}, u32[]{:S(2)}) %collective-permute-start.7) | collective-permute-done | bytes 393248 | tf_op jit(solution)/shard_map/ppermute | solution.py:27
  50.8 1.8 %shard_map.88 = (bf16[4,192,1792]{2,1,0:T(8,128)(2,1)}, f32[8,128]{1,0:T(8,128)S(1)}) custom-call(bf16[48,4096]{1,0:T(8,128)(2,1)S(1)} %get-tuple-element.84.g0, bf16[48,4096]{1,0:T(8,128)(2,1)S(1)} %collective-permute-done.g1, bf16[48,4096]{1,0:T(8,128)(2,1)S(1)} %collective-permute-done.1.g2, bf16[48,4096]{1,0:T(8,128)(2,1)S(1)} %collective-permute-done.2.g3, ...), custom_call_target="tpu_custom_call" | custom-call | bytes 3145728 | tf_op jit(solution)/shard_map/pallas_call | solution.py:345
  52.7 4.6 %all-to-all-start.1 = ((bf16[4,192,1792]{2,1,0:T(8,128)(2,1)}), bf16[4,192,1792]{2,1,0:T(8,128)(2,1)}, u32[]{:S(2)}, u32[]{:S(2)}) async-start(bf16[4,192,1792]{2,1,0:T(8,128)(2,1)} %get-tuple-element.64), calls=%async_computation.1 | async-start | bytes 5505024 | tf_op jit(solution)/shard_map/all_to_all | solution.py:353
  57.3 1.4 collective-permute-start.12
  58.7 2.4 %collective-permute-start.13 = (bf16[2,192,768]{2,1,0:T(8,128)(2,1)S(1)}, bf16[2,192,768]{2,1,0:T(8,128)(2,1)S(1)}, u32[]{:S(2)}, u32[]{:S(2)}) collective-permute-start(bf16[2,192,768]{2,1,0:T(8,128)(2,1)S(1)} %get-tuple-element.42.dact.refs_4_), channel_id=1, source_target_pairs={{0,32},{16,48},{32,0},{48,16},{1,33},{17,49},{33,1},{49,17},{2,34}... | collective-permute-start | bytes 1769480 | tf_op jit(solution)/shard_map/ppermute | solution.py:27
  61.0 1.6 collective-permute-start.14
  62.6 7.6 %shard_map.89 = (bf16[48,4096]{1,0:T(8,128)(2,1)S(1)}, bf16[48,4096]{1,0:T(8,128)(2,1)}, bf16[48,4096]{1,0:T(8,128)(2,1)S(1)}, bf16[48,4096]{1,0:T(8,128)(2,1)S(1)}, f32[8,128]{1,0:T(8,128)}) custom-call(bf16[2,192,768]{2,1,0:T(8,128)(2,1)S(1)} %get-tuple-element.42.dact.refs_4_, bf16[4096,1536]{1,0:T(8,128)(2,1)} %bitcast.25, ...), custom_call_target="tpu_custom_call" | custom-call | flops 2415919104 | bytes 12582912 | tf_op jit(solution)/shard_map/pallas_call | solution.py:355
  71.0 3.4 %collective-permute-start.10 = (bf16[48,4096]{1,0:T(8,128)(2,1)S(1)}, bf16[48,4096]{1,0:T(8,128)(2,1)S(1)}, u32[]{:S(2)}, u32[]{:S(2)}) collective-permute-start(bf16[48,4096]{1,0:T(8,128)(2,1)S(1)} %get-tuple-element.51), channel_id=1, source_target_pairs={{0,2},{1,3},{2,0},{3,1},{4,6},{5,7},{6,4},{7,5},{8,10},{9,11},{10,... | collective-permute-start | bytes 1179656 | tf_op jit(solution)/shard_map/ppermute | solution.py:21
  74.5 12.4 %collective-permute-done.13.refs_6_ = bf16[2,192,768]{2,1,0:T(8,128)(2,1)S(1)} collective-permute-done((bf16[2,192,768]{2,1,0:T(8,128)(2,1)S(1)}, bf16[2,192,768]{2,1,0:T(8,128)(2,1)S(1)}, u32[]{:S(2)}, u32[]{:S(2)}) %collective-permute-start.13) | collective-permute-done | bytes 589856 | tf_op jit(solution)/shard_map/ppermute | solution.py:27
  86.9 3.2 %collective-permute-done.11.a3.refs_9_ = bf16[48,4096]{1,0:T(8,128)(2,1)S(1)} collective-permute-done((bf16[48,4096]{1,0:T(8,128)(2,1)S(1)}, bf16[48,4096]{1,0:T(8,128)(2,1)S(1)}, u32[]{:S(2)}, u32[]{:S(2)}) %collective-permute-start.11) | collective-permute-done | bytes 393248 | tf_op jit(solution)/shard_map/ppermute | solution.py:21
  90.1 5.7 %shard_map.91 = (bf16[4,256,896]{2,1,0:T(8,128)(2,1)}, f32[512,640]{1,0:T(8,128)S(1)}, bf16[512,640]{1,0:T(8,128)(2,1)}, f32[8,128]{1,0:T(8,128)S(1)}) custom-call(s32[4]{0:T(128)S(1)} %pad_add_fusion.at, bf16[192,1024]{1,0:T(8,128)(2,1)S(1)} %copy-done.21, bf16[192,1024]{1,0:T(8,128)(2,1)S(1)} %copy-done.8, bf16[192,1024]{1,0:T(8,128)(2,1)S(1)} %copy-done.10, ...), custom_call_target="tpu_custom_call" | custom-call | flops 2415919104 | bytes 3932160 | tf_op jit(solution)/shard_map/pallas_call | solution.py:194
  98.5 4.4 %all-to-all-start = ((bf16[4,256,896]{2,1,0:T(8,128)(2,1)}), bf16[4,256,896]{2,1,0:T(8,128)(2,1)S(1)}, u32[]{:S(2)}, u32[]{:S(2)}) async-start(bf16[4,256,896]{2,1,0:T(8,128)(2,1)} %get-tuple-element.55), calls=%async_computation | async-start | bytes 3670016 | tf_op jit(solution)/shard_map/all_to_all | solution.py:367
  104.2 5.1 %shard_map.94 = (f32[192,1024]{1,0:T(8,128)S(1)}, bf16[192,1024]{1,0:T(8,128)(2,1)}, bf16[192,1024]{1,0:T(8,128)(2,1)}, bf16[192,1024]{1,0:T(8,128)(2,1)}, f32[8,128]{1,0:T(8,128)}) custom-call(s32[4]{0:T(128)S(1)} %pad_add_fusion.at, bf16[4,192,1792]{2,1,0:T(8,128)(2,1)} %all-to-all-done.1.both, f32[8,128]{1,0:T(8,128)S(1)} %get-tuple-element.65.rest_0_), custom_call_target="tpu_custom_call" | custom-call | flops 1207959552 | bytes 2752512 | tf_op jit(solution)/shard_map/pallas_call | solution.py:368
  112.2 1.9 %collective-permute-start.22 = (bf16[192,1024]{1,0:T(8,128)(2,1)}, bf16[192,1024]{1,0:T(8,128)(2,1)}, u32[]{:S(2)}, u32[]{:S(2)}) collective-permute-start(bf16[192,1024]{1,0:T(8,128)(2,1)} %get-tuple-element.69), channel_id=1, source_target_pairs={{0,48},{16,0},{32,16},{48,32},{1,49},{17,1},{33,17},{49,33},{2,50}... | collective-permute-start | bytes 1179656 | tf_op jit(solution)/shard_map/ppermute | solution.py:27
  114.1 13.1 %all-to-all-done.parts = bf16[4,256,896]{2,1,0:T(8,128)(2,1)S(1)} async-done(((bf16[4,256,896]{2,1,0:T(8,128)(2,1)}), bf16[4,256,896]{2,1,0:T(8,128)(2,1)S(1)}, u32[]{:S(2)}, u32[]{:S(2)}) %all-to-all-start) | async-done | bytes 1835040 | tf_op jit(solution)/shard_map/all_to_all | solution.py:367
  127.2 2.5 %shard_map.92 = (f32[128,896]{1,0:T(8,128)S(1)}, bf16[128,896]{1,0:T(8,128)(2,1)}, f32[8,128]{1,0:T(8,128)}) custom-call(s32[4]{0:T(128)S(1)} %pad_add_fusion.at, bf16[4,256,896]{2,1,0:T(8,128)(2,1)S(1)} %all-to-all-done.parts), custom_call_target="tpu_custom_call" | custom-call | tf_op jit(solution)/shard_map/pallas_call | solution.py:395
  134.7 2.6 %shard_map.90 = (bf16[128,4096]{1,0:T(8,128)(2,1)}, f32[8,128]{1,0:T(8,128)S(1)}) custom-call(bf16[128,192]{1,0:T(8,128)(2,1)S(1)} %copy-done.19, bf16[48,4096]{1,0:T(8,128)(2,1)S(1)} %copy-done.14, bf16[48,4096]{1,0:T(8,128)(2,1)} %collective-permute-done.9.a1, bf16[48,4096]{1,0:T(8,128)(2,1)S(1)} %copy-done.16, bf16[48,4096]{1,0:T(8,128)(2,1)S(1)} %copy-done.18), custom_call_target="tpu_custom_call" | custom-call | tf_op jit(solution)/shard_map/pallas_call | solution.py:383
  139.3 2.1 %collective-permute-start.18 = (bf16[128,640]{1,0:T(8,128)(2,1)S(1)}, bf16[128,640]{1,0:T(8,128)(2,1)S(1)}, u32[]{:S(2)}, u32[]{:S(2)}) collective-permute-start(bf16[128,640]{1,0:T(8,128)(2,1)S(1)} %get-tuple-element.62), channel_id=1, source_target_pairs={{0,8},{4,12},{8,0},{12,4},{1,9},{5,13},{9,1},{13,5},{2,10},{6,14},... | collective-permute-start | bytes 491528 | tf_op jit(solution)/shard_map/ppermute | solution.py:27
  142.0 2.0 %shard_map.95 = (f32[96,1024]{1,0:T(8,128)S(1)}, bf16[96,1024]{1,0:T(8,128)(2,1)S(1)}) custom-call(s32[4]{0:T(128)S(1)} %pad_add_fusion.at, f32[192,1024]{1,0:T(8,128)S(1)} %copy-done.4, bf16[192,1024]{1,0:T(8,128)(2,1)} %collective-permute-done.20.r1, bf16[192,1024]{1,0:T(8,128)(2,1)} %collective-permute-done.21.r2, ...), custom_call_target="tpu_custom_call" | custom-call | tf_op jit(solution)/shard_map/pallas_call | solution.py:276
  145.9 3.2 %collective-permute-done.17.r1 = bf16[128,640]{1,0:T(8,128)(2,1)S(1)} collective-permute-done((bf16[128,640]{1,0:T(8,128)(2,1)S(1)}, bf16[128,640]{1,0:T(8,128)(2,1)S(1)}, u32[]{:S(2)}, u32[]{:S(2)}) %collective-permute-start.17) | collective-permute-done | bytes 163872 | tf_op jit(solution)/shard_map/ppermute | solution.py:27
  151.3 2.6 %collective-permute-start.25 = (bf16[24,1024]{1,0:T(8,128)(2,1)S(1)}, bf16[24,1024]{1,0:T(8,128)(2,1)S(1)}, u32[]{:S(2)}, u32[]{:S(2)}) collective-permute-start(bf16[24,1024]{1,0:T(8,128)(2,1)S(1)} %get-tuple-element.86), channel_id=1, source_target_pairs={{0,8},{4,12},{8,0},{12,4},{1,9},{5,13},{9,1},{13,5},{2,10},{6,14},... | collective-permute-start | bytes 147464 | tf_op jit(solution)/shard_map/ppermute | solution.py:27
  153.9 1.5 collective-permute-start.26
  (115 shorter events, 31.2 us)
Async XLA Ops:
  4.6 9.6 %collective-permute-start.3 = (bf16[48,4096]{1,0:T(8,128)(2,1)S(1)}, bf16[48,4096]{1,0:T(8,128)(2,1)S(1)}, u32[]{:S(2)}, u32[]{:S(2)}) collective-permute-start(bf16[48,4096]{1,0:T(8,128)(2,1)S(1)} %get-tuple-element.79), channel_id=1, source_target_pairs={{0,1},{1,0},{2,3},{3,2},{4,5},{5,4},{6,7},{7,6},{8,9},{9,8},{10,11... | collective-permute-start | bytes 1179656 | tf_op jit(solution)/shard_map/ppermute | solution.py:21
  4.6 14.2 %collective-permute-start.4 = (bf16[48,4096]{1,0:T(8,128)(2,1)}, bf16[48,4096]{1,0:T(8,128)(2,1)}, u32[]{:S(2)}, u32[]{:S(2)}) collective-permute-start(bf16[48,4096]{1,0:T(8,128)(2,1)} %get-tuple-element.78), channel_id=1, source_target_pairs={{0,2},{1,3},{2,0},{3,1},{4,6},{5,7},{6,4},{7,5},{8,10},{9,11},{10,... | collective-permute-start | bytes 1179656 | tf_op jit(solution)/shard_map/ppermute | solution.py:21
  8.6 18.3 %collective-permute-start.5 = (bf16[48,4096]{1,0:T(8,128)(2,1)}, bf16[48,4096]{1,0:T(8,128)(2,1)}, u32[]{:S(2)}, u32[]{:S(2)}) collective-permute-start(bf16[48,4096]{1,0:T(8,128)(2,1)} %get-tuple-element.77), channel_id=1, source_target_pairs={{0,3},{1,2},{2,1},{3,0},{4,7},{5,6},{6,5},{7,4},{8,11},{9,10},{10,... | collective-permute-start | bytes 1179656 | tf_op jit(solution)/shard_map/ppermute | solution.py:21
  10.7 22.6 %collective-permute-start = (bf16[48,4096]{1,0:T(8,128)(2,1)}, bf16[48,4096]{1,0:T(8,128)(2,1)S(1)}, u32[]{:S(2)}, u32[]{:S(2)}) collective-permute-start(bf16[48,4096]{1,0:T(8,128)(2,1)} %get-tuple-element.83), channel_id=1, source_target_pairs={{0,1},{1,0},{2,3},{3,2},{4,5},{5,4},{6,7},{7,6},{8,9},{9,8},{10,11... | collective-permute-start | bytes 1179656 | tf_op jit(solution)/shard_map/ppermute | solution.py:21
  10.7 31.3 %collective-permute-start.1 = (bf16[48,4096]{1,0:T(8,128)(2,1)}, bf16[48,4096]{1,0:T(8,128)(2,1)S(1)}, u32[]{:S(2)}, u32[]{:S(2)}) collective-permute-start(bf16[48,4096]{1,0:T(8,128)(2,1)} %get-tuple-element.82), channel_id=1, source_target_pairs={{0,2},{1,3},{2,0},{3,1},{4,6},{5,7},{6,4},{7,5},{8,10},{9,11},{10,... | collective-permute-start | bytes 1179656 | tf_op jit(solution)/shard_map/ppermute | solution.py:21
  14.2 29.5 %collective-permute-start.2 = (bf16[48,4096]{1,0:T(8,128)(2,1)}, bf16[48,4096]{1,0:T(8,128)(2,1)S(1)}, u32[]{:S(2)}, u32[]{:S(2)}) collective-permute-start(bf16[48,4096]{1,0:T(8,128)(2,1)} %get-tuple-element.81), channel_id=1, source_target_pairs={{0,3},{1,2},{2,1},{3,0},{4,7},{5,6},{6,5},{7,4},{8,11},{9,10},{10,... | collective-permute-start | bytes 1179656 | tf_op jit(solution)/shard_map/ppermute | solution.py:21
  29.0 19.8 %collective-permute-start.6 = (bf16[192,1024]{1,0:T(8,128)(2,1)S(1)}, bf16[192,1024]{1,0:T(8,128)(2,1)S(1)}, u32[]{:S(2)}, u32[]{:S(2)}) collective-permute-start(bf16[192,1024]{1,0:T(8,128)(2,1)S(1)} %get-tuple-element.44), channel_id=1, source_target_pairs={{0,16},{16,32},{32,48},{48,0},{1,17},{17,33},{33,49},{49,1},{2,18}... | collective-permute-start | bytes 1179656 | tf_op jit(solution)/shard_map/ppermute | solution.py:27
  30.5 20.3 %collective-permute-start.7 = (bf16[192,1024]{1,0:T(8,128)(2,1)S(1)}, bf16[192,1024]{1,0:T(8,128)(2,1)S(1)}, u32[]{:S(2)}, u32[]{:S(2)}) collective-permute-start(bf16[192,1024]{1,0:T(8,128)(2,1)S(1)} %get-tuple-element.45), channel_id=1, source_target_pairs={{0,32},{16,48},{32,0},{48,16},{1,33},{17,49},{33,1},{49,17},{2,34}... | collective-permute-start | bytes 1179656 | tf_op jit(solution)/shard_map/ppermute | solution.py:27
  33.2 17.6 %collective-permute-start.8 = (bf16[192,1024]{1,0:T(8,128)(2,1)S(1)}, bf16[192,1024]{1,0:T(8,128)(2,1)S(1)}, u32[]{:S(2)}, u32[]{:S(2)}) collective-permute-start(bf16[192,1024]{1,0:T(8,128)(2,1)S(1)} %get-tuple-element.46), channel_id=1, source_target_pairs={{0,48},{16,0},{32,16},{48,32},{1,49},{17,1},{33,17},{49,33},{2,50}... | collective-permute-start | bytes 1179656 | tf_op jit(solution)/shard_map/ppermute | solution.py:27
  52.7 45.8 %all-to-all-start.1 = ((bf16[4,192,1792]{2,1,0:T(8,128)(2,1)}), bf16[4,192,1792]{2,1,0:T(8,128)(2,1)}, u32[]{:S(2)}, u32[]{:S(2)}) async-start(bf16[4,192,1792]{2,1,0:T(8,128)(2,1)} %get-tuple-element.64), calls=%async_computation.1 | async-start | bytes 5505024 | tf_op jit(solution)/shard_map/all_to_all | solution.py:353
  57.3 17.2 %collective-permute-start.12 = (bf16[2,192,768]{2,1,0:T(8,128)(2,1)S(1)}, bf16[2,192,768]{2,1,0:T(8,128)(2,1)S(1)}, u32[]{:S(2)}, u32[]{:S(2)}) collective-permute-start(bf16[2,192,768]{2,1,0:T(8,128)(2,1)S(1)} %get-tuple-element.42.dact.refs_4_), channel_id=1, source_target_pairs={{0,16},{16,32},{32,48},{48,0},{1,17},{17,33},{33,49},{49,1},{2,18}... | collective-permute-start | bytes 1769480 | tf_op jit(solution)/shard_map/ppermute | solution.py:27
  58.7 28.2 %collective-permute-start.13 = (bf16[2,192,768]{2,1,0:T(8,128)(2,1)S(1)}, bf16[2,192,768]{2,1,0:T(8,128)(2,1)S(1)}, u32[]{:S(2)}, u32[]{:S(2)}) collective-permute-start(bf16[2,192,768]{2,1,0:T(8,128)(2,1)S(1)} %get-tuple-element.42.dact.refs_4_), channel_id=1, source_target_pairs={{0,32},{16,48},{32,0},{48,16},{1,33},{17,49},{33,1},{49,17},{2,34}... | collective-permute-start | bytes 1769480 | tf_op jit(solution)/shard_map/ppermute | solution.py:27
  61.0 25.9 %collective-permute-start.14 = (bf16[2,192,768]{2,1,0:T(8,128)(2,1)S(1)}, bf16[2,192,768]{2,1,0:T(8,128)(2,1)S(1)}, u32[]{:S(2)}, u32[]{:S(2)}) collective-permute-start(bf16[2,192,768]{2,1,0:T(8,128)(2,1)S(1)} %get-tuple-element.42.dact.refs_4_), channel_id=1, source_target_pairs={{0,48},{16,0},{32,16},{48,32},{1,49},{17,1},{33,17},{49,33},{2,50}... | collective-permute-start | bytes 1769480 | tf_op jit(solution)/shard_map/ppermute | solution.py:27
  62.6 27.5 %copy-start.10 = (bf16[192,1024]{1,0:T(8,128)(2,1)S(1)}, bf16[192,1024]{1,0:T(8,128)(2,1)}, u32[]{:S(2)}) copy-start(bf16[192,1024]{1,0:T(8,128)(2,1)} %copy-done.9) | copy-start | bytes 1179652
  62.6 27.5 %copy-start.12 = (bf16[192,1024]{1,0:T(8,128)(2,1)S(1)}, bf16[192,1024]{1,0:T(8,128)(2,1)}, u32[]{:S(2)}) copy-start(bf16[192,1024]{1,0:T(8,128)(2,1)} %copy-done.11) | copy-start | bytes 1179652
  62.6 27.5 %copy-start.21 = (bf16[192,1024]{1,0:T(8,128)(2,1)S(1)}, bf16[192,1024]{1,0:T(8,128)(2,1)}, u32[]{:S(2)}) copy-start(bf16[192,1024]{1,0:T(8,128)(2,1)} %copy-done.20) | copy-start | bytes 1179652
  71.0 15.9 %collective-permute-start.10 = (bf16[48,4096]{1,0:T(8,128)(2,1)S(1)}, bf16[48,4096]{1,0:T(8,128)(2,1)S(1)}, u32[]{:S(2)}, u32[]{:S(2)}) collective-permute-start(bf16[48,4096]{1,0:T(8,128)(2,1)S(1)} %get-tuple-element.51), channel_id=1, source_target_pairs={{0,2},{1,3},{2,0},{3,1},{4,6},{5,7},{6,4},{7,5},{8,10},{9,11},{10,... | collective-permute-start | bytes 1179656 | tf_op jit(solution)/shard_map/ppermute | solution.py:21
  74.5 15.6 %collective-permute-start.11 = (bf16[48,4096]{1,0:T(8,128)(2,1)S(1)}, bf16[48,4096]{1,0:T(8,128)(2,1)S(1)}, u32[]{:S(2)}, u32[]{:S(2)}) collective-permute-start(bf16[48,4096]{1,0:T(8,128)(2,1)S(1)} %get-tuple-element.52), channel_id=1, source_target_pairs={{0,3},{1,2},{2,1},{3,0},{4,7},{5,6},{6,5},{7,4},{8,11},{9,10},{10,... | collective-permute-start | bytes 1179656 | tf_op jit(solution)/shard_map/ppermute | solution.py:21
  98.5 28.7 %all-to-all-start = ((bf16[4,256,896]{2,1,0:T(8,128)(2,1)}), bf16[4,256,896]{2,1,0:T(8,128)(2,1)S(1)}, u32[]{:S(2)}, u32[]{:S(2)}) async-start(bf16[4,256,896]{2,1,0:T(8,128)(2,1)} %get-tuple-element.55), calls=%async_computation | async-start | bytes 3670016 | tf_op jit(solution)/shard_map/all_to_all | solution.py:367
  102.9 34.4 %collective-permute-start.16 = (bf16[512,640]{1,0:T(8,128)(2,1)}, bf16[512,640]{1,0:T(8,128)(2,1)}, u32[]{:S(2)}, u32[]{:S(2)}) collective-permute-start(bf16[512,640]{1,0:T(8,128)(2,1)} %get-tuple-element.59), channel_id=1, source_target_pairs={{0,64},{64,0},{1,65},{65,1},{2,66},{66,2},{3,67},{67,3},{4,68},{68... | collective-permute-start | bytes 1966088 | tf_op jit(solution)/shard_map/ppermute | solution.py:31
  104.0 26.5 %collective-permute-start.9 = (bf16[48,4096]{1,0:T(8,128)(2,1)}, bf16[48,4096]{1,0:T(8,128)(2,1)}, u32[]{:S(2)}, u32[]{:S(2)}) collective-permute-start(bf16[48,4096]{1,0:T(8,128)(2,1)} %get-tuple-element.50), channel_id=1, source_target_pairs={{0,1},{1,0},{2,3},{3,2},{4,5},{5,4},{6,7},{7,6},{8,9},{9,8},{10,11... | collective-permute-start | bytes 1179656 | tf_op jit(solution)/shard_map/ppermute | solution.py:21
  110.2 29.0 %collective-permute-start.20 = (bf16[192,1024]{1,0:T(8,128)(2,1)}, bf16[192,1024]{1,0:T(8,128)(2,1)}, u32[]{:S(2)}, u32[]{:S(2)}) collective-permute-start(bf16[192,1024]{1,0:T(8,128)(2,1)} %get-tuple-element.67), channel_id=1, source_target_pairs={{0,16},{16,32},{32,48},{48,0},{1,17},{17,33},{33,49},{49,1},{2,18}... | collective-permute-start | bytes 1179656 | tf_op jit(solution)/shard_map/ppermute | solution.py:27
  111.2 30.1 %collective-permute-start.21 = (bf16[192,1024]{1,0:T(8,128)(2,1)}, bf16[192,1024]{1,0:T(8,128)(2,1)}, u32[]{:S(2)}, u32[]{:S(2)}) collective-permute-start(bf16[192,1024]{1,0:T(8,128)(2,1)} %get-tuple-element.68), channel_id=1, source_target_pairs={{0,32},{16,48},{32,0},{48,16},{1,33},{17,49},{33,1},{49,17},{2,34}... | collective-permute-start | bytes 1179656 | tf_op jit(solution)/shard_map/ppermute | solution.py:27
  112.2 29.8 %collective-permute-start.22 = (bf16[192,1024]{1,0:T(8,128)(2,1)}, bf16[192,1024]{1,0:T(8,128)(2,1)}, u32[]{:S(2)}, u32[]{:S(2)}) collective-permute-start(bf16[192,1024]{1,0:T(8,128)(2,1)} %get-tuple-element.69), channel_id=1, source_target_pairs={{0,48},{16,0},{32,16},{48,32},{1,49},{17,1},{33,17},{49,33},{2,50}... | collective-permute-start | bytes 1179656 | tf_op jit(solution)/shard_map/ppermute | solution.py:27
  130.5 14.4 %collective-permute-start.15 = (bf16[128,896]{1,0:T(8,128)(2,1)}, bf16[128,896]{1,0:T(8,128)(2,1)}, u32[]{:S(2)}, u32[]{:S(2)}) collective-permute-start(bf16[128,896]{1,0:T(8,128)(2,1)} %get-tuple-element.57), channel_id=1, source_target_pairs={{0,64},{64,0},{1,65},{65,1},{2,66},{66,2},{3,67},{67,3},{4,68},{68... | collective-permute-start | bytes 688136 | tf_op jit(solution)/shard_map/ppermute | solution.py:31
  138.6 10.5 %collective-permute-start.17 = (bf16[128,640]{1,0:T(8,128)(2,1)S(1)}, bf16[128,640]{1,0:T(8,128)(2,1)S(1)}, u32[]{:S(2)}, u32[]{:S(2)}) collective-permute-start(bf16[128,640]{1,0:T(8,128)(2,1)S(1)} %get-tuple-element.61), channel_id=1, source_target_pairs={{0,4},{4,8},{8,12},{12,0},{1,5},{5,9},{9,13},{13,1},{2,6},{6,10},{... | collective-permute-start | bytes 491528 | tf_op jit(solution)/shard_map/ppermute | solution.py:27
  139.3 9.9 %collective-permute-start.18 = (bf16[128,640]{1,0:T(8,128)(2,1)S(1)}, bf16[128,640]{1,0:T(8,128)(2,1)S(1)}, u32[]{:S(2)}, u32[]{:S(2)}) collective-permute-start(bf16[128,640]{1,0:T(8,128)(2,1)S(1)} %get-tuple-element.62), channel_id=1, source_target_pairs={{0,8},{4,12},{8,0},{12,4},{1,9},{5,13},{9,1},{13,5},{2,10},{6,14},... | collective-permute-start | bytes 491528 | tf_op jit(solution)/shard_map/ppermute | solution.py:27
  141.3 8.4 %collective-permute-start.19 = (bf16[128,640]{1,0:T(8,128)(2,1)S(1)}, bf16[128,640]{1,0:T(8,128)(2,1)S(1)}, u32[]{:S(2)}, u32[]{:S(2)}) collective-permute-start(bf16[128,640]{1,0:T(8,128)(2,1)S(1)} %get-tuple-element.63), channel_id=1, source_target_pairs={{0,12},{4,0},{8,4},{12,8},{1,13},{5,1},{9,5},{13,9},{2,14},{6,2},{... | collective-permute-start | bytes 491528 | tf_op jit(solution)/shard_map/ppermute | solution.py:27
  144.1 5.9 %collective-permute-start.23 = (bf16[96,1024]{1,0:T(8,128)(2,1)S(1)}, bf16[96,1024]{1,0:T(8,128)(2,1)S(1)}, u32[]{:S(2)}, u32[]{:S(2)}) collective-permute-start(bf16[96,1024]{1,0:T(8,128)(2,1)S(1)} %get-tuple-element.71.after), channel_id=1, source_target_pairs={{0,64},{64,0},{1,65},{65,1},{2,66},{66,2},{3,67},{67,3},{4,68},{68... | collective-permute-start | bytes 589832 | tf_op jit(solution)/shard_map/ppermute | solution.py:31
  150.1 6.1 %collective-permute-start.24 = (bf16[24,1024]{1,0:T(8,128)(2,1)S(1)}, bf16[24,1024]{1,0:T(8,128)(2,1)S(1)}, u32[]{:S(2)}, u32[]{:S(2)}) collective-permute-start(bf16[24,1024]{1,0:T(8,128)(2,1)S(1)} %get-tuple-element.87), channel_id=1, source_target_pairs={{0,4},{4,8},{8,12},{12,0},{1,5},{5,9},{9,13},{13,1},{2,6},{6,10},{... | collective-permute-start | bytes 147464 | tf_op jit(solution)/shard_map/ppermute | solution.py:27
  151.3 5.6 %collective-permute-start.25 = (bf16[24,1024]{1,0:T(8,128)(2,1)S(1)}, bf16[24,1024]{1,0:T(8,128)(2,1)S(1)}, u32[]{:S(2)}, u32[]{:S(2)}) collective-permute-start(bf16[24,1024]{1,0:T(8,128)(2,1)S(1)} %get-tuple-element.86), channel_id=1, source_target_pairs={{0,8},{4,12},{8,0},{12,4},{1,9},{5,13},{9,1},{13,5},{2,10},{6,14},... | collective-permute-start | bytes 147464 | tf_op jit(solution)/shard_map/ppermute | solution.py:27
  153.9 4.1 %collective-permute-start.26 = (bf16[24,1024]{1,0:T(8,128)(2,1)S(1)}, bf16[24,1024]{1,0:T(8,128)(2,1)S(1)}, u32[]{:S(2)}, u32[]{:S(2)}) collective-permute-start(bf16[24,1024]{1,0:T(8,128)(2,1)S(1)} %get-tuple-element.85), channel_id=1, source_target_pairs={{0,12},{4,0},{8,4},{12,8},{1,13},{5,1},{9,5},{13,9},{2,14},{6,2},{... | collective-permute-start | bytes 147464 | tf_op jit(solution)/shard_map/ppermute | solution.py:27
  (22 other events, 108.1 us)

commit v8 on v6

--- a/solution.py
+++ b/solution.py
@@ -158,12 +158,11 @@
     out[...] = jnp.dot(mask[...], whole[...], preferred_element_type=F32).astype(BF)
 
 
-def tile_step(*refs):
+def tile_step(at, *refs):
     xs, ds = refs[:4], refs[4:8]
-    out, mark, xall, dall, buf, sem, osem = refs[-7:]
-    rows = xs[0].shape[0]
+    own, next0, next1, prev0, prev1, far0, far1, mark, xall, dall, sem = refs[-11:]
+    rows, inner = xs[0].shape[0], ds[0].shape[2]
     part = [pl.ds(p * rows, rows) for p in range(4)]
-    inner = ds[0].shape[2]
     land(
         [(xs[p], xall.at[part[p], :]) for p in range(4)]
         + [
@@ -174,37 +173,36 @@
         sem,
     )
     mark[...] = jnp.zeros_like(mark)
-    copies = []
-    for b in range(2):
-        got = rows_dot(xall[:, b * 512 : b * 512 + 512], dall[...])
-        for j in range(4):
-            i = b * 4 + j
-            buf[i] = got[j * 128 : j * 128 + 128].astype(BF)
-            copies.append(pltpu.make_async_copy(buf.at[i], out.at[i], osem.at[i]))
-            copies[-1].start()
-    for copy in copies:
-        copy.wait()
-
-
-def tile_call(xs, ds, after):
+    for j, out in ((2, (far0, far1)), (1, (next0, next1)), (3, (prev0, prev1)), (0, None)):
+        other = lax.rem(at[2] + j, 4)
+        for b in range(2):
+            got = rows_dot(xall[:, aligned(b * 4 + other, 128)], dall[...])
+            if out is None:
+                own[b * 128 : b * 128 + 128, :] = got
+            else:
+                out[b][...] = got.astype(out[b].dtype)
+
+
+def tile_call(at, xs, ds, after):
     rows, part = xs[0].shape
     wide = 2 * ds[0].shape[2]
+    half, full = shape(128, wide), shape(128, wide, dtype=F32)
     return call(
         tile_step,
-        "a" * (8 + len(after)),
-        [shape(8, 128, wide), MARK],
-        [
-            pltpu.VMEM((4 * rows, part), BF),
-            pltpu.VMEM((4 * rows, wide), BF),
-            pltpu.VMEM((8, 128, wide), BF),
-            sems(12),
-            sems(8),
-        ],
+        "s" + "a" * (8 + len(after)),
+        [shape(256, wide, dtype=F32), full, half, half, full, half, half, MARK],
+        [pltpu.VMEM((4 * rows, part), BF), pltpu.VMEM((4 * rows, wide), BF), sems(12)],
         flops=8 * rows * part * wide,
         moved=8 * rows * (part + wide),
-        limit=24,
-        placed=(0,),
-    )(*xs, *ds, *after)
+        limit=16,
+    )(at, *xs, *ds, *after)
+
+
+def middle_step(next0, next1, prev0, prev1, from_prev, from_next, after, to_next, to_prev):
+    to_next[:128, :] = (next0[...] + from_prev[...].astype(F32)).astype(BF)
+    to_next[128:, :] = next1[...]
+    to_prev[:128, :] = prev0[...]
+    to_prev[128:, :] = (prev1[...] + from_next[...].astype(F32)).astype(BF)
 
 
 def down_step(at, both, *rest):
@@ -227,12 +225,16 @@
             )
 
 
-def gate_sum(parts, out, mark, g, sem):
-    copies = fetch([(parts.at[i], g.at[i]) for i in range(8)], sem)
-    mark[...] = jnp.zeros_like(mark)
-    for copy in copies:
-        copy.wait()
-    out[...] = sum(g[i].astype(F32) for i in range(8)).astype(BF)
+def gate_sum(at, own, r1, r2, keep, send, mark):
+    half = keep.shape[0]
+    mark[...] = jnp.zeros_like(mark)
+
+    def part(i):
+        rows = aligned(i, half)
+        return own[rows, :] + r1[rows, :].astype(F32) + r2[rows, :].astype(F32)
+
+    send[...] = part(1 - at[0]).astype(BF)
+    keep[...] = part(at[0])
 
 
 def sum_step(at, own, r1, r2, r3, *rest):
@@ -339,9 +341,8 @@
         limit=18,
     )(dact, gate_up, sent_mark)
     arrived = [back[0]] + [swap_expert(back[k], k) for k in (1, 2, 3)]
-    parts, mark = tile_call(xa, da, arrived[2:])
-    gate = lax.all_to_all(parts, ("w", "y"), split_axis=0, concat_axis=0, tiled=True)
-    *parts, _ = call(
+    own, next0, next1, prev0, prev1, far0, far1, mark = tile_call(at, xa, da, [arrived[2]])
+    *parts, mark = call(
         down_step,
         "saa",
         [shape(192, part, dtype=F32)] + [shape(192, part)] * 3 + [MARK],
@@ -355,6 +356,10 @@
         moved=8 * rows * (part + inner),
         limit=16,
     )(at, both, mark)
+    to_next, to_prev = call(middle_step, "vvvvvva", [shape(256, 2 * inner)] * 2)(
+        next0, next1, prev0, prev1, shift(far0, "y", 1), shift(far1, "y", 3), mark
+    )
+    gate = [own, shift(to_next, "y", 1), shift(to_prev, "y", 3)]
     down = [parts[0]] + [shift(parts[j], "x", j) for j in (1, 2, 3)]
     token_grad, tok_mark = call(
         tok_step,
@@ -363,13 +368,12 @@
         [pltpu.VMEM((rows, width), BF), sems(4)],
     )(mask, *arrived)
 
-    gate_up_grad, mark = call(
+    gate_keep, gate_send, mark = call(
         gate_sum,
-        "a",
-        [shape(128, 2 * inner), MARK],
-        [pltpu.VMEM((8, 128, 2 * inner), BF), sems(8)],
-        limit=12,
-    )(gate)
+        "svvv",
+        [shape(128, 2 * inner, dtype=F32), shape(128, 2 * inner), MARK],
+    )(at, *gate)
+    gate_up_grad = (gate_keep + swap_w(gate_send).astype(F32)).astype(BF)
     keep, send = sum_call(at, down, [tok_mark])
     down_grad = (keep + swap_w(send).astype(F32)).astype(BF).reshape(4, 24, part)
     cols = [

time: 153 us -> 154 us (level)
  waiting for transfers between devices: 59.5 us -> 48.3 us
  local copies, waits for them, and re-layouts: 3.53 us -> 8.72 us
  starting transfers between devices: 44.9 us -> 47.7 us
  Pallas kernels: 39.6 us -> 42.1 us
  other arithmetic: 1.39 us -> 3.14 us
    ppermute x1 -> x2, waiting for transfers between devices: 12.7 us -> 4.23 us  [swap_w(): return lax.ppermute(a, 'w', [(0, 1), (1, 0)])]
    unnamed x22 -> x50, local copies, waits for them, and re-layouts: 0.82 us -> 5.97 us
    all_to_all x1 -> x0, starting transfers between devices: 4.99 us -> none  [shards(): lax.all_to_all(parts, ('w', 'y'), split_axis=0, concat_axis=0, tiled=True)]
    ppermute x12 -> x16, starting transfers between devices: 21.6 us -> 26.3 us  [shift(): return lax.ppermute(a, axis, [(i, (i + j) % 4) for i in range(4)])]
    ppermute x9, starting transfers between devices: 11.7 us -> 14.7 us  [swap_expert(): return lax.ppermute(a, ('v', 'c'), [(i, i ^ k) for i in range(4)])]
    ppermute x9, waiting for transfers between devices: 14.8 us -> 13 us  [swap_expert(): return lax.ppermute(a, ('v', 'c'), [(i, i ^ k) for i in range(4)])]
    ppermute x12 -> x16, waiting for transfers between devices: 32 us -> 31.1 us  [shift(): return lax.ppermute(a, axis, [(i, (i + j) % 4) for i in range(4)])]
    pallas_call x2 -> x3, Pallas kernels: 7.88 us -> 8.51 us  [the longest x1 4.6 us: tile_call(): call(tile_step, 's' + 'a' * (8 + len(after)), [shape(256, wide, dtype=F32...]
  transfers between devices with their start and end apart: 24 -> 28, of which waited for: 10 -> 11; matrix products, arithmetic and copies ran while one was open for 2% -> 3% of each run, Pallas kernels for 24% -> 26%
where the time goes in v8:
time: 154 us; the launch traced here: 153 us
  waiting for transfers between devices  48.3 us (31%)
  starting transfers between devices  47.7 us (31%)
  Pallas kernels  42.1 us (27%)
  local copies, waits for them, and re-layouts  8.72 us (6%)
  other arithmetic  3.14 us (2%)
  matrix products  2.46 us (2%)
    ppermute x16, waiting for transfers between devices, shift(): return lax.ppermute(a, axis, [(i, (i + j) % 4) for i in range(4)])  31.1 us
    ppermute x16, starting transfers between devices, shift(): return lax.ppermute(a, axis, [(i, (i + j) % 4) for i in range(4)])  26.3 us
    ppermute x9, starting transfers between devices, swap_expert(): return lax.ppermute(a, ('v', 'c'), [(i, i ^ k) for i in range(4)])  14.7 us
    ppermute x9, waiting for transfers between devices, swap_expert(): return lax.ppermute(a, ('v', 'c'), [(i, i ^ k) for i in range(4)])  13 us
    pallas_call x1, Pallas kernels, shards(): call(back_step, 'vaa', [shape(CAP, width)] * 4 + [MARK], [pltpu.VMEM((n,...  7.77 us
    pallas_call x1, Pallas kernels, shards(): call(act_step, 'va', [shape(rows, inner), shape(rows, inner, dtype=F32),...  7.42 us
    unnamed x50, local copies, waits for them, and re-layouts  5.97 us
    pallas_call x1, Pallas kernels, shards(): call(dh_step, 'aaaaaaa', [shape(2, rows, inner), MARK], [pltpu.VMEM((rows...  5.09 us
  transfers between devices with their start and end apart: 28, of which 11 were waited for; matrix products, arithmetic and copies ran while one was open for 3% of the time, Pallas kernels for 26%

profile of v8, /device:TPU:0, one launch (start us, length us, event | category | flops | bytes accessed | tf_op | source)
XLA Modules:
  0.0 153.5 jit_solution(6679895990367242623)
XLA Ops:
  4.0 4.0 %collective-permute-start.4 = (bf16[48,4096]{1,0:T(8,128)(2,1)}, bf16[48,4096]{1,0:T(8,128)(2,1)}, u32[]{:S(2)}, u32[]{:S(2)}) collective-permute-start(bf16[48,4096]{1,0:T(8,128)(2,1)} %get-tuple-element.82), channel_id=1, source_target_pairs={{0,2},{1,3},{2,0},{3,1},{4,6},{5,7},{6,4},{7,5},{8,10},{9,11},{10,... | collective-permute-start | bytes 1179656 | tf_op jit(solution)/shard_map/ppermute | solution.py:21
  8.4 1.8 %fusion = bf16[192,4096]{1,0:T(8,128)(2,1)S(1)} fusion(pred[128,192]{1,0:T(32,128)(4,1)S(1)} %get-tuple-element.80, bf16[128,4096]{1,0:T(8,128)(2,1)} %param.7, f32[192]{0:T(256)S(1)} %mul.14), kind=kOutput, calls=%fused_computation.1 | convolution fusion | flops 202899456 | bytes 2646784 | tf_op jit(solution)/shard_map/dot_general | solution.py:35
  11.4 3.4 %collective-permute-start.1 = (bf16[48,4096]{1,0:T(8,128)(2,1)}, bf16[48,4096]{1,0:T(8,128)(2,1)S(1)}, u32[]{:S(2)}, u32[]{:S(2)}) collective-permute-start(bf16[48,4096]{1,0:T(8,128)(2,1)} %get-tuple-element.86), channel_id=1, source_target_pairs={{0,2},{1,3},{2,0},{3,1},{4,6},{5,7},{6,4},{7,5},{8,10},{9,11},{10,... | collective-permute-start | bytes 1179656 | tf_op jit(solution)/shard_map/ppermute | solution.py:21
  14.9 3.4 %collective-permute-done.4.x2 = bf16[48,4096]{1,0:T(8,128)(2,1)} collective-permute-done((bf16[48,4096]{1,0:T(8,128)(2,1)}, bf16[48,4096]{1,0:T(8,128)(2,1)}, u32[]{:S(2)}, u32[]{:S(2)}) %collective-permute-start.4) | collective-permute-done | bytes 393248 | tf_op jit(solution)/shard_map/ppermute | solution.py:21
  18.3 8.1 %collective-permute-done.5.x3 = bf16[48,4096]{1,0:T(8,128)(2,1)} collective-permute-done((bf16[48,4096]{1,0:T(8,128)(2,1)}, bf16[48,4096]{1,0:T(8,128)(2,1)}, u32[]{:S(2)}, u32[]{:S(2)}) %collective-permute-start.5) | collective-permute-done | bytes 393248 | tf_op jit(solution)/shard_map/ppermute | solution.py:21
  29.9 2.7 %collective-permute-start.7 = (bf16[192,1024]{1,0:T(8,128)(2,1)S(1)}, bf16[192,1024]{1,0:T(8,128)(2,1)S(1)}, u32[]{:S(2)}, u32[]{:S(2)}) collective-permute-start(bf16[192,1024]{1,0:T(8,128)(2,1)S(1)} %get-tuple-element.47), channel_id=1, source_target_pairs={{0,32},{16,48},{32,0},{48,16},{1,33},{17,49},{33,1},{49,17},{2,34}... | collective-permute-start | bytes 1179656 | tf_op jit(solution)/shard_map/ppermute | solution.py:27
  34.1 7.4 %shard_map.86 = (bf16[192,768]{1,0:T(8,128)(2,1)S(1)}, f32[192,768]{1,0:T(8,128)S(1)}, f32[192,768]{1,0:T(8,128)S(1)}) custom-call(bf16[192,4096]{1,0:T(8,128)(2,1)S(1)} %get-tuple-element.41.x, bf16[4096,1536]{1,0:T(8,128)(2,1)} %bitcast.24), custom_call_target="tpu_custom_call" | custom-call | flops 2415919104 | bytes 12582912 | tf_op jit(solution)/shard_map/pallas_call | solution.py:298
  43.1 5.1 %shard_map.87 = (bf16[2,192,768]{2,1,0:T(8,128)(2,1)S(1)}, f32[8,128]{1,0:T(8,128)S(1)}) custom-call(bf16[48,4096]{1,0:T(8,128)(2,1)S(1)} %get-tuple-element.88.g0, bf16[48,4096]{1,0:T(8,128)(2,1)S(1)} %collective-permute-done.g1, bf16[48,4096]{1,0:T(8,128)(2,1)S(1)} %collective-permute-done.1.g2, bf16[48,4096]{1,0:T(8,128)(2,1)S(1)} %collective-permute-done.2.g3, ...), custom_call_target="tpu_custom_call" | custom-call | flops 1207959552 | bytes 6291456 | tf_op jit(solution)/shard_map/pallas_call | solution.py:308
  48.2 2.0 %collective-permute-done.7.rest_1_.refs_2_ = bf16[192,1024]{1,0:T(8,128)(2,1)S(1)} collective-permute-done((bf16[192,1024]{1,0:T(8,128)(2,1)S(1)}, bf16[192,1024]{1,0:T(8,128)(2,1)S(1)}, u32[]{:S(2)}, u32[]{:S(2)}) %collective-permute-start.7) | collective-permute-done | bytes 393248 | tf_op jit(solution)/shard_map/ppermute | solution.py:27
  50.3 1.8 %shard_map.88 = (bf16[4,192,1792]{2,1,0:T(8,128)(2,1)}, f32[8,128]{1,0:T(8,128)S(1)}) custom-call(bf16[48,4096]{1,0:T(8,128)(2,1)S(1)} %get-tuple-element.88.g0, bf16[48,4096]{1,0:T(8,128)(2,1)S(1)} %collective-permute-done.g1, bf16[48,4096]{1,0:T(8,128)(2,1)S(1)} %collective-permute-done.1.g2, bf16[48,4096]{1,0:T(8,128)(2,1)S(1)} %collective-permute-done.2.g3, ...), custom_call_target="tpu_custom_call" | custom-call | bytes 3145728 | tf_op jit(solution)/shard_map/pallas_call | solution.py:324
  52.1 4.6 %all-to-all-start = ((bf16[4,192,1792]{2,1,0:T(8,128)(2,1)}), bf16[4,192,1792]{2,1,0:T(8,128)(2,1)}, u32[]{:S(2)}, u32[]{:S(2)}) async-start(bf16[4,192,1792]{2,1,0:T(8,128)(2,1)} %get-tuple-element.64), calls=%async_computation | async-start | bytes 5505024 | tf_op jit(solution)/shard_map/all_to_all | solution.py:332
  58.0 2.4 %collective-permute-start.13 = (bf16[2,192,768]{2,1,0:T(8,128)(2,1)S(1)}, bf16[2,192,768]{2,1,0:T(8,128)(2,1)S(1)}, u32[]{:S(2)}, u32[]{:S(2)}) collective-permute-start(bf16[2,192,768]{2,1,0:T(8,128)(2,1)S(1)} %get-tuple-element.44.dact.refs_4_), channel_id=1, source_target_pairs={{0,32},{16,48},{32,0},{48,16},{1,33},{17,49},{33,1},{49,17},{2,34}... | collective-permute-start | bytes 1769480 | tf_op jit(solution)/shard_map/ppermute | solution.py:27
  62.0 7.8 %shard_map.89 = (bf16[48,4096]{1,0:T(8,128)(2,1)S(1)}, bf16[48,4096]{1,0:T(8,128)(2,1)}, bf16[48,4096]{1,0:T(8,128)(2,1)S(1)}, bf16[48,4096]{1,0:T(8,128)(2,1)}, f32[8,128]{1,0:T(8,128)}) custom-call(bf16[2,192,768]{2,1,0:T(8,128)(2,1)S(1)} %get-tuple-element.44.dact.refs_4_, bf16[4096,1536]{1,0:T(8,128)(2,1)} %bitcast.25, ...), custom_call_target="tpu_custom_call" | custom-call | flops 2415919104 | bytes 12582912 | tf_op jit(solution)/shard_map/pallas_call | solution.py:334
  70.6 3.5 %collective-permute-start.10 = (bf16[48,4096]{1,0:T(8,128)(2,1)S(1)}, bf16[48,4096]{1,0:T(8,128)(2,1)S(1)}, u32[]{:S(2)}, u32[]{:S(2)}) collective-permute-start(bf16[48,4096]{1,0:T(8,128)(2,1)S(1)} %get-tuple-element.53), channel_id=1, source_target_pairs={{0,2},{1,3},{2,0},{3,1},{4,6},{5,7},{6,4},{7,5},{8,10},{9,11},{10,... | collective-permute-start | bytes 1179656 | tf_op jit(solution)/shard_map/ppermute | solution.py:21
  74.0 12.3 %collective-permute-done.13.refs_6_ = bf16[2,192,768]{2,1,0:T(8,128)(2,1)S(1)} collective-permute-done((bf16[2,192,768]{2,1,0:T(8,128)(2,1)S(1)}, bf16[2,192,768]{2,1,0:T(8,128)(2,1)S(1)}, u32[]{:S(2)}, u32[]{:S(2)}) %collective-permute-start.13) | collective-permute-done | bytes 589856 | tf_op jit(solution)/shard_map/ppermute | solution.py:27
  87.5 4.6 %shard_map.91 = (f32[256,1536]{1,0:T(8,128)S(1)}, f32[128,1536]{1,0:T(8,128)S(1)}, bf16[128,1536]{1,0:T(8,128)(2,1)S(1)}, bf16[128,1536]{1,0:T(8,128)(2,1)S(1)},...) custom-call(s32[4]{0:T(128)S(1)} %pad_add_fusion.at, ...), custom_call_target="tpu_custom_call" | custom-call | flops 2415919104 | bytes 3932160 | tf_op jit(solution)/shard_map/pallas_call | solution.py:190
  94.5 1.6 %collective-permute-start.15 = (bf16[128,1536]{1,0:T(8,128)(2,1)}, bf16[128,1536]{1,0:T(8,128)(2,1)}, u32[]{:S(2)}, u32[]{:S(2)}) collective-permute-start(bf16[128,1536]{1,0:T(8,128)(2,1)} %get-tuple-element.62), channel_id=1, source_target_pairs={{0,4},{4,8},{8,12},{12,0},{1,5},{5,9},{9,13},{13,1},{2,6},{6,10},{... | collective-permute-start | bytes 1179656 | tf_op jit(solution)/shard_map/ppermute | solution.py:27
  96.2 1.6 %collective-permute-start.16 = (bf16[128,1536]{1,0:T(8,128)(2,1)}, bf16[128,1536]{1,0:T(8,128)(2,1)}, u32[]{:S(2)}, u32[]{:S(2)}) collective-permute-start(bf16[128,1536]{1,0:T(8,128)(2,1)} %get-tuple-element.63), channel_id=1, source_target_pairs={{0,12},{4,0},{8,4},{12,8},{1,13},{5,1},{9,5},{13,9},{2,14},{6,2},{... | collective-permute-start | bytes 1179656 | tf_op jit(solution)/shard_map/ppermute | solution.py:27
  97.8 3.6 %collective-permute-start.11 = (bf16[48,4096]{1,0:T(8,128)(2,1)}, bf16[48,4096]{1,0:T(8,128)(2,1)}, u32[]{:S(2)}, u32[]{:S(2)}) collective-permute-start(bf16[48,4096]{1,0:T(8,128)(2,1)} %get-tuple-element.54), channel_id=1, source_target_pairs={{0,3},{1,2},{2,1},{3,0},{4,7},{5,6},{6,5},{7,4},{8,11},{9,10},{10,... | collective-permute-start | bytes 1179656 | tf_op jit(solution)/shard_map/ppermute | solution.py:21
  101.4 4.2 %shard_map.92 = (f32[192,1024]{1,0:T(8,128)S(1)}, bf16[192,1024]{1,0:T(8,128)(2,1)S(1)}, bf16[192,1024]{1,0:T(8,128)(2,1)S(1)}, bf16[192,1024]{1,0:T(8,128)(2,1)S(1)}, f32[8,128]{1,0:T(8,128)S(1)}) custom-call(s32[4]{0:T(128)S(1)} %pad_add_fusion.at, bf16[4,192,1792]{2,1,0:T(8,128)(2,1)} %all-to-all-done.both, f32[8,128]{1,0:T(8,128)S(1)} %get-tuple-element.65.rest_0_), custom_call_target="tpu_custom_call" | custom-call | flops 1207959552 | bytes 2752512 | tf_op jit(solution)/shard_map/pallas_call | solution.py:345
  106.4 2.5 %shard_map.93 = (bf16[256,1536]{1,0:T(8,128)(2,1)}, bf16[256,1536]{1,0:T(8,128)(2,1)}) custom-call(f32[128,1536]{1,0:T(8,128)S(1)} %get-tuple-element.58.next0, bf16[128,1536]{1,0:T(8,128)(2,1)S(1)} %copy-done.12, bf16[128,1536]{1,0:T(8,128)(2,1)S(1)} %copy-done.14, f32[128,1536]{1,0:T(8,128)S(1)} %copy-done.2, ...), custom_call_target="tpu_custom_call" | custom-call | tf_op jit(solution)/shard_map/pallas_call | solution.py:359
  110.1 2.0 %collective-permute-start.18 = (bf16[256,1536]{1,0:T(8,128)(2,1)}, bf16[256,1536]{1,0:T(8,128)(2,1)}, u32[]{:S(2)}, u32[]{:S(2)}) collective-permute-start(bf16[256,1536]{1,0:T(8,128)(2,1)} %get-tuple-element.68), channel_id=1, source_target_pairs={{0,12},{4,0},{8,4},{12,8},{1,13},{5,1},{9,5},{13,9},{2,14},{6,2},{... | collective-permute-start | bytes 2359304 | tf_op jit(solution)/shard_map/ppermute | solution.py:27
  112.1 2.2 %collective-permute-start.20 = (bf16[192,1024]{1,0:T(8,128)(2,1)S(1)}, bf16[192,1024]{1,0:T(8,128)(2,1)S(1)}, u32[]{:S(2)}, u32[]{:S(2)}) collective-permute-start(bf16[192,1024]{1,0:T(8,128)(2,1)S(1)} %get-tuple-element.72), channel_id=1, source_target_pairs={{0,16},{16,32},{32,48},{48,0},{1,17},{17,33},{33,49},{49,1},{2,18}... | collective-permute-start | bytes 1179656 | tf_op jit(solution)/shard_map/ppermute | solution.py:27
  114.3 2.3 %collective-permute-start.21 = (bf16[192,1024]{1,0:T(8,128)(2,1)S(1)}, bf16[192,1024]{1,0:T(8,128)(2,1)S(1)}, u32[]{:S(2)}, u32[]{:S(2)}) collective-permute-start(bf16[192,1024]{1,0:T(8,128)(2,1)S(1)} %get-tuple-element.73), channel_id=1, source_target_pairs={{0,32},{16,48},{32,0},{48,16},{1,33},{17,49},{33,1},{49,17},{2,34}... | collective-permute-start | bytes 1179656 | tf_op jit(solution)/shard_map/ppermute | solution.py:27
  117.0 2.8 %shard_map.90 = (bf16[128,4096]{1,0:T(8,128)(2,1)}, f32[8,128]{1,0:T(8,128)S(1)}) custom-call(bf16[128,192]{1,0:T(8,128)(2,1)S(1)} %get-tuple-element.79.mask, bf16[48,4096]{1,0:T(8,128)(2,1)S(1)} %copy-done.18, bf16[48,4096]{1,0:T(8,128)(2,1)} %collective-permute-done.9.a1, bf16[48,4096]{1,0:T(8,128)(2,1)S(1)} %copy-done.20, ...), custom_call_target="tpu_custom_call" | custom-call | tf_op jit(solution)/shard_map/pallas_call | solution.py:364
  119.8 4.5 %collective-permute-done.20.r1 = bf16[192,1024]{1,0:T(8,128)(2,1)S(1)} collective-permute-done((bf16[192,1024]{1,0:T(8,128)(2,1)S(1)}, bf16[192,1024]{1,0:T(8,128)(2,1)S(1)}, u32[]{:S(2)}, u32[]{:S(2)}) %collective-permute-start.20) | collective-permute-done | bytes 393248 | tf_op jit(solution)/shard_map/ppermute | solution.py:27
  124.3 8.5 %collective-permute-done.21.r2 = bf16[192,1024]{1,0:T(8,128)(2,1)S(1)} collective-permute-done((bf16[192,1024]{1,0:T(8,128)(2,1)S(1)}, bf16[192,1024]{1,0:T(8,128)(2,1)S(1)}, u32[]{:S(2)}, u32[]{:S(2)}) %collective-permute-start.21) | collective-permute-done | bytes 393248 | tf_op jit(solution)/shard_map/ppermute | solution.py:27
  132.8 2.0 %shard_map.95 = (f32[96,1024]{1,0:T(8,128)S(1)}, bf16[96,1024]{1,0:T(8,128)(2,1)}) custom-call(s32[4]{0:T(128)S(1)} %pad_add_fusion.at, f32[192,1024]{1,0:T(8,128)S(1)} %get-tuple-element.71.own, bf16[192,1024]{1,0:T(8,128)(2,1)S(1)} %collective-permute-done.20.r1, bf16[192,1024]{1,0:T(8,128)(2,1)S(1)} %collective-permute-done.21.r2, ...), custom_call_target="tpu_custom_call" | custom-call | tf_op jit(solution)/shard_map/pallas_call | solution.py:255
  135.6 2.0 %collective-permute-start.23 = (bf16[96,1024]{1,0:T(8,128)(2,1)}, bf16[96,1024]{1,0:T(8,128)(2,1)}, u32[]{:S(2)}, u32[]{:S(2)}) collective-permute-start(bf16[96,1024]{1,0:T(8,128)(2,1)} %get-tuple-element.77), channel_id=1, source_target_pairs={{0,64},{64,0},{1,65},{65,1},{2,66},{66,2},{3,67},{67,3},{4,68},{68... | collective-permute-start | bytes 589832 | tf_op jit(solution)/shard_map/ppermute | solution.py:31
  139.1 4.2 %collective-permute-done.23 = bf16[96,1024]{1,0:T(8,128)(2,1)} collective-permute-done((bf16[96,1024]{1,0:T(8,128)(2,1)}, bf16[96,1024]{1,0:T(8,128)(2,1)}, u32[]{:S(2)}, u32[]{:S(2)}) %collective-permute-start.23) | collective-permute-done | bytes 196640 | tf_op jit(solution)/shard_map/ppermute | solution.py:31
  144.4 2.9 %collective-permute-start.25 = (bf16[24,1024]{1,0:T(8,128)(2,1)S(1)}, bf16[24,1024]{1,0:T(8,128)(2,1)S(1)}, u32[]{:S(2)}, u32[]{:S(2)}) collective-permute-start(bf16[24,1024]{1,0:T(8,128)(2,1)S(1)} %get-tuple-element.90), channel_id=1, source_target_pairs={{0,8},{4,12},{8,0},{12,4},{1,9},{5,13},{9,1},{13,5},{2,10},{6,14},... | collective-permute-start | bytes 147464 | tf_op jit(solution)/shard_map/ppermute | solution.py:27
  148.4 1.8 %collective-permute-done.24.c1 = bf16[24,1024]{1,0:T(8,128)(2,1)S(1)} collective-permute-done((bf16[24,1024]{1,0:T(8,128)(2,1)S(1)}, bf16[24,1024]{1,0:T(8,128)(2,1)S(1)}, u32[]{:S(2)}, u32[]{:S(2)}) %collective-permute-start.24) | collective-permute-done | bytes 49184 | tf_op jit(solution)/shard_map/ppermute | solution.py:27
  (111 shorter events, 29.0 us)
Async XLA Ops:
  4.0 10.8 %collective-permute-start.3 = (bf16[48,4096]{1,0:T(8,128)(2,1)}, bf16[48,4096]{1,0:T(8,128)(2,1)S(1)}, u32[]{:S(2)}, u32[]{:S(2)}) collective-permute-start(bf16[48,4096]{1,0:T(8,128)(2,1)} %get-tuple-element.83), channel_id=1, source_target_pairs={{0,1},{1,0},{2,3},{3,2},{4,5},{5,4},{6,7},{7,6},{8,9},{9,8},{10,11... | collective-permute-start | bytes 1179656 | tf_op jit(solution)/shard_map/ppermute | solution.py:21
  4.0 14.2 %collective-permute-start.4 = (bf16[48,4096]{1,0:T(8,128)(2,1)}, bf16[48,4096]{1,0:T(8,128)(2,1)}, u32[]{:S(2)}, u32[]{:S(2)}) collective-permute-start(bf16[48,4096]{1,0:T(8,128)(2,1)} %get-tuple-element.82), channel_id=1, source_target_pairs={{0,2},{1,3},{2,0},{3,1},{4,6},{5,7},{6,4},{7,5},{8,10},{9,11},{10,... | collective-permute-start | bytes 1179656 | tf_op jit(solution)/shard_map/ppermute | solution.py:21
  8.0 18.3 %collective-permute-start.5 = (bf16[48,4096]{1,0:T(8,128)(2,1)}, bf16[48,4096]{1,0:T(8,128)(2,1)}, u32[]{:S(2)}, u32[]{:S(2)}) collective-permute-start(bf16[48,4096]{1,0:T(8,128)(2,1)} %get-tuple-element.81), channel_id=1, source_target_pairs={{0,3},{1,2},{2,1},{3,0},{4,7},{5,6},{6,5},{7,4},{8,11},{9,10},{10,... | collective-permute-start | bytes 1179656 | tf_op jit(solution)/shard_map/ppermute | solution.py:21
  11.3 21.3 %collective-permute-start = (bf16[48,4096]{1,0:T(8,128)(2,1)}, bf16[48,4096]{1,0:T(8,128)(2,1)S(1)}, u32[]{:S(2)}, u32[]{:S(2)}) collective-permute-start(bf16[48,4096]{1,0:T(8,128)(2,1)} %get-tuple-element.87), channel_id=1, source_target_pairs={{0,1},{1,0},{2,3},{3,2},{4,5},{5,4},{6,7},{7,6},{8,9},{9,8},{10,11... | collective-permute-start | bytes 1179656 | tf_op jit(solution)/shard_map/ppermute | solution.py:21
  11.4 30.1 %collective-permute-start.1 = (bf16[48,4096]{1,0:T(8,128)(2,1)}, bf16[48,4096]{1,0:T(8,128)(2,1)S(1)}, u32[]{:S(2)}, u32[]{:S(2)}) collective-permute-start(bf16[48,4096]{1,0:T(8,128)(2,1)} %get-tuple-element.86), channel_id=1, source_target_pairs={{0,2},{1,3},{2,0},{3,1},{4,6},{5,7},{6,4},{7,5},{8,10},{9,11},{10,... | collective-permute-start | bytes 1179656 | tf_op jit(solution)/shard_map/ppermute | solution.py:21
  14.8 28.3 %collective-permute-start.2 = (bf16[48,4096]{1,0:T(8,128)(2,1)}, bf16[48,4096]{1,0:T(8,128)(2,1)S(1)}, u32[]{:S(2)}, u32[]{:S(2)}) collective-permute-start(bf16[48,4096]{1,0:T(8,128)(2,1)} %get-tuple-element.85), channel_id=1, source_target_pairs={{0,3},{1,2},{2,1},{3,0},{4,7},{5,6},{6,5},{7,4},{8,11},{9,10},{10,... | collective-permute-start | bytes 1179656 | tf_op jit(solution)/shard_map/ppermute | solution.py:21
  28.4 19.8 %collective-permute-start.6 = (bf16[192,1024]{1,0:T(8,128)(2,1)S(1)}, bf16[192,1024]{1,0:T(8,128)(2,1)S(1)}, u32[]{:S(2)}, u32[]{:S(2)}) collective-permute-start(bf16[192,1024]{1,0:T(8,128)(2,1)S(1)} %get-tuple-element.46), channel_id=1, source_target_pairs={{0,16},{16,32},{32,48},{48,0},{1,17},{17,33},{33,49},{49,1},{2,18}... | collective-permute-start | bytes 1179656 | tf_op jit(solution)/shard_map/ppermute | solution.py:27
  29.9 20.3 %collective-permute-start.7 = (bf16[192,1024]{1,0:T(8,128)(2,1)S(1)}, bf16[192,1024]{1,0:T(8,128)(2,1)S(1)}, u32[]{:S(2)}, u32[]{:S(2)}) collective-permute-start(bf16[192,1024]{1,0:T(8,128)(2,1)S(1)} %get-tuple-element.47), channel_id=1, source_target_pairs={{0,32},{16,48},{32,0},{48,16},{1,33},{17,49},{33,1},{49,17},{2,34}... | collective-permute-start | bytes 1179656 | tf_op jit(solution)/shard_map/ppermute | solution.py:27
  32.6 17.6 %collective-permute-start.8 = (bf16[192,1024]{1,0:T(8,128)(2,1)S(1)}, bf16[192,1024]{1,0:T(8,128)(2,1)S(1)}, u32[]{:S(2)}, u32[]{:S(2)}) collective-permute-start(bf16[192,1024]{1,0:T(8,128)(2,1)S(1)} %get-tuple-element.48), channel_id=1, source_target_pairs={{0,48},{16,0},{32,16},{48,32},{1,49},{17,1},{33,17},{49,33},{2,50}... | collective-permute-start | bytes 1179656 | tf_op jit(solution)/shard_map/ppermute | solution.py:27
  52.1 49.2 %all-to-all-start = ((bf16[4,192,1792]{2,1,0:T(8,128)(2,1)}), bf16[4,192,1792]{2,1,0:T(8,128)(2,1)}, u32[]{:S(2)}, u32[]{:S(2)}) async-start(bf16[4,192,1792]{2,1,0:T(8,128)(2,1)} %get-tuple-element.64), calls=%async_computation | async-start | bytes 5505024 | tf_op jit(solution)/shard_map/all_to_all | solution.py:332
  56.7 17.3 %collective-permute-start.12 = (bf16[2,192,768]{2,1,0:T(8,128)(2,1)S(1)}, bf16[2,192,768]{2,1,0:T(8,128)(2,1)S(1)}, u32[]{:S(2)}, u32[]{:S(2)}) collective-permute-start(bf16[2,192,768]{2,1,0:T(8,128)(2,1)S(1)} %get-tuple-element.44.dact.refs_4_), channel_id=1, source_target_pairs={{0,16},{16,32},{32,48},{48,0},{1,17},{17,33},{33,49},{49,1},{2,18}... | collective-permute-start | bytes 1769480 | tf_op jit(solution)/shard_map/ppermute | solution.py:27
  58.0 28.2 %collective-permute-start.13 = (bf16[2,192,768]{2,1,0:T(8,128)(2,1)S(1)}, bf16[2,192,768]{2,1,0:T(8,128)(2,1)S(1)}, u32[]{:S(2)}, u32[]{:S(2)}) collective-permute-start(bf16[2,192,768]{2,1,0:T(8,128)(2,1)S(1)} %get-tuple-element.44.dact.refs_4_), channel_id=1, source_target_pairs={{0,32},{16,48},{32,0},{48,16},{1,33},{17,49},{33,1},{49,17},{2,34}... | collective-permute-start | bytes 1769480 | tf_op jit(solution)/shard_map/ppermute | solution.py:27
  60.4 25.9 %collective-permute-start.14 = (bf16[2,192,768]{2,1,0:T(8,128)(2,1)S(1)}, bf16[2,192,768]{2,1,0:T(8,128)(2,1)S(1)}, u32[]{:S(2)}, u32[]{:S(2)}) collective-permute-start(bf16[2,192,768]{2,1,0:T(8,128)(2,1)S(1)} %get-tuple-element.44.dact.refs_4_), channel_id=1, source_target_pairs={{0,48},{16,0},{32,16},{48,32},{1,49},{17,1},{33,17},{49,33},{2,50}... | collective-permute-start | bytes 1769480 | tf_op jit(solution)/shard_map/ppermute | solution.py:27
  62.0 24.3 %copy-start.6 = (bf16[192,1024]{1,0:T(8,128)(2,1)S(1)}, bf16[192,1024]{1,0:T(8,128)(2,1)}, u32[]{:S(2)}) copy-start(bf16[192,1024]{1,0:T(8,128)(2,1)} %copy-done.5) | copy-start | bytes 1179652
  62.0 24.3 %copy-start.8 = (bf16[192,1024]{1,0:T(8,128)(2,1)S(1)}, bf16[192,1024]{1,0:T(8,128)(2,1)}, u32[]{:S(2)}) copy-start(bf16[192,1024]{1,0:T(8,128)(2,1)} %copy-done.7) | copy-start | bytes 1179652
  62.0 24.3 %copy-start.10 = (bf16[192,1024]{1,0:T(8,128)(2,1)S(1)}, bf16[192,1024]{1,0:T(8,128)(2,1)}, u32[]{:S(2)}) copy-start(bf16[192,1024]{1,0:T(8,128)(2,1)} %copy-done.9) | copy-start | bytes 1179652
  62.0 24.3 %copy-start.22 = (bf16[192,1024]{1,0:T(8,128)(2,1)S(1)}, bf16[192,1024]{1,0:T(8,128)(2,1)}, u32[]{:S(2)}) copy-start(bf16[192,1024]{1,0:T(8,128)(2,1)} %copy-done.21) | copy-start | bytes 1179652
  70.6 15.7 %collective-permute-start.10 = (bf16[48,4096]{1,0:T(8,128)(2,1)S(1)}, bf16[48,4096]{1,0:T(8,128)(2,1)S(1)}, u32[]{:S(2)}, u32[]{:S(2)}) collective-permute-start(bf16[48,4096]{1,0:T(8,128)(2,1)S(1)} %get-tuple-element.53), channel_id=1, source_target_pairs={{0,2},{1,3},{2,0},{3,1},{4,6},{5,7},{6,4},{7,5},{8,10},{9,11},{10,... | collective-permute-start | bytes 1179656 | tf_op jit(solution)/shard_map/ppermute | solution.py:21
  94.5 11.8 %collective-permute-start.15 = (bf16[128,1536]{1,0:T(8,128)(2,1)}, bf16[128,1536]{1,0:T(8,128)(2,1)}, u32[]{:S(2)}, u32[]{:S(2)}) collective-permute-start(bf16[128,1536]{1,0:T(8,128)(2,1)} %get-tuple-element.62), channel_id=1, source_target_pairs={{0,4},{4,8},{8,12},{12,0},{1,5},{5,9},{9,13},{13,1},{2,6},{6,10},{... | collective-permute-start | bytes 1179656 | tf_op jit(solution)/shard_map/ppermute | solution.py:27
  96.2 10.2 %collective-permute-start.16 = (bf16[128,1536]{1,0:T(8,128)(2,1)}, bf16[128,1536]{1,0:T(8,128)(2,1)}, u32[]{:S(2)}, u32[]{:S(2)}) collective-permute-start(bf16[128,1536]{1,0:T(8,128)(2,1)} %get-tuple-element.63), channel_id=1, source_target_pairs={{0,12},{4,0},{8,4},{12,8},{1,13},{5,1},{9,5},{13,9},{2,14},{6,2},{... | collective-permute-start | bytes 1179656 | tf_op jit(solution)/shard_map/ppermute | solution.py:27
  97.8 16.5 %collective-permute-start.9 = (bf16[48,4096]{1,0:T(8,128)(2,1)}, bf16[48,4096]{1,0:T(8,128)(2,1)}, u32[]{:S(2)}, u32[]{:S(2)}) collective-permute-start(bf16[48,4096]{1,0:T(8,128)(2,1)} %get-tuple-element.52), channel_id=1, source_target_pairs={{0,1},{1,0},{2,3},{3,2},{4,5},{5,4},{6,7},{7,6},{8,9},{9,8},{10,11... | collective-permute-start | bytes 1179656 | tf_op jit(solution)/shard_map/ppermute | solution.py:21
  97.8 18.9 %collective-permute-start.11 = (bf16[48,4096]{1,0:T(8,128)(2,1)}, bf16[48,4096]{1,0:T(8,128)(2,1)}, u32[]{:S(2)}, u32[]{:S(2)}) collective-permute-start(bf16[48,4096]{1,0:T(8,128)(2,1)} %get-tuple-element.54), channel_id=1, source_target_pairs={{0,3},{1,2},{2,1},{3,0},{4,7},{5,6},{6,5},{7,4},{8,11},{9,10},{10,... | collective-permute-start | bytes 1179656 | tf_op jit(solution)/shard_map/ppermute | solution.py:21
  108.9 28.6 %collective-permute-start.17 = (bf16[256,1536]{1,0:T(8,128)(2,1)}, bf16[256,1536]{1,0:T(8,128)(2,1)S(1)}, u32[]{:S(2)}, u32[]{:S(2)}) collective-permute-start(bf16[256,1536]{1,0:T(8,128)(2,1)} %get-tuple-element.67), channel_id=1, source_target_pairs={{0,4},{4,8},{8,12},{12,0},{1,5},{5,9},{9,13},{13,1},{2,6},{6,10},{... | collective-permute-start | bytes 2359304 | tf_op jit(solution)/shard_map/ppermute | solution.py:27
  110.1 27.4 %collective-permute-start.18 = (bf16[256,1536]{1,0:T(8,128)(2,1)}, bf16[256,1536]{1,0:T(8,128)(2,1)}, u32[]{:S(2)}, u32[]{:S(2)}) collective-permute-start(bf16[256,1536]{1,0:T(8,128)(2,1)} %get-tuple-element.68), channel_id=1, source_target_pairs={{0,12},{4,0},{8,4},{12,8},{1,13},{5,1},{9,5},{13,9},{2,14},{6,2},{... | collective-permute-start | bytes 2359304 | tf_op jit(solution)/shard_map/ppermute | solution.py:27
  112.1 12.2 %collective-permute-start.20 = (bf16[192,1024]{1,0:T(8,128)(2,1)S(1)}, bf16[192,1024]{1,0:T(8,128)(2,1)S(1)}, u32[]{:S(2)}, u32[]{:S(2)}) collective-permute-start(bf16[192,1024]{1,0:T(8,128)(2,1)S(1)} %get-tuple-element.72), channel_id=1, source_target_pairs={{0,16},{16,32},{32,48},{48,0},{1,17},{17,33},{33,49},{49,1},{2,18}... | collective-permute-start | bytes 1179656 | tf_op jit(solution)/shard_map/ppermute | solution.py:27
  114.3 18.5 %collective-permute-start.21 = (bf16[192,1024]{1,0:T(8,128)(2,1)S(1)}, bf16[192,1024]{1,0:T(8,128)(2,1)S(1)}, u32[]{:S(2)}, u32[]{:S(2)}) collective-permute-start(bf16[192,1024]{1,0:T(8,128)(2,1)S(1)} %get-tuple-element.73), channel_id=1, source_target_pairs={{0,32},{16,48},{32,0},{48,16},{1,33},{17,49},{33,1},{49,17},{2,34}... | collective-permute-start | bytes 1179656 | tf_op jit(solution)/shard_map/ppermute | solution.py:27
  116.7 16.2 %collective-permute-start.22 = (bf16[192,1024]{1,0:T(8,128)(2,1)S(1)}, bf16[192,1024]{1,0:T(8,128)(2,1)S(1)}, u32[]{:S(2)}, u32[]{:S(2)}) collective-permute-start(bf16[192,1024]{1,0:T(8,128)(2,1)S(1)} %get-tuple-element.74), channel_id=1, source_target_pairs={{0,48},{16,0},{32,16},{48,32},{1,49},{17,1},{33,17},{49,33},{2,50}... | collective-permute-start | bytes 1179656 | tf_op jit(solution)/shard_map/ppermute | solution.py:27
  135.6 7.8 %collective-permute-start.23 = (bf16[96,1024]{1,0:T(8,128)(2,1)}, bf16[96,1024]{1,0:T(8,128)(2,1)}, u32[]{:S(2)}, u32[]{:S(2)}) collective-permute-start(bf16[96,1024]{1,0:T(8,128)(2,1)} %get-tuple-element.77), channel_id=1, source_target_pairs={{0,64},{64,0},{1,65},{65,1},{2,66},{66,2},{3,67},{67,3},{4,68},{68... | collective-permute-start | bytes 589832 | tf_op jit(solution)/shard_map/ppermute | solution.py:31
  139.0 13.7 %collective-permute-start.19 = (bf16[128,1536]{1,0:T(8,128)(2,1)S(1)}, bf16[128,1536]{1,0:T(8,128)(2,1)S(1)}, u32[]{:S(2)}, u32[]{:S(2)}) collective-permute-start(bf16[128,1536]{1,0:T(8,128)(2,1)S(1)} %get-tuple-element.70), channel_id=1, source_target_pairs={{0,64},{64,0},{1,65},{65,1},{2,66},{66,2},{3,67},{67,3},{4,68},{68... | collective-permute-start | bytes 1179656 | tf_op jit(solution)/shard_map/ppermute | solution.py:31
  144.4 5.9 %collective-permute-start.24 = (bf16[24,1024]{1,0:T(8,128)(2,1)S(1)}, bf16[24,1024]{1,0:T(8,128)(2,1)S(1)}, u32[]{:S(2)}, u32[]{:S(2)}) collective-permute-start(bf16[24,1024]{1,0:T(8,128)(2,1)S(1)} %get-tuple-element.91), channel_id=1, source_target_pairs={{0,4},{4,8},{8,12},{12,0},{1,5},{5,9},{9,13},{13,1},{2,6},{6,10},{... | collective-permute-start | bytes 147464 | tf_op jit(solution)/shard_map/ppermute | solution.py:27
  144.4 5.8 %collective-permute-start.25 = (bf16[24,1024]{1,0:T(8,128)(2,1)S(1)}, bf16[24,1024]{1,0:T(8,128)(2,1)S(1)}, u32[]{:S(2)}, u32[]{:S(2)}) collective-permute-start(bf16[24,1024]{1,0:T(8,128)(2,1)S(1)} %get-tuple-element.90), channel_id=1, source_target_pairs={{0,8},{4,12},{8,0},{12,4},{1,9},{5,13},{9,1},{13,5},{2,10},{6,14},... | collective-permute-start | bytes 147464 | tf_op jit(solution)/shard_map/ppermute | solution.py:27
  147.3 4.1 %collective-permute-start.26 = (bf16[24,1024]{1,0:T(8,128)(2,1)S(1)}, bf16[24,1024]{1,0:T(8,128)(2,1)S(1)}, u32[]{:S(2)}, u32[]{:S(2)}) collective-permute-start(bf16[24,1024]{1,0:T(8,128)(2,1)S(1)} %get-tuple-element.89), channel_id=1, source_target_pairs={{0,12},{4,0},{8,4},{12,8},{1,13},{5,1},{9,5},{13,9},{2,14},{6,2},{... | collective-permute-start | bytes 147464 | tf_op jit(solution)/shard_map/ppermute | solution.py:27
  (21 other events, 98.4 us)

commit v9 on v4

--- a/solution.py
+++ b/solution.py
@@ -265,8 +265,9 @@
     )(at, *parts, *after)
 
 
-def join_step(keep, theirs, mark, out):
-    out[...] = (keep[...] + theirs[...].astype(F32)).astype(BF)
+def join_step(at, c0, c1, c2, c3, mark, out):
+    for j, piece in enumerate((c0, c1, c2, c3)):
+        out[:, aligned(lax.rem(at[2] + 4 - j, 4), piece.shape[1])] = piece[...]
 
 
 def shards(tokens, cotangent, routes, gates, gate_up, down_proj):
@@ -377,15 +378,11 @@
     )(at, gate)
     gate_up_grad = (gate_keep + swap_w(gate_send).astype(F32)).astype(BF)
     keep, send = sum_call(at, down, [tok_mark])
-    down_grad = call(join_step, "vva", [shape(96, part)], moved=800 * part)(
-        keep, swap_w(send), mark
-    )[0].reshape(4, 24, part)
+    down_grad = (keep + swap_w(send).astype(F32)).astype(BF).reshape(4, 24, part)
     cols = [
         shift(lax.dynamic_index_in_dim(down_grad, (y + j) % 4, 0, False), "y", j) for j in range(4)
     ]
-    turned = jnp.stack(cols[::-1] + cols[::-1])
-    mine = lax.dynamic_slice_in_dim(turned, 3 - y, 4, 0)
-    down_grad = jnp.concatenate([mine[i] for i in range(4)], axis=1)
+    down_grad = call(join_step, "svvvva", [shape(24, width)])(at, *cols, mark)[0]
 
     return token_grad, gate_up_grad[None], down_grad[None]
 

time: 150 us -> 149 us (level)
  waiting for transfers between devices: 52.3 us -> 50.4 us
    ppermute x12, waiting for transfers between devices: 34.2 us -> 32.3 us  [shift(): return lax.ppermute(a, axis, [(i, (i + j) % 4) for i in range(4)])]
  transfers between devices with their start and end apart: 25 -> 25, of which waited for: 10 -> 11; matrix products, arithmetic and copies ran while one was open for 3% -> 2% of each run, Pallas kernels for 25% -> 26%
where the time goes in v9:
time: 149 us; the launch traced here: 147 us
  waiting for transfers between devices  50.4 us (34%)
  starting transfers between devices  46.2 us (31%)
  Pallas kernels  39.8 us (27%)
  local copies, waits for them, and re-layouts  5.04 us (3%)
  matrix products  2.46 us (2%)
  other arithmetic  2.22 us (1%)
    ppermute x12, waiting for transfers between devices, shift(): return lax.ppermute(a, axis, [(i, (i + j) % 4) for i in range(4)])  32.3 us
    ppermute x12, starting transfers between devices, shift(): return lax.ppermute(a, axis, [(i, (i + j) % 4) for i in range(4)])  19.4 us
    ppermute x9, starting transfers between devices, swap_expert(): return lax.ppermute(a, ('v', 'c'), [(i, i ^ k) for i in range(4)])  14.7 us
    ppermute x9, waiting for transfers between devices, swap_expert(): return lax.ppermute(a, ('v', 'c'), [(i, i ^ k) for i in range(4)])  13 us
    pallas_call x1, Pallas kernels, shards(): call(act_step, 'va', [shape(rows, inner), shape(rows, inner, dtype=F32),...  7.4 us
    pallas_call x1, Pallas kernels, shards(): call(back_step, 'vaa', [shape(CAP, width)] * 4 + [MARK], [pltpu.VMEM((n,...  6.92 us
    pallas_call x1, Pallas kernels, tile_call(): call(tile_step, 'a' * (8 + len(after)), [shape(4, 256, wide), MARK], [plt...  5.25 us
    pallas_call x1, Pallas kernels, shards(): call(dh_step, 'aaaaaaa', [shape(2, rows, inner), MARK], [pltpu.VMEM((rows...  5.09 us
  transfers between devices with their start and end apart: 25, of which 11 were waited for; matrix products, arithmetic and copies ran while one was open for 2% of the time, Pallas kernels for 26%

profile of v9, /device:TPU:0, one launch (start us, length us, event | category | flops | bytes accessed | tf_op | source)
XLA Modules:
  0.0 147.1 jit_solution(16492013938262376727)
XLA Ops:
  4.0 4.0 %collective-permute-start.4 = (bf16[48,4096]{1,0:T(8,128)(2,1)}, bf16[48,4096]{1,0:T(8,128)(2,1)}, u32[]{:S(2)}, u32[]{:S(2)}) collective-permute-start(bf16[48,4096]{1,0:T(8,128)(2,1)} %get-tuple-element.64), channel_id=1, source_target_pairs={{0,2},{1,3},{2,0},{3,1},{4,6},{5,7},{6,4},{7,5},{8,10},{9,11},{10,... | collective-permute-start | bytes 1179656 | tf_op jit(solution)/shard_map/ppermute | solution.py:21
  8.4 1.8 %fusion = bf16[192,4096]{1,0:T(8,128)(2,1)S(1)} fusion(pred[128,192]{1,0:T(32,128)(4,1)S(1)} %get-tuple-element.62, bf16[128,4096]{1,0:T(8,128)(2,1)} %param.7, f32[192]{0:T(256)S(1)} %mul.14), kind=kOutput, calls=%fused_computation.1 | convolution fusion | flops 202899456 | bytes 2646784 | tf_op jit(solution)/shard_map/dot_general | solution.py:35
  11.4 3.4 %collective-permute-start.1 = (bf16[48,4096]{1,0:T(8,128)(2,1)}, bf16[48,4096]{1,0:T(8,128)(2,1)S(1)}, u32[]{:S(2)}, u32[]{:S(2)}) collective-permute-start(bf16[48,4096]{1,0:T(8,128)(2,1)} %get-tuple-element.68), channel_id=1, source_target_pairs={{0,2},{1,3},{2,0},{3,1},{4,6},{5,7},{6,4},{7,5},{8,10},{9,11},{10,... | collective-permute-start | bytes 1179656 | tf_op jit(solution)/shard_map/ppermute | solution.py:21
  14.9 3.4 %collective-permute-done.4.x2 = bf16[48,4096]{1,0:T(8,128)(2,1)} collective-permute-done((bf16[48,4096]{1,0:T(8,128)(2,1)}, bf16[48,4096]{1,0:T(8,128)(2,1)}, u32[]{:S(2)}, u32[]{:S(2)}) %collective-permute-start.4) | collective-permute-done | bytes 393248 | tf_op jit(solution)/shard_map/ppermute | solution.py:21
  18.3 8.1 %collective-permute-done.5.x3 = bf16[48,4096]{1,0:T(8,128)(2,1)} collective-permute-done((bf16[48,4096]{1,0:T(8,128)(2,1)}, bf16[48,4096]{1,0:T(8,128)(2,1)}, u32[]{:S(2)}, u32[]{:S(2)}) %collective-permute-start.5) | collective-permute-done | bytes 393248 | tf_op jit(solution)/shard_map/ppermute | solution.py:21
  28.4 1.5 %collective-permute-start.6 = (bf16[192,1024]{1,0:T(8,128)(2,1)S(1)}, bf16[192,1024]{1,0:T(8,128)(2,1)S(1)}, u32[]{:S(2)}, u32[]{:S(2)}) collective-permute-start(bf16[192,1024]{1,0:T(8,128)(2,1)S(1)} %get-tuple-element.37), channel_id=1, source_target_pairs={{0,16},{16,32},{32,48},{48,0},{1,17},{17,33},{33,49},{49,1},{2,18}... | collective-permute-start | bytes 1179656 | tf_op jit(solution)/shard_map/ppermute | solution.py:27
  29.9 2.7 %collective-permute-start.7 = (bf16[192,1024]{1,0:T(8,128)(2,1)S(1)}, bf16[192,1024]{1,0:T(8,128)(2,1)S(1)}, u32[]{:S(2)}, u32[]{:S(2)}) collective-permute-start(bf16[192,1024]{1,0:T(8,128)(2,1)S(1)} %get-tuple-element.38), channel_id=1, source_target_pairs={{0,32},{16,48},{32,0},{48,16},{1,33},{17,49},{33,1},{49,17},{2,34}... | collective-permute-start | bytes 1179656 | tf_op jit(solution)/shard_map/ppermute | solution.py:27
  34.1 7.4 %shard_map.86 = (bf16[192,768]{1,0:T(8,128)(2,1)S(1)}, f32[192,768]{1,0:T(8,128)S(1)}, f32[192,768]{1,0:T(8,128)S(1)}) custom-call(bf16[192,4096]{1,0:T(8,128)(2,1)S(1)} %get-tuple-element.32.x, bf16[4096,1536]{1,0:T(8,128)(2,1)} %bitcast.24), custom_call_target="tpu_custom_call" | custom-call | flops 2415919104 | bytes 12582912 | tf_op jit(solution)/shard_map/pallas_call | solution.py:302
  41.5 1.6 %collective-permute-done.2.g3 = bf16[48,4096]{1,0:T(8,128)(2,1)S(1)} collective-permute-done((bf16[48,4096]{1,0:T(8,128)(2,1)}, bf16[48,4096]{1,0:T(8,128)(2,1)S(1)}, u32[]{:S(2)}, u32[]{:S(2)}) %collective-permute-start.2) | collective-permute-done | bytes 393248 | tf_op jit(solution)/shard_map/ppermute | solution.py:21
  43.1 5.1 %shard_map.87 = (bf16[2,192,768]{2,1,0:T(8,128)(2,1)S(1)}, f32[8,128]{1,0:T(8,128)S(1)}) custom-call(bf16[48,4096]{1,0:T(8,128)(2,1)S(1)} %get-tuple-element.70.g0, bf16[48,4096]{1,0:T(8,128)(2,1)S(1)} %collective-permute-done.g1, bf16[48,4096]{1,0:T(8,128)(2,1)S(1)} %collective-permute-done.1.g2, bf16[48,4096]{1,0:T(8,128)(2,1)S(1)} %collective-permute-done.2.g3, ...), custom_call_target="tpu_custom_call" | custom-call | flops 1207959552 | bytes 6291456 | tf_op jit(solution)/shard_map/pallas_call | solution.py:312
  48.2 2.1 %collective-permute-done.7.rest_1_.refs_2_ = bf16[192,1024]{1,0:T(8,128)(2,1)S(1)} collective-permute-done((bf16[192,1024]{1,0:T(8,128)(2,1)S(1)}, bf16[192,1024]{1,0:T(8,128)(2,1)S(1)}, u32[]{:S(2)}, u32[]{:S(2)}) %collective-permute-start.7) | collective-permute-done | bytes 393248 | tf_op jit(solution)/shard_map/ppermute | solution.py:27
  50.3 1.8 %shard_map.88 = (bf16[4,192,1792]{2,1,0:T(8,128)(2,1)}, f32[8,128]{1,0:T(8,128)S(1)}) custom-call(bf16[48,4096]{1,0:T(8,128)(2,1)S(1)} %get-tuple-element.70.g0, bf16[48,4096]{1,0:T(8,128)(2,1)S(1)} %collective-permute-done.g1, bf16[48,4096]{1,0:T(8,128)(2,1)S(1)} %collective-permute-done.1.g2, bf16[48,4096]{1,0:T(8,128)(2,1)S(1)} %collective-permute-done.2.g3, ...), custom_call_target="tpu_custom_call" | custom-call | bytes 3145728 | tf_op jit(solution)/shard_map/pallas_call | solution.py:328
  52.1 4.6 %all-to-all-start.1 = ((bf16[4,192,1792]{2,1,0:T(8,128)(2,1)}), bf16[4,192,1792]{2,1,0:T(8,128)(2,1)}, u32[]{:S(2)}, u32[]{:S(2)}) async-start(bf16[4,192,1792]{2,1,0:T(8,128)(2,1)} %get-tuple-element.51), calls=%async_computation.1 | async-start | bytes 5505024 | tf_op jit(solution)/shard_map/all_to_all | solution.py:336
  58.1 2.4 %collective-permute-start.13 = (bf16[2,192,768]{2,1,0:T(8,128)(2,1)S(1)}, bf16[2,192,768]{2,1,0:T(8,128)(2,1)S(1)}, u32[]{:S(2)}, u32[]{:S(2)}) collective-permute-start(bf16[2,192,768]{2,1,0:T(8,128)(2,1)S(1)} %get-tuple-element.35.dact.refs_4_), channel_id=1, source_target_pairs={{0,32},{16,48},{32,0},{48,16},{1,33},{17,49},{33,1},{49,17},{2,34}... | collective-permute-start | bytes 1769480 | tf_op jit(solution)/shard_map/ppermute | solution.py:27
  60.4 1.6 %collective-permute-start.14 = (bf16[2,192,768]{2,1,0:T(8,128)(2,1)S(1)}, bf16[2,192,768]{2,1,0:T(8,128)(2,1)S(1)}, u32[]{:S(2)}, u32[]{:S(2)}) collective-permute-start(bf16[2,192,768]{2,1,0:T(8,128)(2,1)S(1)} %get-tuple-element.35.dact.refs_4_), channel_id=1, source_target_pairs={{0,48},{16,0},{32,16},{48,32},{1,49},{17,1},{33,17},{49,33},{2,50}... | collective-permute-start | bytes 1769480 | tf_op jit(solution)/shard_map/ppermute | solution.py:27
  62.0 6.9 %shard_map.89 = (bf16[48,4096]{1,0:T(8,128)(2,1)S(1)}, bf16[48,4096]{1,0:T(8,128)(2,1)S(1)}, bf16[48,4096]{1,0:T(8,128)(2,1)S(1)}, bf16[48,4096]{1,0:T(8,128)(2,1)S(1)}, f32[8,128]{1,0:T(8,128)}) custom-call(bf16[2,192,768]{2,1,0:T(8,128)(2,1)S(1)} %get-tuple-element.35.dact.refs_4_, bf16[4096,1536]{1,0:T(8,128)(2,1)} %bitcast.25, ...), custom_call_target="tpu_custom_call" | custom-call | flops 2415919104 | bytes 12582912 | tf_op jit(solution)/shard_map/pallas_call | solution.py:338
  70.5 3.4 %collective-permute-start.10 = (bf16[48,4096]{1,0:T(8,128)(2,1)S(1)}, bf16[48,4096]{1,0:T(8,128)(2,1)S(1)}, u32[]{:S(2)}, u32[]{:S(2)}) collective-permute-start(bf16[48,4096]{1,0:T(8,128)(2,1)S(1)} %get-tuple-element.44), channel_id=1, source_target_pairs={{0,2},{1,3},{2,0},{3,1},{4,6},{5,7},{6,4},{7,5},{8,10},{9,11},{10,... | collective-permute-start | bytes 1179656 | tf_op jit(solution)/shard_map/ppermute | solution.py:21
  73.9 12.4 %collective-permute-done.13.refs_6_ = bf16[2,192,768]{2,1,0:T(8,128)(2,1)S(1)} collective-permute-done((bf16[2,192,768]{2,1,0:T(8,128)(2,1)S(1)}, bf16[2,192,768]{2,1,0:T(8,128)(2,1)S(1)}, u32[]{:S(2)}, u32[]{:S(2)}) %collective-permute-start.13) | collective-permute-done | bytes 589856 | tf_op jit(solution)/shard_map/ppermute | solution.py:27
  86.4 5.3 %shard_map.91 = (bf16[4,256,1536]{2,1,0:T(8,128)(2,1)}, f32[8,128]{1,0:T(8,128)S(1)}) custom-call(bf16[192,1024]{1,0:T(8,128)(2,1)S(1)} %copy-done.8, bf16[192,1024]{1,0:T(8,128)(2,1)S(1)} %copy-done.2, bf16[192,1024]{1,0:T(8,128)(2,1)S(1)} %copy-done.4, bf16[192,1024]{1,0:T(8,128)(2,1)S(1)} %copy-done.6, ...), custom_call_target="tpu_custom_call" | custom-call | flops 2415919104 | bytes 3932160 | tf_op jit(solution)/shard_map/pallas_call | solution.py:192
  91.7 4.8 %all-to-all-start = ((bf16[4,256,1536]{2,1,0:T(8,128)(2,1)}), bf16[4,256,1536]{2,1,0:T(8,128)(2,1)}, u32[]{:S(2)}, u32[]{:S(2)}) async-start(bf16[4,256,1536]{2,1,0:T(8,128)(2,1)} %get-tuple-element.48), calls=%async_computation | async-start | bytes 6291456 | tf_op jit(solution)/shard_map/all_to_all | solution.py:349
  96.5 3.6 %collective-permute-start.11 = (bf16[48,4096]{1,0:T(8,128)(2,1)S(1)}, bf16[48,4096]{1,0:T(8,128)(2,1)S(1)}, u32[]{:S(2)}, u32[]{:S(2)}) collective-permute-start(bf16[48,4096]{1,0:T(8,128)(2,1)S(1)} %copy-done.10), channel_id=1, source_target_pairs={{0,3},{1,2},{2,1},{3,0},{4,7},{5,6},{6,5},{7,4},{8,11},{9,10},{10,... | collective-permute-start | bytes 1179656 | tf_op jit(solution)/shard_map/ppermute | solution.py:21
  100.1 4.5 %shard_map.93 = (f32[192,1024]{1,0:T(8,128)S(1)}, bf16[192,1024]{1,0:T(8,128)(2,1)S(1)}, bf16[192,1024]{1,0:T(8,128)(2,1)S(1)}, bf16[192,1024]{1,0:T(8,128)(2,1)S(1)}, f32[8,128]{1,0:T(8,128)}) custom-call(s32[4]{0:T(128)S(1)} %pad_add_fusion.at, bf16[4,192,1792]{2,1,0:T(8,128)(2,1)} %all-to-all-done.1.both, f32[8,128]{1,0:T(8,128)S(1)} %get-tuple-element.52.rest_0_), custom_call_target="tpu_custom_call" | custom-call | flops 1207959552 | bytes 2752512 | tf_op jit(solution)/shard_map/pallas_call | solution.py:350
  104.6 1.7 %collective-permute-start.16 = (bf16[192,1024]{1,0:T(8,128)(2,1)S(1)}, bf16[192,1024]{1,0:T(8,128)(2,1)S(1)}, u32[]{:S(2)}, u32[]{:S(2)}) collective-permute-start(bf16[192,1024]{1,0:T(8,128)(2,1)S(1)} %get-tuple-element.54), channel_id=1, source_target_pairs={{0,16},{16,32},{32,48},{48,0},{1,17},{17,33},{33,49},{49,1},{2,18}... | collective-permute-start | bytes 1179656 | tf_op jit(solution)/shard_map/ppermute | solution.py:27
  106.3 2.4 %collective-permute-start.17 = (bf16[192,1024]{1,0:T(8,128)(2,1)S(1)}, bf16[192,1024]{1,0:T(8,128)(2,1)S(1)}, u32[]{:S(2)}, u32[]{:S(2)}) collective-permute-start(bf16[192,1024]{1,0:T(8,128)(2,1)S(1)} %get-tuple-element.55), channel_id=1, source_target_pairs={{0,32},{16,48},{32,0},{48,16},{1,33},{17,49},{33,1},{49,17},{2,34}... | collective-permute-start | bytes 1179656 | tf_op jit(solution)/shard_map/ppermute | solution.py:27
  109.6 2.2 %shard_map.90 = (bf16[128,4096]{1,0:T(8,128)(2,1)}, f32[8,128]{1,0:T(8,128)S(1)}) custom-call(bf16[128,192]{1,0:T(8,128)(2,1)S(1)} %get-tuple-element.61.mask, bf16[48,4096]{1,0:T(8,128)(2,1)S(1)} %get-tuple-element.42.a0, bf16[48,4096]{1,0:T(8,128)(2,1)S(1)} %collective-permute-done.9.a1, bf16[48,4096]{1,0:T(8,128)(2,1)S(1)} %collective-permute-done.10.a2.refs_8_, ...), custom_call_target="tpu_custom_call" | custom-call | tf_op jit(solution)/shard_map/pallas_call | solution.py:365
  111.8 5.2 %collective-permute-done.16.r1 = bf16[192,1024]{1,0:T(8,128)(2,1)S(1)} collective-permute-done((bf16[192,1024]{1,0:T(8,128)(2,1)S(1)}, bf16[192,1024]{1,0:T(8,128)(2,1)S(1)}, u32[]{:S(2)}, u32[]{:S(2)}) %collective-permute-start.16) | collective-permute-done | bytes 393248 | tf_op jit(solution)/shard_map/ppermute | solution.py:27
  117.0 9.3 %collective-permute-done.17.r2 = bf16[192,1024]{1,0:T(8,128)(2,1)S(1)} collective-permute-done((bf16[192,1024]{1,0:T(8,128)(2,1)S(1)}, bf16[192,1024]{1,0:T(8,128)(2,1)S(1)}, u32[]{:S(2)}, u32[]{:S(2)}) %collective-permute-start.17) | collective-permute-done | bytes 393248 | tf_op jit(solution)/shard_map/ppermute | solution.py:27
  128.7 5.1 %all-to-all-done.parts = bf16[4,256,1536]{2,1,0:T(8,128)(2,1)} async-done(((bf16[4,256,1536]{2,1,0:T(8,128)(2,1)}), bf16[4,256,1536]{2,1,0:T(8,128)(2,1)}, u32[]{:S(2)}, u32[]{:S(2)}) %all-to-all-start) | async-done | bytes 3145760 | tf_op jit(solution)/shard_map/all_to_all | solution.py:349
  133.8 2.8 %shard_map.92 = (f32[128,1536]{1,0:T(8,128)S(1)}, bf16[128,1536]{1,0:T(8,128)(2,1)S(1)}, f32[8,128]{1,0:T(8,128)S(1)}) custom-call(s32[4]{0:T(128)S(1)} %pad_add_fusion.at, bf16[4,256,1536]{2,1,0:T(8,128)(2,1)} %all-to-all-done.parts), custom_call_target="tpu_custom_call" | custom-call | tf_op jit(solution)/shard_map/pallas_call | solution.py:372
  136.6 1.6 %collective-permute-start.15 = (bf16[128,1536]{1,0:T(8,128)(2,1)S(1)}, bf16[128,1536]{1,0:T(8,128)(2,1)S(1)}, u32[]{:S(2)}, u32[]{:S(2)}) collective-permute-start(bf16[128,1536]{1,0:T(8,128)(2,1)S(1)} %get-tuple-element.50), channel_id=1, source_target_pairs={{0,64},{64,0},{1,65},{65,1},{2,66},{66,2},{3,67},{67,3},{4,68},{68... | collective-permute-start | bytes 1179656 | tf_op jit(solution)/shard_map/ppermute | solution.py:31
  139.0 2.0 %collective-permute-start.21 = (bf16[24,1024]{1,0:T(8,128)(2,1)S(1)}, bf16[24,1024]{1,0:T(8,128)(2,1)S(1)}, u32[]{:S(2)}, u32[]{:S(2)}) collective-permute-start(bf16[24,1024]{1,0:T(8,128)(2,1)S(1)} %get-tuple-element.72), channel_id=1, source_target_pairs={{0,8},{4,12},{8,0},{12,4},{1,9},{5,13},{9,1},{13,5},{2,10},{6,14},... | collective-permute-start | bytes 147464 | tf_op jit(solution)/shard_map/ppermute | solution.py:27
  141.7 1.9 %collective-permute-done.20.c1 = bf16[24,1024]{1,0:T(8,128)(2,1)S(1)} collective-permute-done((bf16[24,1024]{1,0:T(8,128)(2,1)S(1)}, bf16[24,1024]{1,0:T(8,128)(2,1)S(1)}, u32[]{:S(2)}, u32[]{:S(2)}) %collective-permute-start.20) | collective-permute-done | bytes 49184 | tf_op jit(solution)/shard_map/ppermute | solution.py:27
  (84 shorter events, 19.9 us)
Async XLA Ops:
  2.3 5.9 %copy-start.13 = (s32[128,8]{0,1:T(8,128)S(1)}, s32[128,8]{0,1:T(8,128)}, u32[]{:S(2)}) copy-start(s32[128,8]{0,1:T(8,128)} %param.8) | copy-start | bytes 12292
  2.3 5.8 %copy-start.14 = (f32[128,8]{0,1:T(8,128)S(1)}, f32[128,8]{0,1:T(8,128)}, u32[]{:S(2)}) copy-start(f32[128,8]{0,1:T(8,128)} %param.9) | copy-start | bytes 12292
  4.0 10.8 %collective-permute-start.3 = (bf16[48,4096]{1,0:T(8,128)(2,1)}, bf16[48,4096]{1,0:T(8,128)(2,1)S(1)}, u32[]{:S(2)}, u32[]{:S(2)}) collective-permute-start(bf16[48,4096]{1,0:T(8,128)(2,1)} %get-tuple-element.65), channel_id=1, source_target_pairs={{0,1},{1,0},{2,3},{3,2},{4,5},{5,4},{6,7},{7,6},{8,9},{9,8},{10,11... | collective-permute-start | bytes 1179656 | tf_op jit(solution)/shard_map/ppermute | solution.py:21
  4.0 14.2 %collective-permute-start.4 = (bf16[48,4096]{1,0:T(8,128)(2,1)}, bf16[48,4096]{1,0:T(8,128)(2,1)}, u32[]{:S(2)}, u32[]{:S(2)}) collective-permute-start(bf16[48,4096]{1,0:T(8,128)(2,1)} %get-tuple-element.64), channel_id=1, source_target_pairs={{0,2},{1,3},{2,0},{3,1},{4,6},{5,7},{6,4},{7,5},{8,10},{9,11},{10,... | collective-permute-start | bytes 1179656 | tf_op jit(solution)/shard_map/ppermute | solution.py:21
  8.0 18.3 %collective-permute-start.5 = (bf16[48,4096]{1,0:T(8,128)(2,1)}, bf16[48,4096]{1,0:T(8,128)(2,1)}, u32[]{:S(2)}, u32[]{:S(2)}) collective-permute-start(bf16[48,4096]{1,0:T(8,128)(2,1)} %get-tuple-element.63), channel_id=1, source_target_pairs={{0,3},{1,2},{2,1},{3,0},{4,7},{5,6},{6,5},{7,4},{8,11},{9,10},{10,... | collective-permute-start | bytes 1179656 | tf_op jit(solution)/shard_map/ppermute | solution.py:21
  11.3 21.4 %collective-permute-start = (bf16[48,4096]{1,0:T(8,128)(2,1)}, bf16[48,4096]{1,0:T(8,128)(2,1)S(1)}, u32[]{:S(2)}, u32[]{:S(2)}) collective-permute-start(bf16[48,4096]{1,0:T(8,128)(2,1)} %get-tuple-element.69), channel_id=1, source_target_pairs={{0,1},{1,0},{2,3},{3,2},{4,5},{5,4},{6,7},{7,6},{8,9},{9,8},{10,11... | collective-permute-start | bytes 1179656 | tf_op jit(solution)/shard_map/ppermute | solution.py:21
  11.4 30.1 %collective-permute-start.1 = (bf16[48,4096]{1,0:T(8,128)(2,1)}, bf16[48,4096]{1,0:T(8,128)(2,1)S(1)}, u32[]{:S(2)}, u32[]{:S(2)}) collective-permute-start(bf16[48,4096]{1,0:T(8,128)(2,1)} %get-tuple-element.68), channel_id=1, source_target_pairs={{0,2},{1,3},{2,0},{3,1},{4,6},{5,7},{6,4},{7,5},{8,10},{9,11},{10,... | collective-permute-start | bytes 1179656 | tf_op jit(solution)/shard_map/ppermute | solution.py:21
  14.8 28.3 %collective-permute-start.2 = (bf16[48,4096]{1,0:T(8,128)(2,1)}, bf16[48,4096]{1,0:T(8,128)(2,1)S(1)}, u32[]{:S(2)}, u32[]{:S(2)}) collective-permute-start(bf16[48,4096]{1,0:T(8,128)(2,1)} %get-tuple-element.67), channel_id=1, source_target_pairs={{0,3},{1,2},{2,1},{3,0},{4,7},{5,6},{6,5},{7,4},{8,11},{9,10},{10,... | collective-permute-start | bytes 1179656 | tf_op jit(solution)/shard_map/ppermute | solution.py:21
  28.4 19.8 %collective-permute-start.6 = (bf16[192,1024]{1,0:T(8,128)(2,1)S(1)}, bf16[192,1024]{1,0:T(8,128)(2,1)S(1)}, u32[]{:S(2)}, u32[]{:S(2)}) collective-permute-start(bf16[192,1024]{1,0:T(8,128)(2,1)S(1)} %get-tuple-element.37), channel_id=1, source_target_pairs={{0,16},{16,32},{32,48},{48,0},{1,17},{17,33},{33,49},{49,1},{2,18}... | collective-permute-start | bytes 1179656 | tf_op jit(solution)/shard_map/ppermute | solution.py:27
  29.9 20.3 %collective-permute-start.7 = (bf16[192,1024]{1,0:T(8,128)(2,1)S(1)}, bf16[192,1024]{1,0:T(8,128)(2,1)S(1)}, u32[]{:S(2)}, u32[]{:S(2)}) collective-permute-start(bf16[192,1024]{1,0:T(8,128)(2,1)S(1)} %get-tuple-element.38), channel_id=1, source_target_pairs={{0,32},{16,48},{32,0},{48,16},{1,33},{17,49},{33,1},{49,17},{2,34}... | collective-permute-start | bytes 1179656 | tf_op jit(solution)/shard_map/ppermute | solution.py:27
  32.7 17.6 %collective-permute-start.8 = (bf16[192,1024]{1,0:T(8,128)(2,1)S(1)}, bf16[192,1024]{1,0:T(8,128)(2,1)S(1)}, u32[]{:S(2)}, u32[]{:S(2)}) collective-permute-start(bf16[192,1024]{1,0:T(8,128)(2,1)S(1)} %get-tuple-element.39), channel_id=1, source_target_pairs={{0,48},{16,0},{32,16},{48,32},{1,49},{17,1},{33,17},{49,33},{2,50}... | collective-permute-start | bytes 1179656 | tf_op jit(solution)/shard_map/ppermute | solution.py:27
  52.1 39.5 %all-to-all-start.1 = ((bf16[4,192,1792]{2,1,0:T(8,128)(2,1)}), bf16[4,192,1792]{2,1,0:T(8,128)(2,1)}, u32[]{:S(2)}, u32[]{:S(2)}) async-start(bf16[4,192,1792]{2,1,0:T(8,128)(2,1)} %get-tuple-element.51), calls=%async_computation.1 | async-start | bytes 5505024 | tf_op jit(solution)/shard_map/all_to_all | solution.py:336
  56.7 17.2 %collective-permute-start.12 = (bf16[2,192,768]{2,1,0:T(8,128)(2,1)S(1)}, bf16[2,192,768]{2,1,0:T(8,128)(2,1)S(1)}, u32[]{:S(2)}, u32[]{:S(2)}) collective-permute-start(bf16[2,192,768]{2,1,0:T(8,128)(2,1)S(1)} %get-tuple-element.35.dact.refs_4_), channel_id=1, source_target_pairs={{0,16},{16,32},{32,48},{48,0},{1,17},{17,33},{33,49},{49,1},{2,18}... | collective-permute-start | bytes 1769480 | tf_op jit(solution)/shard_map/ppermute | solution.py:27
  58.1 28.2 %collective-permute-start.13 = (bf16[2,192,768]{2,1,0:T(8,128)(2,1)S(1)}, bf16[2,192,768]{2,1,0:T(8,128)(2,1)S(1)}, u32[]{:S(2)}, u32[]{:S(2)}) collective-permute-start(bf16[2,192,768]{2,1,0:T(8,128)(2,1)S(1)} %get-tuple-element.35.dact.refs_4_), channel_id=1, source_target_pairs={{0,32},{16,48},{32,0},{48,16},{1,33},{17,49},{33,1},{49,17},{2,34}... | collective-permute-start | bytes 1769480 | tf_op jit(solution)/shard_map/ppermute | solution.py:27
  60.4 25.9 %collective-permute-start.14 = (bf16[2,192,768]{2,1,0:T(8,128)(2,1)S(1)}, bf16[2,192,768]{2,1,0:T(8,128)(2,1)S(1)}, u32[]{:S(2)}, u32[]{:S(2)}) collective-permute-start(bf16[2,192,768]{2,1,0:T(8,128)(2,1)S(1)} %get-tuple-element.35.dact.refs_4_), channel_id=1, source_target_pairs={{0,48},{16,0},{32,16},{48,32},{1,49},{17,1},{33,17},{49,33},{2,50}... | collective-permute-start | bytes 1769480 | tf_op jit(solution)/shard_map/ppermute | solution.py:27
  62.0 24.3 %copy-start.2 = (bf16[192,1024]{1,0:T(8,128)(2,1)S(1)}, bf16[192,1024]{1,0:T(8,128)(2,1)}, u32[]{:S(2)}) copy-start(bf16[192,1024]{1,0:T(8,128)(2,1)} %copy-done.1) | copy-start | bytes 1179652
  62.0 24.3 %copy-start.4 = (bf16[192,1024]{1,0:T(8,128)(2,1)S(1)}, bf16[192,1024]{1,0:T(8,128)(2,1)}, u32[]{:S(2)}) copy-start(bf16[192,1024]{1,0:T(8,128)(2,1)} %copy-done.3) | copy-start | bytes 1179652
  62.0 24.3 %copy-start.6 = (bf16[192,1024]{1,0:T(8,128)(2,1)S(1)}, bf16[192,1024]{1,0:T(8,128)(2,1)}, u32[]{:S(2)}) copy-start(bf16[192,1024]{1,0:T(8,128)(2,1)} %copy-done.5) | copy-start | bytes 1179652
  62.0 24.3 %copy-start.8 = (bf16[192,1024]{1,0:T(8,128)(2,1)S(1)}, bf16[192,1024]{1,0:T(8,128)(2,1)}, u32[]{:S(2)}) copy-start(bf16[192,1024]{1,0:T(8,128)(2,1)} %copy-done.7) | copy-start | bytes 1179652
  70.5 15.9 %collective-permute-start.10 = (bf16[48,4096]{1,0:T(8,128)(2,1)S(1)}, bf16[48,4096]{1,0:T(8,128)(2,1)S(1)}, u32[]{:S(2)}, u32[]{:S(2)}) collective-permute-start(bf16[48,4096]{1,0:T(8,128)(2,1)S(1)} %get-tuple-element.44), channel_id=1, source_target_pairs={{0,2},{1,3},{2,0},{3,1},{4,6},{5,7},{6,4},{7,5},{8,10},{9,11},{10,... | collective-permute-start | bytes 1179656 | tf_op jit(solution)/shard_map/ppermute | solution.py:21
  91.6 4.9 %copy-start.10 = (bf16[48,4096]{1,0:T(8,128)(2,1)S(1)}, bf16[48,4096]{1,0:T(8,128)(2,1)}, u32[]{:S(2)}) copy-start(bf16[48,4096]{1,0:T(8,128)(2,1)} %copy-done.9) | copy-start | bytes 1179652
  91.7 42.1 %all-to-all-start = ((bf16[4,256,1536]{2,1,0:T(8,128)(2,1)}), bf16[4,256,1536]{2,1,0:T(8,128)(2,1)}, u32[]{:S(2)}, u32[]{:S(2)}) async-start(bf16[4,256,1536]{2,1,0:T(8,128)(2,1)} %get-tuple-element.48), calls=%async_computation | async-start | bytes 6291456 | tf_op jit(solution)/shard_map/all_to_all | solution.py:349
  96.4 13.1 %collective-permute-start.9 = (bf16[48,4096]{1,0:T(8,128)(2,1)S(1)}, bf16[48,4096]{1,0:T(8,128)(2,1)S(1)}, u32[]{:S(2)}, u32[]{:S(2)}) collective-permute-start(bf16[48,4096]{1,0:T(8,128)(2,1)S(1)} %copy-done.12), channel_id=1, source_target_pairs={{0,1},{1,0},{2,3},{3,2},{4,5},{5,4},{6,7},{7,6},{8,9},{9,8},{10,11... | collective-permute-start | bytes 1179656 | tf_op jit(solution)/shard_map/ppermute | solution.py:21
  96.5 13.0 %collective-permute-start.11 = (bf16[48,4096]{1,0:T(8,128)(2,1)S(1)}, bf16[48,4096]{1,0:T(8,128)(2,1)S(1)}, u32[]{:S(2)}, u32[]{:S(2)}) collective-permute-start(bf16[48,4096]{1,0:T(8,128)(2,1)S(1)} %copy-done.10), channel_id=1, source_target_pairs={{0,3},{1,2},{2,1},{3,0},{4,7},{5,6},{6,5},{7,4},{8,11},{9,10},{10,... | collective-permute-start | bytes 1179656 | tf_op jit(solution)/shard_map/ppermute | solution.py:21
  104.6 12.4 %collective-permute-start.16 = (bf16[192,1024]{1,0:T(8,128)(2,1)S(1)}, bf16[192,1024]{1,0:T(8,128)(2,1)S(1)}, u32[]{:S(2)}, u32[]{:S(2)}) collective-permute-start(bf16[192,1024]{1,0:T(8,128)(2,1)S(1)} %get-tuple-element.54), channel_id=1, source_target_pairs={{0,16},{16,32},{32,48},{48,0},{1,17},{17,33},{33,49},{49,1},{2,18}... | collective-permute-start | bytes 1179656 | tf_op jit(solution)/shard_map/ppermute | solution.py:27
  106.3 20.0 %collective-permute-start.17 = (bf16[192,1024]{1,0:T(8,128)(2,1)S(1)}, bf16[192,1024]{1,0:T(8,128)(2,1)S(1)}, u32[]{:S(2)}, u32[]{:S(2)}) collective-permute-start(bf16[192,1024]{1,0:T(8,128)(2,1)S(1)} %get-tuple-element.55), channel_id=1, source_target_pairs={{0,32},{16,48},{32,0},{48,16},{1,33},{17,49},{33,1},{49,17},{2,34}... | collective-permute-start | bytes 1179656 | tf_op jit(solution)/shard_map/ppermute | solution.py:27
  108.7 17.6 %collective-permute-start.18 = (bf16[192,1024]{1,0:T(8,128)(2,1)S(1)}, bf16[192,1024]{1,0:T(8,128)(2,1)S(1)}, u32[]{:S(2)}, u32[]{:S(2)}) collective-permute-start(bf16[192,1024]{1,0:T(8,128)(2,1)S(1)} %get-tuple-element.56), channel_id=1, source_target_pairs={{0,48},{16,0},{32,16},{48,32},{1,49},{17,1},{33,17},{49,33},{2,50}... | collective-permute-start | bytes 1179656 | tf_op jit(solution)/shard_map/ppermute | solution.py:27
  127.6 10.5 %collective-permute-start.19 = (bf16[96,1024]{1,0:T(8,128)(2,1)S(1)}, bf16[96,1024]{1,0:T(8,128)(2,1)S(1)}, u32[]{:S(2)}, u32[]{:S(2)}) collective-permute-start(bf16[96,1024]{1,0:T(8,128)(2,1)S(1)} %get-tuple-element.59), channel_id=1, source_target_pairs={{0,64},{64,0},{1,65},{65,1},{2,66},{66,2},{3,67},{67,3},{4,68},{68... | collective-permute-start | bytes 589832 | tf_op jit(solution)/shard_map/ppermute | solution.py:31
  136.6 9.7 %collective-permute-start.15 = (bf16[128,1536]{1,0:T(8,128)(2,1)S(1)}, bf16[128,1536]{1,0:T(8,128)(2,1)S(1)}, u32[]{:S(2)}, u32[]{:S(2)}) collective-permute-start(bf16[128,1536]{1,0:T(8,128)(2,1)S(1)} %get-tuple-element.50), channel_id=1, source_target_pairs={{0,64},{64,0},{1,65},{65,1},{2,66},{66,2},{3,67},{67,3},{4,68},{68... | collective-permute-start | bytes 1179656 | tf_op jit(solution)/shard_map/ppermute | solution.py:31
  138.2 5.4 %collective-permute-start.20 = (bf16[24,1024]{1,0:T(8,128)(2,1)S(1)}, bf16[24,1024]{1,0:T(8,128)(2,1)S(1)}, u32[]{:S(2)}, u32[]{:S(2)}) collective-permute-start(bf16[24,1024]{1,0:T(8,128)(2,1)S(1)} %get-tuple-element.73), channel_id=1, source_target_pairs={{0,4},{4,8},{8,12},{12,0},{1,5},{5,9},{9,13},{13,1},{2,6},{6,10},{... | collective-permute-start | bytes 147464 | tf_op jit(solution)/shard_map/ppermute | solution.py:27
  139.0 5.6 %collective-permute-start.21 = (bf16[24,1024]{1,0:T(8,128)(2,1)S(1)}, bf16[24,1024]{1,0:T(8,128)(2,1)S(1)}, u32[]{:S(2)}, u32[]{:S(2)}) collective-permute-start(bf16[24,1024]{1,0:T(8,128)(2,1)S(1)} %get-tuple-element.72), channel_id=1, source_target_pairs={{0,8},{4,12},{8,0},{12,4},{1,9},{5,13},{9,1},{13,5},{2,10},{6,14},... | collective-permute-start | bytes 147464 | tf_op jit(solution)/shard_map/ppermute | solution.py:27
  140.9 4.1 %collective-permute-start.22 = (bf16[24,1024]{1,0:T(8,128)(2,1)S(1)}, bf16[24,1024]{1,0:T(8,128)(2,1)S(1)}, u32[]{:S(2)}, u32[]{:S(2)}) collective-permute-start(bf16[24,1024]{1,0:T(8,128)(2,1)S(1)} %get-tuple-element.71), channel_id=1, source_target_pairs={{0,12},{4,0},{8,4},{12,8},{1,13},{5,1},{9,5},{13,9},{2,14},{6,2},{... | collective-permute-start | bytes 147464 | tf_op jit(solution)/shard_map/ppermute | solution.py:27
  (8 other events, 16.2 us)
